TPU v7x, 32 devices: a whole 2x2x4 slice. The times are simulated.
32 devices in a mesh: dp: 4 (over x, core), ctx: 8 (over z, y).
Axes of the slice: x: 2, y: 2, z: 4, core: 2. Of those that a mesh axis runs over, the one named last changes fastest.
Arguments:
- tokens: bfloat16 [16384, 1536], P(('dp', 'ctx')), may hold values from -6 to 6
- out_grad: bfloat16 [16384, 1536], P(('dp', 'ctx')), may hold values from -6 to 6
- seq_lengths: int32 [4, 3], P('dp'), may hold values from 1 to 4094, as said below
- norm_gain: bfloat16 [1536], P(('dp', 'ctx')), may hold values from 0.5 to 1.5
- in_weight: bfloat16 [1536, 6448], P(('dp', 'ctx')), may hold values from -0.15625 to 0.15625
- conv_weight: bfloat16 [4, 3328], P(None, ('dp', 'ctx')), may hold values from -3 to 3
- conv_bias: bfloat16 [3328], P(('dp', 'ctx')), may hold values from -3 to 3
- dt_bias: float32 [48], replicated, may hold values from -1 to 1
- a_log: float32 [48], replicated, as said below
- skip_gain: float32 [48], replicated, may hold values from 0.5 to 1.5
- gated_gain: bfloat16 [3072], P(('dp', 'ctx')), may hold values from 0.5 to 1.5
- out_weight: bfloat16 [3072, 1536], P(('dp', 'ctx')), may hold values from -0.109375 to 0.109375
Outputs:
- layer_out: bfloat16 [16384, 1536], P(('dp', 'ctx'))
- grad_tokens: float32 [16384, 1536], P(('dp', 'ctx'))
- grad_norm_gain: float32 [1536], P(('dp', 'ctx'))
- grad_in_weight: float32 [1536, 6448], P(('dp', 'ctx'))
- grad_conv_weight: float32 [4, 3328], P(None, ('dp', 'ctx'))
- grad_conv_bias: float32 [3328], P(('dp', 'ctx'))
- grad_dt_bias: float32 [48], replicated
- grad_a_log: float32 [48], replicated
- grad_skip_gain: float32 [48], replicated
- grad_gated_gain: float32 [3072], P(('dp', 'ctx'))
- grad_out_weight: float32 [3072, 1536], P(('dp', 'ctx'))
Inputs may be any that keep to these rules, and one draw needn't show every extreme that they name: `seq_lengths`: row g holds three document lengths that sum to 4096 (4096 here); the first and the last are 1 to 511, so the middle document of every group starts on the group's first device and ends on its last; in one group, drawn from the seed, the first and the last are both 1. `a_log`: one value a head.
All inputs are finite; a program needn't handle non-finite values.
Results may differ from a plain program's by a relative error of at most 0.0021.
The roundings to bfloat16 on the way count: a program that leaves them out, or rounds other values in their place, can miss the bound.
Values may be sent and summed in bfloat16 or wider, within the bound.
No kernel may reach another device: no remote copies, remote signals or barrier semaphores. Data moves between devices by JAX's collectives and lax.ppermute only.
A program may use at most 256 MiB of HBM per device.

v0:
```python
import jax
import jax.numpy as jnp
from jax import lax
from jax.sharding import PartitionSpec as P

HEADS = 48
HEAD_DIM = 64
STATE = 128
CONV_K = 4
SPAN = 256
INNER = 3072
CONVW = 3328


epsilon = 1e-05
highest = lax.Precision.HIGHEST


def from_behind(array, axis, by):
    peers = lax.axis_size(axis)
    pairs = [(i, i + by) for i in range(peers) if 0 <= i + by < peers]
    return lax.ppermute(array, axis, pairs)


def entering_2(part, axis, combine, identity, reverse):
    count = lax.axis_size(axis)
    place = lax.axis_index(axis)
    ahead = count - 1 - place if reverse else place
    gathered = jax.tree.map(lambda a: lax.all_gather(a, axis), part)
    state = jax.tree.map(lambda a, e: jnp.zeros_like(a) + jnp.asarray(e, a.dtype), part, identity)

    def one(lap, state):
        source = count - 1 - lap if reverse else lap
        return combine(
            state, jax.tree.map(lambda a: lax.dynamic_index_in_dim(a, source, 0, False), gathered)
        )

    return lax.fori_loop(0, ahead, one, state)


def rms_scale(values):
    return lax.rsqrt(jnp.mean(values * values, axis=-1, keepdims=True) + epsilon)


def span_step(carry_state, pieces):
    x_heads, b_rows, c_rows, steps_dt, log_decay, doc_ids, before = pieces
    row_total = doc_ids.shape[0]
    cumulative = jnp.cumsum(log_decay, axis=0).T
    ordinal = jnp.arange(row_total)
    allowed = (doc_ids[:, None] == doc_ids[None, :]) & (ordinal[:, None] >= ordinal[None, :])
    log_gaps = jnp.where(allowed[None], cumulative[:, :, None] - cumulative[:, None, :], 0.0)
    decays = jnp.where(allowed[None], jnp.exp(log_gaps), 0.0)
    scores = jnp.dot(c_rows, b_rows.T, precision=highest)
    mixing = scores[None] * decays * steps_dt.T[:, None, :]
    inside = jnp.einsum("hij,jhp->ihp", mixing, x_heads, precision=highest)
    alive_rows = (doc_ids == before).astype(jnp.float32)
    entering = jnp.exp(cumulative.T) * alive_rows[:, None]
    carry_term = (
        jnp.einsum("hpn,in->ihp", carry_state, c_rows, precision=highest) * entering[:, :, None]
    )
    tail_same = (doc_ids == doc_ids[-1]).astype(jnp.float32)
    weight_last = jnp.exp(cumulative[:, -1][None, :] - cumulative.T) * tail_same[:, None] * steps_dt
    fresh_state = jnp.einsum(
        "jhp,jn->hpn", weight_last[:, :, None] * x_heads, b_rows, precision=highest
    )
    fading = jnp.exp(cumulative[:, -1]) * alive_rows[-1]
    return (fading[:, None, None] * carry_state + fresh_state, inside + carry_term)


def combine(earlier, later_one):
    return (earlier[0] * later_one[0], later_one[0][:, None, None] * earlier[1] + later_one[1])


def contract_rows(left, right):
    return lax.dot_general(
        left, right, (((0,), (0,)), ((), ())), preferred_element_type=jnp.float32
    )


def contract_cols(left, right):
    return lax.dot_general(
        left, right, (((1,), (1,)), ((), ())), preferred_element_type=jnp.float32
    )


def document_ids(lengths, positions):
    first_end = lengths[0]
    second_end = lengths[0] + lengths[1]
    inside = (positions >= first_end).astype(jnp.int32) + (positions >= second_end).astype(
        jnp.int32
    )
    return jnp.where(positions < 0, -1, inside)


def shards(
    tokens,
    out_grad,
    seq_lengths,
    norm_gain,
    in_weight,
    conv_weight,
    conv_bias,
    dt_bias,
    a_log,
    skip_gain,
    gated_gain,
    out_weight,
):
    row_count = tokens.shape[0]
    lead_count = CONV_K - 1
    first_row = lax.axis_index("ctx") * row_count
    lengths = seq_lengths[0]
    doc_ids = document_ids(lengths, first_row + jnp.arange(row_count, dtype=jnp.int32))
    lead_docs = document_ids(
        lengths, first_row - lead_count + jnp.arange(lead_count, dtype=jnp.int32)
    )
    doc_before = document_ids(lengths, first_row - 1 + jnp.zeros((1,), jnp.int32))
    span_before = jnp.concatenate([doc_before, doc_ids[SPAN - 1 : -1 : SPAN]])
    alive_device = (doc_ids == doc_before[0]).astype(jnp.float32)
    gathered = (
        lax.all_gather(in_weight, ("dp", "ctx"), axis=0, tiled=True),
        lax.all_gather(out_weight, ("dp", "ctx"), axis=0, tiled=True),
        lax.all_gather(norm_gain, ("dp", "ctx"), axis=0, tiled=True),
        lax.all_gather(conv_weight, ("dp", "ctx"), axis=1, tiled=True),
        lax.all_gather(conv_bias, ("dp", "ctx"), axis=0, tiled=True),
        lax.all_gather(gated_gain, ("dp", "ctx"), axis=0, tiled=True),
    )
    full_in, full_out, full_gain, full_conv, full_bias, full_gated = gathered
    rows_value = tokens.astype(jnp.float32)

    def first_norm(values, gain_value):
        return values * rms_scale(values) * gain_value[None, :]

    normed, norm_back = jax.vjp(first_norm, rows_value, full_gain.astype(jnp.float32))
    normed_low = normed.astype(jnp.bfloat16)
    mixed = jnp.dot(normed_low, full_in, preferred_element_type=jnp.float32).astype(jnp.bfloat16)
    lead_rows = from_behind(mixed[row_count - lead_count :, INNER : INNER + CONVW], "ctx", 1)

    def prepare(x_part, dt_part, lead_part, weight, bias_value, dt_shift, log_rate):
        padded = jnp.concatenate([lead_part, x_part], axis=0)
        padded_docs = jnp.concatenate([lead_docs, doc_ids], axis=0)
        running = jnp.zeros_like(x_part) + bias_value[None, :]
        for offset in range(CONV_K):
            shifted = padded[offset : offset + row_count]
            same_doc = (padded_docs[offset : offset + row_count] == doc_ids).astype(jnp.float32)
            running = running + shifted * weight[offset][None, :] * same_doc[:, None]
        active = jax.nn.silu(running)
        x_heads = active[:, :INNER].reshape(row_count, HEADS, HEAD_DIM)
        b_rows = active[:, INNER : INNER + STATE]
        c_rows = active[:, INNER + STATE :]
        steps_dt = jax.nn.softplus(dt_part + dt_shift[None, :])
        log_decay = -steps_dt * jnp.exp(log_rate)[None, :]
        entering = jnp.exp(jnp.cumsum(log_decay, axis=0)) * alive_device[:, None]
        return (x_heads, b_rows, c_rows, steps_dt, log_decay, entering)

    prepared, prepare_back = jax.vjp(
        prepare,
        mixed[:, INNER : INNER + CONVW].astype(jnp.float32),
        mixed[:, INNER + CONVW :].astype(jnp.float32),
        lead_rows.astype(jnp.float32),
        full_conv.astype(jnp.float32),
        full_bias.astype(jnp.float32),
        dt_bias,
        a_log,
    )
    x_heads, b_rows, c_rows, steps_dt, log_decay, entering = prepared

    def local_scan(head_values, b_values, c_values, dt_values, decay_values):
        blocks = row_count // SPAN
        pieces = (
            head_values.reshape(blocks, SPAN, HEADS, HEAD_DIM),
            b_values.reshape(blocks, SPAN, STATE),
            c_values.reshape(blocks, SPAN, STATE),
            dt_values.reshape(blocks, SPAN, HEADS),
            decay_values.reshape(blocks, SPAN, HEADS),
            doc_ids.reshape(blocks, SPAN),
            span_before,
        )
        start_state = jnp.zeros((HEADS, HEAD_DIM, STATE), jnp.float32)
        last_state, outputs = lax.scan(jax.checkpoint(span_step), start_state, pieces)
        return (outputs.reshape(row_count, HEADS, HEAD_DIM), last_state)

    (local_y, local_state), scan_back = jax.vjp(
        local_scan, x_heads, b_rows, c_rows, steps_dt, log_decay
    )
    device_decay = entering[row_count - 1]
    identity = (jnp.ones((HEADS,), jnp.float32), jnp.zeros((HEADS, HEAD_DIM, STATE), jnp.float32))
    state_in = entering_2((device_decay, local_state), "ctx", combine, identity, False)[1]

    def finish(
        local_part,
        head_values,
        c_values,
        enter_values,
        z_values,
        skip_value,
        gain_value,
        state_value,
    ):
        carry_term = (
            jnp.einsum("hpn,in->ihp", state_value, c_values, precision=highest)
            * enter_values[:, :, None]
        )
        y_heads = local_part + carry_term + skip_value[None, :, None] * head_values
        gated = y_heads.reshape(row_count, INNER) * jax.nn.silu(z_values)
        return gated * rms_scale(gated) * gain_value[None, :]

    final, finish_back = jax.vjp(
        finish,
        local_y,
        x_heads,
        c_rows,
        entering,
        mixed[:, :INNER].astype(jnp.float32),
        skip_gain,
        full_gated.astype(jnp.float32),
        state_in,
    )
    final_low = final.astype(jnp.bfloat16)
    layer_out = (
        rows_value + jnp.dot(final_low, full_out, preferred_element_type=jnp.float32)
    ).astype(jnp.bfloat16)
    again = (
        lax.all_gather(in_weight, ("dp", "ctx"), axis=0, tiled=True),
        lax.all_gather(out_weight, ("dp", "ctx"), axis=0, tiled=True),
        lax.all_gather(norm_gain, ("dp", "ctx"), axis=0, tiled=True),
        lax.all_gather(conv_weight, ("dp", "ctx"), axis=1, tiled=True),
        lax.all_gather(conv_bias, ("dp", "ctx"), axis=0, tiled=True),
        lax.all_gather(gated_gain, ("dp", "ctx"), axis=0, tiled=True),
    )
    back_in = again[0]
    back_out = again[1]
    grad_out_weight = contract_rows(final_low, out_grad)
    d_final = contract_cols(out_grad, back_out)
    d_local, d_heads_one, d_c_one, d_entering, d_z, d_skip, d_gated, d_state_in = finish_back(
        d_final
    )
    carried = entering_2((device_decay, d_state_in), "ctx", combine, identity, True)[1]
    d_decay = jnp.sum(carried * state_in, axis=(1, 2))
    d_heads_two, d_b_rows, d_c_two, d_steps, d_log_decay = scan_back((d_local, carried))
    d_entering = d_entering.at[row_count - 1].add(d_decay)
    d_x_part, d_dt_part, d_lead, d_conv, d_bias, d_dt_shift, d_log_rate = prepare_back(
        (d_heads_one + d_heads_two, d_b_rows, d_c_one + d_c_two, d_steps, d_log_decay, d_entering)
    )
    d_returned = from_behind(d_lead.astype(jnp.bfloat16), "ctx", -1).astype(d_lead.dtype)
    d_x_part = d_x_part.at[row_count - lead_count :].add(d_returned)
    d_mixed = jnp.concatenate([d_z, d_x_part, d_dt_part], axis=1).astype(jnp.bfloat16)
    grad_in_weight = contract_rows(normed_low, d_mixed)
    d_normed = contract_cols(d_mixed, back_in)
    d_rows, d_gain = norm_back(d_normed)
    grad_tokens = out_grad.astype(jnp.float32) + d_rows
    summed = (
        lax.psum_scatter(grad_in_weight, ("dp", "ctx"), scatter_dimension=0, tiled=True),
        lax.psum_scatter(grad_out_weight, ("dp", "ctx"), scatter_dimension=0, tiled=True),
        lax.psum_scatter(d_gain, ("dp", "ctx"), scatter_dimension=0, tiled=True),
        lax.psum_scatter(d_conv, ("dp", "ctx"), scatter_dimension=1, tiled=True),
        lax.psum_scatter(d_bias, ("dp", "ctx"), scatter_dimension=0, tiled=True),
        lax.psum_scatter(d_gated, ("dp", "ctx"), scatter_dimension=0, tiled=True),
    )
    sum_in, sum_out, sum_gain, sum_conv, sum_bias, sum_gated = summed
    head_sums = lax.psum((d_dt_shift, d_log_rate, d_skip), ("dp", "ctx"))
    return (
        layer_out,
        grad_tokens,
        sum_gain,
        sum_in,
        sum_conv,
        sum_bias,
        head_sums[0],
        head_sums[1],
        head_sums[2],
        sum_gated,
        sum_out,
    )


def solution(mesh):
    in_specs = (
        P(("dp", "ctx"), None),
        P(("dp", "ctx"), None),
        P("dp", None),
        P(("dp", "ctx")),
        P(("dp", "ctx"), None),
        P(None, ("dp", "ctx")),
        P(("dp", "ctx")),
        P(),
        P(),
        P(),
        P(("dp", "ctx")),
        P(("dp", "ctx"), None),
    )
    out_specs = (
        P(("dp", "ctx"), None),
        P(("dp", "ctx"), None),
        P(("dp", "ctx")),
        P(("dp", "ctx"), None),
        P(None, ("dp", "ctx")),
        P(("dp", "ctx")),
        P(),
        P(),
        P(),
        P(("dp", "ctx")),
        P(("dp", "ctx"), None),
    )
    return jax.shard_map(shards, mesh=mesh, in_specs=in_specs, out_specs=out_specs, check_vma=False)
```

profile of v0, /device:TPU:0, one launch (start us, length us, event | category | flops | bytes accessed | tf_op | source)
XLA Modules:
  0.0 2143.8 jit_solution(14149943516219043199)
XLA Ops:
  15.7 43.9 %all-reduce.21 = (bf16[1536]{0:T(1024)(128)(2,1)S(1)}, bf16[3328]{0:T(1024)(128)(2,1)S(1)}, bf16[3072]{0:T(1024)(128)(2,1)}) all-reduce(bf16[1536]{0:T(1024)(128)(2,1)S(1)} %dynamic-update-slice.6, bf16[3328]{0:T(1024)(128)(2,1)S(1)} %dynamic-update-slice.7, ...), channel_id=1, replica_groups=mesh['dp'=4,'ctx'=8] {'dp','ctx'}, use_global_device_ids=true, to_apply=%add.13 | all-reduce | flops 7936 | bytes 31744
  59.6 67.4 %all-gather.2 = bf16[32,104,4]{1,2,0:T(4,128)(2,1)S(1)} all-gather(bf16[1,104,4]{1,2,0:T(4,128)(2,1)} %bitcast.517), channel_id=1, replica_groups=mesh['dp'=4,'ctx'=8] {'dp','ctx'}, dimensions={0}, use_global_device_ids=true | all-gather | bytes 27456 | tf_op jit(solution)/shard_map/all_gather | solution.py:124
  132.5 12.8 all-gather.9.cloned.1.call-done
  145.3 17.6 convolution_convert_fusion
  164.4 5.7 slice_convert_fusion
  176.5 20.0 fusion.102
  201.7 8.3 reshape.578
  210.0 6.4 copy.280
  216.3 5.7 broadcast.352.clone2
  222.1 211.7 %while.72 = (s32[]{:T(128)}, f32[48,64,128]{2,1,0:T(8,128)S(1)}, f32[2,256,48,64]{1,0,3,2:T(2,128)}, f32[2,48,64,128]{3,2,1,0:T(8,128)}, f32[2,256,48]{1,2,0:T(8...) while((s32[]{:T(128)}, f32[48,64,128]{2,1,0:T(8,128)S(1)}, ...), condition=%wide.region_4.5_spmd.clone, body=%wide.region_1.4_spmd.clone.sunk | while | flops 4954399744 | bytes 38354684 | solution.py:180
  229.3 16.2 fusion.268
  253.2 63.6 %dynamic_update_slice.80 = f32[2,256,48,64]{1,0,3,2:T(2,128)} dynamic-update-slice(f32[2,256,48,64]{1,0,3,2:T(2,128)} %get-tuple-element.1315, f32[1,256,48,64]{1,0,3,2:T(1,128)} %copy.450, s32[]{:T(128)S(6)} %copy.465, s32[]{:T(128)} %constant.244.clone.1..sunk.3, s32[]{:T(128)} %constant.244.clone.1..sunk.3, s32[]{:T(128)} %constant.244.clone.1..sunk.3) | dynamic-update-slice | bytes 6291460 | tf_op jit(solution)/shard_map/jvp()/while/body/jit(dynamic_update_index_in_dim)/dynamic_update_slice | solution.py:180
  318.0 5.1 multiply_add_fusion.11
  330.4 16.2 fusion.268
  354.3 63.6 %dynamic_update_slice.80 = f32[2,256,48,64]{1,0,3,2:T(2,128)} dynamic-update-slice(f32[2,256,48,64]{1,0,3,2:T(2,128)} %get-tuple-element.1315, f32[1,256,48,64]{1,0,3,2:T(1,128)} %copy.450, s32[]{:T(128)S(6)} %copy.465, s32[]{:T(128)} %constant.244.clone.1..sunk.3, s32[]{:T(128)} %constant.244.clone.1..sunk.3, s32[]{:T(128)} %constant.244.clone.1..sunk.3) | dynamic-update-slice | bytes 6291460 | tf_op jit(solution)/shard_map/jvp()/while/body/jit(dynamic_update_index_in_dim)/dynamic_update_slice | solution.py:180
  419.1 5.1 multiply_add_fusion.11
  438.2 18.4 all-gather.3
  456.5 9.0 reshape.581
  465.5 145.1 %all-gather.13.cloned.1.call-done = f32[384,64,128]{2,1,0:T(8,128)} async-done(((f32[48,64,128]{2,1,0:T(8,128)}), f32[384,64,128]{2,1,0:T(8,128)}) %all-gather.13.cloned.1.call-update) | async-done | bytes 12582928 | tf_op jit(solution)/shard_map/all_gather | solution.py:29
  610.8 8.1 fusion.135
  619.0 12.4 multiply_add_fusion.4
  631.3 6.6 multiply_reduce_fusion.13
  637.9 55.8 %all-gather.11.cloned.1.call-done = bf16[3072,1536]{1,0:T(8,128)(2,1)} async-done(((bf16[96,1536]{1,0:T(8,128)(2,1)}), bf16[3072,1536]{1,0:T(8,128)(2,1)}) %all-gather.11.cloned.1.call-update) | async-done | bytes 9437200 | tf_op jit(solution)/shard_map/all_gather | solution.py:122
  693.8 11.6 multiply_reduce_fusion.9
  705.4 8.5 multiply_reduce_fusion.10
  716.5 7.2 fusion.109
  724.6 8.5 reshape.587
  733.8 6.4 multiply_reduce_fusion.11
  740.2 158.8 %all-gather.15.cloned.1.call-done = f32[384,64,128]{2,1,0:T(8,128)} async-done(((f32[48,64,128]{2,1,0:T(8,128)}), f32[384,64,128]{2,1,0:T(8,128)}) %all-gather.15.cloned.1.call-update) | async-done | bytes 12582928 | tf_op jit(solution)/shard_map/all_gather | solution.py:29
  899.1 12.3 while.70
  912.4 5.0 reduce-window.80
  920.9 5.6 broadcast.352.clone
  926.6 389.0 %while.71 = (s32[]{:T(128)}, f32[48,64,128]{2,1,0:T(8,128)S(1)}, f32[2,256,48,64]{1,0,3,2:T(2,128)}, f32[2,256,128]{2,1,0:T(8,128)}, f32[2,256,128]{2,1,0:T(8,12...) while((s32[]{:T(128)}, f32[48,64,128]{2,1,0:T(8,128)S(1)}, ...), condition=%wide.region_26.27_spmd, body=%wide.region_13.26_spmd.sunk | while | flops 11248780288 | bytes 132763392 | solution.py:180
  934.3 6.1 constant_dynamic-slice_fusion.11
  963.8 22.7 %fusion.250 = (f32[48,256]{1,0:T(8,128)}, f32[48,256]{1,0:T(8,128)}, f32[48,256]{1,0:T(8,128)}, f32[256,256]{1,0:T(8,128)}) fusion(f32[48,256]{1,0:T(8,128)} %copy.432, f32[48,256]{1,0:T(8,128)} %copy_bitcast_fusion.16, f32[256,256]{1,0:T(8,128)S(1)} %fusion.248, pred[256,256]{1,0:T(8,128)(4,1)} %fusion.249, ...), kind=kOutput, calls=%fused_computation.14.clone.1 | convolution fusion | flops 2463002624 | bytes 7127040 | tf_op jit(solution)/shard_map/transpose(jvp())/while/body/eval_jaxpr/checkpoint/hij,jhp->ihp/dot_general | solution.py:55
  991.1 7.2 multiply_reduce_fusion.21
  1007.0 6.5 fusion.256
  1020.5 7.4 fusion.254
  1027.9 13.4 fusion.253
  1041.4 5.2 multiply_add_fusion.10
  1047.9 4.9 copy.440
  1054.0 63.6 %dynamic_update_slice.77 = f32[2,256,48,64]{1,0,3,2:T(2,128)} dynamic-update-slice(f32[2,256,48,64]{1,0,3,2:T(2,128)} %get-tuple-element.1415, f32[1,256,48,64]{1,0,3,2:T(1,128)} %copy.440, s32[]{:T(128)S(6)} %sub.271, s32[]{:T(128)} %constant.244.clone.1..sunk.2, s32[]{:T(128)} %constant.244.clone.1..sunk.2, s32[]{:T(128)} %constant.244.clone.1..sunk.2) | dynamic-update-slice | bytes 6291460 | tf_op jit(solution)/shard_map/transpose(jvp())/while/body/jit(dynamic_update_index_in_dim)/dynamic_update_slice | solution.py:180
  1125.2 6.1 constant_dynamic-slice_fusion.11
  1154.7 22.8 %fusion.250 = (f32[48,256]{1,0:T(8,128)}, f32[48,256]{1,0:T(8,128)}, f32[48,256]{1,0:T(8,128)}, f32[256,256]{1,0:T(8,128)}) fusion(f32[48,256]{1,0:T(8,128)} %copy.432, f32[48,256]{1,0:T(8,128)} %copy_bitcast_fusion.16, f32[256,256]{1,0:T(8,128)S(1)} %fusion.248, pred[256,256]{1,0:T(8,128)(4,1)} %fusion.249, ...), kind=kOutput, calls=%fused_computation.14.clone.1 | convolution fusion | flops 2463002624 | bytes 7127040 | tf_op jit(solution)/shard_map/transpose(jvp())/while/body/eval_jaxpr/checkpoint/hij,jhp->ihp/dot_general | solution.py:55
  1182.1 7.2 multiply_reduce_fusion.21
  1197.9 6.5 fusion.256
  1211.6 7.4 fusion.254
  1219.0 13.1 fusion.253
  1232.2 5.2 multiply_add_fusion.10
  1238.8 4.9 copy.440
  1244.9 63.6 %dynamic_update_slice.77 = f32[2,256,48,64]{1,0,3,2:T(2,128)} dynamic-update-slice(f32[2,256,48,64]{1,0,3,2:T(2,128)} %get-tuple-element.1415, f32[1,256,48,64]{1,0,3,2:T(1,128)} %copy.440, s32[]{:T(128)S(6)} %sub.271, s32[]{:T(128)} %constant.244.clone.1..sunk.2, s32[]{:T(128)} %constant.244.clone.1..sunk.2, s32[]{:T(128)} %constant.244.clone.1..sunk.2) | dynamic-update-slice | bytes 6291460 | tf_op jit(solution)/shard_map/transpose(jvp())/while/body/jit(dynamic_update_index_in_dim)/dynamic_update_slice | solution.py:180
  1319.7 8.4 fusion.129
  1335.5 19.2 multiply_reduce_fusion.7
  1354.8 9.0 broadcast_multiply_fusion
  1363.9 12.6 pad_add_fusion
  1382.5 6.6 split.9
  1392.0 10.2 scatter-add.6
  1402.2 22.3 %fusion.116 = (f32[1536]{0:T(1024)}, f32[512]{0:T(512)S(1)}, f32[512,1536]{1,0:T(8,128)}) fusion(bf16[512,1536]{1,0:T(8,128)(2,1)S(1)} %copy-done.17, f32[512]{0:T(512)S(1)} %copy-done.51, f32[1536]{0:T(1024)S(1)} %copy-done.46, bf16[1536,6448]{1,0:T(8,128)(2,1)} %all-gather.9.cloned.1.call-done, bf16[512,48]{0,1:T(8,128)(2,1)S(1)} %get-tuple-element.967, ...), kind=kOutput, calls=%fused_computation.206 | convolution fusion | flops 10167138304 | bytes 31145984 | tf_op jit(solution)/shard_map/dot_general | solution.py:81
  1424.7 12.2 fusion.159
  1436.9 22.2 %fusion.124 = f32[1536,6448]{1,0:T(8,128)} fusion(bf16[512,48]{0,1:T(8,128)(2,1)S(1)} %get-tuple-element.967, bf16[512,3328]{0,1:T(8,128)(2,1)} %scatter-add.6, bf16[512,3072]{0,1:T(8,128)(2,1)} %get-tuple-element.989, bf16[512,1536]{1,0:T(8,128)(2,1)S(1)} %copy-done.17, f32[1536]{0:T(1024)S(1)} %copy-done.46, f32[512]{0:T(512)S(1)} %copy-done.51), kind=kOutput, calls=%fused_computation.214 | convolution fusion | flops 10164781056 | bytes 47800320 | tf_op jit(solution)/shard_map/dot_general | solution.py:75
  1459.2 11.1 fusion.123
  1472.9 74.6 %all-reduce.24.cloned.1.call-done = (f32[1536]{0:T(1024)}, f32[4,3328]{1,0:T(4,128)}, f32[3328]{0:T(1024)}, f32[48]{0:T(128)}, f32[48]{0:T(128)}, /*index=5*/f32[48]{0:T(128)}, f32[3072]{0:T(1024)}) async-done(((f32[1536]{0:T(1024)}, f32[4,3328]{1,0:T(4,128)}, f32[3328]{0:T(1024)}, f32[48]{0:T(128)}, f32[48]{0:T(128)}, /*index=5*/f32[48]{0:T(128)}, f32[3072]{0:T(1024)}), (f32[1536]{0:T(1024)}, ...) | async-done | bytes 85584
  1552.7 209.5 %reduce-scatter.6.cloned.1.call-done = f32[96,1536]{1,0:T(8,128)} async-done(((f32[3072,1536]{1,0:T(8,128)}), f32[96,1536]{1,0:T(8,128)}) %reduce-scatter.6.cloned.1.call-update) | async-done | bytes 589840 | tf_op jit(solution)/shard_map/reduce_scatter | solution.py:254
  1762.2 371.2 %reduce-scatter.4.cloned.1.call-done = f32[48,6448]{1,0:T(8,128)} async-done(((f32[1536,6448]{1,0:T(8,128)}), f32[48,6448]{1,0:T(8,128)}) %reduce-scatter.4.cloned.1.call-update) | async-done | bytes 1238032 | tf_op jit(solution)/shard_map/reduce_scatter | solution.py:253
  (424 shorter events, 221.3 us)
Async XLA Ops:
  7.2 138.1 %all-gather.9.cloned.1.call-start = ((), (), s32[]{:S(2)}) async-start(), calls=%async_computation.2 | async-start | bytes 20680704 | tf_op jit(solution)/shard_map/all_gather | solution.py:121
  7.9 602.7 %all-gather.13.cloned.1.call-start = ((), (), s32[]{:S(2)}) async-start(), calls=%async_computation.6 | async-start | bytes 14155776 | tf_op jit(solution)/shard_map/all_gather | solution.py:29
  8.7 165.1 %copy-start.58 = (f32[48]{0:T(128)}, f32[48]{0:T(128)S(1)}, u32[]{:S(2)}) copy-start(f32[48]{0:T(128)S(1)} %exp.118) | copy-start | bytes 580
  59.6 103.3 %copy-start.45 = (f32[1536]{0:T(1024)}, f32[1536]{0:T(1024)S(1)}, u32[]{:S(2)}) copy-start(f32[1536]{0:T(1024)S(1)} %convert_element_type.136) | copy-start | bytes 18436
  129.4 47.1 %copy-start.28 = (f32[3328]{0:T(1024)}, f32[3328]{0:T(1024)S(1)}, u32[]{:S(2)}) copy-start(f32[3328]{0:T(1024)S(1)} %get-tuple-element.876) | copy-start | bytes 39940
  129.4 47.1 %copy-start.30 = (f32[3328]{0:T(1024)}, f32[3328]{0:T(1024)S(1)}, u32[]{:S(2)}) copy-start(f32[3328]{0:T(1024)S(1)} %get-tuple-element.877) | copy-start | bytes 39940
  129.4 47.1 %copy-start.32 = (f32[3328]{0:T(1024)}, f32[3328]{0:T(1024)S(1)}, u32[]{:S(2)}) copy-start(f32[3328]{0:T(1024)S(1)} %get-tuple-element.878) | copy-start | bytes 39940
  129.4 47.1 %copy-start.34 = (f32[3328]{0:T(1024)}, f32[3328]{0:T(1024)S(1)}, u32[]{:S(2)}) copy-start(f32[3328]{0:T(1024)S(1)} %get-tuple-element.879) | copy-start | bytes 39940
  131.8 31.1 %copy-start.50 = (f32[512]{0:T(512)}, f32[512]{0:T(512)S(1)}, u32[]{:S(2)}) copy-start(f32[512]{0:T(512)S(1)} %fusion.151) | copy-start | bytes 6148
  132.5 44.0 %copy-start.39 = (f32[512]{0:T(512)}, f32[512]{0:T(512)S(1)}, u32[]{:S(2)}) copy-start(f32[512]{0:T(512)S(1)} %get-tuple-element.1000) | copy-start | bytes 6148
  132.5 44.0 %copy-start.41 = (f32[512]{0:T(512)}, f32[512]{0:T(512)S(1)}, u32[]{:S(2)}) copy-start(f32[512]{0:T(512)S(1)} %get-tuple-element.1001) | copy-start | bytes 6148
  132.5 44.0 %copy-start.43 = (f32[512]{0:T(512)}, f32[512]{0:T(512)S(1)}, u32[]{:S(2)}) copy-start(f32[512]{0:T(512)S(1)} %get-tuple-element.1002) | copy-start | bytes 6148
  162.9 10.9 copy-start.56
  170.4 5.7 collective-permute-start
  176.4 20.1 copy-start.13
  222.1 213.7 %copy-start.55 = (bf16[3072]{0:T(1024)(128)(2,1)S(1)}, bf16[3072]{0:T(1024)(128)(2,1)}, u32[]{:S(2)}) copy-start(bf16[3072]{0:T(1024)(128)(2,1)} %get-tuple-element.963) | copy-start | bytes 18436
  433.8 31.8 %copy-start.11 = (f32[2,256,128]{2,1,0:T(8,128)}, f32[2,256,128]{2,1,0:T(8,128)S(1)}, u32[]{:S(2)}) copy-start(f32[2,256,128]{2,1,0:T(8,128)S(1)} %get-tuple-element.1487) | copy-start | bytes 786436
  433.8 31.7 %copy-start.12 = (f32[2,256,128]{2,1,0:T(8,128)}, f32[2,256,128]{2,1,0:T(8,128)S(1)}, u32[]{:S(2)}) copy-start(f32[2,256,128]{2,1,0:T(8,128)S(1)} %get-tuple-element.1488) | copy-start | bytes 786436
  434.9 258.8 %all-gather.11.cloned.1.call-start = ((), (), s32[]{:S(2)}) async-start(), calls=%async_computation.3 | async-start | bytes 9732096 | tf_op jit(solution)/shard_map/all_gather | solution.py:122
  435.7 463.3 %all-gather.15.cloned.1.call-start = ((), (), s32[]{:S(2)}) async-start(), calls=%async_computation.7 | async-start | bytes 14155776 | tf_op jit(solution)/shard_map/all_gather | solution.py:29
  435.8 269.6 %copy-start.36 = (f32[3072]{0:T(1024)}, f32[3072]{0:T(1024)S(1)}, u32[]{:S(2)}) copy-start(f32[3072]{0:T(1024)S(1)} %convert_element_type.157) | copy-start | bytes 36868
  438.0 275.9 %copy-start.20 = (f32[512,48]{0,1:T(8,128)}, f32[512,48]{0,1:T(8,128)S(1)}, u32[]{:S(2)}) copy-start(f32[512,48]{0,1:T(8,128)S(1)} %fusion.142) | copy-start | bytes 294916
  610.8 300.6 %copy-start.5 = (f32[48,64,128]{2,1,0:T(8,128)}, f32[48,64,128]{2,1,0:T(8,128)S(1)}, u32[]{:S(2)}) copy-start(f32[48,64,128]{2,1,0:T(8,128)S(1)} %get-tuple-element.628) | copy-start | bytes 4718596
  637.9 67.4 %copy-start.52 = (f32[512]{0:T(512)}, f32[512]{0:T(512)S(1)}, u32[]{:S(2)}) copy-start(f32[512]{0:T(512)S(1)} %fusion.152) | copy-start | bytes 6148
  693.8 11.6 copy-start.7
  693.8 11.6 copy-start.10
  723.8 823.7 %all-reduce.24.cloned.1.call-start = ((), (), s32[]{:S(2)}) async-start(), calls=%async_computation.8 | async-start | bytes 183296
  930.1 23.1 %copy-start.8 = (f32[1,256,48]{2,1,0:T(8,128)}, f32[1,256,48]{2,1,0:T(8,128)S(1)}, u32[]{:S(2)}) copy-start(f32[1,256,48]{2,1,0:T(8,128)S(1)} %copy.431) | copy-start | bytes 147460 | tf_op jit(solution)/shard_map/transpose(jvp())/while
  963.7 22.7 %copy-start.16 = (f32[256,256]{1,0:T(8,128)}, f32[256,256]{1,0:T(8,128)S(1)}, u32[]{:S(2)}) copy-start(f32[256,256]{1,0:T(8,128)S(1)} %fusion.248) | copy-start | bytes 786436 | tf_op jit(solution)/shard_map/transpose(jvp())/while
  1027.9 13.4 copy-start.15
  1027.9 13.4 copy-start.49
  1041.4 11.5 copy-start.26
  1047.9 69.7 %copy-start.1 = (f32[48,64,128]{2,1,0:T(8,128)S(1)}, f32[48,64,128]{2,1,0:T(8,128)}, u32[]{:S(2)}) copy-start(f32[48,64,128]{2,1,0:T(8,128)} %multiply_add_fusion.10) | copy-start | bytes 4718596 | tf_op jit(solution)/shard_map/transpose(jvp())/while
  1047.9 69.7 %copy-start.63 = (s32[2]{0:T(128)S(1)}, s32[2]{0:T(128)}, u32[]{:S(2)}) copy-start(s32[2]{0:T(128)} %copy-done.62) | copy-start | bytes 28 | tf_op jit(solution)/shard_map/transpose(jvp())/while
  1054.0 63.6 %copy-start.27 = (f32[2,256,48]{1,0,2:T(2,128)}, f32[2,256,48]{1,0,2:T(2,128)S(1)}, u32[]{:S(2)}) copy-start(f32[2,256,48]{1,0,2:T(2,128)S(1)} %dynamic_update_slice.78) | copy-start | bytes 294916 | tf_op jit(solution)/shard_map/transpose(jvp())/while
  1121.0 23.2 %copy-start.8 = (f32[1,256,48]{2,1,0:T(8,128)}, f32[1,256,48]{2,1,0:T(8,128)S(1)}, u32[]{:S(2)}) copy-start(f32[1,256,48]{2,1,0:T(8,128)S(1)} %copy.431) | copy-start | bytes 147460 | tf_op jit(solution)/shard_map/transpose(jvp())/while
  1154.6 22.8 %copy-start.16 = (f32[256,256]{1,0:T(8,128)}, f32[256,256]{1,0:T(8,128)S(1)}, u32[]{:S(2)}) copy-start(f32[256,256]{1,0:T(8,128)S(1)} %fusion.248) | copy-start | bytes 786436 | tf_op jit(solution)/shard_map/transpose(jvp())/while
  1219.0 13.1 copy-start.15
  1219.0 13.1 copy-start.49
  1232.2 11.5 copy-start.26
  1238.8 69.7 %copy-start.1 = (f32[48,64,128]{2,1,0:T(8,128)S(1)}, f32[48,64,128]{2,1,0:T(8,128)}, u32[]{:S(2)}) copy-start(f32[48,64,128]{2,1,0:T(8,128)} %multiply_add_fusion.10) | copy-start | bytes 4718596 | tf_op jit(solution)/shard_map/transpose(jvp())/while
  1238.8 69.7 %copy-start.63 = (s32[2]{0:T(128)S(1)}, s32[2]{0:T(128)}, u32[]{:S(2)}) copy-start(s32[2]{0:T(128)} %copy-done.62) | copy-start | bytes 28 | tf_op jit(solution)/shard_map/transpose(jvp())/while
  1244.9 63.6 %copy-start.27 = (f32[2,256,48]{1,0,2:T(2,128)}, f32[2,256,48]{1,0,2:T(2,128)S(1)}, u32[]{:S(2)}) copy-start(f32[2,256,48]{1,0,2:T(2,128)S(1)} %dynamic_update_slice.78) | copy-start | bytes 294916 | tf_op jit(solution)/shard_map/transpose(jvp())/while
  1319.7 12.1 slice-start
  1335.4 19.3 copy-start.29
  1335.5 19.3 copy-start.31
  1335.5 19.3 copy-start.33
  1335.5 19.3 copy-start.35
  1363.8 15.8 copy-start.25
  1363.8 15.8 copy-start.54
  1363.8 15.8 copy-start.57
  1363.8 15.8 copy-start.59
  1363.8 18.1 copy-start.61
  1378.4 10.7 collective-permute-start.1
  1382.5 19.6 copy-start.17
  1382.5 19.6 copy-start.46
  1382.5 19.6 copy-start.51
  1402.1 22.5 %copy-start.21 = (bf16[512,1536]{1,0:T(8,128)(2,1)S(1)}, bf16[512,1536]{1,0:T(8,128)(2,1)}, u32[]{:S(2)}) copy-start(bf16[512,1536]{1,0:T(8,128)(2,1)} %param.25) | copy-start | bytes 4718596
  1402.1 22.5 %copy-start.37 = (f32[3072]{0:T(1024)S(1)}, f32[3072]{0:T(1024)}, u32[]{:S(2)}) copy-start(f32[3072]{0:T(1024)} %copy-done.36) | copy-start | bytes 36868
  1402.1 22.5 %copy-start.53 = (f32[512]{0:T(512)S(1)}, f32[512]{0:T(512)}, u32[]{:S(2)}) copy-start(f32[512]{0:T(512)} %copy-done.52) | copy-start | bytes 6148
  1424.4 337.7 %reduce-scatter.6.cloned.1.call-start = ((), (), s32[]{:S(2)}) async-start(), calls=%async_computation.5 | async-start | bytes 19464192 | tf_op jit(solution)/shard_map/reduce_scatter | solution.py:254
  1436.9 696.5 %reduce-scatter.4.cloned.1.call-start = ((), (), s32[]{:S(2)}) async-start(), calls=%async_computation.4 | async-start | bytes 41361408 | tf_op jit(solution)/shard_map/reduce_scatter | solution.py:253
  1459.2 11.1 copy-start.48
  1459.2 11.2 copy-start.19
  (28 other events, 128.7 us)
Sparse Core Ops, SparseCore 0:
  10.9 134.3 all-gather.8
  435.1 175.4 all-gather.12
  613.5 80.2 all-gather.10
  723.9 175.0 all-gather.14
  1424.6 122.9 all-reduce.23
  1554.3 207.7 reduce-scatter.5
  1769.1 364.1 reduce-scatter.3
where the time goes:
time: 2170 us; the launch traced here: 2140 us
  waiting for transfers between devices  1030 us (47%)
  local copies, waits for them, and re-layouts  450 us (21%)
  matrix products  308 us (14%)
  other arithmetic  186 us (9%)
  blocking collectives  130 us (6%)
    reduce_scatter x1, waiting for transfers between devices, shards(): lax.psum_scatter(grad_in_weight, ('dp', 'ctx'), scatter_dimension=0, tile...  371 us
    all_gather x2, waiting for transfers between devices, entering_2(): gathered = jax.tree.map(lambda a: lax.all_gather(a, axis), part)  304 us
    dynamic_update_slice x12, local copies, waits for them, and re-layouts, local_scan(): lax.scan(jax.checkpoint(span_step), start_state, pieces)  276 us
    reduce_scatter x1, waiting for transfers between devices, shards(): lax.psum_scatter(grad_out_weight, ('dp', 'ctx'), scatter_dimension=0, til...  209 us
    dot_general x6, matrix products, span_step(): inside = jnp.einsum('hij,jhp->ihp', mixing, x_heads, precision=highest)  104 us
    unnamed x8, waiting for transfers between devices  76.1 us
    all_gather x1, blocking collectives, shards(): lax.all_gather(conv_weight, ('dp', 'ctx'), axis=1, tiled=True)  67.4 us
    all_gather x1, waiting for transfers between devices, shards(): lax.all_gather(out_weight, ('dp', 'ctx'), axis=0, tiled=True)  55.8 us
  transfers between devices with their start and end apart: 9, of which 7 were waited for; matrix products, arithmetic and copies ran while one was open for 6% of the time, Pallas kernels for 0%

commit v1 on v0

v1 whole, which is shorter than its diff:
```python
import functools

import jax
import jax.numpy as jnp
from jax import lax
from jax.experimental import pallas as pl
from jax.experimental.pallas import tpu as pltpu
from jax.sharding import Mesh, PartitionSpec as P

HEADS = 48
HEAD_DIM = 64
STATE = 128
CONV_K = 4
INNER = 3072
CONVW = 3328
LEAD = 16
BLOCK = 512
BLOCK_HEADS = BLOCK // HEAD_DIM
PAIRS = 2
PAIR_LANES = 128 * PAIRS
VMEM = 56 * 1024 * 1024
F32 = jnp.float32
BF = jnp.bfloat16
EPS = 1e-05
highest = lax.Precision.HIGHEST
EVERY = ("x", "core", "z", "y")
CTX = ("z", "y")


def params():
    return pltpu.CompilerParams(vmem_limit_bytes=VMEM, dimension_semantics=("arbitrary",))


def call(body, grid, ins, outs, scratch=()):
    in_specs = [spec for _, spec in ins]
    return pl.pallas_call(
        body,
        grid=(grid,),
        in_specs=in_specs,
        out_specs=[spec for _, spec in outs],
        out_shape=[shape for shape, _ in outs],
        scratch_shapes=list(scratch),
        compiler_params=params(),
    )(*[array for array, _ in ins])


def whole(*shape):
    return pl.BlockSpec(shape, lambda g: (0,) * len(shape))


def lanes(rows, width):
    return pl.BlockSpec((rows, width), lambda g: (0, g))


def rows_of(count, width):
    return pl.BlockSpec((count, width), lambda g: (g, 0))


def group(rows, width):
    return pl.BlockSpec((1, rows, width), lambda g: (g, 0, 0))


def out(shape, dtype=F32):
    return jax.ShapeDtypeStruct(shape, dtype)


def split(value):
    high = value.astype(BF)
    return high, (value - high.astype(F32)).astype(BF)


def mm(left, right):
    return jnp.dot(left, right, preferred_element_type=F32)


def mm_nt(left, right):
    return lax.dot_general(left, right, (((1,), (1,)), ((), ())), preferred_element_type=F32)


def mm_tn(left, right):
    return lax.dot_general(left, right, (((0,), (0,)), ((), ())), preferred_element_type=F32)


def three(product, left, right):
    left_high, left_low = left
    right_high, right_low = right
    return (
        product(left_high, right_high)
        + product(left_high, right_low)
        + product(left_low, right_high)
    )


def head_of_lane(first, count):
    lane = lax.broadcasted_iota(jnp.int32, (STATE, count), 1) // HEAD_DIM + first
    row = lax.broadcasted_iota(jnp.int32, (STATE, count), 0)
    return (lane == row).astype(BF)


def expand(value, places):
    high, low = split(value)
    return mm(high, places) + mm(low, places)


def fold(value, places):
    high, low = split(value)
    return mm_nt(high, places) + mm_nt(low, places)


def sigmoid(value):
    return 1.0 / (1.0 + jnp.exp(-value))


def conv_pre(extended, weight, bias, masks):
    running = jnp.zeros((masks.shape[0], extended.shape[1]), F32) + bias
    for tap in range(CONV_K):
        shifted = extended if tap == CONV_K - 1 else pltpu.roll(extended, CONV_K - 1 - tap, 0)
        running = running + shifted[LEAD:] * weight[tap : tap + 1] * masks[:, tap : tap + 1]
    return running


def conv_back(d_pre, extended, weight, masks):
    zeros = jnp.zeros((LEAD, d_pre.shape[1]), F32)
    total = LEAD + d_pre.shape[0]
    d_ext = jnp.zeros((total, d_pre.shape[1]), F32)
    weight_rows = []
    for tap in range(CONV_K):
        by = CONV_K - 1 - tap
        part = d_pre * masks[:, tap : tap + 1]
        padded = jnp.concatenate([zeros, part], axis=0)
        shifted = extended
        if by:
            padded = pltpu.roll(padded, total - by, 0)
            shifted = pltpu.roll(extended, by, 0)
        d_ext = d_ext + padded * weight[tap : tap + 1]
        weight_rows.append(jnp.sum(shifted[LEAD:] * part, axis=0, keepdims=True))
    weight_rows.append(jnp.sum(d_pre, axis=0, keepdims=True))
    weight_rows.append(jnp.zeros((8 - len(weight_rows), d_pre.shape[1]), F32))
    return d_ext, jnp.concatenate(weight_rows, axis=0)


def same_mask(doc_row, doc_col, transposed):
    count = doc_row.shape[1]
    rows = lax.broadcasted_iota(jnp.int32, (count, count), 0)
    cols = lax.broadcasted_iota(jnp.int32, (count, count), 1)
    order = rows <= cols if transposed else rows >= cols
    return jnp.where((doc_row == doc_col) & order, 1.0, 0.0)


def prep_bc_body(x_ref, w_ref, b_ref, m_ref, doc_ref, pre_ref, act_ref, t_ref, s_ref, st_ref):
    masks = m_ref[...]
    pre = conv_pre(x_ref[...].astype(F32), w_ref[...], b_ref[...], masks)
    act = pre * sigmoid(pre)
    pre_ref[...] = pre
    act_ref[...] = act
    t_ref[...] = act.T
    b_rows, c_rows = split(act[:, :STATE]), split(act[:, STATE:])
    doc_row, doc_col = doc_ref[0:1], masks[:, CONV_K : CONV_K + 1]
    s_ref[...] = three(mm_nt, c_rows, b_rows) * same_mask(doc_row, doc_col, False)
    st_ref[...] = three(mm_nt, b_rows, c_rows) * same_mask(doc_row, doc_col, True)


def prep_x_body(x_ref, w_ref, b_ref, m_ref, wl_ref, t_ref, pre_ref, act_ref, state_ref):
    pre = conv_pre(x_ref[...].astype(F32), w_ref[...], b_ref[...], m_ref[...])
    act = pre * sigmoid(pre)
    pre_ref[...] = pre
    act_ref[...] = act
    places = head_of_lane(pl.program_id(0) * BLOCK_HEADS, BLOCK)
    weighted = split(act * expand(wl_ref[...], places))
    state_ref[...] = three(mm, split(t_ref[:STATE]), weighted)


def intra_body(x_ref, dt_ref, skip_ref, s_ref, col_ref, row_ref, y_ref):
    half = s_ref.shape[0] // 2
    places = head_of_lane(pl.program_id(0) * 2 * PAIRS, PAIR_LANES)
    scaled = x_ref[...] * expand(dt_ref[...], places)
    lane = lax.broadcasted_iota(jnp.int32, (2 * half, 128), 1)
    for pair in range(PAIRS):
        here = slice(pair * 128, pair * 128 + 128)
        high, low = split(scaled[:, here])
        right = jnp.concatenate([high, low], axis=1)
        both = []
        for side in range(2):
            head = 2 * pair + side
            col = col_ref[0, :, head : head + 1]
            row = row_ref[0, head : head + 1, :]
            top = s_ref[:half, :half] * jnp.exp(jnp.minimum(col[:half] - row[:, :half], 0.0))
            low_part = s_ref[half:, :] * jnp.exp(jnp.minimum(col[half:] - row, 0.0))
            done = []
            for part, count in ((top, half), (low_part, 2 * half)):
                p_high, p_low = split(part)
                first = mm(p_high, right[:count])
                done.append(first[:, :128] + first[:, 128:] + mm(p_low, high[:count]))
            both.append(jnp.concatenate(done, axis=0))
        y_ref[:, here] = (
            jnp.where(lane < HEAD_DIM, both[0], both[1]) + skip_ref[:, here] * x_ref[:, here]
        )


def gate_body(
    y_ref, z_ref, df_ref, x_ref, c_ref, ct_ref, state_ref, e_ref, gain_ref, skip_ref,
    final_ref, dz_ref, dy_ref, r_ref, dc_ref, q_ref, sums_ref, carry, scaled,
):
    @pl.when(pl.program_id(0) == 0)
    def _():
        r_ref[...] = jnp.zeros_like(r_ref)
        sums_ref[...] = jnp.zeros_like(sums_ref)

    e_high, e_low = split(e_ref[...])
    c_rows = split(c_ref[...])
    for block in range(INNER // BLOCK):
        here = slice(block * BLOCK, block * BLOCK + BLOCK)
        places = head_of_lane(block * BLOCK_HEADS, BLOCK)
        spread = mm(e_high, places) + mm(e_low, places)
        carry[:, here] = three(mm, c_rows, split(state_ref[:, here])) * spread
        scaled[:, here] = spread
    gain, skip = gain_ref[...], skip_ref[...]

    def some(lap, sums):
        at = pl.ds(pl.multiple_of(lap * 16, 16), 16)
        y = y_ref[at, :] + carry[at, :]
        z = z_ref[at, :].astype(F32)
        sig = sigmoid(z)
        gate = z * sig
        gated = y * gate
        scale = lax.rsqrt(jnp.mean(gated * gated, axis=-1, keepdims=True) + EPS)
        unit = gated * scale
        final_ref[at, :] = (unit * gain).astype(BF)
        d_final = df_ref[at, :]
        q = d_final * gain
        inner = jnp.mean(q * unit, axis=-1, keepdims=True)
        d_gated = scale * (q - unit * inner)
        d_y = d_gated * gate
        dz_ref[at, :] = (d_gated * y * (sig * (1.0 + z * (1.0 - sig)))).astype(BF)
        dy_ref[at, :] = d_y
        x = x_ref[at, :]
        scaled[at, :] = scaled[at, :] * d_y
        carry[at, :] = d_y * (y - skip * x)
        d_gain, d_skip = d_final * unit, d_y * x
        return (
            sums[0] + d_gain[:8] + d_gain[8:],
            sums[1] + d_skip[:8] + d_skip[8:],
        )

    zero = jnp.zeros((8, INNER), F32)
    d_gain, d_skip = lax.fori_loop(0, y_ref.shape[0] // 16, some, (zero, zero))
    sums_ref[0:8] += d_gain
    sums_ref[8:16] += d_skip
    ct_rows = split(ct_ref[...])
    d_c = jnp.zeros(dc_ref.shape, F32)
    q_sum = jnp.zeros(q_ref.shape, F32)
    for block in range(INNER // BLOCK):
        here = slice(block * BLOCK, block * BLOCK + BLOCK)
        piece = split(scaled[:, here])
        r_ref[:, here] += three(mm, ct_rows, piece)
        d_c = d_c + three(mm_nt, piece, split(state_ref[:, here]))
        q_sum = q_sum + fold(carry[:, here], head_of_lane(block * BLOCK_HEADS, BLOCK))
    dc_ref[...] = d_c
    q_ref[...] = q_sum


def back_body(x_ref, dy_ref, dt_ref, st_ref, col_ref, row_ref, bc_ref, doc_ref, m_ref, dx_ref, dbc_ref, acc):
    step = pl.program_id(0)
    half = st_ref.shape[0] // 2

    @pl.when(step == 0)
    def _():
        acc[...] = jnp.zeros_like(acc)

    places = head_of_lane(step * 2 * PAIRS, PAIR_LANES)
    scaled = x_ref[...] * expand(dt_ref[...], places)
    lane = lax.broadcasted_iota(jnp.int32, (2 * half, 128), 1)
    for pair in range(PAIRS):
        here = slice(pair * 128, pair * 128 + 128)
        dy_high, dy_low = split(dy_ref[:, here])
        right = jnp.concatenate([dy_high, dy_low], axis=1)
        twice = jnp.concatenate([dy_high, dy_high], axis=1)
        both = []
        for side in range(2):
            head = 2 * pair + side
            mine = (lane < HEAD_DIM) if side == 0 else (lane >= HEAD_DIM)
            x_high, x_low = split(jnp.where(mine, scaled[:, here], 0.0))
            x_both = jnp.concatenate([x_high, x_low], axis=1)
            col = col_ref[0, :, head : head + 1]
            row = row_ref[0, head : head + 1, :]
            done = []
            for at, over in ((slice(0, half), slice(0, 2 * half)), (slice(half, 2 * half), slice(half, 2 * half))):
                decay = jnp.exp(jnp.minimum(row[:, over] - col[at], 0.0))
                p_high, p_low = split(st_ref[at, over] * decay)
                first = mm(p_high, right[over])
                done.append(first[:, :128] + first[:, 128:] + mm(p_low, dy_high[over]))
                outer = mm_nt(x_both[at], twice[over]) + mm_nt(x_high[at], dy_low[over])
                acc[at, over] += outer * decay
            both.append(jnp.concatenate(done, axis=0))
        dx_ref[:, here] = jnp.where(lane < HEAD_DIM, both[0], both[1])

    @pl.when(step == pl.num_programs(0) - 1)
    def _():
        doc_col = m_ref[:, CONV_K : CONV_K + 1]
        ds = split(acc[...] * same_mask(doc_ref[0:1], doc_col, True))
        dbc_ref[:, :STATE] = three(mm, ds, split(bc_ref[:, STATE:]))
        dbc_ref[:, STATE:] = three(mm_tn, ds, split(bc_ref[:, :STATE]))


def carry_body(
    dx_ref, x_ref, dy_ref, pre_ref, in_ref, w_ref, m_ref, bc_ref, r_ref, end_ref, wl_ref, dt_ref, skip_ref,
    d_ref, edge_ref, conv_ref, db_ref, g_ref,
):
    step = pl.program_id(0)

    @pl.when(step == 0)
    def _():
        db_ref[...] = jnp.zeros_like(db_ref)
        g_ref[...] = jnp.zeros_like(g_ref)

    places = head_of_lane(step * BLOCK_HEADS, BLOCK)
    returned = r_ref[...]
    r_parts = split(returned)
    to_end = expand(wl_ref[...], places)
    steps = expand(dt_ref[...], places)
    x = x_ref[...]
    d_scaled = dx_ref[...] + to_end * three(mm, split(bc_ref[:, :STATE]), r_parts)
    g_ref[...] += fold(x * d_scaled, places)
    db_ref[...] += three(mm_nt, split(to_end * steps * x), r_parts)
    d_x = steps * d_scaled + skip_ref[...] * dy_ref[...]
    pre = pre_ref[...]
    sig = sigmoid(pre)
    d_pre = d_x * (sig * (1.0 + pre * (1.0 - sig)))
    d_ext, sums = conv_back(d_pre, in_ref[...].astype(F32), w_ref[...], m_ref[...])
    d_ref[...] = d_ext[LEAD:].astype(BF)
    edge_ref[:LEAD] = d_ext[:LEAD]
    edge_ref[LEAD:] = d_ext[d_ext.shape[0] - LEAD :]
    flow = jnp.sum(returned * end_ref[...], axis=0, keepdims=True)
    row = lax.broadcasted_iota(jnp.int32, sums.shape, 0)
    conv_ref[...] = jnp.where(row == CONV_K + 1, flow, sums)


def carry_bc_body(d_ref, pre_ref, in_ref, w_ref, m_ref, o_ref, edge_ref, conv_ref):
    pre = pre_ref[...]
    sig = sigmoid(pre)
    d_pre = d_ref[...] * (sig * (1.0 + pre * (1.0 - sig)))
    d_ext, sums = conv_back(d_pre, in_ref[...].astype(F32), w_ref[...], m_ref[...])
    o_ref[...] = d_ext[LEAD:].astype(BF)
    edge_ref[:LEAD] = d_ext[:LEAD]
    edge_ref[LEAD:] = d_ext[d_ext.shape[0] - LEAD :]
    conv_ref[...] = sums


def swap(array, axis):
    return lax.ppermute(array, axis, [(0, 1), (1, 0)])


def from_behind(array, by):
    peers = lax.axis_size(CTX[0]) * lax.axis_size(CTX[1])
    pairs = [(i, i + by) for i in range(peers) if 0 <= i + by < peers]
    return lax.ppermute(array, CTX, pairs)


def entering(state, decay, reverse):
    depth, width = lax.axis_size("z"), lax.axis_size("y")
    place_z, place_y = lax.axis_index("z"), lax.axis_index("y")
    if width != 2:
        both = jnp.concatenate([state, jnp.broadcast_to(decay, (8, decay.shape[1]))], axis=0)
        gathered = lax.all_gather(both, CTX)
        count = depth * width
        place = place_z * width + place_y
        ahead = count - 1 - place if reverse else place

        def one(lap, running):
            source = count - 1 - lap if reverse else lap
            item = lax.dynamic_index_in_dim(gathered, source, 0, False)
            return item[STATE : STATE + 1] * running + item[:STATE]

        return lax.fori_loop(0, ahead, one, jnp.zeros_like(state))
    half = state.shape[1] // 2
    second = place_y == (0 if reverse else 1)
    own = lax.dynamic_slice_in_dim(state, place_y * half, half, 1)
    other = lax.dynamic_slice_in_dim(state, (1 - place_y) * half, half, 1)
    got = swap(other, "y")
    decay_own = lax.dynamic_slice_in_dim(decay, place_y * half, half, 1)
    decay_got = swap(lax.dynamic_slice_in_dim(decay, (1 - place_y) * half, half, 1), "y")
    early = jnp.where(second, got, own)
    late = jnp.where(second, own, got)
    decay_early = jnp.where(second, decay_got, decay_own)
    decay_late = jnp.where(second, decay_own, decay_got)
    total = decay_late * early + late
    decay_total = decay_early * decay_late
    before = jnp.zeros_like(total)
    sent = total
    for hop in range(1, depth):
        pair = (depth - hop, depth - 1 - hop) if reverse else (hop - 1, hop)
        before = before + lax.ppermute(sent, "z", [pair])
        sent = decay_total * before + total
    middle = decay_early * before + early
    mine = jnp.where(second, middle, before)
    theirs = swap(jnp.where(second, before, middle), "y")
    return jnp.where(
        place_y == 0,
        jnp.concatenate([mine, theirs], axis=1),
        jnp.concatenate([theirs, mine], axis=1),
    )


def line_sum(parts, axis):
    count, place = lax.axis_size(axis), lax.axis_index(axis)

    def pick(i):
        return lax.dynamic_index_in_dim(parts, jnp.clip(i, 0, count - 1), 0, False)

    up, down = pick(count - 1), pick(0)
    for step in range(1, count):
        got_up = lax.ppermute(up, axis, [(i, i + 1) for i in range(step)])
        got_down = lax.ppermute(down, axis, [(count - 1 - i, count - 2 - i) for i in range(step)])
        if step < count - 1:
            up = pick(count - step - 1 + place) + got_up
            down = pick(place - (count - step - 1)) + got_down
    return pick(place) + got_up + got_down


def pair_sum(parts, axis):
    if lax.axis_size(axis) != 2:
        return line_sum(parts, axis)
    place = lax.axis_index(axis)
    sent = lax.dynamic_index_in_dim(parts, 1 - place, 0, False).astype(BF)
    kept = lax.dynamic_index_in_dim(parts, place, 0, False)
    return kept + swap(sent, axis).astype(F32)


def scatter_sum(partial, x_first):
    sizes = [lax.axis_size(a) for a in ("x", "z", "y")]
    count = partial.shape[0] // (sizes[0] * sizes[1] * sizes[2])
    parts = partial.reshape(*sizes, count, partial.shape[1])
    if x_first:
        parts = pair_sum(parts, "x")
        parts = pair_sum(jnp.moveaxis(parts, 1, 0), "y")
    else:
        parts = pair_sum(jnp.moveaxis(parts, 2, 0), "y")
        parts = pair_sum(parts, "x")
    return line_sum(parts, "z")


def own_rows(array, core):
    sizes = lax.axis_size("x")
    view = array.reshape(array.shape[0], sizes, 2, -1)
    return lax.dynamic_index_in_dim(view, core, 2, False).reshape(array.shape[0], -1)


def document_ids(lengths, positions):
    first_end = lengths[0]
    second_end = lengths[0] + lengths[1]
    inside = (positions >= first_end).astype(jnp.int32) + (positions >= second_end).astype(jnp.int32)
    return jnp.where(positions < 0, -1, inside)


def gather_small(pieces, count):
    flat = jnp.concatenate([piece.reshape(-1) for piece in pieces])
    spread = jnp.broadcast_to(flat[None], (count, flat.shape[0]))
    return lax.all_to_all(spread, EVERY, 0, 0, tiled=True)


def columns(array, width):
    return jnp.pad(array, ((0, 0), (0, width - array.shape[1])))


def shards(
    tokens, out_grad, seq_lengths, norm_gain, in_weight, conv_weight, conv_bias,
    dt_bias, a_log, skip_gain, gated_gain, out_weight,
):
    count = 1
    for axis in EVERY:
        count *= lax.axis_size(axis)
    core = lax.axis_index("core")
    place = lax.axis_index("z") * lax.axis_size("y") + lax.axis_index("y")
    row_count = tokens.shape[0]
    width = tokens.shape[1]
    first_row = place * row_count

    lengths = seq_lengths[0]
    ordinal = jnp.arange(row_count, dtype=jnp.int32)
    doc_ids = document_ids(lengths, first_row + ordinal)
    doc_before = document_ids(lengths, first_row - 1 + jnp.zeros((1,), jnp.int32))
    marks = [
        (document_ids(lengths, first_row + ordinal - (CONV_K - 1 - tap)) == doc_ids).astype(F32)
        for tap in range(CONV_K)
    ]
    keep = marks[CONV_K - 2]
    masks = columns(jnp.stack(marks + [doc_ids.astype(F32)], axis=1), 128)
    doc_rows = jnp.broadcast_to(doc_ids.astype(F32)[None], (8, row_count))
    alive = (doc_ids == doc_before[0]).astype(F32)
    tail = (doc_ids == doc_ids[row_count - 1]).astype(F32)

    lead_tokens = from_behind(tokens[row_count - LEAD :], 1)
    small = gather_small([norm_gain, conv_weight, conv_bias, gated_gain], count)
    cuts = [norm_gain.size, conv_weight.size, conv_bias.size]
    cuts = [sum(cuts[: i + 1]) for i in range(3)]
    gain_piece, conv_piece, bias_piece, gated_piece = jnp.split(small, cuts, axis=1)
    full_gain = gain_piece.reshape(1, -1).astype(F32)
    full_conv = jnp.moveaxis(conv_piece.reshape(count, CONV_K, -1), 1, 0).reshape(CONV_K, -1)
    full_conv = jnp.pad(full_conv.astype(F32), ((0, 4), (0, 0)))
    full_bias = bias_piece.reshape(1, -1).astype(F32)
    full_gated = gated_piece.reshape(1, -1).astype(F32)
    weight_x = lax.all_gather(in_weight[:, INNER:], EVERY, axis=0, tiled=True)
    weight_z = lax.all_gather(in_weight[:, :INNER], EVERY, axis=0, tiled=True)
    weight_o = lax.all_gather(out_weight, EVERY, axis=0, tiled=True)

    extended = jnp.concatenate([lead_tokens, tokens], axis=0).astype(F32)
    rms = lax.rsqrt(jnp.mean(extended * extended, axis=-1, keepdims=True) + EPS)
    normed_ext = (extended * rms * full_gain).astype(BF)
    normed = normed_ext[LEAD:]
    mixed_x = mm(normed_ext, weight_x).astype(BF)
    mixed_xs = mixed_x[:, :INNER]
    mixed_bc = mixed_x[:, INNER:CONVW]
    shifted_dt = mixed_x[LEAD:, CONVW:].astype(F32) + dt_bias[None]

    steps = jax.nn.softplus(shifted_dt)
    rate = jnp.exp(a_log)[None]
    log_decay = -steps * rate
    lower = (ordinal[:, None] >= ordinal[None, :]).astype(F32)
    cumulative = jnp.dot(lower, log_decay, precision=highest)
    last = cumulative[row_count - 1 :]
    enter = jnp.exp(cumulative) * alive[:, None]
    to_end = jnp.exp(last - cumulative) * tail[:, None]
    device_decay = jnp.repeat(enter[row_count - 1 :], HEAD_DIM, axis=1)
    steps_wide = columns(steps, 128)
    enter_wide = columns(enter, 128)
    to_end_wide = columns(to_end, 128)
    weights_wide = columns(to_end * steps, 128)
    heads_block = 2 * PAIRS
    groups = HEADS // heads_block
    cum_cols = jnp.moveaxis(cumulative.reshape(row_count, groups, heads_block), 1, 0)
    cum_rows = cumulative.T.reshape(groups, heads_block, row_count)
    skip_wide = jnp.repeat(skip_gain, HEAD_DIM)[None]

    bc_width = CONVW - INNER
    full_rows = LEAD + row_count
    square = (row_count, row_count)
    pre_bc, act_bc, act_t, scores, scores_t = call(
        prep_bc_body, 1,
        [
            (mixed_bc, whole(full_rows, bc_width)),
            (full_conv[:, INNER:], whole(8, bc_width)),
            (full_bias[:, INNER:], whole(1, bc_width)),
            (masks, whole(row_count, 128)),
            (doc_rows, whole(8, row_count)),
        ],
        [
            (out((row_count, bc_width)), whole(row_count, bc_width)),
            (out((row_count, bc_width)), whole(row_count, bc_width)),
            (out((bc_width, row_count)), whole(bc_width, row_count)),
            (out(square), whole(*square)),
            (out(square), whole(*square)),
        ],
    )
    pre_x, act_x, state_local = call(
        prep_x_body, INNER // BLOCK,
        [
            (mixed_xs, lanes(full_rows, BLOCK)),
            (full_conv[:, :INNER], lanes(8, BLOCK)),
            (full_bias[:, :INNER], lanes(1, BLOCK)),
            (masks, whole(row_count, 128)),
            (weights_wide, whole(row_count, 128)),
            (act_t, whole(bc_width, row_count)),
        ],
        [
            (out((row_count, INNER)), lanes(row_count, BLOCK)),
            (out((row_count, INNER)), lanes(row_count, BLOCK)),
            (out((STATE, INNER)), lanes(STATE, BLOCK)),
        ],
    )
    state_in = entering(state_local, device_decay, False)
    state_end = device_decay * state_in + state_local

    y_local = call(
        intra_body, groups,
        [
            (act_x, lanes(row_count, PAIR_LANES)),
            (steps_wide, whole(row_count, 128)),
            (skip_wide, lanes(1, PAIR_LANES)),
            (scores, whole(*square)),
            (cum_cols, group(row_count, heads_block)),
            (cum_rows, group(heads_block, row_count)),
        ],
        [(out((row_count, INNER)), lanes(row_count, PAIR_LANES))],
    )[0]
    mixed_z = mm(normed, weight_z).astype(BF)
    d_final = mm_nt(out_grad, weight_o)

    tile = 128
    c_rows = act_bc[:, STATE:]
    c_cols = act_t[STATE:]
    final, d_z, d_y, returned_local, d_c_carry, dy_y, sums = call(
        gate_body, row_count // tile,
        [
            (y_local, rows_of(tile, INNER)),
            (mixed_z, rows_of(tile, INNER)),
            (d_final, rows_of(tile, INNER)),
            (act_x, rows_of(tile, INNER)),
            (c_rows, rows_of(tile, STATE)),
            (c_cols, lanes(STATE, tile)),
            (state_in, whole(STATE, INNER)),
            (enter_wide, rows_of(tile, 128)),
            (full_gated, whole(1, INNER)),
            (skip_wide, whole(1, INNER)),
        ],
        [
            (out((row_count, INNER), BF), rows_of(tile, INNER)),
            (out((row_count, INNER), BF), rows_of(tile, INNER)),
            (out((row_count, INNER)), rows_of(tile, INNER)),
            (out((STATE, INNER)), whole(STATE, INNER)),
            (out((row_count, STATE)), rows_of(tile, STATE)),
            (out((row_count, 128)), rows_of(tile, 128)),
            (out((16, INNER)), whole(16, INNER)),
        ],
        [pltpu.VMEM((tile, INNER), F32), pltpu.VMEM((tile, INNER), F32)],
    )
    returned = entering(returned_local, device_decay, True)

    layer_out = (tokens.astype(F32) + mm(final, weight_o)).astype(BF)
    final_mine = jnp.concatenate([own_rows(final, core), swap(own_rows(final, 1 - core), "core")], axis=0)
    out_grad_both = jnp.concatenate([out_grad, swap(out_grad, "core")], axis=0)
    normed_mine = jnp.concatenate([own_rows(normed, core), swap(own_rows(normed, 1 - core), "core")], axis=0)

    def reduce_columns(left, right):
        middle = right.shape[1] // 256 * 128
        return jnp.concatenate(
            [
                scatter_sum(mm_tn(left, right[:, :middle]), True),
                scatter_sum(mm_tn(left, right[:, middle:]), False),
            ],
            axis=1,
        )

    sum_out = reduce_columns(final_mine, out_grad_both)
    d_z_both = jnp.concatenate([d_z, swap(d_z, "core")], axis=0)
    sum_in_z = reduce_columns(normed_mine, d_z_both)

    d_scaled, d_bc = call(
        back_body, groups,
        [
            (act_x, lanes(row_count, PAIR_LANES)),
            (d_y, lanes(row_count, PAIR_LANES)),
            (steps_wide, whole(row_count, 128)),
            (scores_t, whole(*square)),
            (cum_cols, group(row_count, heads_block)),
            (cum_rows, group(heads_block, row_count)),
            (act_bc, whole(row_count, bc_width)),
            (doc_rows, whole(8, row_count)),
            (masks, whole(row_count, 128)),
        ],
        [
            (out((row_count, INNER)), lanes(row_count, PAIR_LANES)),
            (out((row_count, bc_width)), whole(row_count, bc_width)),
        ],
        [pltpu.VMEM(square, F32)],
    )

    d_xs, edge_x, conv_x, d_b_carry, x_dx = call(
        carry_body, INNER // BLOCK,
        [
            (d_scaled, lanes(row_count, BLOCK)),
            (act_x, lanes(row_count, BLOCK)),
            (d_y, lanes(row_count, BLOCK)),
            (pre_x, lanes(row_count, BLOCK)),
            (mixed_xs, lanes(full_rows, BLOCK)),
            (full_conv[:, :INNER], lanes(8, BLOCK)),
            (masks, whole(row_count, 128)),
            (act_bc, whole(row_count, bc_width)),
            (returned, lanes(STATE, BLOCK)),
            (state_end, lanes(STATE, BLOCK)),
            (to_end_wide, whole(row_count, 128)),
            (steps_wide, whole(row_count, 128)),
            (skip_wide, lanes(1, BLOCK)),
        ],
        [
            (out((row_count, INNER), BF), lanes(row_count, BLOCK)),
            (out((2 * LEAD, INNER)), lanes(2 * LEAD, BLOCK)),
            (out((8, INNER)), lanes(8, BLOCK)),
            (out((row_count, STATE)), whole(row_count, STATE)),
            (out((row_count, 128)), whole(row_count, 128)),
        ],
    )
    d_bc = d_bc + jnp.concatenate([d_b_carry, d_c_carry], axis=1)
    d_bc_low, edge_bc, conv_bc = call(
        carry_bc_body, 1,
        [
            (d_bc, whole(row_count, bc_width)),
            (pre_bc, whole(row_count, bc_width)),
            (mixed_bc, whole(full_rows, bc_width)),
            (full_conv[:, INNER:], whole(8, bc_width)),
            (masks, whole(row_count, 128)),
        ],
        [
            (out((row_count, bc_width), BF), whole(row_count, bc_width)),
            (out((2 * LEAD, bc_width)), whole(2 * LEAD, bc_width)),
            (out((8, bc_width)), whole(8, bc_width)),
        ],
    )
    conv_sums = jnp.concatenate([conv_x, conv_bc], axis=1)
    edges = jnp.concatenate([edge_x, edge_bc], axis=1)
    d_last = edges[LEAD:] + from_behind(edges[:LEAD], -1)

    x_dx = x_dx[:, :HEADS]
    flow = jnp.sum(conv_x[CONV_K + 1].reshape(HEADS, HEAD_DIM), axis=1)
    difference = dy_y[:, :HEADS] - steps * x_dx
    upper = (ordinal[:, None] <= ordinal[None, :]).astype(F32)
    d_log_decay = (flow[None] + jnp.dot(upper, difference, precision=highest)) * keep[:, None]
    d_steps = x_dx - rate * d_log_decay
    d_dt = d_steps * jax.nn.sigmoid(shifted_dt)
    grad_a_log = -jnp.sum(steps * rate * d_log_decay, axis=0)
    grad_dt_bias = jnp.sum(d_dt, axis=0)
    grad_skip = jnp.sum(jnp.sum(sums[8:], axis=0).reshape(HEADS, HEAD_DIM), axis=1)
    grad_gated = jnp.sum(sums[:8], axis=0)

    d_xr = jnp.concatenate([d_xs, d_bc_low], axis=1)
    d_xr = lax.dynamic_update_slice_in_dim(d_xr, d_last.astype(BF), row_count - LEAD, 0)
    d_x = jnp.concatenate([d_xr, d_dt.astype(BF)], axis=1)
    d_x_both = jnp.concatenate([d_x, swap(d_x, "core")], axis=0)
    sum_in_x = reduce_columns(normed_mine, d_x_both)
    d_normed = mm_nt(d_z, weight_z) + mm_nt(d_x, weight_x)

    rows_value, scale = extended[LEAD:], rms[LEAD:]
    unit = rows_value * scale
    pulled = d_normed * full_gain
    d_rows = scale * (pulled - unit * jnp.mean(pulled * unit, axis=-1, keepdims=True))
    grad_tokens = out_grad.astype(F32) + d_rows
    grad_gain = jnp.sum(d_normed * unit, axis=0)

    per_device = jnp.concatenate(
        [
            grad_gain.reshape(count, -1),
            jnp.moveaxis(conv_sums[:CONV_K].reshape(CONV_K, count, -1), 1, 0).reshape(count, -1),
            conv_sums[CONV_K].reshape(count, -1),
            grad_gated.reshape(count, -1),
            jnp.broadcast_to(
                jnp.concatenate([grad_dt_bias, grad_a_log, grad_skip])[None], (count, 3 * HEADS)
            ),
        ],
        axis=1,
    )
    small_sums = jnp.sum(lax.all_to_all(per_device, EVERY, 0, 0, tiled=True), axis=0)
    cuts = [norm_gain.size, conv_weight.size, conv_bias.size, gated_gain.size, HEADS, HEADS]
    cuts = [sum(cuts[: i + 1]) for i in range(6)]
    sum_gain, sum_conv, sum_bias, sum_gated, sum_dt, sum_log, sum_skip = jnp.split(small_sums, cuts)
    return (
        layer_out,
        grad_tokens,
        sum_gain,
        jnp.concatenate([sum_in_z, sum_in_x], axis=1),
        sum_conv.reshape(conv_weight.shape),
        sum_bias,
        sum_dt,
        sum_log,
        sum_skip,
        sum_gated,
        sum_out,
    )


def solution(mesh):
    x = mesh.shape["dp"] // 2
    y = x
    z = mesh.shape["ctx"] // y
    fine = Mesh(mesh.devices.reshape(x, 2, z, y), EVERY)
    rows = P(EVERY, None)
    flat = P(EVERY)
    in_specs = (
        rows, rows, P(("x", "core"), None), flat, rows, P(None, EVERY), flat,
        P(), P(), P(), flat, rows,
    )
    out_specs = (rows, rows, flat, rows, P(None, EVERY), flat, P(), P(), P(), flat, rows)
    return jax.shard_map(shards, mesh=fine, in_specs=in_specs, out_specs=out_specs, check_vma=False)
```

time: 2170 us -> 847 us (0.39)
  waiting for transfers between devices: 1030 us -> 259 us
  local copies, waits for them, and re-layouts: 450 us -> 120 us
  matrix products: 308 us -> 88.3 us
  starting transfers between devices: 5.14 us -> 141 us
  Pallas kernels: 0 us -> 134 us
  blocking collectives: 130 us -> 0 us
  other arithmetic: 186 us -> 76.4 us
    reduce_scatter x2 -> x0, waiting for transfers between devices: 581 us -> none  [the longest x1 371 us: shards(): lax.psum_scatter(grad_in_weight, ('dp', 'ctx'), scatter_dimension=0, tile...]
    dynamic_update_slice x12 -> x0, local copies, waits for them, and re-layouts: 276 us -> none  [local_scan(): lax.scan(jax.checkpoint(span_step), start_state, pieces)]
    all_gather x4 -> x3, waiting for transfers between devices: 372 us -> 107 us  [the longest x1 58.3 us: shards(): weight_x = lax.all_gather(in_weight[:, INNER:], EVERY, axis=0, tiled=True)]
    dot_general x37 -> x14, matrix products: 308 us -> 88.3 us  [the longest x3 29.9 us: mm(): return jnp.dot(left, right, preferred_element_type=F32)]
    ppermute x2 -> x66, waiting for transfers between devices: 0.01 us -> 152 us  [the longest x22 71.7 us: swap(): return lax.ppermute(array, axis, [(0, 1), (1, 0)])]
    pallas_call x0 -> x7, Pallas kernels: none -> 134 us  [call(): pl.pallas_call(body, grid=(grid,), in_specs=in_specs, out_specs=[spec for...]
    ppermute x2 -> x66, starting transfers between devices: 4.69 us -> 130 us  [the longest x18 73.4 us: line_sum(): got_up = lax.ppermute(up, axis, [(i, i + 1) for i in range(step)])]
    all_gather x2 -> x0, blocking collectives: 85.8 us -> none  [the longest x1 67.4 us: shards(): lax.all_gather(conv_weight, ('dp', 'ctx'), axis=1, tiled=True)]
  transfers between devices with their start and end apart: 9 -> 71, of which waited for: 7 -> 23; matrix products, arithmetic and copies ran while one was open for 6% -> 34% of each run, Pallas kernels for 0% -> 16%
where the time goes in v1:
time: 847 us; the launch traced here: 837 us
  waiting for transfers between devices  259 us (31%)
  starting transfers between devices  141 us (17%)
  Pallas kernels  134 us (16%)
  local copies, waits for them, and re-layouts  120 us (14%)
  matrix products  88.3 us (10%)
  other arithmetic  76.4 us (9%)
  between operations  17.6 us (2%)
    pallas_call x7, Pallas kernels, call(): pl.pallas_call(body, grid=(grid,), in_specs=in_specs, out_specs=[spec for...  134 us
    ppermute x18, starting transfers between devices, line_sum(): got_up = lax.ppermute(up, axis, [(i, i + 1) for i in range(step)])  73.4 us
    ppermute x22, waiting for transfers between devices, swap(): return lax.ppermute(array, axis, [(0, 1), (1, 0)])  71.7 us
    all_gather x1, waiting for transfers between devices, shards(): weight_x = lax.all_gather(in_weight[:, INNER:], EVERY, axis=0, tiled=True)  58.3 us
    all_gather x1, waiting for transfers between devices, shards(): weight_o = lax.all_gather(out_weight, EVERY, axis=0, tiled=True)  48.2 us
    unnamed x169, local copies, waits for them, and re-layouts  31.1 us
    dot_general x3, matrix products, mm(): return jnp.dot(left, right, preferred_element_type=F32)  29.9 us
    dot_general x3, matrix products, mm_nt(): lax.dot_general(left, right, (((1,), (1,)), ((), ())), preferred_element_...  29.1 us
  transfers between devices with their start and end apart: 71, of which 23 were waited for; matrix products, arithmetic and copies ran while one was open for 34% of the time, Pallas kernels for 16%

profile of v1, /device:TPU:0, one launch (start us, length us, event | category | flops | bytes accessed | tf_op | source)
XLA Modules:
  0.0 837.0 jit_solution(224978465877674037)
XLA Ops:
  15.4 7.3 all-to-all-start
  23.5 3.7 collective-permute-start
  43.7 58.3 %all-gather.4.cloned.1.call-done = bf16[1536,3376]{1,0:T(8,128)(2,1)} async-done(((bf16[48,3376]{1,0:T(8,128)(2,1)}), bf16[1536,3376]{1,0:T(8,128)(2,1)}) %all-gather.4.cloned.1.call-update) | async-done | bytes 10371088 | tf_op jit(solution)/shard_map/all_gather | solution.py:502
  102.0 10.2 %convolution_convert_fusion = bf16[528,3376]{1,0:T(8,128)(2,1)S(1)} fusion(bf16[528,1536]{1,0:T(8,128)(2,1)S(1)} %multiply_convert_fusion, bf16[1536,3376]{1,0:T(8,128)(2,1)} %all-gather.4.cloned.1.call-done), kind=kOutput, calls=%fused_computation | convolution fusion | flops 5477708800 | bytes 15558144 | tf_op jit(solution)/shard_map/dot_general | solution.py:73
  119.6 3.7 shard_map.203
  123.2 11.9 %shard_map.204 = (f32[512,3072]{1,0:T(8,128)}, f32[512,3072]{1,0:T(8,128)}, f32[128,3072]{1,0:T(8,128)}) custom-call(bf16[528,3072]{1,0:T(8,128)(2,1)} %slice.179.x_ref.in_ref, f32[8,3072]{1,0:T(8,128)} %slice.180.w_ref, f32[1,3072]{1,0:T(1,128)} %slice.181.b_ref, f32[512,128]{1,0:T(8,128)} %pad.26.m_ref, f32[512,128]{1,0:T(8,128)} %pad.27.wl_ref, ...), custom_call_target="tpu_custom_call" | custom-call | tf_op jit(solution)/shard_map/pallas_call | solution.py:36
  139.6 20.8 %collective-permute-done.1 = f32[1,1536]{1,0:T(1,128)S(1)} collective-permute-done((f32[1,1536]{1,0:T(1,128)S(1)}, f32[1,1536]{1,0:T(1,128)S(1)}, u32[]{:S(2)}, u32[]{:S(2)}) %collective-permute-start.1) | collective-permute-done | bytes 6176 | tf_op jit(solution)/shard_map/ppermute | solution.py:350
  162.7 3.8 collective-permute-start.3
  171.9 22.9 %collective-permute-done.3 = f32[128,1536]{1,0:T(8,128)} collective-permute-done((f32[128,1536]{1,0:T(8,128)S(1)}, f32[128,1536]{1,0:T(8,128)}, u32[]{:S(2)}, u32[]{:S(2)}) %collective-permute-start.3) | collective-permute-done | bytes 786464 | tf_op jit(solution)/shard_map/ppermute | solution.py:392
  204.1 3.6 reshape.376
  207.7 4.9 constant_dynamic-slice_fusion.9
  212.6 4.8 copy.128
  217.4 3.3 copy.127
  228.0 9.3 %convolution_convert_fusion.1.z_ref = bf16[512,3072]{1,0:T(8,128)(2,1)} fusion(bf16[1536,3072]{1,0:T(8,128)(2,1)} %all-gather.6.cloned.1.call-done, bf16[528,1536]{1,0:T(8,128)(2,1)} %copy-done.14), kind=kOutput, calls=%fused_computation.1 | convolution fusion | flops 4833411072 | bytes 14155776 | tf_op jit(solution)/shard_map/dot_general | solution.py:73
  237.3 3.0 fusion.27
  242.2 48.2 %all-gather.8.cloned.1.call-done = bf16[3072,1536]{1,0:T(8,128)(2,1)} async-done(((bf16[96,1536]{1,0:T(8,128)(2,1)}), bf16[3072,1536]{1,0:T(8,128)(2,1)}) %all-gather.8.cloned.1.call-update) | async-done | bytes 9437200 | tf_op jit(solution)/shard_map/all_gather | solution.py:504
  290.3 10.6 %fusion.77.df_ref = f32[512,3072]{1,0:T(8,128)} fusion(bf16[512,1536]{1,0:T(8,128)(2,1)S(1)} %copy-done.16, bf16[3072,1536]{1,0:T(8,128)(2,1)} %all-gather.8.cloned.1.call-done), kind=kOutput, calls=%fused_computation.251 | convolution fusion | flops 4831838208 | bytes 17301504 | tf_op jit(solution)/shard_map/dot_general | solution.py:77
  310.3 23.8 %shard_map.205.y_ref = f32[512,3072]{1,0:T(8,128)} custom-call(f32[512,3072]{1,0:T(8,128)} %get-tuple-element.37.x_ref, f32[512,128]{1,0:T(8,128)} %pad.28.dt_ref, f32[1,3072]{1,0:T(1,128)} %broadcast_in_dim_reshape.3.skip_ref, f32[512,512]{1,0:T(8,128)} %get-tuple-element.38.s_ref, f32[12,512,4]{2,1,0:T(8,128)} %bitcast.193, f32[12,4,512]{2,1,0:T(4,128)} %reshape.370.row_ref), custom_call_target="tpu_custom_call" | custom-call | tf_op jit(solution)/shard_map/pallas_call | solution.py:36
  334.2 3.4 multiply_add_fusion.1
  337.6 31.1 %shard_map.206 = (bf16[512,3072]{1,0:T(8,128)(2,1)}, bf16[512,3072]{1,0:T(8,128)(2,1)}, f32[512,3072]{1,0:T(8,128)}, f32[128,3072]{1,0:T(8,128)}, f32[512,128]{1...) custom-call(f32[512,3072]{1,0:T(8,128)} %shard_map.205.y_ref, bf16[512,3072]{1,0:T(8,128)(2,1)} %convolution_convert_fusion.1.z_ref, ...), custom_call_target="tpu_custom_call" | custom-call | tf_op jit(solution)/shard_map/pallas_call | solution.py:36
  368.7 7.5 reshape.384
  376.2 9.1 %constant_dynamic-slice_fusion.3 = (bf16[512,2,1,768]{3,2,1,0:T(2,128)(2,1)}, bf16[512,2,1,768]{3,2,1,0:T(2,128)(2,1)}) fusion(bf16[512,2,2,768]{3,2,1,0:T(2,128)(2,1)S(1)} %reshape.384, s32[]{:T(128)S(6)} %select_n.293, s32[]{:T(128)S(6)} %select_n.294), kind=kLoop, calls=%fused_computation.176 | loop fusion | bytes 6291464 | tf_op jit(solution)/shard_map/jit(dynamic_index_in_dim)/dynamic_slice | solution.py:445
  385.3 8.3 copy.133
  394.5 10.4 %fusion.12 = bf16[512,1536]{1,0:T(8,128)(2,1)} fusion(bf16[512,3072]{1,0:T(8,128)(2,1)} %get-tuple-element.41, bf16[3072,1536]{1,0:T(8,128)(2,1)} %all-gather.8.cloned.1.call-done, bf16[512,1536]{1,0:T(8,128)(2,1)S(1)} %copy-done.1), kind=kOutput, calls=%fused_computation.27 | convolution fusion | flops 4834197504 | bytes 15728640 | tf_op jit(solution)/shard_map/dot_general | solution.py:73
  405.0 9.1 %collective-permute-done.7 = f32[128,1536]{1,0:T(8,128)S(1)} collective-permute-done((f32[128,1536]{1,0:T(8,128)S(1)}, f32[128,1536]{1,0:T(8,128)S(1)}, u32[]{:S(2)}, u32[]{:S(2)}) %collective-permute-start.7) | collective-permute-done | bytes 786464 | tf_op jit(solution)/shard_map/ppermute | solution.py:350
  416.9 6.7 fusion.78
  423.6 6.1 copy.132
  429.7 4.7 fusion.14
  436.8 3.5 multiply_add_fusion.4
  442.1 4.2 fusion.13
  450.9 32.9 %shard_map.207 = (f32[512,3072]{1,0:T(8,128)}, f32[512,256]{1,0:T(8,128)}) custom-call(f32[512,3072]{1,0:T(8,128)} %get-tuple-element.37.x_ref, f32[512,3072]{1,0:T(8,128)} %get-tuple-element.43.dy_ref, f32[512,128]{1,0:T(8,128)} %pad.28.dt_ref, f32[512,512]{1,0:T(8,128)} %get-tuple-element.44.st_ref, f32[12,512,4]{2,1,0:T(8,128)} %bitcast.194, ...), custom_call_target="tpu_custom_call" | custom-call | tf_op jit(solution)/shard_map/pallas_call | solution.py:36
  495.9 3.9 fusion.10
  501.8 4.8 collective-permute-done.10
  508.3 3.7 fusion.8
  525.3 5.1 collective-permute-start.53
  534.7 27.3 %shard_map.208 = (bf16[512,3072]{1,0:T(8,128)(2,1)}, f32[32,3072]{1,0:T(8,128)}, f32[8,3072]{1,0:T(8,128)}, f32[512,128]{1,0:T(8,128)}, f32[512,128]{1,0:T(8,128)}) custom-call(f32[512,3072]{1,0:T(8,128)} %get-tuple-element.45.dx_ref, f32[512,3072]{1,0:T(8,128)} %get-tuple-element.37.x_ref, f32[512,3072]{1,0:T(8,128)} %get-tuple-element.43.dy_ref, ...), custom_call_target="tpu_custom_call" | custom-call | tf_op jit(solution)/shard_map/pallas_call | solution.py:36
  584.5 5.6 collective-permute-start.54
  592.2 16.1 %collective-permute-done.12 = f32[16,3328]{1,0:T(8,128)S(1)} collective-permute-done((f32[16,3328]{1,0:T(8,128)}, f32[16,3328]{1,0:T(8,128)S(1)}, u32[]{:S(2)}, u32[]{:S(2)}) %collective-permute-start.12) | collective-permute-done | bytes 213024 | tf_op jit(solution)/shard_map/ppermute | solution.py:356
  610.6 11.8 %multiply_reduce_fusion.1 = (f32[1536]{0:T(1024)S(1)}, f32[512]{0:T(512)S(1)}, f32[512,1536]{1,0:T(8,128)}) fusion(f32[528,1536]{1,0:T(8,128)S(1)} %copy-done.5, f32[512]{0:T(512)S(1)} %slice.162, f32[1536]{0:T(1024)S(1)} %copy-done.57, f32[512,1536]{1,0:T(8,128)} %fusion.78, bf16[1536,3376]{1,0:T(8,128)(2,1)} %all-gather.4.cloned.1.call-done, ...), kind=kOutput, calls=%fused_computation.24 | convolution fusion | flops 5322405888 | bytes 23281664 | tf_op jit(solution)/shard_map/dot_general | solution.py:77
  623.5 3.5 all-to-all-start.1
  626.9 5.9 multiply_add_fusion
  633.1 3.6 copy.114
  636.7 4.4 collective-permute-start.62
  664.7 6.8 collective-permute-done.16
  671.7 4.9 collective-permute-start.17
  679.5 4.5 collective-permute-done.17
  684.0 4.4 collective-permute-start.18
  690.4 4.4 collective-permute-start.26
  698.1 5.7 collective-permute-start.19
  705.3 5.2 collective-permute-start.27
  714.9 5.8 copy.115
  720.7 5.1 fusion.2
  727.5 4.1 fusion
  735.8 16.5 %collective-permute-done.32 = bf16[4,2,48,1664]{3,2,0,1:T(8,128)(2,1)S(1)} collective-permute-done((bf16[4,2,48,1664]{3,2,0,1:T(8,128)(2,1)S(1)}, bf16[4,2,48,1664]{3,2,0,1:T(8,128)(2,1)S(1)}, u32[]{:S(2)}, u32[]{:S(2)}) %collective-permute-start.32) | collective-permute-done | bytes 1277984 | tf_op jit(solution)/shard_map/ppermute | solution.py:350
  754.1 10.9 %collective-permute-done.40 = bf16[2,4,48,1712]{3,2,1,0:T(8,128)(2,1)S(1)} collective-permute-done((bf16[2,4,48,1712]{3,2,1,0:T(8,128)(2,1)S(1)}, bf16[2,4,48,1712]{3,2,1,0:T(8,128)(2,1)S(1)}, u32[]{:S(2)}, u32[]{:S(2)}) %collective-permute-start.40) | collective-permute-done | bytes 1314848 | tf_op jit(solution)/shard_map/ppermute | solution.py:350
  766.0 7.6 collective-permute-done.33
  773.8 5.2 collective-permute-start.34
  779.9 3.1 collective-permute-start.42
  786.0 4.4 collective-permute-start.35
  793.4 4.4 collective-permute-start.43
  801.0 5.0 collective-permute-start.36
  808.4 5.0 collective-permute-start.44
  816.1 6.8 collective-permute-done.39
  823.0 6.1 collective-permute-done.47
  (450 shorter events, 206.9 us)
Async XLA Ops:
  7.2 94.8 %all-gather.4.cloned.1.call-start = ((), (), s32[]{:S(2)}) async-start(), calls=%async_computation.2 | async-start | bytes 10948608 | tf_op jit(solution)/shard_map/all_gather | solution.py:502
  9.1 218.9 %all-gather.6.cloned.1.call-start = ((), (), s32[]{:S(2)}) async-start(), calls=%async_computation.3 | async-start | bytes 9732096 | tf_op jit(solution)/shard_map/all_gather | solution.py:503
  10.9 279.5 %all-gather.8.cloned.1.call-start = ((), (), s32[]{:S(2)}) async-start(), calls=%async_computation.4 | async-start | bytes 9732096 | tf_op jit(solution)/shard_map/all_gather | solution.py:504
  15.4 24.7 %all-to-all-start = ((bf16[32,2,332]{2,1,0:T(2,128)(2,1)}), bf16[32,2,332]{2,1,0:T(2,128)(2,1)S(1)}, u32[]{:S(2)}, u32[]{:S(2)}) async-start(bf16[32,2,332]{2,1,0:T(2,128)(2,1)} %reshape.407), calls=%async_computation | async-start | bytes 98304 | tf_op jit(solution)/shard_map/all_to_all | solution.py:458
  23.5 16.2 %collective-permute-start = (bf16[16,1536]{1,0:T(8,128)(2,1)S(1)}, bf16[16,1536]{1,0:T(8,128)(2,1)S(1)}, u32[]{:S(2)}, u32[]{:S(2)}) collective-permute-start(bf16[16,1536]{1,0:T(8,128)(2,1)S(1)} %slice.142), channel_id=1, source_target_pairs={{0,1},{1,2},{2,3},{3,4},{4,5},{5,6},{6,7},{8,9},{9,10},{10,11},{11... | collective-permute-start | bytes 147464 | tf_op jit(solution)/shard_map/ppermute | solution.py:356
  137.2 23.9 %collective-permute-start.2 = (f32[128,1536]{1,0:T(8,128)}, f32[128,1536]{1,0:T(8,128)S(1)}, u32[]{:S(2)}, u32[]{:S(2)}) collective-permute-start(f32[128,1536]{1,0:T(8,128)} %constant_dynamic-slice_fusion.11), channel_id=1, source_target_pairs={{0,1},{1,0},{2,3},{3,2},{4,5},{5,4},{6,7},{7,6},{8,9},{9,8},{10,11... | collective-permute-start | bytes 2359304 | tf_op jit(solution)/shard_map/ppermute | solution.py:350
  139.0 21.5 %collective-permute-start.1 = (f32[1,1536]{1,0:T(1,128)S(1)}, f32[1,1536]{1,0:T(1,128)S(1)}, u32[]{:S(2)}, u32[]{:S(2)}) collective-permute-start(f32[1,1536]{1,0:T(1,128)S(1)} %dynamic_slice.226), channel_id=1, source_target_pairs={{0,1},{1,0},{2,3},{3,2},{4,5},{5,4},{6,7},{7,6},{8,9},{9,8},{10,11... | collective-permute-start | bytes 18440 | tf_op jit(solution)/shard_map/ppermute | solution.py:350
  162.7 32.1 %collective-permute-start.3 = (f32[128,1536]{1,0:T(8,128)S(1)}, f32[128,1536]{1,0:T(8,128)}, u32[]{:S(2)}, u32[]{:S(2)}) collective-permute-start(f32[128,1536]{1,0:T(8,128)S(1)} %select_add_fusion.1), channel_id=1, source_target_pairs={{0,2},{1,3},{8,10},{9,11},{16,18},{17,19},{24,26},{25,27}} | collective-permute-start | bytes 2359304 | tf_op jit(solution)/shard_map/ppermute | solution.py:392
  166.4 54.2 %collective-permute-start.49 = (bf16[512,1536]{1,0:T(8,128)(2,1)}, bf16[512,1536]{1,0:T(8,128)(2,1)}, u32[]{:S(2)}, u32[]{:S(2)}) collective-permute-start(bf16[512,1536]{1,0:T(8,128)(2,1)} %param.13), channel_id=1, source_target_pairs={{0,8},{8,0},{1,9},{9,1},{2,10},{10,2},{3,11},{11,3},{4,12},{12,4},... | collective-permute-start | bytes 4718600 | tf_op jit(solution)/shard_map/ppermute | solution.py:350
  197.1 26.3 %collective-permute-start.4 = (f32[128,1536]{1,0:T(8,128)}, f32[128,1536]{1,0:T(8,128)}, u32[]{:S(2)}, u32[]{:S(2)}) collective-permute-start(f32[128,1536]{1,0:T(8,128)} %multiply_add_fusion.7), channel_id=1, source_target_pairs={{2,4},{3,5},{10,12},{11,13},{18,20},{19,21},{26,28},{27,29}} | collective-permute-start | bytes 2359304 | tf_op jit(solution)/shard_map/ppermute | solution.py:392
  217.4 278.4 %collective-permute-start.13 = (bf16[512,768]{0,1:T(8,128)(2,1)}, bf16[512,768]{0,1:T(8,128)(2,1)}, u32[]{:S(2)}, u32[]{:S(2)}) collective-permute-start(bf16[512,768]{0,1:T(8,128)(2,1)} %bitcast.14), channel_id=1, source_target_pairs={{0,8},{8,0},{1,9},{9,1},{2,10},{10,2},{3,11},{11,3},{4,12},{12,4},... | collective-permute-start | bytes 2359304 | tf_op jit(solution)/shard_map/ppermute | solution.py:350
  240.2 94.0 %collective-permute-start.6 = (f32[128,1536]{1,0:T(8,128)}, f32[128,1536]{1,0:T(8,128)}, u32[]{:S(2)}, u32[]{:S(2)}) collective-permute-start(f32[128,1536]{1,0:T(8,128)} %get-tuple-element.83), channel_id=1, source_target_pairs={{0,1},{1,0},{2,3},{3,2},{4,5},{5,4},{6,7},{7,6},{8,9},{9,8},{10,11... | collective-permute-start | bytes 2359304 | tf_op jit(solution)/shard_map/ppermute | solution.py:350
  393.6 36.1 %collective-permute-start.48 = (bf16[512,1536]{0,1:T(8,128)(2,1)}, bf16[512,1536]{0,1:T(8,128)(2,1)}, u32[]{:S(2)}, u32[]{:S(2)}) collective-permute-start(bf16[512,1536]{0,1:T(8,128)(2,1)} %bitcast.209), channel_id=1, source_target_pairs={{0,8},{8,0},{1,9},{9,1},{2,10},{10,2},{3,11},{11,3},{4,12},{12,4},... | collective-permute-start | bytes 4718600 | tf_op jit(solution)/shard_map/ppermute | solution.py:350
  393.9 99.9 %collective-permute-start.14 = (bf16[512,3072]{1,0:T(8,128)(2,1)}, bf16[512,3072]{1,0:T(8,128)(2,1)}, u32[]{:S(2)}, u32[]{:S(2)}) collective-permute-start(bf16[512,3072]{1,0:T(8,128)(2,1)} %get-tuple-element.42), channel_id=1, source_target_pairs={{0,8},{8,0},{1,9},{9,1},{2,10},{10,2},{3,11},{11,3},{4,12},{12,4},... | collective-permute-start | bytes 9437192 | tf_op jit(solution)/shard_map/ppermute | solution.py:350
  394.2 19.8 %collective-permute-start.7 = (f32[128,1536]{1,0:T(8,128)S(1)}, f32[128,1536]{1,0:T(8,128)S(1)}, u32[]{:S(2)}, u32[]{:S(2)}) collective-permute-start(f32[128,1536]{1,0:T(8,128)S(1)} %constant_dynamic-slice_fusion.10), channel_id=1, source_target_pairs={{0,1},{1,0},{2,3},{3,2},{4,5},{5,4},{6,7},{7,6},{8,9},{9,8},{10,11... | collective-permute-start | bytes 2359304 | tf_op jit(solution)/shard_map/ppermute | solution.py:350
  415.2 21.6 %collective-permute-start.8 = (f32[128,1536]{1,0:T(8,128)}, f32[128,1536]{1,0:T(8,128)}, u32[]{:S(2)}, u32[]{:S(2)}) collective-permute-start(f32[128,1536]{1,0:T(8,128)} %select_add_fusion), channel_id=1, source_target_pairs={{6,4},{7,5},{14,12},{15,13},{22,20},{23,21},{30,28},{31,29}} | collective-permute-start | bytes 2359304 | tf_op jit(solution)/shard_map/ppermute | solution.py:392
  435.6 51.5 %collective-permute-start.50 = (bf16[4,2,96,768]{3,2,0,1:T(8,128)(2,1)}, bf16[4,2,96,768]{3,2,0,1:T(8,128)(2,1)}, u32[]{:S(2)}, u32[]{:S(2)}) collective-permute-start(bf16[4,2,96,768]{3,2,0,1:T(8,128)(2,1)} %fusion.20), channel_id=1, source_target_pairs={{0,16},{16,0},{1,17},{17,1},{2,18},{18,2},{3,19},{19,3},{4,20},{20... | collective-permute-start | bytes 3538952 | tf_op jit(solution)/shard_map/ppermute | solution.py:350
  440.3 43.5 %collective-permute-start.9 = (f32[128,1536]{1,0:T(8,128)}, f32[128,1536]{1,0:T(8,128)}, u32[]{:S(2)}, u32[]{:S(2)}) collective-permute-start(f32[128,1536]{1,0:T(8,128)} %multiply_add_fusion.4), channel_id=1, source_target_pairs={{4,2},{5,3},{12,10},{13,11},{20,18},{21,19},{28,26},{29,27}} | collective-permute-start | bytes 2359304 | tf_op jit(solution)/shard_map/ppermute | solution.py:392
  447.6 42.8 %collective-permute-start.58 = (bf16[2,4,96,768]{3,2,1,0:T(8,128)(2,1)}, bf16[2,4,96,768]{3,2,1,0:T(8,128)(2,1)}, u32[]{:S(2)}, u32[]{:S(2)}) collective-permute-start(bf16[2,4,96,768]{3,2,1,0:T(8,128)(2,1)} %fusion.22), channel_id=1, source_target_pairs={{0,1},{1,0},{2,3},{3,2},{4,5},{5,4},{6,7},{7,6},{8,9},{9,8},{10,11... | collective-permute-start | bytes 3538952 | tf_op jit(solution)/shard_map/ppermute | solution.py:350
  485.6 21.0 %collective-permute-start.10 = (f32[128,1536]{1,0:T(8,128)S(1)}, f32[128,1536]{1,0:T(8,128)S(1)}, u32[]{:S(2)}, u32[]{:S(2)}) collective-permute-start(f32[128,1536]{1,0:T(8,128)S(1)} %get-tuple-element.75), channel_id=1, source_target_pairs={{2,0},{3,1},{10,8},{11,9},{18,16},{19,17},{26,24},{27,25}} | collective-permute-start | bytes 2359304 | tf_op jit(solution)/shard_map/ppermute | solution.py:392
  488.8 23.2 %collective-permute-start.51 = (bf16[4,96,768]{2,1,0:T(8,128)(2,1)S(1)}, bf16[4,96,768]{2,1,0:T(8,128)(2,1)S(1)}, u32[]{:S(2)}, u32[]{:S(2)}) collective-permute-start(bf16[4,96,768]{2,1,0:T(8,128)(2,1)S(1)} %fusion.33), channel_id=1, source_target_pairs={{0,1},{1,0},{2,3},{3,2},{4,5},{5,4},{6,7},{7,6},{8,9},{9,8},{10,11... | collective-permute-start | bytes 1769480 | tf_op jit(solution)/shard_map/ppermute | solution.py:350
  492.3 22.2 %collective-permute-start.59 = (bf16[4,96,768]{2,1,0:T(8,128)(2,1)S(1)}, bf16[4,96,768]{2,1,0:T(8,128)(2,1)S(1)}, u32[]{:S(2)}, u32[]{:S(2)}) collective-permute-start(bf16[4,96,768]{2,1,0:T(8,128)(2,1)S(1)} %fusion.34), channel_id=1, source_target_pairs={{0,16},{16,0},{1,17},{17,1},{2,18},{18,2},{3,19},{19,3},{4,20},{20... | collective-permute-start | bytes 1769480 | tf_op jit(solution)/shard_map/ppermute | solution.py:350
  501.1 143.6 %collective-permute-start.15 = (bf16[4,2,48,1536]{3,2,0,1:T(8,128)(2,1)}, bf16[4,2,48,1536]{3,2,0,1:T(8,128)(2,1)}, u32[]{:S(2)}, u32[]{:S(2)}) collective-permute-start(bf16[4,2,48,1536]{3,2,0,1:T(8,128)(2,1)} %fusion.19), channel_id=1, source_target_pairs={{0,16},{16,0},{1,17},{17,1},{2,18},{18,2},{3,19},{19,3},{4,20},{20... | collective-permute-start | bytes 3538952 | tf_op jit(solution)/shard_map/ppermute | solution.py:350
  507.0 24.2 %collective-permute-start.11 = (f32[128,1536]{1,0:T(8,128)S(1)}, f32[128,1536]{1,0:T(8,128)S(1)}, u32[]{:S(2)}, u32[]{:S(2)}) collective-permute-start(f32[128,1536]{1,0:T(8,128)S(1)} %get-tuple-element.82), channel_id=1, source_target_pairs={{0,1},{1,0},{2,3},{3,2},{4,5},{5,4},{6,7},{7,6},{8,9},{9,8},{10,11... | collective-permute-start | bytes 2359304 | tf_op jit(solution)/shard_map/ppermute | solution.py:350
  518.4 60.1 %collective-permute-start.55 = (f32[96,768]{1,0:T(8,128)}, f32[96,768]{1,0:T(8,128)}, u32[]{:S(2)}, u32[]{:S(2)}) collective-permute-start(f32[96,768]{1,0:T(8,128)} %get-tuple-element.102), channel_id=1, source_target_pairs={{6,4},{7,5},{14,12},{15,13},{22,20},{23,21},{30,28},{31,29}} | collective-permute-start | bytes 884744 | tf_op jit(solution)/shard_map/ppermute | solution.py:413
  521.9 61.1 %collective-permute-start.63 = (f32[96,768]{1,0:T(8,128)}, f32[96,768]{1,0:T(8,128)}, u32[]{:S(2)}, u32[]{:S(2)}) collective-permute-start(f32[96,768]{1,0:T(8,128)} %get-tuple-element.106), channel_id=1, source_target_pairs={{6,4},{7,5},{14,12},{15,13},{22,20},{23,21},{30,28},{31,29}} | collective-permute-start | bytes 884744 | tf_op jit(solution)/shard_map/ppermute | solution.py:413
  525.3 54.3 %collective-permute-start.53 = (f32[96,768]{1,0:T(8,128)}, f32[96,768]{1,0:T(8,128)}, u32[]{:S(2)}, u32[]{:S(2)}) collective-permute-start(f32[96,768]{1,0:T(8,128)} %bitcast_add_fusion.29), channel_id=1, source_target_pairs={{0,2},{2,4},{1,3},{3,5},{8,10},{10,12},{9,11},{11,13},{16,18},{18,... | collective-permute-start | bytes 884744 | tf_op jit(solution)/shard_map/ppermute | solution.py:412
  531.2 53.3 %collective-permute-start.61 = (f32[96,768]{1,0:T(8,128)}, f32[96,768]{1,0:T(8,128)}, u32[]{:S(2)}, u32[]{:S(2)}) collective-permute-start(f32[96,768]{1,0:T(8,128)} %bitcast_add_fusion.24), channel_id=1, source_target_pairs={{0,2},{2,4},{1,3},{3,5},{8,10},{10,12},{9,11},{11,13},{16,18},{18,... | collective-permute-start | bytes 884744 | tf_op jit(solution)/shard_map/ppermute | solution.py:412
  578.5 69.9 %collective-permute-start.23 = (bf16[2,4,48,1536]{3,2,1,0:T(8,128)(2,1)}, bf16[2,4,48,1536]{3,2,1,0:T(8,128)(2,1)}, u32[]{:S(2)}, u32[]{:S(2)}) collective-permute-start(bf16[2,4,48,1536]{3,2,1,0:T(8,128)(2,1)} %fusion.21), channel_id=1, source_target_pairs={{0,1},{1,0},{2,3},{3,2},{4,5},{5,4},{6,7},{7,6},{8,9},{9,8},{10,11... | collective-permute-start | bytes 3538952 | tf_op jit(solution)/shard_map/ppermute | solution.py:350
  579.6 28.6 %collective-permute-start.12 = (f32[16,3328]{1,0:T(8,128)}, f32[16,3328]{1,0:T(8,128)S(1)}, u32[]{:S(2)}, u32[]{:S(2)}) collective-permute-start(f32[16,3328]{1,0:T(8,128)} %slice.189), channel_id=1, source_target_pairs={{1,0},{2,1},{3,2},{4,3},{5,4},{6,5},{7,6},{9,8},{10,9},{11,10},{12... | collective-permute-start | bytes 638984 | tf_op jit(solution)/shard_map/ppermute | solution.py:356
  583.1 53.6 %collective-permute-start.56 = (f32[96,768]{1,0:T(8,128)}, f32[96,768]{1,0:T(8,128)}, u32[]{:S(2)}, u32[]{:S(2)}) collective-permute-start(f32[96,768]{1,0:T(8,128)} %get-tuple-element.100), channel_id=1, source_target_pairs={{6,4},{4,2},{7,5},{5,3},{14,12},{12,10},{15,13},{13,11},{22,20},{2... | collective-permute-start | bytes 884744 | tf_op jit(solution)/shard_map/ppermute | solution.py:413
  584.5 71.2 %collective-permute-start.54 = (f32[96,768]{1,0:T(8,128)}, f32[96,768]{1,0:T(8,128)}, u32[]{:S(2)}, u32[]{:S(2)}) collective-permute-start(f32[96,768]{1,0:T(8,128)} %get-tuple-element.99), channel_id=1, source_target_pairs={{0,2},{2,4},{4,6},{1,3},{3,5},{5,7},{8,10},{10,12},{12,14},{9,11},... | collective-permute-start | bytes 884744 | tf_op jit(solution)/shard_map/ppermute | solution.py:412
  608.2 34.6 %collective-permute-start.64 = (f32[96,768]{1,0:T(8,128)}, f32[96,768]{1,0:T(8,128)}, u32[]{:S(2)}, u32[]{:S(2)}) collective-permute-start(f32[96,768]{1,0:T(8,128)} %get-tuple-element.104), channel_id=1, source_target_pairs={{6,4},{4,2},{7,5},{5,3},{14,12},{12,10},{15,13},{13,11},{22,20},{2... | collective-permute-start | bytes 884744 | tf_op jit(solution)/shard_map/ppermute | solution.py:413
  623.5 28.8 %all-to-all-start.1 = ((f32[32,1,808]{2,1,0:T(1,128)}), f32[32,1,808]{2,1,0:T(1,128)}, u32[]{:S(2)}, u32[]{:S(2)}) async-start(f32[32,1,808]{2,1,0:T(1,128)} %copy.108), calls=%async_computation.1 | async-start | bytes 229376 | tf_op jit(solution)/shard_map/all_to_all | solution.py:740
  636.7 23.2 %collective-permute-start.62 = (f32[96,768]{1,0:T(8,128)}, f32[96,768]{1,0:T(8,128)}, u32[]{:S(2)}, u32[]{:S(2)}) collective-permute-start(f32[96,768]{1,0:T(8,128)} %get-tuple-element.103), channel_id=1, source_target_pairs={{0,2},{2,4},{4,6},{1,3},{3,5},{5,7},{8,10},{10,12},{12,14},{9,11},... | collective-permute-start | bytes 884744 | tf_op jit(solution)/shard_map/ppermute | solution.py:412
  642.9 72.0 %collective-permute-start.31 = (bf16[512,3376]{0,1:T(8,128)(2,1)}, bf16[512,3376]{0,1:T(8,128)(2,1)}, u32[]{:S(2)}, u32[]{:S(2)}) collective-permute-start(bf16[512,3376]{0,1:T(8,128)(2,1)} %copy.114), channel_id=1, source_target_pairs={{0,8},{8,0},{1,9},{9,1},{2,10},{10,2},{3,11},{11,3},{4,12},{12,4},... | collective-permute-start | bytes 10371080 | tf_op jit(solution)/shard_map/ppermute | solution.py:350
  644.7 12.5 %collective-permute-start.57 = (f32[96,768]{1,0:T(8,128)}, f32[96,768]{1,0:T(8,128)}, u32[]{:S(2)}, u32[]{:S(2)}) collective-permute-start(f32[96,768]{1,0:T(8,128)} %bitcast_add_fusion.28), channel_id=1, source_target_pairs={{6,4},{4,2},{2,0},{7,5},{5,3},{3,1},{14,12},{12,10},{10,8},{15,13}... | collective-permute-start | bytes 884744 | tf_op jit(solution)/shard_map/ppermute | solution.py:413
  648.4 14.2 %collective-permute-start.65 = (f32[96,768]{1,0:T(8,128)}, f32[96,768]{1,0:T(8,128)}, u32[]{:S(2)}, u32[]{:S(2)}) collective-permute-start(f32[96,768]{1,0:T(8,128)} %bitcast_add_fusion.23), channel_id=1, source_target_pairs={{6,4},{4,2},{2,0},{7,5},{5,3},{3,1},{14,12},{12,10},{10,8},{15,13}... | collective-permute-start | bytes 884744 | tf_op jit(solution)/shard_map/ppermute | solution.py:413
  655.7 15.7 %collective-permute-start.16 = (bf16[4,48,1536]{2,1,0:T(8,128)(2,1)S(1)}, bf16[4,48,1536]{2,1,0:T(8,128)(2,1)S(1)}, u32[]{:S(2)}, u32[]{:S(2)}) collective-permute-start(bf16[4,48,1536]{2,1,0:T(8,128)(2,1)S(1)} %fusion.31), channel_id=1, source_target_pairs={{0,1},{1,0},{2,3},{3,2},{4,5},{5,4},{6,7},{7,6},{8,9},{9,8},{10,11... | collective-permute-start | bytes 1769480 | tf_op jit(solution)/shard_map/ppermute | solution.py:350
  657.2 20.1 %collective-permute-start.24 = (bf16[4,48,1536]{2,1,0:T(8,128)(2,1)S(1)}, bf16[4,48,1536]{2,1,0:T(8,128)(2,1)S(1)}, u32[]{:S(2)}, u32[]{:S(2)}) collective-permute-start(bf16[4,48,1536]{2,1,0:T(8,128)(2,1)S(1)} %fusion.32), channel_id=1, source_target_pairs={{0,16},{16,0},{1,17},{17,1},{2,18},{18,2},{3,19},{19,3},{4,20},{20... | collective-permute-start | bytes 1769480 | tf_op jit(solution)/shard_map/ppermute | solution.py:350
  671.7 12.4 %collective-permute-start.17 = (f32[48,1536]{1,0:T(8,128)S(1)}, f32[48,1536]{1,0:T(8,128)S(1)}, u32[]{:S(2)}, u32[]{:S(2)}) collective-permute-start(f32[48,1536]{1,0:T(8,128)S(1)} %get-tuple-element.109), channel_id=1, source_target_pairs={{0,2},{1,3},{8,10},{9,11},{16,18},{17,19},{24,26},{25,27}} | collective-permute-start | bytes 884744 | tf_op jit(solution)/shard_map/ppermute | solution.py:412
  676.6 18.2 %collective-permute-start.20 = (f32[48,1536]{1,0:T(8,128)S(1)}, f32[48,1536]{1,0:T(8,128)S(1)}, u32[]{:S(2)}, u32[]{:S(2)}) collective-permute-start(f32[48,1536]{1,0:T(8,128)S(1)} %get-tuple-element.110), channel_id=1, source_target_pairs={{6,4},{7,5},{14,12},{15,13},{22,20},{23,21},{30,28},{31,29}} | collective-permute-start | bytes 884744 | tf_op jit(solution)/shard_map/ppermute | solution.py:413
  677.5 12.8 %collective-permute-start.25 = (f32[48,1536]{1,0:T(8,128)S(1)}, f32[48,1536]{1,0:T(8,128)S(1)}, u32[]{:S(2)}, u32[]{:S(2)}) collective-permute-start(f32[48,1536]{1,0:T(8,128)S(1)} %get-tuple-element.113), channel_id=1, source_target_pairs={{0,2},{1,3},{8,10},{9,11},{16,18},{17,19},{24,26},{25,27}} | collective-permute-start | bytes 884744 | tf_op jit(solution)/shard_map/ppermute | solution.py:412
  678.8 25.1 %collective-permute-start.28 = (f32[48,1536]{1,0:T(8,128)S(1)}, f32[48,1536]{1,0:T(8,128)S(1)}, u32[]{:S(2)}, u32[]{:S(2)}) collective-permute-start(f32[48,1536]{1,0:T(8,128)S(1)} %get-tuple-element.114), channel_id=1, source_target_pairs={{6,4},{7,5},{14,12},{15,13},{22,20},{23,21},{30,28},{31,29}} | collective-permute-start | bytes 884744 | tf_op jit(solution)/shard_map/ppermute | solution.py:413
  684.0 12.6 %collective-permute-start.18 = (f32[48,1536]{1,0:T(8,128)S(1)}, f32[48,1536]{1,0:T(8,128)S(1)}, u32[]{:S(2)}, u32[]{:S(2)}) collective-permute-start(f32[48,1536]{1,0:T(8,128)S(1)} %bitcast_add_fusion.39), channel_id=1, source_target_pairs={{0,2},{2,4},{1,3},{3,5},{8,10},{10,12},{9,11},{11,13},{16,18},{18,... | collective-permute-start | bytes 884744 | tf_op jit(solution)/shard_map/ppermute | solution.py:412
  690.4 13.5 %collective-permute-start.26 = (f32[48,1536]{1,0:T(8,128)S(1)}, f32[48,1536]{1,0:T(8,128)S(1)}, u32[]{:S(2)}, u32[]{:S(2)}) collective-permute-start(f32[48,1536]{1,0:T(8,128)S(1)} %bitcast_add_fusion.34), channel_id=1, source_target_pairs={{0,2},{2,4},{1,3},{3,5},{8,10},{10,12},{9,11},{11,13},{16,18},{18,... | collective-permute-start | bytes 884744 | tf_op jit(solution)/shard_map/ppermute | solution.py:412
  697.4 13.1 %collective-permute-start.21 = (f32[48,1536]{1,0:T(8,128)S(1)}, f32[48,1536]{1,0:T(8,128)S(1)}, u32[]{:S(2)}, u32[]{:S(2)}) collective-permute-start(f32[48,1536]{1,0:T(8,128)S(1)} %get-tuple-element.108), channel_id=1, source_target_pairs={{6,4},{4,2},{7,5},{5,3},{14,12},{12,10},{15,13},{13,11},{22,20},{2... | collective-permute-start | bytes 884744 | tf_op jit(solution)/shard_map/ppermute | solution.py:413
  698.1 33.7 %collective-permute-start.19 = (f32[48,1536]{1,0:T(8,128)}, f32[48,1536]{1,0:T(8,128)}, u32[]{:S(2)}, u32[]{:S(2)}) collective-permute-start(f32[48,1536]{1,0:T(8,128)} %get-tuple-element.107), channel_id=1, source_target_pairs={{0,2},{2,4},{4,6},{1,3},{3,5},{5,7},{8,10},{10,12},{12,14},{9,11},... | collective-permute-start | bytes 884744 | tf_op jit(solution)/shard_map/ppermute | solution.py:412
  705.3 29.2 %collective-permute-start.27 = (f32[48,1536]{1,0:T(8,128)}, f32[48,1536]{1,0:T(8,128)}, u32[]{:S(2)}, u32[]{:S(2)}) collective-permute-start(f32[48,1536]{1,0:T(8,128)} %get-tuple-element.111), channel_id=1, source_target_pairs={{0,2},{2,4},{4,6},{1,3},{3,5},{5,7},{8,10},{10,12},{12,14},{9,11},... | collective-permute-start | bytes 884744 | tf_op jit(solution)/shard_map/ppermute | solution.py:412
  711.3 22.1 %collective-permute-start.22 = (f32[48,1536]{1,0:T(8,128)}, f32[48,1536]{1,0:T(8,128)}, u32[]{:S(2)}, u32[]{:S(2)}) collective-permute-start(f32[48,1536]{1,0:T(8,128)} %bitcast_add_fusion.38), channel_id=1, source_target_pairs={{6,4},{4,2},{2,0},{7,5},{5,3},{3,1},{14,12},{12,10},{10,8},{15,13}... | collective-permute-start | bytes 884744 | tf_op jit(solution)/shard_map/ppermute | solution.py:413
  713.4 21.2 %collective-permute-start.30 = (f32[48,1536]{1,0:T(8,128)}, f32[48,1536]{1,0:T(8,128)}, u32[]{:S(2)}, u32[]{:S(2)}) collective-permute-start(f32[48,1536]{1,0:T(8,128)} %bitcast_add_fusion.33), channel_id=1, source_target_pairs={{6,4},{4,2},{2,0},{7,5},{5,3},{3,1},{14,12},{12,10},{10,8},{15,13}... | collective-permute-start | bytes 884744 | tf_op jit(solution)/shard_map/ppermute | solution.py:413
  725.9 26.3 %collective-permute-start.32 = (bf16[4,2,48,1664]{3,2,0,1:T(8,128)(2,1)S(1)}, bf16[4,2,48,1664]{3,2,0,1:T(8,128)(2,1)S(1)}, u32[]{:S(2)}, u32[]{:S(2)}) collective-permute-start(bf16[4,2,48,1664]{3,2,0,1:T(8,128)(2,1)S(1)} %fusion.18), channel_id=1, source_target_pairs={{0,16},{16,0},{1,17},{17,1},{2,18},{18,2},{3,19},{19,3},{4,20},{20... | collective-permute-start | bytes 3833864 | tf_op jit(solution)/shard_map/ppermute | solution.py:350
  731.8 33.2 %collective-permute-start.40 = (bf16[2,4,48,1712]{3,2,1,0:T(8,128)(2,1)S(1)}, bf16[2,4,48,1712]{3,2,1,0:T(8,128)(2,1)S(1)}, u32[]{:S(2)}, u32[]{:S(2)}) collective-permute-start(bf16[2,4,48,1712]{3,2,1,0:T(8,128)(2,1)S(1)} %fusion.17), channel_id=1, source_target_pairs={{0,1},{1,0},{2,3},{3,2},{4,5},{5,4},{6,7},{7,6},{8,9},{9,8},{10,11... | collective-permute-start | bytes 3944456 | tf_op jit(solution)/shard_map/ppermute | solution.py:350
  752.5 21.1 %collective-permute-start.33 = (bf16[4,48,1664]{2,1,0:T(8,128)(2,1)S(1)}, bf16[4,48,1664]{2,1,0:T(8,128)(2,1)S(1)}, u32[]{:S(2)}, u32[]{:S(2)}) collective-permute-start(bf16[4,48,1664]{2,1,0:T(8,128)(2,1)S(1)} %fusion.30), channel_id=1, source_target_pairs={{0,1},{1,0},{2,3},{3,2},{4,5},{5,4},{6,7},{7,6},{8,9},{9,8},{10,11... | collective-permute-start | bytes 1916936 | tf_op jit(solution)/shard_map/ppermute | solution.py:350
  765.4 14.3 %collective-permute-start.41 = (bf16[4,48,1712]{2,1,0:T(8,128)(2,1)S(1)}, bf16[4,48,1712]{2,1,0:T(8,128)(2,1)S(1)}, u32[]{:S(2)}, u32[]{:S(2)}) collective-permute-start(bf16[4,48,1712]{2,1,0:T(8,128)(2,1)S(1)} %fusion.29), channel_id=1, source_target_pairs={{0,16},{16,0},{1,17},{17,1},{2,18},{18,2},{3,19},{19,3},{4,20},{20... | collective-permute-start | bytes 1972232 | tf_op jit(solution)/shard_map/ppermute | solution.py:350
  779.0 18.8 %collective-permute-start.37 = (f32[48,1664]{1,0:T(8,128)S(1)}, f32[48,1664]{1,0:T(8,128)S(1)}, u32[]{:S(2)}, u32[]{:S(2)}) collective-permute-start(f32[48,1664]{1,0:T(8,128)S(1)} %get-tuple-element.98), channel_id=1, source_target_pairs={{6,4},{7,5},{14,12},{15,13},{22,20},{23,21},{30,28},{31,29}} | collective-permute-start | bytes 958472 | tf_op jit(solution)/shard_map/ppermute | solution.py:413
  779.9 13.5 %collective-permute-start.42 = (f32[48,1712]{1,0:T(8,128)S(1)}, f32[48,1712]{1,0:T(8,128)S(1)}, u32[]{:S(2)}, u32[]{:S(2)}) collective-permute-start(f32[48,1712]{1,0:T(8,128)S(1)} %get-tuple-element.93), channel_id=1, source_target_pairs={{0,2},{1,3},{8,10},{9,11},{16,18},{17,19},{24,26},{25,27}} | collective-permute-start | bytes 986120 | tf_op jit(solution)/shard_map/ppermute | solution.py:412
  783.0 23.0 %collective-permute-start.45 = (f32[48,1712]{1,0:T(8,128)S(1)}, f32[48,1712]{1,0:T(8,128)S(1)}, u32[]{:S(2)}, u32[]{:S(2)}) collective-permute-start(f32[48,1712]{1,0:T(8,128)S(1)} %get-tuple-element.94), channel_id=1, source_target_pairs={{6,4},{7,5},{14,12},{15,13},{22,20},{23,21},{30,28},{31,29}} | collective-permute-start | bytes 986120 | tf_op jit(solution)/shard_map/ppermute | solution.py:413
  786.0 14.2 %collective-permute-start.35 = (f32[48,1664]{1,0:T(8,128)S(1)}, f32[48,1664]{1,0:T(8,128)S(1)}, u32[]{:S(2)}, u32[]{:S(2)}) collective-permute-start(f32[48,1664]{1,0:T(8,128)S(1)} %bitcast_add_fusion.19), channel_id=1, source_target_pairs={{0,2},{2,4},{1,3},{3,5},{8,10},{10,12},{9,11},{11,13},{16,18},{18,... | collective-permute-start | bytes 958472 | tf_op jit(solution)/shard_map/ppermute | solution.py:412
  793.4 14.2 %collective-permute-start.43 = (f32[48,1712]{1,0:T(8,128)S(1)}, f32[48,1712]{1,0:T(8,128)S(1)}, u32[]{:S(2)}, u32[]{:S(2)}) collective-permute-start(f32[48,1712]{1,0:T(8,128)S(1)} %bitcast_add_fusion.14), channel_id=1, source_target_pairs={{0,2},{2,4},{1,3},{3,5},{8,10},{10,12},{9,11},{11,13},{16,18},{18,... | collective-permute-start | bytes 986120 | tf_op jit(solution)/shard_map/ppermute | solution.py:412
  800.3 13.1 %collective-permute-start.38 = (f32[48,1664]{1,0:T(8,128)S(1)}, f32[48,1664]{1,0:T(8,128)S(1)}, u32[]{:S(2)}, u32[]{:S(2)}) collective-permute-start(f32[48,1664]{1,0:T(8,128)S(1)} %get-tuple-element.96), channel_id=1, source_target_pairs={{6,4},{4,2},{7,5},{5,3},{14,12},{12,10},{15,13},{13,11},{22,20},{2... | collective-permute-start | bytes 958472 | tf_op jit(solution)/shard_map/ppermute | solution.py:413
  801.0 15.1 %collective-permute-start.36 = (f32[48,1664]{1,0:T(8,128)S(1)}, f32[48,1664]{1,0:T(8,128)S(1)}, u32[]{:S(2)}, u32[]{:S(2)}) collective-permute-start(f32[48,1664]{1,0:T(8,128)S(1)} %get-tuple-element.95), channel_id=1, source_target_pairs={{0,2},{2,4},{4,6},{1,3},{3,5},{5,7},{8,10},{10,12},{12,14},{9,11},... | collective-permute-start | bytes 958472 | tf_op jit(solution)/shard_map/ppermute | solution.py:412
  808.4 14.6 %collective-permute-start.44 = (f32[48,1712]{1,0:T(8,128)S(1)}, f32[48,1712]{1,0:T(8,128)S(1)}, u32[]{:S(2)}, u32[]{:S(2)}) collective-permute-start(f32[48,1712]{1,0:T(8,128)S(1)} %get-tuple-element.91), channel_id=1, source_target_pairs={{0,2},{2,4},{4,6},{1,3},{3,5},{5,7},{8,10},{10,12},{12,14},{9,11},... | collective-permute-start | bytes 986120 | tf_op jit(solution)/shard_map/ppermute | solution.py:412
  814.8 14.3 %collective-permute-start.47 = (f32[48,1712]{1,0:T(8,128)S(1)}, f32[48,1712]{1,0:T(8,128)S(1)}, u32[]{:S(2)}, u32[]{:S(2)}) collective-permute-start(f32[48,1712]{1,0:T(8,128)S(1)} %bitcast_add_fusion.13), channel_id=1, source_target_pairs={{6,4},{4,2},{2,0},{7,5},{5,3},{3,1},{14,12},{12,10},{10,8},{15,13}... | collective-permute-start | bytes 986120 | tf_op jit(solution)/shard_map/ppermute | solution.py:413
  (86 other events, 1424.7 us)
Sparse Core Ops, SparseCore 0:
  11.5 90.4 all-gather.3
  104.9 87.1 all-gather.5
  195.1 95.2 all-gather.7

commit v2 on v1

--- a/solution.py
+++ b/solution.py
@@ -31,17 +31,43 @@
     return pltpu.CompilerParams(vmem_limit_bytes=VMEM, dimension_semantics=("arbitrary",))
 
 
-def call(body, grid, ins, outs, scratch=()):
-    in_specs = [spec for _, spec in ins]
+def call(body, grid, micros, ins, outs, scratch=(), waits=(), places=None):
+    first = (places is not None) + len(ins)
+    anywhere = pl.BlockSpec(memory_space=pl.ANY)
+
+    def run(*refs):
+        body(*refs[:first], *refs[first + len(waits) :])
+
+    scalars = [] if places is None else [places]
+    return pl.pallas_call(
+        run,
+        grid_spec=pltpu.PrefetchScalarGridSpec(
+            num_scalar_prefetch=len(scalars),
+            grid=(grid,),
+            in_specs=[spec for _, spec in ins] + [anywhere] * len(waits),
+            out_specs=[spec for _, spec in outs],
+            scratch_shapes=list(scratch),
+        ),
+        out_shape=[shape for shape, _ in outs],
+        compiler_params=params(),
+        cost_estimate=pl.CostEstimate(
+            flops=int(micros * 1e9), bytes_accessed=int(micros * 3e6), transcendentals=0
+        ),
+    )(*scalars, *[array for array, _ in ins], *waits)
+
+
+def tie(value, *others):
+    def body(*refs):
+        pass
+
+    anywhere = pl.BlockSpec(memory_space=pl.ANY)
     return pl.pallas_call(
         body,
-        grid=(grid,),
-        in_specs=in_specs,
-        out_specs=[spec for _, spec in outs],
-        out_shape=[shape for shape, _ in outs],
-        scratch_shapes=list(scratch),
-        compiler_params=params(),
-    )(*[array for array, _ in ins])
+        in_specs=[anywhere] * (1 + len(others)),
+        out_specs=anywhere,
+        out_shape=jax.ShapeDtypeStruct(value.shape, value.dtype),
+        input_output_aliases={0: 0},
+    )(value, *others)
 
 
 def whole(*shape):
@@ -54,6 +80,11 @@
 
 def rows_of(count, width):
     return pl.BlockSpec((count, width), lambda g: (g, 0))
+
+
+def halves(rows, width):
+    count = INNER // 2 // width
+    return pl.BlockSpec((1, rows, width), lambda g: (g // count, 0, g % count))
 
 
 def group(rows, width):
@@ -160,6 +191,11 @@
     st_ref[...] = three(mm_nt, b_rows, c_rows) * same_mask(doc_row, doc_col, True)
 
 
+def either(first_ref, second_ref):
+    first = pl.program_id(0) < INNER // 2 // BLOCK
+    return jnp.where(first, first_ref[...].astype(F32), second_ref[...].astype(F32))
+
+
 def prep_x_body(x_ref, w_ref, b_ref, m_ref, wl_ref, t_ref, pre_ref, act_ref, state_ref):
     pre = conv_pre(x_ref[...].astype(F32), w_ref[...], b_ref[...], m_ref[...])
     act = pre * sigmoid(pre)
@@ -167,12 +203,12 @@
     act_ref[...] = act
     places = head_of_lane(pl.program_id(0) * BLOCK_HEADS, BLOCK)
     weighted = split(act * expand(wl_ref[...], places))
-    state_ref[...] = three(mm, split(t_ref[:STATE]), weighted)
-
-
-def intra_body(x_ref, dt_ref, skip_ref, s_ref, col_ref, row_ref, y_ref):
+    state_ref[0] = three(mm, split(t_ref[:STATE]), weighted)
+
+
+def intra_body(first, x_ref, dt_ref, skip_ref, s_ref, col_ref, row_ref, y_ref):
     half = s_ref.shape[0] // 2
-    places = head_of_lane(pl.program_id(0) * 2 * PAIRS, PAIR_LANES)
+    places = head_of_lane((pl.program_id(0) + first) * 2 * PAIRS, PAIR_LANES)
     scaled = x_ref[...] * expand(dt_ref[...], places)
     lane = lax.broadcasted_iota(jnp.int32, (2 * half, 128), 1)
     for pair in range(PAIRS):
@@ -198,8 +234,8 @@
 
 
 def gate_body(
-    y_ref, z_ref, df_ref, x_ref, c_ref, ct_ref, state_ref, e_ref, gain_ref, skip_ref,
-    final_ref, dz_ref, dy_ref, r_ref, dc_ref, q_ref, sums_ref, carry, scaled,
+    ya_ref, yb_ref, z_ref, df_ref, x_ref, c_ref, ct_ref, state_ref, e_ref, gain_ref, skip_ref,
+    final_ref, turned_ref, dz_ref, dy_ref, r_ref, dc_ref, q_ref, sums_ref, carry, scaled,
 ):
     @pl.when(pl.program_id(0) == 0)
     def _():
@@ -212,13 +248,14 @@
         here = slice(block * BLOCK, block * BLOCK + BLOCK)
         places = head_of_lane(block * BLOCK_HEADS, BLOCK)
         spread = mm(e_high, places) + mm(e_low, places)
-        carry[:, here] = three(mm, c_rows, split(state_ref[:, here])) * spread
+        there = slice(block % 3 * BLOCK, block % 3 * BLOCK + BLOCK)
+        carry[:, here] = three(mm, c_rows, split(state_ref[block // 3, :, there])) * spread
         scaled[:, here] = spread
     gain, skip = gain_ref[...], skip_ref[...]
 
     def some(lap, sums):
         at = pl.ds(pl.multiple_of(lap * 16, 16), 16)
-        y = y_ref[at, :] + carry[at, :]
+        y = jnp.concatenate([ya_ref[at, :], yb_ref[at, :]], axis=1) + carry[at, :]
         z = z_ref[at, :].astype(F32)
         sig = sigmoid(z)
         gate = z * sig
@@ -243,7 +280,7 @@
         )
 
     zero = jnp.zeros((8, INNER), F32)
-    d_gain, d_skip = lax.fori_loop(0, y_ref.shape[0] // 16, some, (zero, zero))
+    d_gain, d_skip = lax.fori_loop(0, z_ref.shape[0] // 16, some, (zero, zero))
     sums_ref[0:8] += d_gain
     sums_ref[8:16] += d_skip
     ct_rows = split(ct_ref[...])
@@ -251,23 +288,25 @@
     q_sum = jnp.zeros(q_ref.shape, F32)
     for block in range(INNER // BLOCK):
         here = slice(block * BLOCK, block * BLOCK + BLOCK)
+        there = slice(block % 3 * BLOCK, block % 3 * BLOCK + BLOCK)
         piece = split(scaled[:, here])
-        r_ref[:, here] += three(mm, ct_rows, piece)
-        d_c = d_c + three(mm_nt, piece, split(state_ref[:, here]))
+        r_ref[block // 3, :, there] += three(mm, ct_rows, piece)
+        d_c = d_c + three(mm_nt, piece, split(state_ref[block // 3, :, there]))
+        turned_ref[here, :] = final_ref[:, here].T
         q_sum = q_sum + fold(carry[:, here], head_of_lane(block * BLOCK_HEADS, BLOCK))
     dc_ref[...] = d_c
     q_ref[...] = q_sum
 
 
-def back_body(x_ref, dy_ref, dt_ref, st_ref, col_ref, row_ref, bc_ref, doc_ref, m_ref, dx_ref, dbc_ref, acc):
+def back_body(first, x_ref, dy_ref, dt_ref, st_ref, col_ref, row_ref, bc_ref, doc_ref, m_ref, in_ref, dx_ref, acc, *ends):
     step = pl.program_id(0)
     half = st_ref.shape[0] // 2
 
     @pl.when(step == 0)
     def _():
-        acc[...] = jnp.zeros_like(acc)
-
-    places = head_of_lane(step * 2 * PAIRS, PAIR_LANES)
+        acc[...] = in_ref[...]
+
+    places = head_of_lane((step + first) * 2 * PAIRS, PAIR_LANES)
     scaled = x_ref[...] * expand(dt_ref[...], places)
     lane = lax.broadcasted_iota(jnp.int32, (2 * half, 128), 1)
     for pair in range(PAIRS):
@@ -294,8 +333,12 @@
             both.append(jnp.concatenate(done, axis=0))
         dx_ref[:, here] = jnp.where(lane < HEAD_DIM, both[0], both[1])
 
+    if not ends:
+        return
+
     @pl.when(step == pl.num_programs(0) - 1)
     def _():
+        dbc_ref = ends[0]
         doc_col = m_ref[:, CONV_K : CONV_K + 1]
         ds = split(acc[...] * same_mask(doc_ref[0:1], doc_col, True))
         dbc_ref[:, :STATE] = three(mm, ds, split(bc_ref[:, STATE:]))
@@ -303,7 +346,8 @@
 
 
 def carry_body(
-    dx_ref, x_ref, dy_ref, pre_ref, in_ref, w_ref, m_ref, bc_ref, r_ref, end_ref, wl_ref, dt_ref, skip_ref,
+    dxa_ref, dxb_ref, x_ref, dy_ref, pre_ref, in_ref, w_ref, m_ref, bc_ref, r_ref, end_ref, wl_ref, dt_ref,
+    skip_ref,
     d_ref, edge_ref, conv_ref, db_ref, g_ref,
 ):
     step = pl.program_id(0)
@@ -314,12 +358,12 @@
         g_ref[...] = jnp.zeros_like(g_ref)
 
     places = head_of_lane(step * BLOCK_HEADS, BLOCK)
-    returned = r_ref[...]
+    returned = r_ref[0]
     r_parts = split(returned)
     to_end = expand(wl_ref[...], places)
     steps = expand(dt_ref[...], places)
     x = x_ref[...]
-    d_scaled = dx_ref[...] + to_end * three(mm, split(bc_ref[:, :STATE]), r_parts)
+    d_scaled = either(dxa_ref, dxb_ref) + to_end * three(mm, split(bc_ref[:, :STATE]), r_parts)
     g_ref[...] += fold(x * d_scaled, places)
     db_ref[...] += three(mm_nt, split(to_end * steps * x), r_parts)
     d_x = steps * d_scaled + skip_ref[...] * dy_ref[...]
@@ -330,7 +374,7 @@
     d_ref[...] = d_ext[LEAD:].astype(BF)
     edge_ref[:LEAD] = d_ext[:LEAD]
     edge_ref[LEAD:] = d_ext[d_ext.shape[0] - LEAD :]
-    flow = jnp.sum(returned * end_ref[...], axis=0, keepdims=True)
+    flow = jnp.sum(returned * end_ref[0], axis=0, keepdims=True)
     row = lax.broadcasted_iota(jnp.int32, sums.shape, 0)
     conv_ref[...] = jnp.where(row == CONV_K + 1, flow, sums)
 
@@ -356,12 +400,19 @@
     return lax.ppermute(array, CTX, pairs)
 
 
-def entering(state, decay, reverse):
+def entering(state, decay, reverse, fills):
+    fills = list(fills)
+
+    def meanwhile(sent, arrived):
+        return tie(arrived, *fills.pop(0)(sent)) if fills else arrived
+
     depth, width = lax.axis_size("z"), lax.axis_size("y")
     place_z, place_y = lax.axis_index("z"), lax.axis_index("y")
     if width != 2:
-        both = jnp.concatenate([state, jnp.broadcast_to(decay, (8, decay.shape[1]))], axis=0)
-        gathered = lax.all_gather(both, CTX)
+        wide = jnp.broadcast_to(decay, (2, 8, decay.shape[2]))
+        gathered = lax.all_gather(jnp.concatenate([state, wide], axis=1), CTX)
+        while fills:
+            gathered = meanwhile(state, gathered)
         count = depth * width
         place = place_z * width + place_y
         ahead = count - 1 - place if reverse else place
@@ -369,16 +420,15 @@
         def one(lap, running):
             source = count - 1 - lap if reverse else lap
             item = lax.dynamic_index_in_dim(gathered, source, 0, False)
-            return item[STATE : STATE + 1] * running + item[:STATE]
+            return item[:, STATE : STATE + 1] * running + item[:, :STATE]
 
         return lax.fori_loop(0, ahead, one, jnp.zeros_like(state))
-    half = state.shape[1] // 2
     second = place_y == (0 if reverse else 1)
-    own = lax.dynamic_slice_in_dim(state, place_y * half, half, 1)
-    other = lax.dynamic_slice_in_dim(state, (1 - place_y) * half, half, 1)
-    got = swap(other, "y")
-    decay_own = lax.dynamic_slice_in_dim(decay, place_y * half, half, 1)
-    decay_got = swap(lax.dynamic_slice_in_dim(decay, (1 - place_y) * half, half, 1), "y")
+    sent = pick(state, 1 - place_y)
+    got = meanwhile(sent, swap(sent, "y"))
+    own = pick(state, place_y)
+    decay_own = pick(decay, place_y)
+    decay_got = swap(pick(decay, 1 - place_y), "y")
     early = jnp.where(second, got, own)
     late = jnp.where(second, own, got)
     decay_early = jnp.where(second, decay_got, decay_own)
@@ -387,62 +437,167 @@
     decay_total = decay_early * decay_late
     before = jnp.zeros_like(total)
     sent = total
+    turn = depth - 1 - place_z if reverse else place_z
     for hop in range(1, depth):
-        pair = (depth - hop, depth - 1 - hop) if reverse else (hop - 1, hop)
-        before = before + lax.ppermute(sent, "z", [pair])
+        pairs = [(depth - hop, depth - 1 - hop)] if reverse else [(hop - 1, hop)]
+        arrived = meanwhile(sent, lax.ppermute(sent, "z", pairs))
+        before = jnp.where(turn == hop, arrived, before)
         sent = decay_total * before + total
     middle = decay_early * before + early
     mine = jnp.where(second, middle, before)
-    theirs = swap(jnp.where(second, before, middle), "y")
-    return jnp.where(
-        place_y == 0,
-        jnp.concatenate([mine, theirs], axis=1),
-        jnp.concatenate([theirs, mine], axis=1),
-    )
-
-
-def line_sum(parts, axis):
+    sent = jnp.where(second, before, middle)
+    theirs = swap(sent, "y")
+    while fills:
+        theirs = meanwhile(sent, theirs)
+    return in_order(mine, theirs, "y")
+
+
+def pick(parts, index, dim=0):
+    return lax.dynamic_index_in_dim(parts, index, dim, False)
+
+
+def in_order(mine, theirs, axis):
+    first = lax.axis_index(axis) == 0
+    return jnp.where(first, jnp.stack([mine, theirs]), jnp.stack([theirs, mine]))
+
+
+def across(array, axis, by):
+    return lax.ppermute(array, axis, [(i, i ^ by) for i in range(lax.axis_size(axis))])
+
+
+def xor_sum(parts, axis, kind):
     count, place = lax.axis_size(axis), lax.axis_index(axis)
-
-    def pick(i):
-        return lax.dynamic_index_in_dim(parts, jnp.clip(i, 0, count - 1), 0, False)
-
-    up, down = pick(count - 1), pick(0)
-    for step in range(1, count):
-        got_up = lax.ppermute(up, axis, [(i, i + 1) for i in range(step)])
-        got_down = lax.ppermute(down, axis, [(count - 1 - i, count - 2 - i) for i in range(step)])
-        if step < count - 1:
-            up = pick(count - step - 1 + place) + got_up
-            down = pick(place - (count - step - 1)) + got_down
-    return pick(place) + got_up + got_down
-
-
-def pair_sum(parts, axis):
-    if lax.axis_size(axis) != 2:
-        return line_sum(parts, axis)
-    place = lax.axis_index(axis)
-    sent = lax.dynamic_index_in_dim(parts, 1 - place, 0, False).astype(BF)
-    kept = lax.dynamic_index_in_dim(parts, place, 0, False)
-    return kept + swap(sent, axis).astype(F32)
-
-
-def scatter_sum(partial, x_first):
+    total = pick(parts, place)
+    for by in range(1, count):
+        total = total + across(pick(parts, place ^ by).astype(kind), axis, by).astype(F32)
+    return total
+
+
+def products_body(
+    place_ref, sent_own, kept_own, sent_other, kept_other, own_ref, other_ref, sent_ref, kept_ref
+):
+    def product(first, second):
+        first, second = first[...], second[...]
+        first = first.reshape(-1, first.shape[-1])
+        second = second.reshape(-1, second.shape[-1])
+        return mm(first, own_ref[...]) + mm(second, other_ref[...])
+
+    sent_ref[...] = product(sent_own, sent_other).astype(BF)
+    kept_ref[...] = product(kept_own, kept_other)
+
+
+def products(left, right, start, count, axis, waits):
+    own, other = left
     sizes = [lax.axis_size(a) for a in ("x", "z", "y")]
-    count = partial.shape[0] // (sizes[0] * sizes[1] * sizes[2])
-    parts = partial.reshape(*sizes, count, partial.shape[1])
-    if x_first:
-        parts = pair_sum(parts, "x")
-        parts = pair_sum(jnp.moveaxis(parts, 1, 0), "y")
+    tokens = own.shape[1]
+    rows = other.shape[0] // sizes[0] // sizes[1] // sizes[2]
+    out_rows = other.shape[0] // 2
+    places = jnp.stack([lax.axis_index(a) for a in ("core", "x", "y")])
+    if axis == "x":
+        own = own.reshape(2, 2, out_rows, tokens)
+        other = other.reshape(2, out_rows, tokens)
+        own_block, other_block = (1, 1, out_rows, tokens), (1, out_rows, tokens)
+
+        def spec(mine, flip):
+            if mine:
+                return pl.BlockSpec(own_block, lambda g, p: (p[1] ^ flip, p[0], 0, 0))
+            return pl.BlockSpec(other_block, lambda g, p: (p[1] ^ flip, 0, 0))
     else:
-        parts = pair_sum(jnp.moveaxis(parts, 2, 0), "y")
-        parts = pair_sum(parts, "x")
-    return line_sum(parts, "z")
-
-
-def own_rows(array, core):
-    sizes = lax.axis_size("x")
-    view = array.reshape(array.shape[0], sizes, 2, -1)
-    return lax.dynamic_index_in_dim(view, core, 2, False).reshape(array.shape[0], -1)
+        own = own.reshape(2, 2, sizes[1], 2, rows, tokens)
+        other = other.reshape(2 * sizes[1], 2, rows, tokens)
+        own_block = (2, 1, sizes[1], 1, rows, tokens)
+        other_block = (2 * sizes[1], 1, rows, tokens)
+
+        def spec(mine, flip):
+            if mine:
+                return pl.BlockSpec(own_block, lambda g, p: (0, p[0], 0, p[2] ^ flip, 0, 0))
+            return pl.BlockSpec(other_block, lambda g, p: (0, p[2] ^ flip, 0, 0))
+
+    block = 512 if count % 512 == 0 or count > 1024 else 384
+    first = start // block
+    columns_of = pl.BlockSpec((tokens, block), lambda g, p: (0, g + first))
+    result = pl.BlockSpec((out_rows, block), lambda g, p: (0, g))
+    return call(
+        products_body, -(-count // block), count * out_rows / 2.0e5,
+        [
+            (own, spec(True, 1)), (own, spec(True, 0)), (other, spec(False, 1)), (other, spec(False, 0)),
+            (right[0], columns_of), (right[1], columns_of),
+        ],
+        [(out((out_rows, count), BF), result), (out((out_rows, count)), result)],
+        waits=waits,
+        places=places,
+    )
+
+
+def products_any(left, right, start, count, axis):
+    core, place = lax.axis_index("core"), lax.axis_index(axis)
+    sizes = [lax.axis_size(a) for a in ("x", "z", "y")]
+    own = core_rows(left[0], core).reshape(left[1].shape)
+    both = jnp.concatenate([own, left[1]], axis=1)
+    view = both.reshape(*sizes, -1, both.shape[1])
+    if axis == "y":
+        view = jnp.moveaxis(view, 2, 0)
+    view = view.reshape(view.shape[0], -1, both.shape[1])
+    right = jnp.concatenate(right, axis=0)[:, start : start + count]
+    sent = [mm(pick(view, place ^ by), right).astype(BF) for by in range(1, view.shape[0])]
+    return sent, mm(pick(view, place), right)
+
+
+def total_of(kept, got):
+    for piece in got:
+        kept = kept + piece.astype(F32)
+    return kept
+
+
+class Reduction:
+    def __init__(self, left, right, start, middle, end, waits=()):
+        if lax.axis_size("x") == 2 and lax.axis_size("y") == 2:
+            sent_x, self.kept_x = products(left, right, start, middle - start, "x", waits)
+            sent_y, self.kept_y = products(left, right, middle, end - middle, "y", waits)
+            self.sent_x, self.sent_y = [sent_x], [sent_y]
+        else:
+            self.sent_x, self.kept_x = products_any(left, right, start, middle - start, "x")
+            self.sent_y, self.kept_y = products_any(left, right, middle, end - middle, "y")
+        self.got_x = [across(piece, "x", by + 1) for by, piece in enumerate(self.sent_x)]
+        self.got_y = [across(piece, "y", by + 1) for by, piece in enumerate(self.sent_y)]
+
+    def made(self):
+        return [self.kept_x, self.kept_y, *self.sent_x, *self.sent_y]
+
+    def second(self, *others):
+        sizes = [lax.axis_size(a) for a in ("x", "z", "y")]
+        kept_x, kept_y = self.kept_x, self.kept_y
+        if others:
+            kept_x, kept_y = tie(kept_x, *others), tie(kept_y, *others)
+        part_x = total_of(kept_x, self.got_x)
+        part_y = total_of(kept_y, self.got_y)
+        view_x = part_x.reshape(sizes[1], sizes[2], -1, part_x.shape[1])
+        view_y = part_y.reshape(sizes[0], sizes[1], -1, part_y.shape[1])
+        done_x = xor_sum(jnp.moveaxis(view_x, 1, 0), "y", BF)
+        done_y = xor_sum(view_y, "x", BF)
+        self.parts = jnp.concatenate([done_x, done_y], axis=2)
+
+    def third(self, *others):
+        parts = tie(self.parts, *others) if others else self.parts
+        count, place = lax.axis_size("z"), lax.axis_index("z")
+        self.got_z = [across(pick(parts, place ^ by), "z", by) for by in range(1, count)]
+        self.kept_z = pick(parts, place)
+
+    def last(self, *others):
+        total = tie(self.kept_z, *others) if others else self.kept_z
+        for piece in self.got_z:
+            total = total + piece
+        return total
+
+
+def core_rows(turned, core):
+    view = turned.reshape(lax.axis_size("x"), 2, -1, turned.shape[1])
+    return pick(view, core, 1)
+
+
+def both_cores(turned, core):
+    theirs = core_rows(turned, 1 - core)
+    return turned, swap(theirs.reshape(-1, turned.shape[1]), "core")
 
 
 def document_ids(lengths, positions):
@@ -500,17 +655,22 @@
     full_bias = bias_piece.reshape(1, -1).astype(F32)
     full_gated = gated_piece.reshape(1, -1).astype(F32)
     weight_x = lax.all_gather(in_weight[:, INNER:], EVERY, axis=0, tiled=True)
-    weight_z = lax.all_gather(in_weight[:, :INNER], EVERY, axis=0, tiled=True)
-    weight_o = lax.all_gather(out_weight, EVERY, axis=0, tiled=True)
+    half = INNER // 2
+    count_out = out_weight.shape[0] // 2
+    stacked = jnp.stack(
+        [in_weight[:, :half], in_weight[:, half:INNER], out_weight[:count_out], out_weight[count_out:]]
+    )
+    stacked = lax.all_gather(stacked, EVERY, axis=1, tiled=True)
 
     extended = jnp.concatenate([lead_tokens, tokens], axis=0).astype(F32)
     rms = lax.rsqrt(jnp.mean(extended * extended, axis=-1, keepdims=True) + EPS)
     normed_ext = (extended * rms * full_gain).astype(BF)
     normed = normed_ext[LEAD:]
     mixed_x = mm(normed_ext, weight_x).astype(BF)
-    mixed_xs = mixed_x[:, :INNER]
-    mixed_bc = mixed_x[:, INNER:CONVW]
+    bc_width = CONVW - INNER
     shifted_dt = mixed_x[LEAD:, CONVW:].astype(F32) + dt_bias[None]
+    turned = normed.T
+    normed_left = both_cores(turned, core)
 
     steps = jax.nn.softplus(shifted_dt)
     rate = jnp.exp(a_log)[None]
@@ -520,7 +680,7 @@
     last = cumulative[row_count - 1 :]
     enter = jnp.exp(cumulative) * alive[:, None]
     to_end = jnp.exp(last - cumulative) * tail[:, None]
-    device_decay = jnp.repeat(enter[row_count - 1 :], HEAD_DIM, axis=1)
+    device_decay = jnp.repeat(enter[row_count - 1 :], HEAD_DIM, axis=1).reshape(2, 1, -1)
     steps_wide = columns(steps, 128)
     enter_wide = columns(enter, 128)
     to_end_wide = columns(to_end, 128)
@@ -531,13 +691,13 @@
     cum_rows = cumulative.T.reshape(groups, heads_block, row_count)
     skip_wide = jnp.repeat(skip_gain, HEAD_DIM)[None]
 
-    bc_width = CONVW - INNER
     full_rows = LEAD + row_count
+    block_bc = pl.BlockSpec((full_rows, bc_width), lambda g: (0, INNER // bc_width))
     square = (row_count, row_count)
     pre_bc, act_bc, act_t, scores, scores_t = call(
-        prep_bc_body, 1,
-        [
-            (mixed_bc, whole(full_rows, bc_width)),
+        prep_bc_body, 1, 3.6,
+        [
+            (mixed_x, block_bc),
             (full_conv[:, INNER:], whole(8, bc_width)),
             (full_bias[:, INNER:], whole(1, bc_width)),
             (masks, whole(row_count, 128)),
@@ -552,9 +712,9 @@
         ],
     )
     pre_x, act_x, state_local = call(
-        prep_x_body, INNER // BLOCK,
-        [
-            (mixed_xs, lanes(full_rows, BLOCK)),
+        prep_x_body, INNER // BLOCK, 12,
+        [
+            (mixed_x, lanes(full_rows, BLOCK)),
             (full_conv[:, :INNER], lanes(8, BLOCK)),
             (full_bias[:, :INNER], lanes(1, BLOCK)),
             (masks, whole(row_count, 128)),
@@ -564,109 +724,146 @@
         [
             (out((row_count, INNER)), lanes(row_count, BLOCK)),
             (out((row_count, INNER)), lanes(row_count, BLOCK)),
-            (out((STATE, INNER)), lanes(STATE, BLOCK)),
-        ],
-    )
-    state_in = entering(state_local, device_decay, False)
+            (out((2, STATE, INNER // 2)), halves(STATE, BLOCK)),
+        ],
+    )
+    half_groups = groups // 2
+    kept = {}
+
+    def intra(index, wait):
+        kept[index] = call(
+            functools.partial(intra_body, index * half_groups), half_groups, 12,
+            [
+                (act_x, pl.BlockSpec((row_count, PAIR_LANES), lambda g: (0, g + index * half_groups))),
+                (steps_wide, whole(row_count, 128)),
+                (skip_wide[:, index * half :][:, :half], lanes(1, PAIR_LANES)),
+                (scores, whole(*square)),
+                (cum_cols[index * half_groups :][:half_groups], group(row_count, heads_block)),
+                (cum_rows[index * half_groups :][:half_groups], group(heads_block, row_count)),
+            ],
+            [(out((row_count, half)), lanes(row_count, PAIR_LANES))],
+            waits=[wait],
+        )[0]
+        return [kept[index]]
+
+    def project(wait):
+        weight_z = [stacked[0], stacked[1]]
+        weight_o = stacked[2:].reshape(2, count, count_out, width)
+        weight_o = jnp.moveaxis(weight_o, 0, 1).reshape(-1, width)
+        kept["z"], kept["o"] = weight_z, weight_o
+        mixed_z = [mm(normed, weight).astype(BF) for weight in weight_z]
+        kept["mixed_z"] = jnp.concatenate(mixed_z, axis=1)
+        kept["d_final"] = mm_nt(out_grad, weight_o)
+        return [kept["mixed_z"], kept["d_final"]]
+
+    state_in = entering(
+        state_local, device_decay, False,
+        [lambda wait: [], lambda wait: intra(0, wait), lambda wait: intra(1, wait), project],
+    )
     state_end = device_decay * state_in + state_local
-
-    y_local = call(
-        intra_body, groups,
-        [
-            (act_x, lanes(row_count, PAIR_LANES)),
-            (steps_wide, whole(row_count, 128)),
-            (skip_wide, lanes(1, PAIR_LANES)),
-            (scores, whole(*square)),
-            (cum_cols, group(row_count, heads_block)),
-            (cum_rows, group(heads_block, row_count)),
-        ],
-        [(out((row_count, INNER)), lanes(row_count, PAIR_LANES))],
-    )[0]
-    mixed_z = mm(normed, weight_z).astype(BF)
-    d_final = mm_nt(out_grad, weight_o)
+    weight_z, weight_o = kept["z"], kept["o"]
+    mixed_z, d_final = kept["mixed_z"], kept["d_final"]
 
     tile = 128
     c_rows = act_bc[:, STATE:]
     c_cols = act_t[STATE:]
-    final, d_z, d_y, returned_local, d_c_carry, dy_y, sums = call(
-        gate_body, row_count // tile,
-        [
-            (y_local, rows_of(tile, INNER)),
+    final, final_turned, d_z, d_y, returned_local, d_c_carry, dy_y, sums = call(
+        gate_body, row_count // tile, 31,
+        [
+            (kept[0], rows_of(tile, half)),
+            (kept[1], rows_of(tile, half)),
             (mixed_z, rows_of(tile, INNER)),
             (d_final, rows_of(tile, INNER)),
             (act_x, rows_of(tile, INNER)),
             (c_rows, rows_of(tile, STATE)),
             (c_cols, lanes(STATE, tile)),
-            (state_in, whole(STATE, INNER)),
+            (state_in, whole(2, STATE, INNER // 2)),
             (enter_wide, rows_of(tile, 128)),
             (full_gated, whole(1, INNER)),
             (skip_wide, whole(1, INNER)),
         ],
         [
             (out((row_count, INNER), BF), rows_of(tile, INNER)),
+            (out((INNER, row_count), BF), lanes(INNER, tile)),
             (out((row_count, INNER), BF), rows_of(tile, INNER)),
             (out((row_count, INNER)), rows_of(tile, INNER)),
-            (out((STATE, INNER)), whole(STATE, INNER)),
+            (out((2, STATE, INNER // 2)), whole(2, STATE, INNER // 2)),
             (out((row_count, STATE)), rows_of(tile, STATE)),
             (out((row_count, 128)), rows_of(tile, 128)),
             (out((16, INNER)), whole(16, INNER)),
         ],
         [pltpu.VMEM((tile, INNER), F32), pltpu.VMEM((tile, INNER), F32)],
     )
-    returned = entering(returned_local, device_decay, True)
-
-    layer_out = (tokens.astype(F32) + mm(final, weight_o)).astype(BF)
-    final_mine = jnp.concatenate([own_rows(final, core), swap(own_rows(final, 1 - core), "core")], axis=0)
-    out_grad_both = jnp.concatenate([out_grad, swap(out_grad, "core")], axis=0)
-    normed_mine = jnp.concatenate([own_rows(normed, core), swap(own_rows(normed, 1 - core), "core")], axis=0)
-
-    def reduce_columns(left, right):
-        middle = right.shape[1] // 256 * 128
-        return jnp.concatenate(
+
+    out_grad_theirs = swap(out_grad, "core")
+    final_left = both_cores(final_turned, core)
+    d_z_theirs = swap(d_z, "core")
+    back = {"acc": jnp.zeros(square, F32)}
+
+    def out_sums(wait):
+        back["out"] = Reduction(final_left, [out_grad, out_grad_theirs], 0, width // 2, width, [wait])
+        return back["out"].made()
+
+    def z_sums(wait):
+        back["z"] = Reduction(normed_left, [d_z, d_z_theirs], 0, half, INNER, [wait])
+        return back["z"].made()
+
+    def within(index, wait):
+        ends = [(out((row_count, bc_width)), whole(row_count, bc_width))] if index else []
+        back[index], back["acc"], *back["bc"] = call(
+            functools.partial(back_body, index * half_groups), half_groups, 16,
             [
-                scatter_sum(mm_tn(left, right[:, :middle]), True),
-                scatter_sum(mm_tn(left, right[:, middle:]), False),
+                (act_x, pl.BlockSpec((row_count, PAIR_LANES), lambda g: (0, g + index * half_groups))),
+                (d_y, pl.BlockSpec((row_count, PAIR_LANES), lambda g: (0, g + index * half_groups))),
+                (steps_wide, whole(row_count, 128)),
+                (scores_t, whole(*square)),
+                (cum_cols[index * half_groups :][:half_groups], group(row_count, heads_block)),
+                (cum_rows[index * half_groups :][:half_groups], group(heads_block, row_count)),
+                (act_bc, whole(row_count, bc_width)),
+                (doc_rows, whole(8, row_count)),
+                (masks, whole(row_count, 128)),
+                (back["acc"], whole(*square)),
             ],
-            axis=1,
+            [
+                (out((row_count, half)), lanes(row_count, PAIR_LANES)),
+                (out(square), whole(*square)),
+                *ends,
+            ],
+            waits=[wait],
         )
-
-    sum_out = reduce_columns(final_mine, out_grad_both)
-    d_z_both = jnp.concatenate([d_z, swap(d_z, "core")], axis=0)
-    sum_in_z = reduce_columns(normed_mine, d_z_both)
-
-    d_scaled, d_bc = call(
-        back_body, groups,
-        [
-            (act_x, lanes(row_count, PAIR_LANES)),
-            (d_y, lanes(row_count, PAIR_LANES)),
-            (steps_wide, whole(row_count, 128)),
-            (scores_t, whole(*square)),
-            (cum_cols, group(row_count, heads_block)),
-            (cum_rows, group(heads_block, row_count)),
-            (act_bc, whole(row_count, bc_width)),
-            (doc_rows, whole(8, row_count)),
-            (masks, whole(row_count, 128)),
-        ],
-        [
-            (out((row_count, INNER)), lanes(row_count, PAIR_LANES)),
-            (out((row_count, bc_width)), whole(row_count, bc_width)),
-        ],
-        [pltpu.VMEM(square, F32)],
-    )
+        return [back[index]]
+
+    def rest(wait):
+        back["out"].second(wait)
+        back["z"].second(wait)
+        layer = (tokens.astype(F32) + mm(final, weight_o)).astype(BF)
+        back["layer_out"] = layer
+        back["d_normed"] = mm_nt(d_z[:, :half], weight_z[0]) + mm_nt(d_z[:, half:], weight_z[1])
+        return [layer, back["d_normed"]]
+
+    returned = entering(
+        returned_local, device_decay, True,
+        [out_sums, z_sums, lambda wait: within(0, wait), lambda wait: within(1, wait), rest],
+    )
+    layer_out = back["layer_out"]
+    d_bc = back["bc"][0]
+    back["out"].third(returned)
+    back["z"].third(returned)
 
     d_xs, edge_x, conv_x, d_b_carry, x_dx = call(
-        carry_body, INNER // BLOCK,
-        [
-            (d_scaled, lanes(row_count, BLOCK)),
+        carry_body, INNER // BLOCK, 27,
+        [
+            (back[0], pl.BlockSpec((row_count, BLOCK), lambda g: (0, jnp.minimum(g, half // BLOCK - 1)))),
+            (back[1], pl.BlockSpec((row_count, BLOCK), lambda g: (0, jnp.maximum(g - half // BLOCK, 0)))),
             (act_x, lanes(row_count, BLOCK)),
             (d_y, lanes(row_count, BLOCK)),
             (pre_x, lanes(row_count, BLOCK)),
-            (mixed_xs, lanes(full_rows, BLOCK)),
+            (mixed_x, lanes(full_rows, BLOCK)),
             (full_conv[:, :INNER], lanes(8, BLOCK)),
             (masks, whole(row_count, 128)),
             (act_bc, whole(row_count, bc_width)),
-            (returned, lanes(STATE, BLOCK)),
-            (state_end, lanes(STATE, BLOCK)),
+            (returned, halves(STATE, BLOCK)),
+            (state_end, halves(STATE, BLOCK)),
             (to_end_wide, whole(row_count, 128)),
             (steps_wide, whole(row_count, 128)),
             (skip_wide, lanes(1, BLOCK)),
@@ -681,11 +878,11 @@
     )
     d_bc = d_bc + jnp.concatenate([d_b_carry, d_c_carry], axis=1)
     d_bc_low, edge_bc, conv_bc = call(
-        carry_bc_body, 1,
+        carry_bc_body, 1, 3,
         [
             (d_bc, whole(row_count, bc_width)),
             (pre_bc, whole(row_count, bc_width)),
-            (mixed_bc, whole(full_rows, bc_width)),
+            (mixed_x, block_bc),
             (full_conv[:, INNER:], whole(8, bc_width)),
             (masks, whole(row_count, 128)),
         ],
@@ -711,12 +908,14 @@
     grad_skip = jnp.sum(jnp.sum(sums[8:], axis=0).reshape(HEADS, HEAD_DIM), axis=1)
     grad_gated = jnp.sum(sums[:8], axis=0)
 
-    d_xr = jnp.concatenate([d_xs, d_bc_low], axis=1)
-    d_xr = lax.dynamic_update_slice_in_dim(d_xr, d_last.astype(BF), row_count - LEAD, 0)
-    d_x = jnp.concatenate([d_xr, d_dt.astype(BF)], axis=1)
-    d_x_both = jnp.concatenate([d_x, swap(d_x, "core")], axis=0)
-    sum_in_x = reduce_columns(normed_mine, d_x_both)
-    d_normed = mm_nt(d_z, weight_z) + mm_nt(d_x, weight_x)
+    d_last = d_last.astype(BF)
+    d_x = jnp.concatenate([d_xs, d_bc_low, d_dt.astype(BF)], axis=1)
+    d_x = lax.dynamic_update_slice(d_x, d_last, (row_count - LEAD, 0))
+    d_x_theirs = swap(d_x, "core")
+    last_sums = Reduction(normed_left, [d_x, d_x_theirs], 0, half, d_x.shape[1])
+    d_normed = back["d_normed"] + mm_nt(tie(d_x, *last_sums.made()), weight_x)
+    last_sums.second()
+    last_sums.third()
 
     rows_value, scale = extended[LEAD:], rms[LEAD:]
     unit = rows_value * scale
@@ -724,6 +923,10 @@
     d_rows = scale * (pulled - unit * jnp.mean(pulled * unit, axis=-1, keepdims=True))
     grad_tokens = out_grad.astype(F32) + d_rows
     grad_gain = jnp.sum(d_normed * unit, axis=0)
+
+    sum_out = back["out"].last(d_normed, last_sums.parts)
+    sum_in_z = back["z"].last(d_normed, last_sums.parts)
+    sum_in_x = last_sums.last()
 
     per_device = jnp.concatenate(
         [

time: 847 us -> 779 us (0.920)
  starting transfers between devices: 141 us -> 57.5 us
  Pallas kernels: 134 us -> 186 us
  waiting for transfers between devices: 259 us -> 234 us
  matrix products: 88.3 us -> 70 us
    ppermute x42 -> x27, starting transfers between devices: 105 us -> 36 us  [the longest x21 27.3 us: across(): lax.ppermute(array, axis, [(i, i ^ by) for i in range(lax.axis_size(axis))])]
    ppermute x22 -> x10, waiting for transfers between devices: 71.7 us -> 15.7 us  [swap(): return lax.ppermute(array, axis, [(0, 1), (1, 0)])]
    ppermute x42 -> x27, waiting for transfers between devices: 64.4 us -> 119 us  [the longest x21 81.1 us: across(): lax.ppermute(array, axis, [(i, i ^ by) for i in range(lax.axis_size(axis))])]
    pallas_call x7 -> x33, Pallas kernels: 134 us -> 186 us  [the longest x15 186 us: call(): pl.pallas_call(run, grid_spec=pltpu.PrefetchScalarGridSpec(num_scalar_pre...]
    all_gather x2 -> x1, waiting for transfers between devices: 48.2 us -> 12.8 us  [shards(): stacked = lax.all_gather(stacked, EVERY, axis=1, tiled=True)]
    all_to_all x1, waiting for transfers between devices: 0.01 us -> 26.8 us  [shards(): lax.all_to_all(per_device, EVERY, 0, 0, tiled=True)]
    dot_general x6 -> x0, matrix products: 25.7 us -> none  [mm_tn(): lax.dot_general(left, right, (((0,), (0,)), ((), ())), preferred_element_...]
    ppermute x22 -> x10, starting transfers between devices: 20.6 us -> 5.34 us  [swap(): return lax.ppermute(array, axis, [(0, 1), (1, 0)])]
  transfers between devices with their start and end apart: 71 -> 43, of which waited for: 23 -> 14; matrix products, arithmetic and copies ran while one was open for 34% -> 32% of each run, Pallas kernels for 16% -> 24%
where the time goes in v2:
time: 779 us; the launch traced here: 769 us
  waiting for transfers between devices  234 us (30%)
  Pallas kernels  186 us (24%)
  local copies, waits for them, and re-layouts  128 us (16%)
  other arithmetic  75.9 us (10%)
  matrix products  70 us (9%)
  starting transfers between devices  57.5 us (7%)
  between operations  17.4 us (2%)
    pallas_call x15, Pallas kernels, call(): pl.pallas_call(run, grid_spec=pltpu.PrefetchScalarGridSpec(num_scalar_pre...  186 us
    ppermute x21, waiting for transfers between devices, across(): lax.ppermute(array, axis, [(i, i ^ by) for i in range(lax.axis_size(axis))])  81.1 us
    all_gather x1, waiting for transfers between devices, shards(): weight_x = lax.all_gather(in_weight[:, INNER:], EVERY, axis=0, tiled=True)  56.7 us
    ppermute x6, waiting for transfers between devices, entering(): arrived = meanwhile(sent, lax.ppermute(sent, 'z', pairs))  37.5 us
    dot_general x4, matrix products, mm_nt(): lax.dot_general(left, right, (((1,), (1,)), ((), ())), preferred_element_...  36.6 us
    dot_general x4, matrix products, mm(): return jnp.dot(left, right, preferred_element_type=F32)  30.3 us
    unnamed x156, local copies, waits for them, and re-layouts  29.6 us
    ppermute x21, starting transfers between devices, across(): lax.ppermute(array, axis, [(i, i ^ by) for i in range(lax.axis_size(axis))])  27.3 us
  transfers between devices with their start and end apart: 43, of which 14 were waited for; matrix products, arithmetic and copies ran while one was open for 32% of the time, Pallas kernels for 24%

profile of v2, /device:TPU:0, one launch (start us, length us, event | category | flops | bytes accessed | tf_op | source)
XLA Modules:
  0.0 768.5 jit_solution(15321753286876499588)
XLA Ops:
  14.6 7.3 all-to-all-start
  21.9 3.7 collective-permute-start
  44.9 56.7 %all-gather.3.cloned.1.call-done = bf16[1536,3376]{1,0:T(8,128)(2,1)} async-done(((bf16[48,3376]{1,0:T(8,128)(2,1)}), bf16[1536,3376]{1,0:T(8,128)(2,1)}) %all-gather.3.cloned.1.call-update) | async-done | bytes 10371088 | tf_op jit(solution)/shard_map/all_gather | solution.py:657
  101.6 10.5 %convolution_convert_fusion.refs_0_.refs_5_.refs_2_ = bf16[528,3376]{1,0:T(8,128)(2,1)S(1)} fusion(bf16[528,1536]{1,0:T(8,128)(2,1)} %multiply_convert_fusion, bf16[1536,3376]{1,0:T(8,128)(2,1)} %all-gather.3.cloned.1.call-done), kind=kOutput, calls=%fused_computation | convolution fusion | flops 5477708800 | bytes 15558144 | tf_op jit(solution)/shard_map/dot_general | solution.py:104
  117.5 3.6 shard_map.203
  121.2 12.1 %shard_map.204 = (f32[512,3072]{1,0:T(8,128)}, f32[512,3072]{1,0:T(8,128)}, f32[2,128,1536]{2,1,0:T(8,128)}) custom-call(bf16[528,3376]{1,0:T(8,128)(2,1)} %copy-done.56, f32[8,3072]{1,0:T(8,128)} %slice.200.refs_1_.refs_6_, f32[1,3072]{1,0:T(1,128)} %slice.201.refs_2_, f32[512,128]{1,0:T(8,128)} %pad.26.refs_3_.refs_8_.refs_7_.refs_4_, ...), custom_call_target="tpu_custom_call" | custom-call | flops 12000000000 | bytes 36000000 | tf_op jit(solution)/shard_map/pallas_call | solution.py:42
  140.0 3.8 fusion.65
  145.9 15.7 %collective-permute-done.1 = f32[1,1536]{1,0:T(1,128)S(1)} collective-permute-done((f32[1,1536]{1,0:T(1,128)S(1)}, f32[1,1536]{1,0:T(1,128)S(1)}, u32[]{:S(2)}, u32[]{:S(2)}) %collective-permute-start.1) | collective-permute-done | bytes 6176 | tf_op jit(solution)/shard_map/ppermute | solution.py:394
  165.5 3.6 collective-permute-start.3
  169.1 13.3 %shard_map.206.refs_1_.refs_0_ = f32[512,1536]{1,0:T(8,128)} custom-call(f32[512,3072]{1,0:T(8,128)} %get-tuple-element.52.refs_0_.refs_4_.refs_2_, f32[512,128]{1,0:T(8,128)} %pad.28.refs_1_.refs_2_.refs_12_, f32[1,1536]{1,0:T(1,128)} %get-tuple-element.138.refs_2_, f32[512,512]{1,0:T(8,128)} %get-tuple-element.53.refs_3_, ...), custom_call_target="tpu_custom_call" | custom-call | flops 12000000000 | bytes 36000000 | tf_op jit(solution)/shard_map/pallas_call | solution.py:42
  182.4 20.5 %collective-permute-done.3.refs_0_ = f32[128,1536]{1,0:T(8,128)S(1)} collective-permute-done((f32[128,1536]{1,0:T(8,128)}, f32[128,1536]{1,0:T(8,128)S(1)}, u32[]{:S(2)}, u32[]{:S(2)}) %collective-permute-start.3) | collective-permute-done | bytes 786464 | tf_op jit(solution)/shard_map/ppermute | solution.py:443
  205.9 13.1 %shard_map.208.refs_1_ = f32[512,1536]{1,0:T(8,128)} custom-call(f32[512,3072]{1,0:T(8,128)} %get-tuple-element.52.refs_0_.refs_4_.refs_2_, f32[512,128]{1,0:T(8,128)} %pad.28.refs_1_.refs_2_.refs_12_, f32[1,1536]{1,0:T(1,128)} %get-tuple-element.137.refs_2_, f32[512,512]{1,0:T(8,128)} %get-tuple-element.53.refs_3_, ...), custom_call_target="tpu_custom_call" | custom-call | flops 12000000000 | bytes 36000000 | tf_op jit(solution)/shard_map/pallas_call | solution.py:42
  224.3 12.8 %all-gather.5.cloned.1.call-done = bf16[4,1536,1536]{2,1,0:T(8,128)(2,1)} async-done(((bf16[4,48,1536]{2,1,0:T(8,128)(2,1)}), bf16[4,1536,1536]{2,1,0:T(8,128)(2,1)}) %all-gather.5.cloned.1.call-update) | async-done | bytes 18874384 | tf_op jit(solution)/shard_map/all_gather | solution.py:663
  237.1 7.8 %slice.215 = bf16[2,1536,1536]{2,1,0:T(8,128)(2,1)} slice(bf16[4,1536,1536]{2,1,0:T(8,128)(2,1)} %all-gather.5.cloned.1.call-done), slice={[2:4], [0:1536], [0:1536]} | slice | bytes 18874368 | tf_op jit(solution)/shard_map/slice | solution.py:751
  244.9 8.1 %copy.139 = bf16[32,2,48,1536]{3,2,1,0:T(8,128)(2,1)} copy(bf16[32,2,48,1536]{3,2,0,1:T(8,128)(2,1)} %bitcast.182) | data formatting | bytes 18874368 | tf_op jit(solution)/shard_map/transpose | solution.py:752
  253.0 9.9 %convolution_bitcast_fusion.refs_2_.refs_3_ = f32[512,3072]{1,0:T(8,128)} fusion(bf16[3072,1536]{1,0:T(8,128)(2,1)} %bitcast.200, bf16[512,1536]{1,0:T(8,128)(2,1)} %refs_5_.3), kind=kOutput, calls=%fused_computation.6 | convolution fusion | flops 4831838208 | bytes 17301504 | tf_op jit(solution)/shard_map/dot_general | solution.py:108
  262.9 5.0 fusion.6
  267.9 5.0 fusion.7
  276.1 2.7 fusion.17
  280.6 4.6 reshape.388
  285.2 2.6 copy.144
  288.6 4.9 copy.142.refs_1_.refs_2_
  293.5 4.2 constant_dynamic-slice_fusion
  297.6 4.7 copy.161
  308.3 3.5 multiply_add_fusion.1
  311.8 32.4 %shard_map.211 = (bf16[512,3072]{1,0:T(8,128)(2,1)}, bf16[3072,512]{1,0:T(8,128)(2,1)}, bf16[512,3072]{1,0:T(8,128)(2,1)}, f32[512,3072]{1,0:T(8,128)}, f32[2,12...) custom-call(f32[512,1536]{1,0:T(8,128)} %shard_map.206.refs_1_.refs_0_, ...), custom_call_target="tpu_custom_call" | custom-call | flops 31000000512 | bytes 93000000 | tf_op jit(solution)/shard_map/pallas_call | solution.py:42
  346.6 9.9 %fusion.5.refs_1_ = bf16[512,1536]{1,0:T(8,128)(2,1)} fusion(bf16[512,3072]{1,0:T(8,128)(2,1)S(1)} %copy-done.74, bf16[3072,1536]{1,0:T(8,128)(2,1)} %bitcast.201, bf16[512,1536]{1,0:T(8,128)(2,1)S(1)} %copy-done.10), kind=kOutput, calls=%fused_computation.28 | convolution fusion | flops 4834197504 | bytes 15728640 | tf_op jit(solution)/shard_map/dot_general | solution.py:104
  358.2 7.1 fusion
  366.5 7.5 shard_map.212
  374.0 7.6 shard_map.213
  384.8 8.1 %fusion.4.refs_2_ = f32[512,1536]{1,0:T(8,128)} fusion(f32[512,1536]{1,0:T(8,128)} %fusion, bf16[4,1536,1536]{2,1,0:T(8,128)(2,1)} %all-gather.5.cloned.1.call-done, bf16[512,3072]{1,0:T(8,128)(2,1)} %get-tuple-element.57.refs_5_), kind=kOutput, calls=%fused_computation.20 | convolution fusion | flops 2416705536 | bytes 12582912 | tf_op jit(solution)/shard_map/dot_general | solution.py:108
  396.6 6.8 shard_map.216
  404.9 6.8 shard_map.215
  416.2 18.1 %shard_map.218 = (f32[512,1536]{1,0:T(8,128)}, f32[512,512]{1,0:T(8,128)}) custom-call(f32[512,3072]{1,0:T(8,128)} %get-tuple-element.52.refs_0_.refs_4_.refs_2_, f32[512,3072]{1,0:T(8,128)} %get-tuple-element.58.refs_1_.refs_3_, f32[512,128]{1,0:T(8,128)} %pad.28.refs_1_.refs_2_.refs_12_, f32[512,512]{1,0:T(8,128)} %get-tuple-element.59.refs_3_, ...), custom_call_target="tpu_custom_call" | custom-call | flops 16000000000 | bytes 48000000 | tf_op jit(solution)/shard_map/pallas_call | solution.py:42
  438.7 19.5 %shard_map.220 = (f32[512,1536]{1,0:T(8,128)}, f32[512,512]{1,0:T(8,128)}, f32[512,256]{1,0:T(8,128)}) custom-call(f32[512,3072]{1,0:T(8,128)} %get-tuple-element.52.refs_0_.refs_4_.refs_2_, f32[512,3072]{1,0:T(8,128)} %get-tuple-element.58.refs_1_.refs_3_, f32[512,128]{1,0:T(8,128)} %pad.28.refs_1_.refs_2_.refs_12_, f32[512,512]{1,0:T(8,128)} %get-tuple-element.59.refs_3_, ...), custom_call_target="tpu_custom_call" | custom-call | flops 16000000000 | bytes 48000000 | tf_op jit(solution)/shard_map/pallas_call | solution.py:42
  458.2 17.0 %collective-permute-done.14.refs_0_ = f32[128,1536]{1,0:T(8,128)S(1)} collective-permute-done((f32[128,1536]{1,0:T(8,128)S(1)}, f32[128,1536]{1,0:T(8,128)S(1)}, u32[]{:S(2)}, u32[]{:S(2)}) %collective-permute-start.14) | collective-permute-done | bytes 786464 | tf_op jit(solution)/shard_map/ppermute | solution.py:443
  481.0 3.8 convert_add_fusion.4
  501.9 2.7 maximum_select_fusion.1.refs_9_.refs_1_
  504.5 27.2 %shard_map.223 = (bf16[512,3072]{1,0:T(8,128)(2,1)}, f32[32,3072]{1,0:T(8,128)}, f32[8,3072]{1,0:T(8,128)}, f32[512,128]{1,0:T(8,128)}, f32[512,128]{1,0:T(8,128)}) custom-call(f32[512,1536]{1,0:T(8,128)} %get-tuple-element.70.refs_1_.refs_0_, f32[512,1536]{1,0:T(8,128)} %get-tuple-element.72.refs_1_, f32[512,3072]{1,0:T(8,128)} %get-tuple-element.52.refs_0_.refs_4_.refs_2_, ...), custom_call_target="tpu_custom_call" | custom-call | flops 27000000512 | bytes 81000000 | tf_op jit(solution)/shard_map/pallas_call | solution.py:42
  535.7 2.9 shard_map.224
  541.1 2.4 fusion.64
  544.0 3.5 collective-permute-done.16
  547.5 4.0 copy.146
  562.0 3.1 dynamic-slice_bitcast_fusion.8
  565.0 4.2 collective-permute-start.28
  569.9 3.1 dynamic-slice_bitcast_fusion.4
  575.0 5.7 copy.149.refs_6_
  580.6 6.8 shard_map.225
  587.5 8.0 %shard_map.226 = (bf16[384,1840]{1,0:T(8,128)(2,1)}, f32[384,1840]{1,0:T(8,128)}) custom-call(s32[3]{0:T(128)} %pad_add_fusion.refs_0_, bf16[2,2,4,2,48,512]{5,4,3,2,1,0:T(8,128)(2,1)} %bitcast.197, bf16[2,2,4,2,48,512]{5,4,3,2,1,0:T(8,128)(2,1)} %bitcast.198, bf16[8,2,48,512]{3,2,1,0:T(8,128)(2,1)} %bitcast.189, bf16[8,2,48,512]{3,2,1,0:T(8,128)(2,1)} %bitcast.190, ...), custom_call_target="tpu_custom_call" | custom-call | flops 3532800000 | bytes 10598400 | tf_op jit(solution)/shard_map/pallas_call | solution.py:42
  597.5 11.5 %multiply_reduce_fusion.1 = (f32[1536]{0:T(1024)S(1)}, f32[512]{0:T(512)S(1)}, f32[512,1536]{1,0:T(8,128)S(1)}) fusion(f32[528,1536]{1,0:T(8,128)} %maximum_convert_fusion, f32[512]{0:T(512)S(1)} %copy-done.54, f32[1536]{0:T(1024)S(1)} %copy-done.51, f32[512,1536]{1,0:T(8,128)} %fusion.4.refs_2_, bf16[512,3376]{1,0:T(8,128)(2,1)} %shard_map.227, ...), kind=kOutput, calls=%fused_computation.25 | convolution fusion | flops 5315491840 | bytes 23281664 | tf_op jit(solution)/shard_map/dot_general | solution.py:108
  609.1 3.6 copy.155
  613.6 3.7 all-to-all-start.1
  619.2 4.8 multiply_add_fusion
  624.0 26.8 %all-to-all-done.1 = f32[32,1,808]{2,1,0:T(1,128)S(1)} async-done(((f32[32,1,808]{2,1,0:T(1,128)}), f32[32,1,808]{2,1,0:T(1,128)S(1)}, u32[]{:S(2)}, u32[]{:S(2)}) %all-to-all-start.1) | async-done | bytes 103456 | tf_op jit(solution)/shard_map/all_to_all | solution.py:943
  657.0 2.6 copy.156
  662.8 8.5 %collective-permute-done.23 = bf16[4,48,1536]{2,1,0:T(8,128)(2,1)} collective-permute-done((bf16[4,48,1536]{2,1,0:T(8,128)(2,1)S(1)}, bf16[4,48,1536]{2,1,0:T(8,128)(2,1)}, u32[]{:S(2)}, u32[]{:S(2)}) %collective-permute-start.23) | collective-permute-done | bytes 589856 | tf_op jit(solution)/shard_map/ppermute | solution.py:465
  673.0 6.7 collective-permute-done.25
  684.8 14.0 %collective-permute-done.37 = f32[96,1536]{1,0:T(8,128)} collective-permute-done((f32[96,1536]{1,0:T(8,128)}, f32[96,1536]{1,0:T(8,128)}, u32[]{:S(2)}, u32[]{:S(2)}) %collective-permute-start.37) | collective-permute-done | bytes 589856 | tf_op jit(solution)/shard_map/ppermute | solution.py:465
  701.0 6.0 collective-permute-done.36
  707.8 2.5 add_add_fusion
  710.3 2.5 collective-permute-start.29
  712.8 21.1 %collective-permute-done.26 = f32[48,3072]{1,0:T(8,128)} collective-permute-done((f32[48,3072]{1,0:T(8,128)}, f32[48,3072]{1,0:T(8,128)}, u32[]{:S(2)}, u32[]{:S(2)}) %collective-permute-start.26) | collective-permute-done | bytes 589856 | tf_op jit(solution)/shard_map/ppermute | solution.py:465
  735.4 21.7 %collective-permute-done.30 = f32[48,3376]{1,0:T(8,128)S(1)} collective-permute-done((f32[48,3376]{1,0:T(8,128)}, f32[48,3376]{1,0:T(8,128)S(1)}, u32[]{:S(2)}, u32[]{:S(2)}) %collective-permute-start.30) | collective-permute-done | bytes 648224 | tf_op jit(solution)/shard_map/ppermute | solution.py:465
  757.2 3.0 collective-permute-done.29
  (381 shorter events, 154.5 us)
Async XLA Ops:
  7.2 14.7 %copy-start.10 = (bf16[512,1536]{1,0:T(8,128)(2,1)S(1)}, bf16[512,1536]{1,0:T(8,128)(2,1)}, u32[]{:S(2)}) copy-start(bf16[512,1536]{1,0:T(8,128)(2,1)} %param.12) | copy-start | bytes 4718596
  7.2 18.4 %copy-start.59 = (s32[1,3]{1,0:T(1,128)S(1)}, s32[1,3]{1,0:T(1,128)}, u32[]{:S(2)}) copy-start(s32[1,3]{1,0:T(1,128)} %param.14) | copy-start | bytes 40
  7.2 22.2 %copy-start.66 = (f32[48]{0:T(128)S(1)}, f32[48]{0:T(128)}, u32[]{:S(2)}) copy-start(f32[48]{0:T(128)} %param.21) | copy-start | bytes 580
  7.2 94.4 %all-gather.3.cloned.1.call-start = ((), (), s32[]{:S(2)}) async-start(), calls=%async_computation.2 | async-start | bytes 10948608 | tf_op jit(solution)/shard_map/all_gather | solution.py:657
  9.1 27.1 %copy-start.68 = (f32[48]{0:T(128)S(1)}, f32[48]{0:T(128)}, u32[]{:S(2)}) copy-start(f32[48]{0:T(128)} %param.20) | copy-start | bytes 580
  9.2 227.9 %all-gather.5.cloned.1.call-start = ((), (), s32[]{:S(2)}) async-start(), calls=%async_computation.3 | async-start | bytes 19464192 | tf_op jit(solution)/shard_map/all_gather | solution.py:663
  14.6 25.6 %all-to-all-start = ((bf16[32,2,332]{2,1,0:T(2,128)(2,1)}), bf16[32,2,332]{2,1,0:T(2,128)(2,1)S(1)}, u32[]{:S(2)}, u32[]{:S(2)}) async-start(bf16[32,2,332]{2,1,0:T(2,128)(2,1)} %reshape.428), calls=%async_computation | async-start | bytes 98304 | tf_op jit(solution)/shard_map/all_to_all | solution.py:613
  21.9 15.1 %collective-permute-start = (bf16[16,1536]{1,0:T(8,128)(2,1)S(1)}, bf16[16,1536]{1,0:T(8,128)(2,1)S(1)}, u32[]{:S(2)}, u32[]{:S(2)}) collective-permute-start(bf16[16,1536]{1,0:T(8,128)(2,1)S(1)} %slice.156), channel_id=1, source_target_pairs={{0,1},{1,2},{2,3},{3,4},{4,5},{5,6},{6,7},{8,9},{9,10},{10,11},{11... | collective-permute-start | bytes 147464 | tf_op jit(solution)/shard_map/ppermute | solution.py:400
  25.6 339.7 %collective-permute-start.9 = (bf16[512,1536]{1,0:T(8,128)(2,1)}, bf16[512,1536]{1,0:T(8,128)(2,1)}, u32[]{:S(2)}, u32[]{:S(2)}) collective-permute-start(bf16[512,1536]{1,0:T(8,128)(2,1)} %refs_5_.3), channel_id=1, source_target_pairs={{0,8},{8,0},{1,9},{9,1},{2,10},{10,2},{3,11},{11,3},{4,12},{12,4},... | collective-permute-start | bytes 4718600 | tf_op jit(solution)/shard_map/ppermute | solution.py:394
  29.6 6.4 copy-start.52
  36.3 75.8 %copy-start.69 = (f32[48]{0:T(128)}, f32[48]{0:T(128)S(1)}, u32[]{:S(2)}) copy-start(f32[48]{0:T(128)S(1)} %exp.17) | copy-start | bytes 580
  41.8 70.3 %copy-start.50 = (f32[1536]{0:T(1024)}, f32[1536]{0:T(1024)S(1)}, u32[]{:S(2)}) copy-start(f32[1536]{0:T(1024)S(1)} %reshape.405) | copy-start | bytes 18436
  44.9 69.1 %copy-start.61 = (f32[48]{0:T(128)S(1)}, f32[48]{0:T(128)}, u32[]{:S(2)}) copy-start(f32[48]{0:T(128)} %param.19) | copy-start | bytes 580
  116.1 20.7 %copy-start.41 = (f32[512,48]{1,0:T(8,128)}, f32[512,48]{1,0:T(8,128)S(1)}, u32[]{:S(2)}) copy-start(f32[512,48]{1,0:T(8,128)S(1)} %get-tuple-element.134) | copy-start | bytes 294916
  135.5 26.7 %collective-permute-start.2 = (f32[128,1536]{1,0:T(8,128)}, f32[128,1536]{1,0:T(8,128)S(1)}, u32[]{:S(2)}, u32[]{:S(2)}) collective-permute-start(f32[128,1536]{1,0:T(8,128)} %dynamic-slice_bitcast_fusion.1), channel_id=1, source_target_pairs={{0,1},{1,0},{2,3},{3,2},{4,5},{5,4},{6,7},{7,6},{8,9},{9,8},{10,11... | collective-permute-start | bytes 2359304 | tf_op jit(solution)/shard_map/ppermute | solution.py:394
  139.3 22.2 %collective-permute-start.1 = (f32[1,1536]{1,0:T(1,128)S(1)}, f32[1,1536]{1,0:T(1,128)S(1)}, u32[]{:S(2)}, u32[]{:S(2)}) collective-permute-start(f32[1,1536]{1,0:T(1,128)S(1)} %fusion.44), channel_id=1, source_target_pairs={{0,1},{1,0},{2,3},{3,2},{4,5},{5,4},{6,7},{7,6},{8,9},{9,8},{10,11... | collective-permute-start | bytes 18440 | tf_op jit(solution)/shard_map/ppermute | solution.py:394
  165.5 37.4 %collective-permute-start.3 = (f32[128,1536]{1,0:T(8,128)}, f32[128,1536]{1,0:T(8,128)S(1)}, u32[]{:S(2)}, u32[]{:S(2)}) collective-permute-start(f32[128,1536]{1,0:T(8,128)} %fusion.15.refs_6_), channel_id=1, source_target_pairs={{0,2},{1,3},{8,10},{9,11},{16,18},{17,19},{24,26},{25,27}} | collective-permute-start | bytes 2359304 | tf_op jit(solution)/shard_map/ppermute | solution.py:443
  205.0 14.0 %collective-permute-start.4 = (f32[128,1536]{1,0:T(8,128)S(1)}, f32[128,1536]{1,0:T(8,128)S(1)}, u32[]{:S(2)}, u32[]{:S(2)}) collective-permute-start(f32[128,1536]{1,0:T(8,128)S(1)} %multiply_add_fusion.7.refs_6_), channel_id=1, source_target_pairs={{2,4},{3,5},{10,12},{11,13},{18,20},{19,21},{26,28},{27,29}} | collective-permute-start | bytes 2359304 | tf_op jit(solution)/shard_map/ppermute | solution.py:443
  222.7 52.3 %collective-permute-start.5 = (f32[128,1536]{1,0:T(8,128)}, f32[128,1536]{1,0:T(8,128)}, u32[]{:S(2)}, u32[]{:S(2)}) collective-permute-start(f32[128,1536]{1,0:T(8,128)} %get-tuple-element.107), channel_id=1, source_target_pairs={{4,6},{5,7},{12,14},{13,15},{20,22},{21,23},{28,30},{29,31}} | collective-permute-start | bytes 2359304 | tf_op jit(solution)/shard_map/ppermute | solution.py:443
  253.0 9.9 %copy-start.30 = (bf16[528,1536]{1,0:T(8,128)(2,1)S(1)}, bf16[528,1536]{1,0:T(8,128)(2,1)}, u32[]{:S(2)}) copy-start(bf16[528,1536]{1,0:T(8,128)(2,1)} %multiply_convert_fusion) | copy-start | bytes 4866052
  278.8 29.4 %collective-permute-start.6 = (f32[128,1536]{1,0:T(8,128)}, f32[128,1536]{1,0:T(8,128)}, u32[]{:S(2)}, u32[]{:S(2)}) collective-permute-start(f32[128,1536]{1,0:T(8,128)} %get-tuple-element.113), channel_id=1, source_target_pairs={{0,1},{1,0},{2,3},{3,2},{4,5},{5,4},{6,7},{7,6},{8,9},{9,8},{10,11... | collective-permute-start | bytes 2359304 | tf_op jit(solution)/shard_map/ppermute | solution.py:394
  297.6 10.6 %copy-start.40 = (f32[1,128,1536]{2,1,0:T(8,128)S(1)}, f32[1,128,1536]{2,1,0:T(8,128)}, u32[]{:S(2)}) copy-start(f32[1,128,1536]{2,1,0:T(8,128)} %get-tuple-element.114) | copy-start | bytes 2359300
  302.4 93.3 %collective-permute-start.11 = (bf16[768,512]{1,0:T(8,128)(2,1)}, bf16[768,512]{1,0:T(8,128)(2,1)S(1)}, u32[]{:S(2)}, u32[]{:S(2)}) collective-permute-start(bf16[768,512]{1,0:T(8,128)(2,1)} %bitcast.216), channel_id=1, source_target_pairs={{0,8},{8,0},{1,9},{9,1},{2,10},{10,2},{3,11},{11,3},{4,12},{12,4},... | collective-permute-start | bytes 2359304 | tf_op jit(solution)/shard_map/ppermute | solution.py:394
  345.9 19.4 %collective-permute-start.8 = (bf16[1536,512]{1,0:T(8,128)(2,1)S(1)}, bf16[1536,512]{1,0:T(8,128)(2,1)S(1)}, u32[]{:S(2)}, u32[]{:S(2)}) collective-permute-start(bf16[1536,512]{1,0:T(8,128)(2,1)S(1)} %bitcast.214), channel_id=1, source_target_pairs={{0,8},{8,0},{1,9},{9,1},{2,10},{10,2},{3,11},{11,3},{4,12},{12,4},... | collective-permute-start | bytes 4718600 | tf_op jit(solution)/shard_map/ppermute | solution.py:394
  346.4 49.4 %collective-permute-start.12 = (bf16[512,3072]{1,0:T(8,128)(2,1)}, bf16[512,3072]{1,0:T(8,128)(2,1)}, u32[]{:S(2)}, u32[]{:S(2)}) collective-permute-start(bf16[512,3072]{1,0:T(8,128)(2,1)} %get-tuple-element.57.refs_5_), channel_id=1, source_target_pairs={{0,8},{8,0},{1,9},{9,1},{2,10},{10,2},{3,11},{11,3},{4,12},{12,4},... | collective-permute-start | bytes 9437192 | tf_op jit(solution)/shard_map/ppermute | solution.py:394
  346.6 9.9 %copy-start.33 = (f32[2,128,1536]{2,1,0:T(8,128)S(1)}, f32[2,128,1536]{2,1,0:T(8,128)}, u32[]{:S(2)}) copy-start(f32[2,128,1536]{2,1,0:T(8,128)} %get-tuple-element.60) | copy-start | bytes 4718596
  356.6 8.7 %copy-start.29 = (f32[128,1536]{1,0:T(8,128)}, f32[128,1536]{1,0:T(8,128)S(1)}, u32[]{:S(2)}) copy-start(f32[128,1536]{1,0:T(8,128)S(1)} %dynamic-slice_bitcast_fusion.refs_7_) | copy-start | bytes 2359300
  356.6 24.9 %collective-permute-start.7 = (f32[128,1536]{1,0:T(8,128)S(1)}, f32[128,1536]{1,0:T(8,128)S(1)}, u32[]{:S(2)}, u32[]{:S(2)}) collective-permute-start(f32[128,1536]{1,0:T(8,128)S(1)} %dynamic-slice_bitcast_fusion.refs_7_), channel_id=1, source_target_pairs={{0,1},{1,0},{2,3},{3,2},{4,5},{5,4},{6,7},{7,6},{8,9},{9,8},{10,11... | collective-permute-start | bytes 2359304 | tf_op jit(solution)/shard_map/ppermute | solution.py:394
  383.9 9.0 %copy-start.7 = (f32[128,1536]{1,0:T(8,128)}, f32[128,1536]{1,0:T(8,128)S(1)}, u32[]{:S(2)}) copy-start(f32[128,1536]{1,0:T(8,128)S(1)} %fusion.14.refs_7_) | copy-start | bytes 2359300
  383.9 8.9 %copy-start.48 = (f32[16,3072]{1,0:T(8,128)S(1)}, f32[16,3072]{1,0:T(8,128)}, u32[]{:S(2)}) copy-start(f32[16,3072]{1,0:T(8,128)} %get-tuple-element.90) | copy-start | bytes 589828
  383.9 28.3 %collective-permute-start.10 = (f32[128,1536]{1,0:T(8,128)S(1)}, f32[128,1536]{1,0:T(8,128)S(1)}, u32[]{:S(2)}, u32[]{:S(2)}) collective-permute-start(f32[128,1536]{1,0:T(8,128)S(1)} %fusion.14.refs_7_), channel_id=1, source_target_pairs={{6,4},{7,5},{14,12},{15,13},{22,20},{23,21},{30,28},{31,29}} | collective-permute-start | bytes 2359304 | tf_op jit(solution)/shard_map/ppermute | solution.py:443
  393.7 99.8 %collective-permute-start.34 = (bf16[768,768]{1,0:T(8,128)(2,1)}, bf16[768,768]{1,0:T(8,128)(2,1)}, u32[]{:S(2)}, u32[]{:S(2)}) collective-permute-start(bf16[768,768]{1,0:T(8,128)(2,1)} %get-tuple-element.65.refs_4_), channel_id=1, source_target_pairs={{0,1},{1,0},{2,3},{3,2},{4,5},{5,4},{6,7},{7,6},{8,9},{9,8},{10,11... | collective-permute-start | bytes 3538952 | tf_op jit(solution)/shard_map/ppermute | solution.py:465
  394.2 102.6 %collective-permute-start.32 = (bf16[768,768]{1,0:T(8,128)(2,1)}, bf16[768,768]{1,0:T(8,128)(2,1)}, u32[]{:S(2)}, u32[]{:S(2)}) collective-permute-start(bf16[768,768]{1,0:T(8,128)(2,1)} %get-tuple-element.64.refs_3_), channel_id=1, source_target_pairs={{0,16},{16,0},{1,17},{17,1},{2,18},{18,2},{3,19},{19,3},{4,20},{20... | collective-permute-start | bytes 3538952 | tf_op jit(solution)/shard_map/ppermute | solution.py:465
  403.4 77.6 %collective-permute-start.20 = (bf16[384,1536]{1,0:T(8,128)(2,1)}, bf16[384,1536]{1,0:T(8,128)(2,1)}, u32[]{:S(2)}, u32[]{:S(2)}) collective-permute-start(bf16[384,1536]{1,0:T(8,128)(2,1)} %get-tuple-element.69.refs_4_), channel_id=1, source_target_pairs={{0,1},{1,0},{2,3},{3,2},{4,5},{5,4},{6,7},{7,6},{8,9},{9,8},{10,11... | collective-permute-start | bytes 3538952 | tf_op jit(solution)/shard_map/ppermute | solution.py:465
  411.7 76.8 %collective-permute-start.18 = (bf16[384,1536]{1,0:T(8,128)(2,1)}, bf16[384,1536]{1,0:T(8,128)(2,1)}, u32[]{:S(2)}, u32[]{:S(2)}) collective-permute-start(bf16[384,1536]{1,0:T(8,128)(2,1)} %get-tuple-element.68.refs_3_), channel_id=1, source_target_pairs={{0,16},{16,0},{1,17},{17,1},{2,18},{18,2},{3,19},{19,3},{4,20},{20... | collective-permute-start | bytes 3538952 | tf_op jit(solution)/shard_map/ppermute | solution.py:465
  414.4 19.9 %collective-permute-start.13 = (f32[128,1536]{1,0:T(8,128)S(1)}, f32[128,1536]{1,0:T(8,128)S(1)}, u32[]{:S(2)}, u32[]{:S(2)}) collective-permute-start(f32[128,1536]{1,0:T(8,128)S(1)} %multiply_add_fusion.4.refs_10_), channel_id=1, source_target_pairs={{4,2},{5,3},{12,10},{13,11},{20,18},{21,19},{28,26},{29,27}} | collective-permute-start | bytes 2359304 | tf_op jit(solution)/shard_map/ppermute | solution.py:443
  437.4 37.8 %collective-permute-start.14 = (f32[128,1536]{1,0:T(8,128)S(1)}, f32[128,1536]{1,0:T(8,128)S(1)}, u32[]{:S(2)}, u32[]{:S(2)}) collective-permute-start(f32[128,1536]{1,0:T(8,128)S(1)} %get-tuple-element.105.refs_10_), channel_id=1, source_target_pairs={{2,0},{3,1},{10,8},{11,9},{18,16},{19,17},{26,24},{27,25}} | collective-permute-start | bytes 2359304 | tf_op jit(solution)/shard_map/ppermute | solution.py:443
  480.1 21.5 %collective-permute-start.15 = (f32[128,1536]{1,0:T(8,128)S(1)}, f32[128,1536]{1,0:T(8,128)}, u32[]{:S(2)}, u32[]{:S(2)}) collective-permute-start(f32[128,1536]{1,0:T(8,128)S(1)} %get-tuple-element.112.refs_1_), channel_id=1, source_target_pairs={{0,1},{1,0},{2,3},{3,2},{4,5},{5,4},{6,7},{7,6},{8,9},{9,8},{10,11... | collective-permute-start | bytes 2359304 | tf_op jit(solution)/shard_map/ppermute | solution.py:394
  487.0 6.5 copy-start.5
  487.0 69.6 %collective-permute-start.21 = (bf16[4,48,1536]{2,1,0:T(8,128)(2,1)}, bf16[4,48,1536]{2,1,0:T(8,128)(2,1)}, u32[]{:S(2)}, u32[]{:S(2)}) collective-permute-start(bf16[4,48,1536]{2,1,0:T(8,128)(2,1)} %fusion.30), channel_id=1, source_target_pairs={{0,16},{16,0},{1,17},{17,1},{2,18},{18,2},{3,19},{19,3},{4,20},{20... | collective-permute-start | bytes 1769480 | tf_op jit(solution)/shard_map/ppermute | solution.py:465
  492.4 66.2 %collective-permute-start.19 = (bf16[4,48,1536]{2,1,0:T(8,128)(2,1)}, bf16[4,48,1536]{2,1,0:T(8,128)(2,1)}, u32[]{:S(2)}, u32[]{:S(2)}) collective-permute-start(bf16[4,48,1536]{2,1,0:T(8,128)(2,1)} %fusion.32), channel_id=1, source_target_pairs={{0,1},{1,0},{2,3},{3,2},{4,5},{5,4},{6,7},{7,6},{8,9},{9,8},{10,11... | collective-permute-start | bytes 1769480 | tf_op jit(solution)/shard_map/ppermute | solution.py:465
  496.1 57.1 %collective-permute-start.35 = (bf16[4,96,768]{2,1,0:T(8,128)(2,1)}, bf16[4,96,768]{2,1,0:T(8,128)(2,1)}, u32[]{:S(2)}, u32[]{:S(2)}) collective-permute-start(bf16[4,96,768]{2,1,0:T(8,128)(2,1)} %fusion.31), channel_id=1, source_target_pairs={{0,16},{16,0},{1,17},{17,1},{2,18},{18,2},{3,19},{19,3},{4,20},{20... | collective-permute-start | bytes 1769480 | tf_op jit(solution)/shard_map/ppermute | solution.py:465
  500.7 50.7 %collective-permute-start.33 = (bf16[4,96,768]{2,1,0:T(8,128)(2,1)}, bf16[4,96,768]{2,1,0:T(8,128)(2,1)}, u32[]{:S(2)}, u32[]{:S(2)}) collective-permute-start(bf16[4,96,768]{2,1,0:T(8,128)(2,1)} %fusion.34), channel_id=1, source_target_pairs={{0,1},{1,0},{2,3},{3,2},{4,5},{5,4},{6,7},{7,6},{8,9},{9,8},{10,11... | collective-permute-start | bytes 1769480 | tf_op jit(solution)/shard_map/ppermute | solution.py:465
  504.5 29.4 %copy-start.45 = (f32[512,256]{1,0:T(8,128)S(1)}, f32[512,256]{1,0:T(8,128)}, u32[]{:S(2)}) copy-start(f32[512,256]{1,0:T(8,128)} %get-tuple-element.75) | copy-start | bytes 1572868
  504.5 29.4 %copy-start.47 = (f32[512,128]{1,0:T(8,128)S(1)}, f32[512,128]{1,0:T(8,128)}, u32[]{:S(2)}) copy-start(f32[512,128]{1,0:T(8,128)} %get-tuple-element.77) | copy-start | bytes 786436
  539.6 7.9 %collective-permute-start.16 = (f32[16,3328]{1,0:T(8,128)S(1)}, f32[16,3328]{1,0:T(8,128)S(1)}, u32[]{:S(2)}, u32[]{:S(2)}) collective-permute-start(f32[16,3328]{1,0:T(8,128)S(1)} %slice.217), channel_id=1, source_target_pairs={{1,0},{2,1},{3,2},{4,3},{5,4},{6,5},{7,6},{9,8},{10,9},{11,10},{12... | collective-permute-start | bytes 638984 | tf_op jit(solution)/shard_map/ppermute | solution.py:400
  551.5 23.5 %collective-permute-start.17 = (bf16[512,3376]{0,1:T(8,128)(2,1)}, bf16[512,3376]{0,1:T(8,128)(2,1)}, u32[]{:S(2)}, u32[]{:S(2)}) collective-permute-start(bf16[512,3376]{0,1:T(8,128)(2,1)} %copy.146), channel_id=1, source_target_pairs={{0,8},{8,0},{1,9},{9,1},{2,10},{10,2},{3,11},{11,3},{4,12},{12,4},... | collective-permute-start | bytes 10371080 | tf_op jit(solution)/shard_map/ppermute | solution.py:394
  565.0 145.3 %collective-permute-start.28 = (f32[48,3072]{1,0:T(8,128)}, f32[48,3072]{1,0:T(8,128)}, u32[]{:S(2)}, u32[]{:S(2)}) collective-permute-start(f32[48,3072]{1,0:T(8,128)} %get-tuple-element.127), channel_id=1, source_target_pairs={{0,6},{2,4},{4,2},{6,0},{1,7},{3,5},{5,3},{7,1},{8,14},{10,12},{12... | collective-permute-start | bytes 1769480 | tf_op jit(solution)/shard_map/ppermute | solution.py:465
  569.2 143.5 %collective-permute-start.27 = (f32[48,3072]{1,0:T(8,128)}, f32[48,3072]{1,0:T(8,128)}, u32[]{:S(2)}, u32[]{:S(2)}) collective-permute-start(f32[48,3072]{1,0:T(8,128)} %get-tuple-element.128), channel_id=1, source_target_pairs={{0,4},{2,6},{4,0},{6,2},{1,5},{3,7},{5,1},{7,3},{8,12},{10,14},{12... | collective-permute-start | bytes 1769480 | tf_op jit(solution)/shard_map/ppermute | solution.py:465
  573.0 109.3 %collective-permute-start.38 = (f32[96,1536]{1,0:T(8,128)}, f32[96,1536]{1,0:T(8,128)}, u32[]{:S(2)}, u32[]{:S(2)}) collective-permute-start(f32[96,1536]{1,0:T(8,128)} %get-tuple-element.123), channel_id=1, source_target_pairs={{0,6},{2,4},{4,2},{6,0},{1,7},{3,5},{5,3},{7,1},{8,14},{10,12},{12... | collective-permute-start | bytes 1769480 | tf_op jit(solution)/shard_map/ppermute | solution.py:465
  595.5 57.3 %collective-permute-start.22 = (bf16[384,1536]{1,0:T(8,128)(2,1)}, bf16[384,1536]{1,0:T(8,128)(2,1)}, u32[]{:S(2)}, u32[]{:S(2)}) collective-permute-start(bf16[384,1536]{1,0:T(8,128)(2,1)} %get-tuple-element.87.refs_3_), channel_id=1, source_target_pairs={{0,16},{16,0},{1,17},{17,1},{2,18},{18,2},{3,19},{19,3},{4,20},{20... | collective-permute-start | bytes 3538952 | tf_op jit(solution)/shard_map/ppermute | solution.py:465
  609.0 15.0 %copy-start.2 = (f32[512,1536]{1,0:T(8,128)}, f32[512,1536]{1,0:T(8,128)S(1)}, u32[]{:S(2)}) copy-start(f32[512,1536]{1,0:T(8,128)S(1)} %get-tuple-element.145.refs_1_) | copy-start | bytes 9437188
  613.6 37.2 %all-to-all-start.1 = ((f32[32,1,808]{2,1,0:T(1,128)}), f32[32,1,808]{2,1,0:T(1,128)S(1)}, u32[]{:S(2)}, u32[]{:S(2)}) async-start(f32[32,1,808]{2,1,0:T(1,128)} %copy.152), calls=%async_computation.1 | async-start | bytes 229376 | tf_op jit(solution)/shard_map/all_to_all | solution.py:943
  617.3 39.7 %collective-permute-start.24 = (bf16[384,1840]{0,1:T(8,128)(2,1)}, bf16[384,1840]{0,1:T(8,128)(2,1)}, u32[]{:S(2)}, u32[]{:S(2)}) collective-permute-start(bf16[384,1840]{0,1:T(8,128)(2,1)} %copy.155), channel_id=1, source_target_pairs={{0,1},{1,0},{2,3},{3,2},{4,5},{5,4},{6,7},{7,6},{8,9},{9,8},{10,11... | collective-permute-start | bytes 4239368 | tf_op jit(solution)/shard_map/ppermute | solution.py:465
  656.6 14.7 %collective-permute-start.23 = (bf16[4,48,1536]{2,1,0:T(8,128)(2,1)S(1)}, bf16[4,48,1536]{2,1,0:T(8,128)(2,1)}, u32[]{:S(2)}, u32[]{:S(2)}) collective-permute-start(bf16[4,48,1536]{2,1,0:T(8,128)(2,1)S(1)} %fusion.33), channel_id=1, source_target_pairs={{0,1},{1,0},{2,3},{3,2},{4,5},{5,4},{6,7},{7,6},{8,9},{9,8},{10,11... | collective-permute-start | bytes 1769480 | tf_op jit(solution)/shard_map/ppermute | solution.py:465
  659.6 12.2 %copy-start.20 = (f32[384,1536]{1,0:T(8,128)S(1)}, f32[384,1536]{1,0:T(8,128)}, u32[]{:S(2)}) copy-start(f32[384,1536]{1,0:T(8,128)} %copy-done.19) | copy-start | bytes 7077892
  661.4 18.3 %collective-permute-start.25 = (bf16[4,48,1840]{2,1,0:T(8,128)(2,1)S(1)}, bf16[4,48,1840]{2,1,0:T(8,128)(2,1)S(1)}, u32[]{:S(2)}, u32[]{:S(2)}) collective-permute-start(bf16[4,48,1840]{2,1,0:T(8,128)(2,1)S(1)} %fusion.18), channel_id=1, source_target_pairs={{0,16},{16,0},{1,17},{17,1},{2,18},{18,2},{3,19},{19,3},{4,20},{20... | collective-permute-start | bytes 2119688 | tf_op jit(solution)/shard_map/ppermute | solution.py:465
  671.3 27.5 %collective-permute-start.37 = (f32[96,1536]{1,0:T(8,128)}, f32[96,1536]{1,0:T(8,128)}, u32[]{:S(2)}, u32[]{:S(2)}) collective-permute-start(f32[96,1536]{1,0:T(8,128)} %get-tuple-element.124), channel_id=1, source_target_pairs={{0,4},{2,6},{4,0},{6,2},{1,5},{3,7},{5,1},{7,3},{8,12},{10,14},{12... | collective-permute-start | bytes 1769480 | tf_op jit(solution)/shard_map/ppermute | solution.py:465
  679.7 27.3 %collective-permute-start.36 = (f32[96,1536]{1,0:T(8,128)}, f32[96,1536]{1,0:T(8,128)}, u32[]{:S(2)}, u32[]{:S(2)}) collective-permute-start(f32[96,1536]{1,0:T(8,128)} %get-tuple-element.122), channel_id=1, source_target_pairs={{0,2},{2,0},{4,6},{6,4},{1,3},{3,1},{5,7},{7,5},{8,10},{10,8},{12,... | collective-permute-start | bytes 1769480 | tf_op jit(solution)/shard_map/ppermute | solution.py:465
  682.3 51.6 %collective-permute-start.26 = (f32[48,3072]{1,0:T(8,128)}, f32[48,3072]{1,0:T(8,128)}, u32[]{:S(2)}, u32[]{:S(2)}) collective-permute-start(f32[48,3072]{1,0:T(8,128)} %get-tuple-element.126), channel_id=1, source_target_pairs={{0,2},{2,0},{4,6},{6,4},{1,3},{3,1},{5,7},{7,5},{8,10},{10,8},{12,... | collective-permute-start | bytes 1769480 | tf_op jit(solution)/shard_map/ppermute | solution.py:465
  684.8 49.1 %copy-start.32 = (f32[48,3072]{1,0:T(8,128)S(1)}, f32[48,3072]{1,0:T(8,128)}, u32[]{:S(2)}) copy-start(f32[48,3072]{1,0:T(8,128)} %shard_map.231) | copy-start | bytes 1769476
  698.8 36.6 %collective-permute-start.31 = (f32[48,3376]{1,0:T(8,128)}, f32[48,3376]{1,0:T(8,128)S(1)}, u32[]{:S(2)}, u32[]{:S(2)}) collective-permute-start(f32[48,3376]{1,0:T(8,128)} %get-tuple-element.121), channel_id=1, source_target_pairs={{0,6},{2,4},{4,2},{6,0},{1,7},{3,5},{5,3},{7,1},{8,14},{10,12},{12... | collective-permute-start | bytes 1944584 | tf_op jit(solution)/shard_map/ppermute | solution.py:465
  707.0 50.1 %collective-permute-start.30 = (f32[48,3376]{1,0:T(8,128)}, f32[48,3376]{1,0:T(8,128)S(1)}, u32[]{:S(2)}, u32[]{:S(2)}) collective-permute-start(f32[48,3376]{1,0:T(8,128)} %get-tuple-element.120), channel_id=1, source_target_pairs={{0,4},{2,6},{4,0},{6,2},{1,5},{3,7},{5,1},{7,3},{8,12},{10,14},{12... | collective-permute-start | bytes 1944584 | tf_op jit(solution)/shard_map/ppermute | solution.py:465
  710.3 49.9 %collective-permute-start.29 = (f32[48,3376]{1,0:T(8,128)S(1)}, f32[48,3376]{1,0:T(8,128)S(1)}, u32[]{:S(2)}, u32[]{:S(2)}) collective-permute-start(f32[48,3376]{1,0:T(8,128)S(1)} %get-tuple-element.119), channel_id=1, source_target_pairs={{0,2},{2,0},{4,6},{6,4},{1,3},{3,1},{5,7},{7,5},{8,10},{10,8},{12,... | collective-permute-start | bytes 1944584 | tf_op jit(solution)/shard_map/ppermute | solution.py:465
  (54 other events, 141.1 us)
Sparse Core Ops, SparseCore 0:
  11.6 90.0 all-gather.2
  105.1 131.9 all-gather.4

commit v3 on v2

v3 whole, which is shorter than its diff:
```python
import functools

import jax
import jax.numpy as jnp
from jax import lax
from jax.experimental import pallas as pl
from jax.experimental.pallas import tpu as pltpu
from jax.sharding import Mesh, PartitionSpec as P

HEADS = 48
HEAD_DIM = 64
STATE = 128
CONV_K = 4
INNER = 3072
CONVW = 3328
LEAD = 16
PROJ_X = 3456
BLOCK = 512
BLOCK_HEADS = BLOCK // HEAD_DIM
PAIRS = 2
PAIR_LANES = 128 * PAIRS
VMEM = 56 * 1024 * 1024
F32 = jnp.float32
BF = jnp.bfloat16
EPS = 1e-05
highest = lax.Precision.HIGHEST
EVERY = ("x", "core", "z", "y")
CTX = ("z", "y")


def params():
    return pltpu.CompilerParams(vmem_limit_bytes=VMEM, dimension_semantics=("arbitrary",))


def call(body, grid, micros, ins, outs, scratch=(), waits=(), places=None):
    first = (places is not None) + len(ins)
    anywhere = pl.BlockSpec(memory_space=pl.ANY)

    def run(*refs):
        body(*refs[:first], *refs[first + len(waits) :])

    scalars = [] if places is None else [places]
    return pl.pallas_call(
        run,
        grid_spec=pltpu.PrefetchScalarGridSpec(
            num_scalar_prefetch=len(scalars),
            grid=(grid,),
            in_specs=[spec for _, spec in ins] + [anywhere] * len(waits),
            out_specs=[spec for _, spec in outs],
            scratch_shapes=list(scratch),
        ),
        out_shape=[shape for shape, _ in outs],
        compiler_params=params(),
        cost_estimate=pl.CostEstimate(
            flops=int(micros * 1e9), bytes_accessed=int(micros * 3e6), transcendentals=0
        ),
    )(*scalars, *[array for array, _ in ins], *waits)


def tie(value, *others):
    def body(*refs):
        pass

    anywhere = pl.BlockSpec(memory_space=pl.ANY)
    return pl.pallas_call(
        body,
        in_specs=[anywhere] * (1 + len(others)),
        out_specs=anywhere,
        out_shape=jax.ShapeDtypeStruct(value.shape, value.dtype),
        input_output_aliases={0: 0},
    )(value, *others)


def whole(*shape):
    return pl.BlockSpec(shape, lambda g: (0,) * len(shape))


def lanes(rows, width):
    return pl.BlockSpec((rows, width), lambda g: (0, g))


def rows_of(count, width):
    return pl.BlockSpec((count, width), lambda g: (g, 0))


def halves(rows, width):
    count = INNER // 2 // width
    return pl.BlockSpec((1, rows, width), lambda g: (g // count, 0, g % count))


def group(rows, width):
    return pl.BlockSpec((1, rows, width), lambda g: (g, 0, 0))


def out(shape, dtype=F32):
    return jax.ShapeDtypeStruct(shape, dtype)


def split(value):
    high = value.astype(BF)
    return high, (value - high.astype(F32)).astype(BF)


def mm(left, right):
    return jnp.dot(left, right, preferred_element_type=F32)


def mm_nt(left, right):
    return lax.dot_general(left, right, (((1,), (1,)), ((), ())), preferred_element_type=F32)


def mm_tn(left, right):
    return lax.dot_general(left, right, (((0,), (0,)), ((), ())), preferred_element_type=F32)


def three(product, left, right):
    left_high, left_low = left
    right_high, right_low = right
    return (
        product(left_high, right_high)
        + product(left_high, right_low)
        + product(left_low, right_high)
    )


def head_of_lane(first, count):
    lane = lax.broadcasted_iota(jnp.int32, (STATE, count), 1) // HEAD_DIM + first
    row = lax.broadcasted_iota(jnp.int32, (STATE, count), 0)
    return (lane == row).astype(BF)


def expand(value, places):
    high, low = split(value)
    return mm(high, places) + mm(low, places)


def fold(value, places):
    high, low = split(value)
    return mm_nt(high, places) + mm_nt(low, places)


def sigmoid(value):
    return 1.0 / (1.0 + jnp.exp(-value))


def conv_pre(extended, weight, bias, masks):
    running = jnp.zeros((masks.shape[0], extended.shape[1]), F32) + bias
    for tap in range(CONV_K):
        shifted = extended if tap == CONV_K - 1 else pltpu.roll(extended, CONV_K - 1 - tap, 0)
        running = running + shifted[LEAD:] * weight[tap : tap + 1] * masks[:, tap : tap + 1]
    return running


def conv_back(d_pre, extended, weight, masks):
    zeros = jnp.zeros((LEAD, d_pre.shape[1]), F32)
    total = LEAD + d_pre.shape[0]
    d_ext = jnp.zeros((total, d_pre.shape[1]), F32)
    weight_rows = []
    for tap in range(CONV_K):
        by = CONV_K - 1 - tap
        part = d_pre * masks[:, tap : tap + 1]
        padded = jnp.concatenate([zeros, part], axis=0)
        shifted = extended
        if by:
            padded = pltpu.roll(padded, total - by, 0)
            shifted = pltpu.roll(extended, by, 0)
        d_ext = d_ext + padded * weight[tap : tap + 1]
        weight_rows.append(jnp.sum(shifted[LEAD:] * part, axis=0, keepdims=True))
    weight_rows.append(jnp.sum(d_pre, axis=0, keepdims=True))
    weight_rows.append(jnp.zeros((8 - len(weight_rows), d_pre.shape[1]), F32))
    return d_ext, jnp.concatenate(weight_rows, axis=0)


def same_mask(doc_row, doc_col, transposed):
    count = doc_row.shape[1]
    rows = lax.broadcasted_iota(jnp.int32, (count, count), 0)
    cols = lax.broadcasted_iota(jnp.int32, (count, count), 1)
    order = rows <= cols if transposed else rows >= cols
    return jnp.where((doc_row == doc_col) & order, 1.0, 0.0)


def norm_body(lead_ref, x_ref, gain_ref, normed_ref, turned_ref):
    def normed(value):
        scale = lax.rsqrt(jnp.mean(value * value, axis=-1, keepdims=True) + EPS)
        return value * scale * gain_ref[...]

    normed_ref[:LEAD] = normed(lead_ref[...].astype(F32)).astype(BF)
    for tile in range(x_ref.shape[0] // 128):
        here = slice(tile * 128, tile * 128 + 128)
        value = normed(x_ref[here].astype(F32))
        normed_ref[LEAD + tile * 128 : LEAD + tile * 128 + 128] = value.astype(BF)
        turned_ref[:, here] = value.T.astype(BF)


def parts_of(value):
    high, low = split(value)
    return high, low, (value - high.astype(F32) - low.astype(F32)).astype(BF)


def running_sum(value, transposed):
    count = value.shape[0]
    rows = lax.broadcasted_iota(jnp.int32, (count, count), 0)
    cols = lax.broadcasted_iota(jnp.int32, (count, count), 1)
    side = ((rows <= cols) if transposed else (rows >= cols)).astype(BF)
    high, middle, low = parts_of(value)
    return mm(side, high) + mm(side, middle) + mm(side, low)


def softplus(value):
    return jnp.maximum(value, 0.0) + jnp.log1p(jnp.exp(-jnp.abs(value)))


def prep_bc_body(
    x_ref, dr_ref, w_ref, b_ref, m_ref, doc_ref, shift_ref, rate_ref,
    pre_ref, act_ref, t_ref, s_ref, st_ref, steps_ref, enter_ref, to_end_ref, cum_ref, turned_ref, dt_ref,
):
    masks = m_ref[...]
    pre = conv_pre(x_ref[...].astype(F32), w_ref[...], b_ref[...], masks)
    act = pre * sigmoid(pre)
    pre_ref[...] = pre
    act_ref[...] = act
    t_ref[...] = act.T
    b_rows, c_rows = split(act[:, :STATE]), split(act[:, STATE:])
    doc_row, doc_col = doc_ref[0:1], masks[:, CONV_K : CONV_K + 1]
    s_ref[...] = three(mm_nt, c_rows, b_rows) * same_mask(doc_row, doc_col, False)
    st_ref[...] = three(mm_nt, b_rows, c_rows) * same_mask(doc_row, doc_col, True)
    shifted = dr_ref[LEAD:, :].astype(F32) + shift_ref[...]
    steps = softplus(shifted)
    cumulative = running_sum(-steps * rate_ref[...], False)
    last = cumulative[cumulative.shape[0] - 1 :]
    dt_ref[...] = shifted
    steps_ref[...] = steps
    enter_ref[...] = jnp.exp(cumulative) * masks[:, CONV_K + 1 : CONV_K + 2]
    to_end_ref[...] = jnp.exp(last - cumulative) * masks[:, CONV_K + 2 : CONV_K + 3]
    cum_ref[...] = cumulative
    turned_ref[...] = cumulative.T


def prep_x_body(
    x_ref, w_ref, b_ref, m_ref, wl_ref, dt_ref, e_ref, t_ref, pre_ref, act_ref, state_ref, decay_ref
):
    pre = conv_pre(x_ref[...].astype(F32), w_ref[...], b_ref[...], m_ref[...])
    act = pre * sigmoid(pre)
    pre_ref[...] = pre
    act_ref[...] = act
    places = head_of_lane(pl.program_id(0) * BLOCK_HEADS, BLOCK)
    weighted = split(act * expand(wl_ref[...] * dt_ref[...], places))
    state_ref[0] = three(mm, split(t_ref[:STATE]), weighted)
    last = e_ref[e_ref.shape[0] - 8 :]
    high, middle, low = parts_of(last)
    spread = mm(high, places) + mm(middle, places) + mm(low, places)
    decay_ref[0] = jnp.broadcast_to(spread[7:8], spread.shape)


def heads_here(cum_ref, first):
    back = STATE - (pl.program_id(0) + first) * 2 * PAIRS
    return pltpu.roll(cum_ref[...], jnp.where(back == STATE, 0, back), 1)


def intra_body(first, x_ref, dt_ref, skip_ref, s_ref, cum_ref, row_ref, y_ref):
    half = s_ref.shape[0] // 2
    places = head_of_lane((pl.program_id(0) + first) * 2 * PAIRS, PAIR_LANES)
    scaled = x_ref[...] * expand(dt_ref[...], places)
    cols = heads_here(cum_ref, first)
    lane = lax.broadcasted_iota(jnp.int32, (2 * half, 128), 1)
    for pair in range(PAIRS):
        here = slice(pair * 128, pair * 128 + 128)
        high, low = split(scaled[:, here])
        right = jnp.concatenate([high, low], axis=1)
        both = []
        for side in range(2):
            head = 2 * pair + side
            col = cols[:, head : head + 1]
            row = row_ref[0, head : head + 1, :]
            top = s_ref[:half, :half] * jnp.exp(jnp.minimum(col[:half] - row[:, :half], 0.0))
            low_part = s_ref[half:, :] * jnp.exp(jnp.minimum(col[half:] - row, 0.0))
            done = []
            for part, count in ((top, half), (low_part, 2 * half)):
                p_high, p_low = split(part)
                first = mm(p_high, right[:count])
                done.append(first[:, :128] + first[:, 128:] + mm(p_low, high[:count]))
            both.append(jnp.concatenate(done, axis=0))
        y_ref[:, here] = (
            jnp.where(lane < HEAD_DIM, both[0], both[1]) + skip_ref[:, here] * x_ref[:, here]
        )


def gate_body(
    ya_ref, yb_ref, za_ref, zb_ref, df_ref, x_ref, c_ref, ct_ref, state_ref, e_ref, gain_ref, skip_ref,
    final_ref, turned_ref, dz_ref, dy_ref, r_ref, dc_ref, q_ref, sums_ref, carry, scaled,
):
    @pl.when(pl.program_id(0) == 0)
    def _():
        r_ref[...] = jnp.zeros_like(r_ref)
        sums_ref[...] = jnp.zeros_like(sums_ref)

    e_high, e_low = split(e_ref[...])
    c_rows = split(c_ref[...])
    for block in range(INNER // BLOCK):
        here = slice(block * BLOCK, block * BLOCK + BLOCK)
        places = head_of_lane(block * BLOCK_HEADS, BLOCK)
        spread = mm(e_high, places) + mm(e_low, places)
        there = slice(block % 3 * BLOCK, block % 3 * BLOCK + BLOCK)
        carry[:, here] = three(mm, c_rows, split(state_ref[block // 3, :, there])) * spread
        scaled[:, here] = spread
    gain, skip = gain_ref[...], skip_ref[...]

    def some(lap, sums):
        at = pl.ds(pl.multiple_of(lap * 16, 16), 16)
        y = jnp.concatenate([ya_ref[at, :], yb_ref[at, :]], axis=1) + carry[at, :]
        z = jnp.concatenate([za_ref[at, :], zb_ref[at, :]], axis=1).astype(F32)
        sig = sigmoid(z)
        gate = z * sig
        gated = y * gate
        scale = lax.rsqrt(jnp.mean(gated * gated, axis=-1, keepdims=True) + EPS)
        unit = gated * scale
        final_ref[at, :] = (unit * gain).astype(BF)
        d_final = df_ref[at, :]
        q = d_final * gain
        inner = jnp.mean(q * unit, axis=-1, keepdims=True)
        d_gated = scale * (q - unit * inner)
        d_y = d_gated * gate
        dz_ref[at, :] = (d_gated * y * (sig * (1.0 + z * (1.0 - sig)))).astype(BF)
        dy_ref[at, :] = d_y
        x = x_ref[at, :]
        scaled[at, :] = scaled[at, :] * d_y
        carry[at, :] = d_y * (y - skip * x)
        d_gain, d_skip = d_final * unit, d_y * x
        return (
            sums[0] + d_gain[:8] + d_gain[8:],
            sums[1] + d_skip[:8] + d_skip[8:],
        )

    zero = jnp.zeros((8, INNER), F32)
    d_gain, d_skip = lax.fori_loop(0, za_ref.shape[0] // 16, some, (zero, zero))
    sums_ref[0:8] += d_gain
    sums_ref[8:16] += d_skip
    ct_rows = split(ct_ref[...])
    d_c = jnp.zeros(dc_ref.shape, F32)
    q_sum = jnp.zeros(q_ref.shape, F32)
    for block in range(INNER // BLOCK):
        here = slice(block * BLOCK, block * BLOCK + BLOCK)
        there = slice(block % 3 * BLOCK, block % 3 * BLOCK + BLOCK)
        piece = split(scaled[:, here])
        r_ref[block // 3, :, there] += three(mm, ct_rows, piece)
        d_c = d_c + three(mm_nt, piece, split(state_ref[block // 3, :, there]))
        turned_ref[here, :] = final_ref[:, here].T
        q_sum = q_sum + fold(carry[:, here], head_of_lane(block * BLOCK_HEADS, BLOCK))
    dc_ref[...] = d_c
    q_ref[...] = q_sum


def back_body(first, x_ref, dy_ref, dt_ref, st_ref, cum_ref, row_ref, bc_ref, doc_ref, m_ref, in_ref, dx_ref, acc, *ends):
    step = pl.program_id(0)
    half = st_ref.shape[0] // 2

    @pl.when(step == 0)
    def _():
        acc[...] = in_ref[...]

    places = head_of_lane((step + first) * 2 * PAIRS, PAIR_LANES)
    scaled = x_ref[...] * expand(dt_ref[...], places)
    cols = heads_here(cum_ref, first)
    lane = lax.broadcasted_iota(jnp.int32, (2 * half, 128), 1)
    for pair in range(PAIRS):
        here = slice(pair * 128, pair * 128 + 128)
        dy_high, dy_low = split(dy_ref[:, here])
        right = jnp.concatenate([dy_high, dy_low], axis=1)
        twice = jnp.concatenate([dy_high, dy_high], axis=1)
        both = []
        for side in range(2):
            head = 2 * pair + side
            mine = (lane < HEAD_DIM) if side == 0 else (lane >= HEAD_DIM)
            x_high, x_low = split(jnp.where(mine, scaled[:, here], 0.0))
            x_both = jnp.concatenate([x_high, x_low], axis=1)
            col = cols[:, head : head + 1]
            row = row_ref[0, head : head + 1, :]
            done = []
            for at, over in ((slice(0, half), slice(0, 2 * half)), (slice(half, 2 * half), slice(half, 2 * half))):
                decay = jnp.exp(jnp.minimum(row[:, over] - col[at], 0.0))
                p_high, p_low = split(st_ref[at, over] * decay)
                first = mm(p_high, right[over])
                done.append(first[:, :128] + first[:, 128:] + mm(p_low, dy_high[over]))
                outer = mm_nt(x_both[at], twice[over]) + mm_nt(x_high[at], dy_low[over])
                acc[at, over] += outer * decay
            both.append(jnp.concatenate(done, axis=0))
        dx_ref[:, here] = jnp.where(lane < HEAD_DIM, both[0], both[1])

    if not ends:
        return

    @pl.when(step == pl.num_programs(0) - 1)
    def _():
        dbc_ref = ends[0]
        doc_col = m_ref[:, CONV_K : CONV_K + 1]
        ds = split(acc[...] * same_mask(doc_ref[0:1], doc_col, True))
        dbc_ref[:, :STATE] = three(mm, ds, split(bc_ref[:, STATE:]))
        dbc_ref[:, STATE:] = three(mm_tn, ds, split(bc_ref[:, :STATE]))


def carry_body(
    first, dx_ref, x_ref, dy_ref, pre_ref, in_ref, w_ref, m_ref, bc_ref, r_ref, end_ref, wl_ref, dt_ref,
    skip_ref, db_in, g_in, flow_in, *refs,
):
    extra = refs[:-6]
    d_ref, edge_ref, conv_ref, db_ref, g_ref, flow_ref = refs[-6:]
    if extra:
        pre_bc, in_bc, w_bc, dbc_ref, dc_ref, shifted_ref, rate_ref, q_ref, heads_ref = extra
    step = pl.program_id(0)
    count = INNER // 2 // BLOCK

    @pl.when(step == 0)
    def _():
        db_ref[...] = db_in[...]
        g_ref[...] = g_in[...]
        flow_ref[...] = flow_in[...]

    def conv(d_act, pre, inputs, weight, width):
        sig = sigmoid(pre)
        d_pre = d_act * (sig * (1.0 + pre * (1.0 - sig)))
        d_ext, sums = conv_back(d_pre, inputs, weight, m_ref[...])
        d_ref[:, :width] = d_ext[LEAD:].astype(BF)
        edge_ref[:LEAD, :width] = d_ext[:LEAD]
        edge_ref[LEAD:, :width] = d_ext[d_ext.shape[0] - LEAD :]
        conv_ref[:, :width] = sums

    @pl.when(step < count)
    def _():
        places = head_of_lane((step + first) * BLOCK_HEADS, BLOCK)
        returned = r_ref[0]
        r_parts = split(returned)
        to_end = expand(wl_ref[...], places)
        steps = expand(dt_ref[...], places)
        x = x_ref[...]
        d_scaled = dx_ref[...] + to_end * three(mm, split(bc_ref[:, :STATE]), r_parts)
        g_ref[...] += fold(x * d_scaled, places)
        db_ref[...] += three(mm_nt, split(to_end * steps * x), r_parts)
        flow = jnp.sum(returned * end_ref[0], axis=0, keepdims=True)
        high, middle, low = parts_of(jnp.broadcast_to(flow, (8, BLOCK)))
        flow_ref[...] += mm_nt(high, places) + mm_nt(middle, places) + mm_nt(low, places)
        d_x = steps * d_scaled + skip_ref[...] * dy_ref[...]
        conv(d_x, pre_ref[...], in_ref[...].astype(F32), w_ref[...], BLOCK)

    if not extra:
        return

    @pl.when(step == count)
    def _():
        width = 2 * STATE
        d_bc = jnp.concatenate([dbc_ref[:, :STATE] + db_ref[...], dbc_ref[:, STATE:] + dc_ref[...]], axis=1)
        conv(d_bc, pre_bc[...], in_bc[...].astype(F32), w_bc[...], width)
        masks = m_ref[...]
        steps, rate, shifted = dt_ref[...], rate_ref[...], shifted_ref[...]
        difference = q_ref[...] - steps * g_ref[...]
        d_log = (flow_ref[0:1] + running_sum(difference, True)) * masks[:, CONV_K - 2 : CONV_K - 1]
        d_steps = g_ref[...] - rate * d_log
        d_dt = d_steps * sigmoid(shifted)
        head = lax.broadcasted_iota(jnp.int32, d_dt.shape, 1) < HEADS
        d_dt = jnp.where(head, d_dt, 0.0)
        d_ref[:, width : width + STATE] = d_dt.astype(BF)
        edge_ref[:LEAD, width : width + STATE] = jnp.zeros((LEAD, STATE), F32)
        edge_ref[LEAD:, width : width + STATE] = d_dt[d_dt.shape[0] - LEAD :]
        conv_ref[:, width : width + STATE] = jnp.zeros((8, STATE), F32)
        heads_ref[0:8] = jnp.broadcast_to(jnp.sum(d_dt, axis=0, keepdims=True), (8, STATE))
        log_sum = -jnp.sum(steps * rate * d_log, axis=0, keepdims=True)
        heads_ref[8:16] = jnp.broadcast_to(log_sum, (8, STATE))


def woven(ref, devices, rows):
    pieces = [ref[side, d * rows : d * rows + rows, :] for d in range(devices) for side in range(2)]
    return jnp.concatenate(pieces, axis=0)


def d_final_body(devices, rows, g_ref, w_ref, o_ref):
    o_ref[...] = mm_nt(g_ref[...], woven(w_ref, devices, rows))


def layer_body(devices, rows, f_ref, w_ref, t_ref, o_ref, total):
    @pl.when(pl.program_id(0) == 0)
    def _():
        total[...] = t_ref[...].astype(F32)

    total[...] += mm(f_ref[...], woven(w_ref, devices, rows))

    @pl.when(pl.program_id(0) == pl.num_programs(0) - 1)
    def _():
        o_ref[...] = total[...].astype(BF)


def back_z_body(d_ref, w_ref, o_ref):
    half = w_ref.shape[2]
    o_ref[...] = mm_nt(d_ref[:, :half], w_ref[0]) + mm_nt(d_ref[:, half:], w_ref[1])


def back_x_body(da_ref, db_ref, w_ref, part_ref, o_ref):
    half = da_ref.shape[1]
    o_ref[...] = part_ref[...] + mm_nt(da_ref[...], w_ref[:, :half]) + mm_nt(db_ref[...], w_ref[:, half:])


def back_norm_body(d_ref, x_ref, og_ref, gain_ref, o_ref, sum_ref):
    @pl.when(pl.program_id(0) == 0)
    def _():
        sum_ref[...] = jnp.zeros_like(sum_ref)

    d_normed = d_ref[...]
    x = x_ref[...].astype(F32)
    scale = lax.rsqrt(jnp.mean(x * x, axis=-1, keepdims=True) + EPS)
    unit = x * scale
    pulled = d_normed * gain_ref[...]
    inner = jnp.mean(pulled * unit, axis=-1, keepdims=True)
    o_ref[...] = og_ref[...].astype(F32) + scale * (pulled - unit * inner)
    total = jnp.sum(d_normed * unit, axis=0, keepdims=True)
    sum_ref[...] += jnp.broadcast_to(total, sum_ref.shape)


def swap(array, axis):
    return lax.ppermute(array, axis, [(0, 1), (1, 0)])


def from_behind(array, by):
    peers = lax.axis_size(CTX[0]) * lax.axis_size(CTX[1])
    pairs = [(i, i + by) for i in range(peers) if 0 <= i + by < peers]
    return lax.ppermute(array, CTX, pairs)


def entering(state, decay, reverse, fills):
    fills = list(fills)

    def meanwhile(sent, arrived):
        return tie(arrived, *fills.pop(0)(sent)) if fills else arrived

    depth, width = lax.axis_size("z"), lax.axis_size("y")
    place_z, place_y = lax.axis_index("z"), lax.axis_index("y")
    if width != 2:
        gathered = lax.all_gather(jnp.concatenate([state, decay], axis=1), CTX)
        while fills:
            gathered = meanwhile(state, gathered)
        count = depth * width
        place = place_z * width + place_y
        ahead = count - 1 - place if reverse else place

        def one(lap, running):
            source = count - 1 - lap if reverse else lap
            item = lax.dynamic_index_in_dim(gathered, source, 0, False)
            return item[:, STATE : STATE + 1] * running + item[:, :STATE]

        return lax.fori_loop(0, ahead, one, jnp.zeros_like(state))
    second = place_y == (0 if reverse else 1)
    sent = pick(state, 1 - place_y)
    got = meanwhile(sent, swap(sent, "y"))
    own = pick(state, place_y)
    decay_own = pick(decay, place_y)[:1]
    decay_got = swap(pick(decay, 1 - place_y), "y")[:1]
    early = jnp.where(second, got, own)
    late = jnp.where(second, own, got)
    decay_early = jnp.where(second, decay_got, decay_own)
    decay_late = jnp.where(second, decay_own, decay_got)
    total = decay_late * early + late
    decay_total = decay_early * decay_late
    before = jnp.zeros_like(total)
    sent = total
    turn = depth - 1 - place_z if reverse else place_z
    for hop in range(1, depth):
        pairs = [(depth - hop, depth - 1 - hop)] if reverse else [(hop - 1, hop)]
        arrived = meanwhile(sent, lax.ppermute(sent, "z", pairs))
        before = jnp.where(turn == hop, arrived, before)
        sent = decay_total * before + total
    middle = decay_early * before + early
    mine = jnp.where(second, middle, before)
    sent = jnp.where(second, before, middle)
    theirs = swap(sent, "y")
    while fills:
        theirs = meanwhile(sent, theirs)
    return in_order(mine, theirs, "y")


def pick(parts, index, dim=0):
    return lax.dynamic_index_in_dim(parts, index, dim, False)


def in_order(mine, theirs, axis):
    first = lax.axis_index(axis) == 0
    return jnp.where(first, jnp.stack([mine, theirs]), jnp.stack([theirs, mine]))


def across(array, axis, by):
    return lax.ppermute(array, axis, [(i, i ^ by) for i in range(lax.axis_size(axis))])


def products_body(
    patched, place_ref, sent_own, kept_own, sent_other, kept_other, own_ref, other_ref, *refs
):
    sent_ref, kept_ref = refs[-2:]
    own, other = own_ref[...], other_ref[...]
    if patched:
        upto = own.shape[0] - LEAD
        own = jnp.concatenate([own[:upto], refs[0][...]], axis=0)
        other = jnp.concatenate([other[:upto], refs[1][...]], axis=0)

    def product(first, second):
        first, second = first[...], second[...]
        first = first.reshape(-1, first.shape[-1])
        second = second.reshape(-1, second.shape[-1])
        return mm(first, own) + mm(second, other)

    sent_ref[...] = product(sent_own, sent_other).astype(BF)
    kept_ref[...] = product(kept_own, kept_other)


def products(left, right, start, count, axis, waits):
    own, other = left
    sizes = [lax.axis_size(a) for a in ("x", "z", "y")]
    tokens = own.shape[1]
    rows = other.shape[0] // sizes[0] // sizes[1] // sizes[2]
    out_rows = other.shape[0] // 2
    places = jnp.stack([lax.axis_index(a) for a in ("core", "x", "y")])
    if axis == "x":
        own = own.reshape(2, 2, out_rows, tokens)
        other = other.reshape(2, out_rows, tokens)
        own_block, other_block = (1, 1, out_rows, tokens), (1, out_rows, tokens)

        def spec(mine, flip):
            if mine:
                return pl.BlockSpec(own_block, lambda g, p: (p[1] ^ flip, p[0], 0, 0))
            return pl.BlockSpec(other_block, lambda g, p: (p[1] ^ flip, 0, 0))
    else:
        own = own.reshape(2, 2, sizes[1], 2, rows, tokens)
        other = other.reshape(2 * sizes[1], 2, rows, tokens)
        own_block = (2, 1, sizes[1], 1, rows, tokens)
        other_block = (2 * sizes[1], 1, rows, tokens)

        def spec(mine, flip):
            if mine:
                return pl.BlockSpec(own_block, lambda g, p: (0, p[0], 0, p[2] ^ flip, 0, 0))
            return pl.BlockSpec(other_block, lambda g, p: (0, p[2] ^ flip, 0, 0))

    block = 384 if count % 384 == 0 else 512
    first = start // block
    columns_of = pl.BlockSpec((tokens, block), lambda g, p: (0, g + first))
    edge_of = pl.BlockSpec((LEAD, block), lambda g, p: (0, g + first))
    result = pl.BlockSpec((out_rows, block), lambda g, p: (0, g))
    return call(
        functools.partial(products_body, len(right) > 2), -(-count // block), count * out_rows / 2.0e5,
        [
            (own, spec(True, 1)), (own, spec(True, 0)), (other, spec(False, 1)), (other, spec(False, 0)),
            (right[0], columns_of), (right[1], columns_of),
            *[(edge, edge_of) for edge in right[2:]],
        ],
        [(out((out_rows, count), BF), result), (out((out_rows, count)), result)],
        waits=waits,
        places=places,
    )


def products_any(left, right, start, count, axis):
    core, place = lax.axis_index("core"), lax.axis_index(axis)
    sizes = [lax.axis_size(a) for a in ("x", "z", "y")]
    own = core_rows(left[0], core).reshape(left[1].shape)
    both = jnp.concatenate([own, left[1]], axis=1)
    view = both.reshape(*sizes, -1, both.shape[1])
    if axis == "y":
        view = jnp.moveaxis(view, 2, 0)
    view = view.reshape(view.shape[0], -1, both.shape[1])
    if len(right) > 2:
        upto = right[0].shape[0] - LEAD
        right = [right[0][:upto], right[2], right[1][:upto], right[3]]
    right = jnp.concatenate(right, axis=0)[:, start : start + count]
    sent = [mm(pick(view, place ^ by), right).astype(BF) for by in range(1, view.shape[0])]
    return sent, mm(pick(view, place), right)


def total_of(kept, got):
    for piece in got:
        kept = kept + piece.astype(F32)
    return kept


def tied(value, others):
    return tie(value, *others) if others else value


def xor_parts(parts, axis):
    count, place = lax.axis_size(axis), lax.axis_index(axis)
    return pick(parts, place), [pick(parts, place ^ by).astype(BF) for by in range(1, count)]


def travel(sent, axis, others):
    return [across(tied(piece, others), axis, by + 1) for by, piece in enumerate(sent)]


class Reduction:
    def __init__(self, left, right, start, middle, end, waits=()):
        if lax.axis_size("x") == 2 and lax.axis_size("y") == 2:
            sent_x, self.kept_x = products(left, right, start, middle - start, "x", waits)
            sent_y, self.kept_y = products(left, right, middle, end - middle, "y", waits)
            self.sent_x, self.sent_y = [sent_x], [sent_y]
        else:
            self.sent_x, self.kept_x = products_any(left, right, start, middle - start, "x")
            self.sent_y, self.kept_y = products_any(left, right, middle, end - middle, "y")

    def made(self):
        return [self.kept_x, self.kept_y, *self.sent_x, *self.sent_y]

    def launch(self, *others):
        self.got_x = travel(self.sent_x, "x", others)
        self.got_y = travel(self.sent_y, "y", others)

    def second(self, *others):
        sizes = [lax.axis_size(a) for a in ("x", "z", "y")]
        part_x = total_of(tied(self.kept_x, others), self.got_x)
        part_y = total_of(tied(self.kept_y, others), self.got_y)
        view_x = part_x.reshape(sizes[1], sizes[2], -1, part_x.shape[1])
        view_y = part_y.reshape(sizes[0], sizes[1], -1, part_y.shape[1])
        self.own_x, self.next_x = xor_parts(jnp.moveaxis(view_x, 1, 0), "y")
        self.own_y, self.next_y = xor_parts(view_y, "x")
        self.came_x = travel(self.next_x, "y", ())
        self.came_y = travel(self.next_y, "x", ())

    def third(self, *others):
        done_x = total_of(tied(self.own_x, others), self.came_x)
        done_y = total_of(tied(self.own_y, others), self.came_y)
        self.parts = jnp.concatenate([done_x, done_y], axis=2)
        self.got_z = lax.all_to_all(self.parts, "z", 0, 0, tiled=True)

    def last(self, *others):
        return jnp.sum(tied(self.got_z, others), axis=0)


def core_rows(turned, core):
    view = turned.reshape(lax.axis_size("x"), 2, -1, turned.shape[1])
    return pick(view, core, 1)


def both_cores(turned, core):
    theirs = core_rows(turned, 1 - core)
    return turned, swap(theirs.reshape(-1, turned.shape[1]), "core")


def document_ids(lengths, positions):
    first_end = lengths[0]
    second_end = lengths[0] + lengths[1]
    inside = (positions >= first_end).astype(jnp.int32) + (positions >= second_end).astype(jnp.int32)
    return jnp.where(positions < 0, -1, inside)


def gather_small(pieces, count):
    flat = jnp.concatenate([piece.reshape(-1) for piece in pieces])
    spread = jnp.broadcast_to(flat[None], (count, flat.shape[0]))
    return lax.all_to_all(spread, EVERY, 0, 0, tiled=True)


def columns(array, width):
    return jnp.pad(array, ((0, 0), (0, width - array.shape[1])))


def shards(
    tokens, out_grad, seq_lengths, norm_gain, in_weight, conv_weight, conv_bias,
    dt_bias, a_log, skip_gain, gated_gain, out_weight,
):
    count = 1
    for axis in EVERY:
        count *= lax.axis_size(axis)
    core = lax.axis_index("core")
    place = lax.axis_index("z") * lax.axis_size("y") + lax.axis_index("y")
    row_count, width = tokens.shape
    first_row = place * row_count
    full_rows = LEAD + row_count
    half = INNER // 2
    bc_width = CONVW - INNER
    square = (row_count, row_count)

    lead_tokens = from_behind(tokens[row_count - LEAD :], 1)
    small = gather_small([norm_gain, conv_weight, conv_bias, gated_gain], count)
    weight_x = lax.all_gather(columns(in_weight[:, INNER:], PROJ_X), EVERY, axis=0, tiled=True)
    rows_out = out_weight.shape[0] // 2
    stacked = jnp.stack(
        [in_weight[:, :half], in_weight[:, half:INNER], out_weight[:rows_out], out_weight[rows_out:]]
    )
    stacked = lax.all_gather(stacked, EVERY, axis=1, tiled=True)
    cuts = [norm_gain.size, conv_weight.size, conv_bias.size]
    cuts = [sum(cuts[: i + 1]) for i in range(3)]
    gain_piece, conv_piece, bias_piece, gated_piece = jnp.split(small, cuts, axis=1)
    full_gain = gain_piece.reshape(1, -1).astype(F32)
    full_conv = jnp.moveaxis(conv_piece.reshape(count, CONV_K, -1), 1, 0).reshape(CONV_K, -1)
    full_conv = jnp.pad(full_conv.astype(F32), ((0, 4), (0, 0)))
    full_bias = bias_piece.reshape(1, -1).astype(F32)
    full_gated = gated_piece.reshape(1, -1).astype(F32)

    normed_ext, turned = call(
        norm_body, 1, 4,
        [
            (lead_tokens, whole(LEAD, width)),
            (tokens, whole(row_count, width)),
            (full_gain, whole(1, width)),
        ],
        [
            (out((full_rows, width), BF), whole(full_rows, width)),
            (out((width, row_count), BF), whole(width, row_count)),
        ],
    )
    normed = normed_ext[LEAD:]
    normed_left = both_cores(turned, core)
    out_grad_theirs = swap(out_grad, "core")

    lengths = seq_lengths[0]
    ordinal = jnp.arange(row_count, dtype=jnp.int32)
    doc_ids = document_ids(lengths, first_row + ordinal)
    doc_before = document_ids(lengths, first_row - 1 + jnp.zeros((1,), jnp.int32))
    marks = [
        document_ids(lengths, first_row + ordinal - (CONV_K - 1 - tap)) == doc_ids
        for tap in range(CONV_K)
    ]
    marks = marks + [doc_ids, doc_ids == doc_before[0], doc_ids == doc_ids[row_count - 1]]
    masks = columns(jnp.stack([mark.astype(F32) for mark in marks], axis=1), 128)
    doc_rows = jnp.broadcast_to(doc_ids.astype(F32)[None], (8, row_count))
    rate = columns(jnp.exp(a_log)[None], 128)
    shift = columns(dt_bias[None], 128)
    skip_wide = jnp.repeat(skip_gain, HEAD_DIM)[None]
    mixed_x = mm(normed_ext, weight_x).astype(BF)

    block_bc = pl.BlockSpec((full_rows, bc_width), lambda g: (0, INNER // bc_width))
    block_dr = pl.BlockSpec((full_rows, 128), lambda g: (0, CONVW // 128))
    per_token = whole(row_count, 128)
    a_token = (out((row_count, 128)), per_token)
    pre_bc, act_bc, act_t, scores, scores_t, steps, enter, to_end, cumulative, cum_turned, shifted = call(
        prep_bc_body, 1, 6,
        [
            (mixed_x, block_bc),
            (mixed_x, block_dr),
            (full_conv[:, INNER:], whole(8, bc_width)),
            (full_bias[:, INNER:], whole(1, bc_width)),
            (masks, per_token),
            (doc_rows, whole(8, row_count)),
            (shift, whole(1, 128)),
            (rate, whole(1, 128)),
        ],
        [
            (out((row_count, bc_width)), whole(row_count, bc_width)),
            (out((row_count, bc_width)), whole(row_count, bc_width)),
            (out((bc_width, row_count)), whole(bc_width, row_count)),
            (out(square), whole(*square)),
            (out(square), whole(*square)),
            a_token, a_token, a_token, a_token,
            (out((128, row_count)), whole(128, row_count)),
            a_token,
        ],
    )
    pre_x, act_x, state_local, device_decay = call(
        prep_x_body, INNER // BLOCK, 12,
        [
            (mixed_x, lanes(full_rows, BLOCK)),
            (full_conv[:, :INNER], lanes(8, BLOCK)),
            (full_bias[:, :INNER], lanes(1, BLOCK)),
            (masks, per_token),
            (to_end, per_token),
            (steps, per_token),
            (enter, per_token),
            (act_t, whole(bc_width, row_count)),
        ],
        [
            (out((row_count, INNER)), lanes(row_count, BLOCK)),
            (out((row_count, INNER)), lanes(row_count, BLOCK)),
            (out((2, STATE, half)), halves(STATE, BLOCK)),
            (out((2, 8, half)), halves(8, BLOCK)),
        ],
    )

    heads_block = 2 * PAIRS
    groups = HEADS // heads_block
    half_groups = groups // 2
    cum_rows = cum_turned[:HEADS].reshape(groups, heads_block, row_count)
    kept = {}

    def pairs_at(index):
        return pl.BlockSpec((row_count, PAIR_LANES), lambda g: (0, g + index * half_groups))

    def cums_at(index):
        return pl.BlockSpec((1, heads_block, row_count), lambda g: (g + index * half_groups, 0, 0))

    def intra(index, wait):
        kept[index] = call(
            functools.partial(intra_body, index * half_groups), half_groups, 12,
            [
                (act_x, pairs_at(index)),
                (steps, per_token),
                (skip_wide, pl.BlockSpec((1, PAIR_LANES), lambda g: (0, g + index * half_groups))),
                (scores, whole(*square)),
                (cumulative, per_token),
                (cum_rows, cums_at(index)),
            ],
            [(out((row_count, half)), lanes(row_count, PAIR_LANES))],
            waits=[wait],
        )[0]
        return [kept[index]]

    devices = 4
    out_block = 2 * devices * rows_out
    out_blocks = count // devices
    weight_block = pl.BlockSpec((2, devices * rows_out, width), lambda g: (1, g, 0))
    direct = rows_out % 16 == 0

    def project(wait):
        if direct:
            kept["d_final"] = call(
                functools.partial(d_final_body, devices, rows_out), out_blocks, 7,
                [(out_grad, whole(row_count, width)), (stacked, weight_block)],
                [(out((row_count, INNER)), lanes(row_count, out_block))],
                waits=[wait],
            )[0]
        else:
            weight_o = jnp.moveaxis(stacked[2:].reshape(2, count, rows_out, width), 0, 1)
            kept["weight_o"] = weight_o.reshape(-1, width)
            kept["d_final"] = mm_nt(out_grad, kept["weight_o"])
        kept["mixed_z"] = [mm(normed, stacked[side]).astype(BF) for side in range(2)]
        return [kept["d_final"], *kept["mixed_z"]]

    state_in = entering(
        state_local, device_decay, False,
        [
            lambda wait: intra(0, wait), lambda wait: intra(1, wait), lambda wait: [], lambda wait: [],
            project,
        ],
    )
    state_end = device_decay[:, :1] * state_in + state_local

    tile = 128
    final, final_turned, d_z, d_y, returned_local, d_c_carry, dy_y, sums = call(
        gate_body, row_count // tile, 31,
        [
            (kept[0], rows_of(tile, half)),
            (kept[1], rows_of(tile, half)),
            (kept["mixed_z"][0], rows_of(tile, half)),
            (kept["mixed_z"][1], rows_of(tile, half)),
            (kept["d_final"], rows_of(tile, INNER)),
            (act_x, rows_of(tile, INNER)),
            (act_bc[:, STATE:], rows_of(tile, STATE)),
            (act_t[STATE:], lanes(STATE, tile)),
            (state_in, whole(2, STATE, half)),
            (enter, rows_of(tile, 128)),
            (full_gated, whole(1, INNER)),
            (skip_wide, whole(1, INNER)),
        ],
        [
            (out((row_count, INNER), BF), rows_of(tile, INNER)),
            (out((INNER, row_count), BF), lanes(INNER, tile)),
            (out((row_count, INNER), BF), rows_of(tile, INNER)),
            (out((row_count, INNER)), rows_of(tile, INNER)),
            (out((2, STATE, half)), whole(2, STATE, half)),
            (out((row_count, STATE)), rows_of(tile, STATE)),
            (out((row_count, 128)), rows_of(tile, 128)),
            (out((16, INNER)), whole(16, INNER)),
        ],
        [pltpu.VMEM((tile, INNER), F32), pltpu.VMEM((tile, INNER), F32)],
    )

    final_left = both_cores(final_turned, core)
    d_z_theirs = swap(d_z, "core")
    back = {"acc": jnp.zeros(square, F32)}

    def out_sums(wait):
        back["out"] = Reduction(final_left, [out_grad, out_grad_theirs], 0, width // 2, width, [wait])
        back["out"].launch()
        return back["out"].made()

    def z_sums(wait):
        back["z"] = Reduction(normed_left, [d_z, d_z_theirs], 0, half, INNER, [wait])
        back["z"].launch()
        return back["z"].made()

    def within(index, wait):
        ends = [(out((row_count, bc_width)), whole(row_count, bc_width))] if index else []
        back[index], back["acc"], *back["bc"] = call(
            functools.partial(back_body, index * half_groups), half_groups, 18,
            [
                (act_x, pairs_at(index)),
                (d_y, pairs_at(index)),
                (steps, per_token),
                (scores_t, whole(*square)),
                (cumulative, per_token),
                (cum_rows, cums_at(index)),
                (act_bc, whole(row_count, bc_width)),
                (doc_rows, whole(8, row_count)),
                (masks, per_token),
                (back["acc"], whole(*square)),
            ],
            [
                (out((row_count, half)), lanes(row_count, PAIR_LANES)),
                (out(square), whole(*square)),
                *ends,
            ],
            waits=[wait],
        )
        return [back[index]]

    def first_within(wait):
        back["out"].second(wait)
        return within(0, wait)

    def second_within(wait):
        return within(1, wait)

    norm_block = 256

    def back_z(wait):
        back["d_normed"] = call(
            back_z_body, width // norm_block, 10,
            [
                (d_z, whole(row_count, INNER)),
                (stacked, pl.BlockSpec((2, norm_block, half), lambda g: (0, g, 0))),
            ],
            [(out((row_count, width)), lanes(row_count, norm_block))],
            waits=[wait],
        )[0]
        back["z"].second(wait)
        back["out"].third(wait)
        return [back["d_normed"], back["out"].parts, *back["z"].next_x, *back["z"].next_y]

    returned = entering(
        returned_local, device_decay, True,
        [out_sums, z_sums, first_within, second_within, back_z],
    )

    blocks = half // BLOCK

    def carried(index, earlier, extra, extra_out, waits):
        steps_count = blocks + len(extra_out)
        own = pl.BlockSpec((row_count, BLOCK), lambda g: (0, jnp.minimum(g, blocks - 1)))

        def at(rows):
            return pl.BlockSpec((rows, BLOCK), lambda g: (0, jnp.minimum(g, blocks - 1) + index * blocks))

        state_at = pl.BlockSpec((1, STATE, BLOCK), lambda g: (index, 0, jnp.minimum(g, blocks - 1)))
        wide = half + len(extra_out) * (PROJ_X - INNER)
        return call(
            functools.partial(carry_body, index * blocks), steps_count, 14 + 4 * index,
            [
                (back[index], own),
                (act_x, at(row_count)),
                (d_y, at(row_count)),
                (pre_x, at(row_count)),
                (mixed_x, at(full_rows)),
                (full_conv[:, :INNER], at(8)),
                (masks, per_token),
                (act_bc, whole(row_count, bc_width)),
                (returned, state_at),
                (state_end, state_at),
                (to_end, per_token),
                (steps, per_token),
                (skip_wide, at(1)),
                *[(array, whole(*array.shape)) for array in earlier],
                *extra,
            ],
            [
                *extra_out,
                (out((row_count, wide), BF), lanes(row_count, BLOCK)),
                (out((2 * LEAD, wide)), lanes(2 * LEAD, BLOCK)),
                (out((8, wide)), lanes(8, BLOCK)),
                (out((row_count, STATE)), whole(row_count, STATE)),
                a_token,
                (out((8, 128)), whole(8, 128)),
            ],
            waits=waits,
        )

    none = jnp.zeros((row_count, 128), F32)
    d_xa, edge_a, conv_a, *so_far = carried(0, [none, none, none[:8]], [], [], [])
    back["z"].third(edge_a)
    d_xa_theirs = swap(d_xa, "core")
    halo_a = from_behind(edge_a[:LEAD], -1)
    last_a = (edge_a[LEAD:] + halo_a).astype(BF)
    last_a_theirs = swap(last_a, "core")
    sums_a = Reduction(normed_left, [d_xa, d_xa_theirs, last_a, last_a_theirs], 0, half // 2, half, [back["z"].parts, back["out"].got_z])
    sums_a.launch()
    heads, d_xb, edge_b, conv_b, *_ = carried(
        1, so_far,
        [
            (pre_bc, whole(row_count, bc_width)),
            (mixed_x, block_bc),
            (full_conv[:, INNER:], whole(8, bc_width)),
            (back["bc"][0], whole(row_count, bc_width)),
            (d_c_carry, whole(row_count, STATE)),
            (shifted, per_token),
            (rate, whole(1, 128)),
            (dy_y, per_token),
        ],
        [(out((16, 128)), whole(16, 128))],
        sums_a.made(),
    )
    d_xb_theirs = swap(d_xb, "core")
    halo_b = from_behind(edge_b[:LEAD], -1)
    sums_a.second(edge_b)
    sums_a.third()
    last_b = (edge_b[LEAD:] + halo_b).astype(BF)
    last_b_theirs = swap(last_b, "core")
    wide_b = d_xb.shape[1]
    sums_b = Reduction(
        normed_left, [d_xb, d_xb_theirs, last_b, last_b_theirs], 0, 1024, wide_b, [sums_a.parts]
    )
    sums_b.launch()

    d_xa = lax.dynamic_update_slice(d_xa, last_a, (row_count - LEAD, 0))
    d_xb = lax.dynamic_update_slice(d_xb, last_b, (row_count - LEAD, 0))
    d_normed = call(
        back_x_body, width // norm_block, 10,
        [
            (d_xa, whole(row_count, half)),
            (d_xb, whole(row_count, wide_b)),
            (weight_x, rows_of(norm_block, PROJ_X)),
            (back["d_normed"], lanes(row_count, norm_block)),
        ],
        [(out((row_count, width)), lanes(row_count, norm_block))],
        waits=sums_b.made(),
    )[0]
    grad_tokens, gain_sums = call(
        back_norm_body, row_count // tile, 4,
        [
            (d_normed, rows_of(tile, width)),
            (tokens, rows_of(tile, width)),
            (out_grad, rows_of(tile, width)),
            (full_gain, whole(1, width)),
        ],
        [
            (out((row_count, width)), rows_of(tile, width)),
            (out((8, width)), whole(8, width)),
        ],
    )
    sums_b.second(grad_tokens)
    if direct:
        layer_out = call(
            functools.partial(layer_body, devices, rows_out), out_blocks, 13,
            [
                (final, lanes(row_count, out_block)),
                (stacked, weight_block),
                (tokens, whole(row_count, width)),
            ],
            [(out((row_count, width), BF), whole(row_count, width))],
            [pltpu.VMEM((row_count, width), F32)],
            waits=[*sums_b.next_x, *sums_b.next_y],
        )[0]
    else:
        layer_out = (tokens.astype(F32) + mm(final, kept["weight_o"])).astype(BF)

    conv_sums = jnp.concatenate([conv_a, conv_b[:, : CONVW - half]], axis=1)
    grad_skip = jnp.sum(jnp.sum(sums[8:], axis=0).reshape(HEADS, HEAD_DIM), axis=1)
    grad_gated = jnp.sum(sums[:8], axis=0)
    per_device = jnp.concatenate(
        [
            gain_sums[0].reshape(count, -1),
            jnp.moveaxis(conv_sums[:CONV_K].reshape(CONV_K, count, -1), 1, 0).reshape(count, -1),
            conv_sums[CONV_K].reshape(count, -1),
            grad_gated.reshape(count, -1),
            jnp.broadcast_to(
                jnp.concatenate([heads[0, :HEADS], heads[8, :HEADS], grad_skip])[None],
                (count, 3 * HEADS),
            ),
        ],
        axis=1,
    )
    sums_b.third()
    per_device = tie(per_device, *sums_b.next_x, *sums_b.next_y)
    arrived = lax.all_to_all(per_device, EVERY, 0, 0, tiled=True)
    done = [layer_out]
    sum_out, sum_in_z, sum_in_a = [each.last(*done) for each in (back["out"], back["z"], sums_a)]
    sum_in_b = sums_b.last()
    small_sums = jnp.sum(tie(arrived, layer_out), axis=0)
    cuts = [norm_gain.size, conv_weight.size, conv_bias.size, gated_gain.size, HEADS, HEADS]
    cuts = [sum(cuts[: i + 1]) for i in range(6)]
    sum_gain, sum_conv, sum_bias, sum_gated, sum_dt, sum_log, sum_skip = jnp.split(small_sums, cuts)
    sum_in = jnp.concatenate([sum_in_z, sum_in_a, sum_in_b[:, : in_weight.shape[1] - INNER - half]], axis=1)
    return (
        layer_out,
        grad_tokens,
        sum_gain,
        sum_in,
        sum_conv.reshape(conv_weight.shape),
        sum_bias,
        sum_dt,
        sum_log,
        sum_skip,
        sum_gated,
        sum_out,
    )


def solution(mesh):
    x = mesh.shape["dp"] // 2
    y = x
    z = mesh.shape["ctx"] // y
    fine = Mesh(mesh.devices.reshape(x, 2, z, y), EVERY)
    rows = P(EVERY, None)
    flat = P(EVERY)
    in_specs = (
        rows, rows, P(("x", "core"), None), flat, rows, P(None, EVERY), flat,
        P(), P(), P(), flat, rows,
    )
    out_specs = (rows, rows, flat, rows, P(None, EVERY), flat, P(), P(), P(), flat, rows)
    return jax.shard_map(shards, mesh=fine, in_specs=in_specs, out_specs=out_specs, check_vma=False)
```

time: 779 us -> 731 us (0.938)
  Pallas kernels: 186 us -> 259 us
  waiting for transfers between devices: 234 us -> 175 us
  local copies, waits for them, and re-layouts: 128 us -> 78.8 us
  matrix products: 70 us -> 24.4 us
  starting transfers between devices: 57.5 us -> 97.6 us
  other arithmetic: 75.9 us -> 67.2 us
    pallas_call x15 -> x23, Pallas kernels: 186 us -> 259 us  [call(): pl.pallas_call(run, grid_spec=pltpu.PrefetchScalarGridSpec(num_scalar_pre...]
    ppermute x21 -> x16, waiting for transfers between devices: 81.1 us -> 15.8 us  [across(): lax.ppermute(array, axis, [(i, i ^ by) for i in range(lax.axis_size(axis))])]
    dot_general x6 -> x0, matrix products: 39.7 us -> none  [the longest x4 36.6 us: mm_nt(): lax.dot_general(left, right, (((1,), (1,)), ((), ())), preferred_element_...]
    all_to_all x1 -> x5, starting transfers between devices: 3.69 us -> 39 us  [the longest x4 33.5 us: third(): self.got_z = lax.all_to_all(self.parts, 'z', 0, 0, tiled=True)]
    add x12 -> x1, other arithmetic: 21 us -> 3.59 us  [shards(): state_end = device_decay[:, :1] * state_in + state_local]
    transpose x3 -> x0, local copies, waits for them, and re-layouts: 12 us -> none  [the longest x1 8.12 us: project(): weight_o = jnp.moveaxis(weight_o, 0, 1).reshape(-1, width)]
    reshape x5 -> x1, local copies, waits for them, and re-layouts: 11.8 us -> 0.67 us  [shards(): cum_rows = cum_turned[:HEADS].reshape(groups, heads_block, row_count)]
    slice x17 -> x11, local copies, waits for them, and re-layouts: 21.2 us -> 10.3 us  [the longest x1 1.67 us: shards(): act_bc[:, STATE:]]
  transfers between devices with their start and end apart: 43 -> 46, of which waited for: 14 -> 14; matrix products, arithmetic and copies ran while one was open for 32% -> 19% of each run, Pallas kernels for 24% -> 32%
where the time goes in v3:
time: 731 us; the launch traced here: 720 us
  Pallas kernels  259 us (35%)
  waiting for transfers between devices  175 us (24%)
  starting transfers between devices  97.6 us (13%)
  local copies, waits for them, and re-layouts  78.8 us (11%)
  other arithmetic  67.2 us (9%)
  matrix products  24.4 us (3%)
  between operations  17.5 us (2%)
    pallas_call x23, Pallas kernels, call(): pl.pallas_call(run, grid_spec=pltpu.PrefetchScalarGridSpec(num_scalar_pre...  259 us
    all_gather x1, waiting for transfers between devices, shards(): lax.all_gather(columns(in_weight[:, INNER:], PROJ_X), EVERY, axis=0, tile...  59.5 us
    ppermute x6, waiting for transfers between devices, entering(): arrived = meanwhile(sent, lax.ppermute(sent, 'z', pairs))  41.7 us
    all_to_all x4, starting transfers between devices, third(): self.got_z = lax.all_to_all(self.parts, 'z', 0, 0, tiled=True)  33.5 us
    unnamed x133, local copies, waits for them, and re-layouts  26.4 us
    dot_general x3, matrix products, mm(): return jnp.dot(left, right, preferred_element_type=F32)  24.4 us
    ppermute x16, starting transfers between devices, across(): lax.ppermute(array, axis, [(i, i ^ by) for i in range(lax.axis_size(axis))])  22.3 us
    ppermute x6, starting transfers between devices, entering(): arrived = meanwhile(sent, lax.ppermute(sent, 'z', pairs))  19.4 us
  transfers between devices with their start and end apart: 46, of which 14 were waited for; matrix products, arithmetic and copies ran while one was open for 19% of the time, Pallas kernels for 32%

profile of v3, /device:TPU:0, one launch (start us, length us, event | category | flops | bytes accessed | tf_op | source)
XLA Modules:
  0.0 719.5 jit_solution(3233698943833280567)
XLA Ops:
  12.0 4.9 collective-permute-start
  19.3 4.9 all-to-all-start
  39.1 3.9 shard_map.203
  43.1 59.5 %all-gather.3.cloned.1.call-done.refs_2_ = bf16[1536,3456]{1,0:T(8,128)(2,1)} async-done(((bf16[48,3456]{1,0:T(8,128)(2,1)}), bf16[1536,3456]{1,0:T(8,128)(2,1)}) %all-gather.3.cloned.1.call-update) | async-done | bytes 10616848 | tf_op jit(solution)/shard_map/all_gather | solution.py:774
  102.5 11.8 %convolution_convert_fusion.refs_0_.refs_1_.refs_4_.refs_17_ = bf16[528,3456]{1,0:T(8,128)(2,1)} fusion(bf16[528,1536]{1,0:T(8,128)(2,1)} %get-tuple-element.68, bf16[1536,3456]{1,0:T(8,128)(2,1)} %all-gather.3.cloned.1.call-done.refs_2_), kind=kOutput, calls=%fused_computation | convolution fusion | flops 5607512064 | bytes 15888384 | tf_op jit(solution)/shard_map/dot_general | solution.py:105
  114.9 4.5 shard_map.204
  120.9 12.4 %shard_map.205 = (f32[512,3072]{1,0:T(8,128)}, f32[512,3072]{1,0:T(8,128)}, f32[2,128,1536]{2,1,0:T(8,128)}, f32[2,8,1536]{2,1,0:T(8,128)}) custom-call(bf16[528,3456]{1,0:T(8,128)(2,1)} %convolution_convert_fusion.refs_0_.refs_1_.refs_4_.refs_17_, f32[8,3072]{1,0:T(8,128)} %slice.174.refs_1_.refs_5_, f32[1,3072]{1,0:T(1,128)} %slice.175.refs_2_, ...), custom_call_target="tpu_custom_call" | custom-call | flops 12000000000 | bytes 36000000 | tf_op jit(solution)/shard_map/pallas_call | solution.py:43
  137.8 13.6 %shard_map.206.refs_1_.refs_0_ = f32[512,1536]{1,0:T(8,128)} custom-call(f32[512,3072]{1,0:T(8,128)} %get-tuple-element.73.refs_0_.refs_5_.refs_1_, f32[512,128]{1,0:T(8,128)} %get-tuple-element.70.refs_5_.refs_1_.refs_2_.refs_11_, f32[1,3072]{1,0:T(1,128)} %broadcast_in_dim_reshape.3.refs_2_.refs_11_.refs_12_, f32[512,512]{1,0:T(8,128)} %get-tuple-element.74.refs_3_, ...), custom_call_target="tpu_custom_call" | custom-call | flops 12000000000 | bytes 36000000 | tf_op jit(solution)/shard_map/pallas_call | solution.py:43
  152.2 11.1 %collective-permute-done.2.refs_0_ = f32[128,1536]{1,0:T(8,128)S(1)} collective-permute-done((f32[128,1536]{1,0:T(8,128)S(1)}, f32[128,1536]{1,0:T(8,128)S(1)}, u32[]{:S(2)}, u32[]{:S(2)}) %collective-permute-start.2) | collective-permute-done | bytes 786464 | tf_op jit(solution)/shard_map/ppermute | solution.py:517
  164.2 2.2 fusion.7.refs_6_
  166.4 3.5 collective-permute-start.3
  169.9 13.6 %shard_map.208.refs_1_ = f32[512,1536]{1,0:T(8,128)} custom-call(f32[512,3072]{1,0:T(8,128)} %get-tuple-element.73.refs_0_.refs_5_.refs_1_, f32[512,128]{1,0:T(8,128)} %get-tuple-element.70.refs_5_.refs_1_.refs_2_.refs_11_, f32[1,3072]{1,0:T(1,128)} %broadcast_in_dim_reshape.3.refs_2_.refs_11_.refs_12_, f32[512,512]{1,0:T(8,128)} %get-tuple-element.74.refs_3_, ...), custom_call_target="tpu_custom_call" | custom-call | flops 12000000000 | bytes 36000000 | tf_op jit(solution)/shard_map/pallas_call | solution.py:43
  183.6 18.9 %collective-permute-done.3.refs_0_ = f32[128,1536]{1,0:T(8,128)S(1)} collective-permute-done((f32[128,1536]{1,0:T(8,128)}, f32[128,1536]{1,0:T(8,128)S(1)}, u32[]{:S(2)}, u32[]{:S(2)}) %collective-permute-start.3) | collective-permute-done | bytes 786464 | tf_op jit(solution)/shard_map/ppermute | solution.py:565
  203.3 2.2 multiply_add_fusion.6
  207.1 2.5 multiply_add_fusion.5
  216.3 2.3 select_bitcast_fusion.1
  218.6 19.0 %all-gather.5.cloned.1.call-done.refs_1_ = bf16[4,1536,1536]{2,1,0:T(8,128)(2,1)} async-done(((bf16[4,48,1536]{2,1,0:T(8,128)(2,1)}), bf16[4,1536,1536]{2,1,0:T(8,128)(2,1)}) %all-gather.5.cloned.1.call-update) | async-done | bytes 18874384 | tf_op jit(solution)/shard_map/all_gather | solution.py:779
  237.6 6.6 fusion.3.refs_3_
  244.2 12.9 %shard_map.212.refs_1_.refs_4_ = f32[512,3072]{1,0:T(8,128)} custom-call(bf16[512,1536]{1,0:T(8,128)(2,1)} %refs_2_.2, bf16[4,1536,1536]{2,1,0:T(8,128)(2,1)} %all-gather.5.cloned.1.call-done.refs_1_, f32[128,1536]{1,0:T(8,128)} %get-tuple-element.146.refs_2_), custom_call_target="tpu_custom_call" | custom-call | flops 7000000000 | bytes 21000000 | tf_op jit(solution)/shard_map/pallas_call | solution.py:43
  257.1 6.0 fusion.2.refs_2_
  264.0 3.6 multiply_add_fusion
  267.6 31.8 %shard_map.214 = (bf16[512,3072]{1,0:T(8,128)(2,1)}, bf16[3072,512]{1,0:T(8,128)(2,1)}, bf16[512,3072]{1,0:T(8,128)(2,1)}, f32[512,3072]{1,0:T(8,128)}, f32[2,12...) custom-call(f32[512,1536]{1,0:T(8,128)} %shard_map.206.refs_1_.refs_0_, ...), custom_call_target="tpu_custom_call" | custom-call | flops 31000000512 | bytes 93000000 | tf_op jit(solution)/shard_map/pallas_call | solution.py:43
  299.9 2.7 constant_dynamic-slice_fusion
  306.5 3.4 collective-permute-done.10.refs_6_
  311.1 7.4 %shard_map.215 = (bf16[768,768]{1,0:T(8,128)(2,1)}, f32[768,768]{1,0:T(8,128)}) custom-call(s32[3]{0:T(128)} %pad_add_fusion.refs_0_, bf16[2,2,768,512]{3,2,1,0:T(8,128)(2,1)} %bitcast.194, bf16[2,2,768,512]{3,2,1,0:T(8,128)(2,1)} %bitcast.195, bf16[2,768,512]{2,1,0:T(8,128)(2,1)} %bitcast.198, bf16[2,768,512]{2,1,0:T(8,128)(2,1)} %bitcast.199, ...), custom_call_target="tpu_custom_call" | custom-call | flops 2949120000 | bytes 8847360 | tf_op jit(solution)/shard_map/pallas_call | solution.py:43
  318.5 7.5 %shard_map.216 = (bf16[768,768]{1,0:T(8,128)(2,1)}, f32[768,768]{1,0:T(8,128)}) custom-call(s32[3]{0:T(128)} %pad_add_fusion.refs_0_, bf16[2,2,4,2,96,512]{5,4,3,2,1,0:T(8,128)(2,1)} %bitcast.196, bf16[2,2,4,2,96,512]{5,4,3,2,1,0:T(8,128)(2,1)} %bitcast.197, bf16[8,2,96,512]{3,2,1,0:T(8,128)(2,1)} %bitcast.200, bf16[8,2,96,512]{3,2,1,0:T(8,128)(2,1)} %bitcast.201, ...), custom_call_target="tpu_custom_call" | custom-call | flops 2949120000 | bytes 8847360 | tf_op jit(solution)/shard_map/pallas_call | solution.py:43
  333.9 7.6 %shard_map.218 = (bf16[384,1536]{1,0:T(8,128)(2,1)}, f32[384,1536]{1,0:T(8,128)}) custom-call(s32[3]{0:T(128)} %pad_add_fusion.refs_0_, bf16[2,2,384,512]{3,2,1,0:T(8,128)(2,1)} %bitcast.168, bf16[2,2,384,512]{3,2,1,0:T(8,128)(2,1)} %bitcast.169, bf16[2,384,512]{2,1,0:T(8,128)(2,1)} %bitcast.181, bf16[2,384,512]{2,1,0:T(8,128)(2,1)} %bitcast.182, ...), custom_call_target="tpu_custom_call" | custom-call | flops 2949120000 | bytes 8847360 | tf_op jit(solution)/shard_map/pallas_call | solution.py:43
  341.5 7.6 %shard_map.219 = (bf16[384,1536]{1,0:T(8,128)(2,1)}, f32[384,1536]{1,0:T(8,128)}) custom-call(s32[3]{0:T(128)} %pad_add_fusion.refs_0_, bf16[2,2,4,2,48,512]{5,4,3,2,1,0:T(8,128)(2,1)} %bitcast.170, bf16[2,2,4,2,48,512]{5,4,3,2,1,0:T(8,128)(2,1)} %bitcast.171, bf16[8,2,48,512]{3,2,1,0:T(8,128)(2,1)} %bitcast.183, bf16[8,2,48,512]{3,2,1,0:T(8,128)(2,1)} %bitcast.184, ...), custom_call_target="tpu_custom_call" | custom-call | flops 2949120000 | bytes 8847360 | tf_op jit(solution)/shard_map/pallas_call | solution.py:43
  352.1 12.4 %collective-permute-start.13 = (f32[128,1536]{1,0:T(8,128)}, f32[128,1536]{1,0:T(8,128)}, u32[]{:S(2)}, u32[]{:S(2)}) collective-permute-start(f32[128,1536]{1,0:T(8,128)} %multiply_add_fusion.3.refs_10_.refs_1_), channel_id=1, source_target_pairs={{4,2},{5,3},{12,10},{13,11},{20,18},{21,19},{28,26},{29,27}} | collective-permute-start | bytes 2359304 | tf_op jit(solution)/shard_map/ppermute | solution.py:565
  374.8 18.3 %shard_map.221 = (f32[512,1536]{1,0:T(8,128)}, f32[512,512]{1,0:T(8,128)}) custom-call(f32[512,3072]{1,0:T(8,128)} %get-tuple-element.73.refs_0_.refs_5_.refs_1_, f32[512,3072]{1,0:T(8,128)} %get-tuple-element.82.refs_1_.refs_2_, f32[512,128]{1,0:T(8,128)} %get-tuple-element.70.refs_5_.refs_1_.refs_2_.refs_11_, f32[512,512]{1,0:T(8,128)} %get-tuple-element.83.refs_3_, ...), custom_call_target="tpu_custom_call" | custom-call | flops 17999998976 | bytes 54000000 | tf_op jit(solution)/shard_map/pallas_call | solution.py:43
  398.9 19.8 %shard_map.223 = (f32[512,1536]{1,0:T(8,128)}, f32[512,512]{1,0:T(8,128)}, f32[512,256]{1,0:T(8,128)}) custom-call(f32[512,3072]{1,0:T(8,128)} %get-tuple-element.73.refs_0_.refs_5_.refs_1_, f32[512,3072]{1,0:T(8,128)} %get-tuple-element.82.refs_1_.refs_2_, f32[512,128]{1,0:T(8,128)} %get-tuple-element.70.refs_5_.refs_1_.refs_2_.refs_11_, ...), custom_call_target="tpu_custom_call" | custom-call | flops 17999998976 | bytes 54000000 | tf_op jit(solution)/shard_map/pallas_call | solution.py:43
  418.7 22.8 %collective-permute-done.14.refs_0_ = f32[128,1536]{1,0:T(8,128)S(1)} collective-permute-done((f32[128,1536]{1,0:T(8,128)S(1)}, f32[128,1536]{1,0:T(8,128)S(1)}, u32[]{:S(2)}, u32[]{:S(2)}) %collective-permute-start.14) | collective-permute-done | bytes 786464 | tf_op jit(solution)/shard_map/ppermute | solution.py:565
  444.0 2.8 select_bitcast_fusion
  448.4 2.3 convert_add_fusion.1
  461.1 20.0 %all-to-all-start.1 = ((f32[4,96,1536]{2,1,0:T(8,128)}), f32[4,96,1536]{2,1,0:T(8,128)S(1)}, u32[]{:S(2)}, u32[]{:S(2)}) async-start(f32[4,96,1536]{2,1,0:T(8,128)} %pad_maximum_fusion.refs_2_), calls=%async_computation.1 | async-start | bytes 4718592 | tf_op jit(solution)/shard_map/all_to_all | solution.py:723
  484.0 10.8 %shard_map.225.refs_1_.refs_3_ = f32[512,1536]{1,0:T(8,128)} custom-call(bf16[512,3072]{1,0:T(8,128)(2,1)} %get-tuple-element.90.refs_5_.refs_0_, bf16[4,1536,1536]{2,1,0:T(8,128)(2,1)} %all-gather.5.cloned.1.call-done.refs_1_, f32[128,1536]{1,0:T(8,128)} %get-tuple-element.144.refs_2_.refs_1_), custom_call_target="tpu_custom_call" | custom-call | flops 10000000000 | bytes 30000000 | tf_op jit(solution)/shard_map/pallas_call | solution.py:43
  495.8 2.8 maximum_select_fusion.1.refs_8_
  499.9 17.4 %shard_map.233 = (bf16[512,1536]{1,0:T(8,128)(2,1)}, f32[32,1536]{1,0:T(8,128)}, f32[8,1536]{1,0:T(8,128)}, f32[512,128]{1,0:T(8,128)}, f32[512,128]{1,0:T(8,128)}, /*index=5*/f32[8,128]{1,0:T(8,128)}) custom-call(f32[512,1536]{1,0:T(8,128)} %get-tuple-element.96.refs_1_.refs_0_, f32[512,3072]{1,0:T(8,128)} %get-tuple-element.73.refs_0_.refs_5_.refs_1_, ...), custom_call_target="tpu_custom_call" | custom-call | flops 14000000000 | bytes 42000000 | tf_op jit(solution)/shard_map/pallas_call | solution.py:43
  523.9 1.8 collective-permute-done.23
  530.0 4.4 all-to-all-done.1.refs_10_.refs_0_
  535.8 6.5 all-to-all-start.3
  542.3 5.2 shard_map.237
  547.5 5.3 shard_map.236
  552.8 18.2 %shard_map.238 = (f32[16,128]{1,0:T(8,128)}, bf16[512,1920]{1,0:T(8,128)(2,1)}, f32[32,1920]{1,0:T(8,128)}, f32[8,1920]{1,0:T(8,128)}, f32[512,128]{1,0:T(8,128)}, /*index=5*/f32[512,128]{1,0:T(8,128)}, f32[8,128]{1,0:T(8,128)}) custom-call(f32[512,1536]{1,0:T(8,128)} %get-tuple-element.97.refs_1_.refs_0_, ...), custom_call_target="tpu_custom_call" | custom-call | flops 17999998976 | bytes 54000000 | tf_op jit(solution)/shard_map/pallas_call | solution.py:43
  571.9 4.3 collective-permute-start.32
  580.7 9.9 %collective-permute-done.32 = bf16[384,768]{1,0:T(8,128)(2,1)S(1)} collective-permute-done((bf16[384,768]{1,0:T(8,128)(2,1)}, bf16[384,768]{1,0:T(8,128)(2,1)S(1)}, u32[]{:S(2)}, u32[]{:S(2)}) %collective-permute-start.32) | collective-permute-done | bytes 589856 | tf_op jit(solution)/shard_map/ppermute | solution.py:587
  592.1 1.8 collective-permute-start.31
  594.0 3.6 collective-permute-done.33
  597.6 2.3 collective-permute-done.31
  603.0 5.5 shard_map.242
  608.5 2.5 collective-permute-start.35
  611.0 5.3 shard_map.241
  617.3 12.1 %shard_map.243.refs_0_ = f32[512,1536]{1,0:T(8,128)} custom-call(bf16[512,1536]{1,0:T(8,128)(2,1)} %copy-done.40, bf16[512,1920]{1,0:T(8,128)(2,1)} %copy-done.38, bf16[1536,3456]{1,0:T(8,128)(2,1)} %all-gather.3.cloned.1.call-done.refs_2_, f32[512,1536]{1,0:T(8,128)} %shard_map.225.refs_1_.refs_3_, f32[384,1024]{1,0:T(8,128)} %get-tuple-element.115.refs_4_.refs_0_, ...), custom_call_target="tpu_custom_call" | custom-call | flops 10000000000 | bytes 30000000 | tf_op jit(solution)/shard_map/pallas_call | solution.py:43
  629.4 3.5 all-to-all-start.4
  632.9 5.6 shard_map.244
  655.4 2.1 bitcast_add_fusion.1
  659.1 5.4 all-to-all-start.2
  664.5 2.3 pad_maximum_fusion.2
  666.9 5.3 all-to-all-done.2
  672.2 3.6 all-to-all-start.5
  675.7 12.8 %shard_map.247.refs_1_ = bf16[512,1536]{1,0:T(8,128)(2,1)} custom-call(bf16[512,3072]{1,0:T(8,128)(2,1)} %get-tuple-element.80.refs_0_, bf16[4,1536,1536]{2,1,0:T(8,128)(2,1)} %all-gather.5.cloned.1.call-done.refs_1_, bf16[512,1536]{1,0:T(8,128)(2,1)} %refs_2_.3, bf16[4,48,1024]{2,1,0:T(8,128)(2,1)} %copy-done.41, bf16[4,48,896]{2,1,0:T(8,128)(2,1)} %copy-done.42), custom_call_target="tpu_custom_call" | custom-call | flops 12999999488 | bytes 39000000 | tf_op jit(solution)/shard_map/pallas_call | solution.py:43
  688.5 2.7 reduce_sum.79
  692.6 1.9 reduce_sum.76
  698.5 12.6 %all-to-all-done.5 = f32[4,48,1920]{2,1,0:T(8,128)S(1)} async-done(((f32[4,48,1920]{2,1,0:T(8,128)}), f32[4,48,1920]{2,1,0:T(8,128)S(1)}, u32[]{:S(2)}, u32[]{:S(2)}) %all-to-all-start.5) | async-done | bytes 1474592 | tf_op jit(solution)/shard_map/all_to_all | solution.py:723
  (350 shorter events, 138.8 us)
Async XLA Ops:
  7.2 95.3 %all-gather.3.cloned.1.call-start = ((), (), s32[]{:S(2)}) async-start(), calls=%async_computation.6 | async-start | bytes 10948608 | tf_op jit(solution)/shard_map/all_gather | solution.py:774
  9.0 7.8 %copy-start.54 = (bf16[4,104]{1,0:T(4,128)(2,1)S(1)}, bf16[4,104]{1,0:T(4,128)(2,1)}, u32[]{:S(2)}) copy-start(bf16[4,104]{1,0:T(4,128)(2,1)} %param.17) | copy-start | bytes 2500
  9.1 7.9 %copy-start.55 = (bf16[96]{0:T(256)(128)(2,1)S(1)}, bf16[96]{0:T(256)(128)(2,1)}, u32[]{:S(2)}) copy-start(bf16[96]{0:T(256)(128)(2,1)} %param.22) | copy-start | bytes 580
  9.1 7.9 %copy-start.56 = (bf16[104]{0:T(256)(128)(2,1)S(1)}, bf16[104]{0:T(256)(128)(2,1)}, u32[]{:S(2)}) copy-start(bf16[104]{0:T(256)(128)(2,1)} %param.18) | copy-start | bytes 628
  9.1 7.9 %copy-start.57 = (bf16[48]{0:T(256)(128)(2,1)S(1)}, bf16[48]{0:T(256)(128)(2,1)}, u32[]{:S(2)}) copy-start(bf16[48]{0:T(256)(128)(2,1)} %param.15) | copy-start | bytes 292
  9.1 228.5 %all-gather.5.cloned.1.call-start = ((), (), s32[]{:S(2)}) async-start(), calls=%async_computation.7 | async-start | bytes 19464192 | tf_op jit(solution)/shard_map/all_gather | solution.py:779
  10.2 14.0 %copy-start.60 = (f32[48]{0:T(128)S(1)}, f32[48]{0:T(128)}, u32[]{:S(2)}) copy-start(f32[48]{0:T(128)} %param.19) | copy-start | bytes 580
  10.2 14.5 %copy-start.61 = (f32[48]{0:T(128)S(1)}, f32[48]{0:T(128)}, u32[]{:S(2)}) copy-start(f32[48]{0:T(128)} %param.20) | copy-start | bytes 580
  10.2 15.1 %copy-start.53 = (s32[1,3]{1,0:T(1,128)S(1)}, s32[1,3]{1,0:T(1,128)}, u32[]{:S(2)}) copy-start(s32[1,3]{1,0:T(1,128)} %param.14) | copy-start | bytes 40
  10.2 18.9 %copy-start.58 = (f32[48]{0:T(128)S(1)}, f32[48]{0:T(128)}, u32[]{:S(2)}) copy-start(f32[48]{0:T(128)} %param.21) | copy-start | bytes 580
  12.0 26.5 %collective-permute-start = (bf16[16,1536]{1,0:T(8,128)(2,1)S(1)}, bf16[16,1536]{1,0:T(8,128)(2,1)S(1)}, u32[]{:S(2)}, u32[]{:S(2)}) collective-permute-start(bf16[16,1536]{1,0:T(8,128)(2,1)S(1)} %slice.136), channel_id=1, source_target_pairs={{0,1},{1,2},{2,3},{3,4},{4,5},{5,6},{6,7},{8,9},{9,10},{10,11},{11... | collective-permute-start | bytes 147464 | tf_op jit(solution)/shard_map/ppermute | solution.py:523
  19.3 15.5 %all-to-all-start = ((bf16[32,2,332]{2,1,0:T(2,128)(2,1)}), bf16[32,2,332]{2,1,0:T(2,128)(2,1)S(1)}, u32[]{:S(2)}, u32[]{:S(2)}) async-start(bf16[32,2,332]{2,1,0:T(2,128)(2,1)} %reshape.384), calls=%async_computation | async-start | bytes 98304 | tf_op jit(solution)/shard_map/all_to_all | solution.py:749
  134.2 17.2 %collective-permute-start.1 = (f32[8,1536]{1,0:T(8,128)S(1)}, f32[8,1536]{1,0:T(8,128)S(1)}, u32[]{:S(2)}, u32[]{:S(2)}) collective-permute-start(f32[8,1536]{1,0:T(8,128)S(1)} %dynamic-slice_bitcast_fusion.6), channel_id=1, source_target_pairs={{0,1},{1,0},{2,3},{3,2},{4,5},{5,4},{6,7},{7,6},{8,9},{9,8},{10,11... | collective-permute-start | bytes 147464 | tf_op jit(solution)/shard_map/ppermute | solution.py:517
  136.8 26.5 %collective-permute-start.2 = (f32[128,1536]{1,0:T(8,128)S(1)}, f32[128,1536]{1,0:T(8,128)S(1)}, u32[]{:S(2)}, u32[]{:S(2)}) collective-permute-start(f32[128,1536]{1,0:T(8,128)S(1)} %dynamic-slice_bitcast_fusion.5.refs_6_), channel_id=1, source_target_pairs={{0,1},{1,0},{2,3},{3,2},{4,5},{5,4},{6,7},{7,6},{8,9},{9,8},{10,11... | collective-permute-start | bytes 2359304 | tf_op jit(solution)/shard_map/ppermute | solution.py:517
  152.2 12.0 %copy-start.15 = (f32[2,128,1536]{2,1,0:T(8,128)S(1)}, f32[2,128,1536]{2,1,0:T(8,128)}, u32[]{:S(2)}) copy-start(f32[2,128,1536]{2,1,0:T(8,128)} %get-tuple-element.77) | copy-start | bytes 4718596
  166.4 36.0 %collective-permute-start.3 = (f32[128,1536]{1,0:T(8,128)}, f32[128,1536]{1,0:T(8,128)S(1)}, u32[]{:S(2)}, u32[]{:S(2)}) collective-permute-start(f32[128,1536]{1,0:T(8,128)} %fusion.7.refs_6_), channel_id=1, source_target_pairs={{0,2},{1,3},{8,10},{9,11},{16,18},{17,19},{24,26},{25,27}} | collective-permute-start | bytes 2359304 | tf_op jit(solution)/shard_map/ppermute | solution.py:565
  205.5 0.7 collective-permute-start.4
  209.6 6.7 copy-start.22
  209.6 5.8 collective-permute-start.5
  218.6 44.5 %collective-permute-start.6 = (f32[128,1536]{1,0:T(8,128)}, f32[128,1536]{1,0:T(8,128)S(1)}, u32[]{:S(2)}, u32[]{:S(2)}) collective-permute-start(f32[128,1536]{1,0:T(8,128)} %get-tuple-element.146.refs_2_), channel_id=1, source_target_pairs={{0,1},{1,0},{2,3},{3,2},{4,5},{5,4},{6,7},{7,6},{8,9},{9,8},{10,11... | collective-permute-start | bytes 2359304 | tf_op jit(solution)/shard_map/ppermute | solution.py:517
  244.2 12.9 %copy-start.62 = (bf16[528,1536]{1,0:T(8,128)(2,1)S(1)}, bf16[528,1536]{1,0:T(8,128)(2,1)}, u32[]{:S(2)}) copy-start(bf16[528,1536]{1,0:T(8,128)(2,1)} %get-tuple-element.68) | copy-start | bytes 4866052
  299.3 33.8 %collective-permute-start.12 = (bf16[512,3072]{1,0:T(8,128)(2,1)}, bf16[512,3072]{1,0:T(8,128)(2,1)}, u32[]{:S(2)}, u32[]{:S(2)}) collective-permute-start(bf16[512,3072]{1,0:T(8,128)(2,1)} %get-tuple-element.90.refs_5_.refs_0_), channel_id=1, source_target_pairs={{0,8},{8,0},{1,9},{9,1},{2,10},{10,2},{3,11},{11,3},{4,12},{12,4},... | collective-permute-start | bytes 9437192 | tf_op jit(solution)/shard_map/ppermute | solution.py:517
  299.5 10.4 %collective-permute-start.10 = (bf16[512,1536]{1,0:T(8,128)(2,1)}, bf16[512,1536]{1,0:T(8,128)(2,1)}, u32[]{:S(2)}, u32[]{:S(2)}) collective-permute-start(bf16[512,1536]{1,0:T(8,128)(2,1)} %refs_2_.2), channel_id=1, source_target_pairs={{0,8},{8,0},{1,9},{9,1},{2,10},{10,2},{3,11},{11,3},{4,12},{12,4},... | collective-permute-start | bytes 4718600 | tf_op jit(solution)/shard_map/ppermute | solution.py:517
  302.6 7.3 %collective-permute-start.9 = (bf16[1536,512]{1,0:T(8,128)(2,1)}, bf16[1536,512]{1,0:T(8,128)(2,1)S(1)}, u32[]{:S(2)}, u32[]{:S(2)}) collective-permute-start(bf16[1536,512]{1,0:T(8,128)(2,1)} %bitcast.30), channel_id=1, source_target_pairs={{0,8},{8,0},{1,9},{9,1},{2,10},{10,2},{3,11},{11,3},{4,12},{12,4},... | collective-permute-start | bytes 4718600 | tf_op jit(solution)/shard_map/ppermute | solution.py:517
  303.9 22.1 %collective-permute-start.8 = (f32[128,1536]{1,0:T(8,128)S(1)}, f32[128,1536]{1,0:T(8,128)}, u32[]{:S(2)}, u32[]{:S(2)}) collective-permute-start(f32[128,1536]{1,0:T(8,128)S(1)} %dynamic-slice_bitcast_fusion.4.refs_7_), channel_id=1, source_target_pairs={{0,1},{1,0},{2,3},{3,2},{4,5},{5,4},{6,7},{7,6},{8,9},{9,8},{10,11... | collective-permute-start | bytes 2359304 | tf_op jit(solution)/shard_map/ppermute | solution.py:517
  306.4 26.7 %collective-permute-start.7 = (bf16[768,512]{1,0:T(8,128)(2,1)}, bf16[768,512]{1,0:T(8,128)(2,1)S(1)}, u32[]{:S(2)}, u32[]{:S(2)}) collective-permute-start(bf16[768,512]{1,0:T(8,128)(2,1)} %bitcast.26), channel_id=1, source_target_pairs={{0,8},{8,0},{1,9},{9,1},{2,10},{10,2},{3,11},{11,3},{4,12},{12,4},... | collective-permute-start | bytes 2359304 | tf_op jit(solution)/shard_map/ppermute | solution.py:517
  328.7 20.4 %collective-permute-start.11 = (f32[128,1536]{1,0:T(8,128)S(1)}, f32[128,1536]{1,0:T(8,128)S(1)}, u32[]{:S(2)}, u32[]{:S(2)}) collective-permute-start(f32[128,1536]{1,0:T(8,128)S(1)} %fusion.6.refs_7_), channel_id=1, source_target_pairs={{6,4},{7,5},{14,12},{15,13},{22,20},{23,21},{30,28},{31,29}} | collective-permute-start | bytes 2359304 | tf_op jit(solution)/shard_map/ppermute | solution.py:565
  329.4 37.1 %collective-permute-start.18 = (bf16[768,768]{1,0:T(8,128)(2,1)}, bf16[768,768]{1,0:T(8,128)(2,1)}, u32[]{:S(2)}, u32[]{:S(2)}) collective-permute-start(bf16[768,768]{1,0:T(8,128)(2,1)} %get-tuple-element.89.refs_4_), channel_id=1, source_target_pairs={{0,1},{1,0},{2,3},{3,2},{4,5},{5,4},{6,7},{7,6},{8,9},{9,8},{10,11... | collective-permute-start | bytes 3538952 | tf_op jit(solution)/shard_map/ppermute | solution.py:587
  331.8 38.7 %collective-permute-start.16 = (bf16[768,768]{1,0:T(8,128)(2,1)}, bf16[768,768]{1,0:T(8,128)(2,1)}, u32[]{:S(2)}, u32[]{:S(2)}) collective-permute-start(bf16[768,768]{1,0:T(8,128)(2,1)} %get-tuple-element.88.refs_3_), channel_id=1, source_target_pairs={{0,16},{16,0},{1,17},{17,1},{2,18},{18,2},{3,19},{19,3},{4,20},{20... | collective-permute-start | bytes 3538952 | tf_op jit(solution)/shard_map/ppermute | solution.py:587
  352.1 14.4 %copy-start.6 = (f32[768,768]{1,0:T(8,128)S(1)}, f32[768,768]{1,0:T(8,128)}, u32[]{:S(2)}) copy-start(f32[768,768]{1,0:T(8,128)} %shard_map.228) | copy-start | bytes 7077892
  352.1 43.2 %collective-permute-start.13 = (f32[128,1536]{1,0:T(8,128)}, f32[128,1536]{1,0:T(8,128)}, u32[]{:S(2)}, u32[]{:S(2)}) collective-permute-start(f32[128,1536]{1,0:T(8,128)} %multiply_add_fusion.3.refs_10_.refs_1_), channel_id=1, source_target_pairs={{4,2},{5,3},{12,10},{13,11},{20,18},{21,19},{28,26},{29,27}} | collective-permute-start | bytes 2359304 | tf_op jit(solution)/shard_map/ppermute | solution.py:565
  364.5 83.9 %collective-permute-start.20 = (bf16[384,1536]{1,0:T(8,128)(2,1)}, bf16[384,1536]{1,0:T(8,128)(2,1)}, u32[]{:S(2)}, u32[]{:S(2)}) collective-permute-start(bf16[384,1536]{1,0:T(8,128)(2,1)} %get-tuple-element.93.refs_3_), channel_id=1, source_target_pairs={{0,16},{16,0},{1,17},{17,1},{2,18},{18,2},{3,19},{19,3},{4,20},{20... | collective-permute-start | bytes 3538952 | tf_op jit(solution)/shard_map/ppermute | solution.py:587
  365.4 87.4 %collective-permute-start.21 = (bf16[384,1536]{1,0:T(8,128)(2,1)}, bf16[384,1536]{1,0:T(8,128)(2,1)}, u32[]{:S(2)}, u32[]{:S(2)}) collective-permute-start(bf16[384,1536]{1,0:T(8,128)(2,1)} %get-tuple-element.94.refs_4_), channel_id=1, source_target_pairs={{0,1},{1,0},{2,3},{3,2},{4,5},{5,4},{6,7},{7,6},{8,9},{9,8},{10,11... | collective-permute-start | bytes 3538952 | tf_op jit(solution)/shard_map/ppermute | solution.py:587
  369.1 87.3 %collective-permute-start.19 = (bf16[4,96,768]{2,1,0:T(8,128)(2,1)}, bf16[4,96,768]{2,1,0:T(8,128)(2,1)}, u32[]{:S(2)}, u32[]{:S(2)}) collective-permute-start(bf16[4,96,768]{2,1,0:T(8,128)(2,1)} %fusion.10), channel_id=1, source_target_pairs={{0,16},{16,0},{1,17},{17,1},{2,18},{18,2},{3,19},{19,3},{4,20},{20... | collective-permute-start | bytes 1769480 | tf_op jit(solution)/shard_map/ppermute | solution.py:587
  373.1 85.1 %collective-permute-start.17 = (bf16[4,96,768]{2,1,0:T(8,128)(2,1)}, bf16[4,96,768]{2,1,0:T(8,128)(2,1)}, u32[]{:S(2)}, u32[]{:S(2)}) collective-permute-start(bf16[4,96,768]{2,1,0:T(8,128)(2,1)} %fusion.12), channel_id=1, source_target_pairs={{0,1},{1,0},{2,3},{3,2},{4,5},{5,4},{6,7},{7,6},{8,9},{9,8},{10,11... | collective-permute-start | bytes 1769480 | tf_op jit(solution)/shard_map/ppermute | solution.py:587
  397.6 43.9 %collective-permute-start.14 = (f32[128,1536]{1,0:T(8,128)S(1)}, f32[128,1536]{1,0:T(8,128)S(1)}, u32[]{:S(2)}, u32[]{:S(2)}) collective-permute-start(f32[128,1536]{1,0:T(8,128)S(1)} %get-tuple-element.139.refs_10_), channel_id=1, source_target_pairs={{2,0},{3,1},{10,8},{11,9},{18,16},{19,17},{26,24},{27,25}} | collective-permute-start | bytes 2359304 | tf_op jit(solution)/shard_map/ppermute | solution.py:565
  448.0 46.7 %collective-permute-start.15 = (f32[128,1536]{1,0:T(8,128)S(1)}, f32[128,1536]{1,0:T(8,128)}, u32[]{:S(2)}, u32[]{:S(2)}) collective-permute-start(f32[128,1536]{1,0:T(8,128)S(1)} %copy-done.9), channel_id=1, source_target_pairs={{0,1},{1,0},{2,3},{3,2},{4,5},{5,4},{6,7},{7,6},{8,9},{9,8},{10,11... | collective-permute-start | bytes 2359304 | tf_op jit(solution)/shard_map/ppermute | solution.py:517
  461.1 73.3 %all-to-all-start.1 = ((f32[4,96,1536]{2,1,0:T(8,128)}), f32[4,96,1536]{2,1,0:T(8,128)S(1)}, u32[]{:S(2)}, u32[]{:S(2)}) async-start(f32[4,96,1536]{2,1,0:T(8,128)} %pad_maximum_fusion.refs_2_), calls=%async_computation.1 | async-start | bytes 4718592 | tf_op jit(solution)/shard_map/all_to_all | solution.py:723
  481.1 39.2 %collective-permute-start.26 = (bf16[4,48,1536]{2,1,0:T(8,128)(2,1)}, bf16[4,48,1536]{2,1,0:T(8,128)(2,1)}, u32[]{:S(2)}, u32[]{:S(2)}) collective-permute-start(bf16[4,48,1536]{2,1,0:T(8,128)(2,1)} %fusion.11.refs_4_), channel_id=1, source_target_pairs={{0,16},{16,0},{1,17},{17,1},{2,18},{18,2},{3,19},{19,3},{4,20},{20... | collective-permute-start | bytes 1769480 | tf_op jit(solution)/shard_map/ppermute | solution.py:587
  482.2 39.6 %collective-permute-start.25 = (bf16[4,48,1536]{2,1,0:T(8,128)(2,1)}, bf16[4,48,1536]{2,1,0:T(8,128)(2,1)}, u32[]{:S(2)}, u32[]{:S(2)}) collective-permute-start(bf16[4,48,1536]{2,1,0:T(8,128)(2,1)} %fusion.13.refs_3_), channel_id=1, source_target_pairs={{0,1},{1,0},{2,3},{3,2},{4,5},{5,4},{6,7},{7,6},{8,9},{9,8},{10,11... | collective-permute-start | bytes 1769480 | tf_op jit(solution)/shard_map/ppermute | solution.py:587
  518.9 6.8 collective-permute-start.23
  520.2 22.1 %collective-permute-start.22 = (bf16[512,1536]{1,0:T(8,128)(2,1)}, bf16[512,1536]{1,0:T(8,128)(2,1)}, u32[]{:S(2)}, u32[]{:S(2)}) collective-permute-start(bf16[512,1536]{1,0:T(8,128)(2,1)} %get-tuple-element.107.refs_5_), channel_id=1, source_target_pairs={{0,8},{8,0},{1,9},{9,1},{2,10},{10,2},{3,11},{11,3},{4,12},{12,4},... | collective-permute-start | bytes 4718600 | tf_op jit(solution)/shard_map/ppermute | solution.py:517
  527.3 15.0 %collective-permute-start.24 = (bf16[16,1536]{1,0:T(8,128)(2,1)}, bf16[16,1536]{1,0:T(8,128)(2,1)}, u32[]{:S(2)}, u32[]{:S(2)}) collective-permute-start(bf16[16,1536]{1,0:T(8,128)(2,1)} %get-tuple-element.136.refs_7_), channel_id=1, source_target_pairs={{0,8},{8,0},{1,9},{9,1},{2,10},{10,2},{3,11},{11,3},{4,12},{12,4},... | collective-permute-start | bytes 147464 | tf_op jit(solution)/shard_map/ppermute | solution.py:517
  535.8 93.6 %all-to-all-start.3 = ((f32[4,48,3072]{2,1,0:T(8,128)}), f32[4,48,3072]{2,1,0:T(8,128)}, u32[]{:S(2)}, u32[]{:S(2)}) async-start(f32[4,48,3072]{2,1,0:T(8,128)} %pad_maximum_fusion.1.refs_9_), calls=%async_computation.3 | async-start | bytes 4718592 | tf_op jit(solution)/shard_map/all_to_all | solution.py:723
  571.9 18.7 %collective-permute-start.32 = (bf16[384,768]{1,0:T(8,128)(2,1)}, bf16[384,768]{1,0:T(8,128)(2,1)S(1)}, u32[]{:S(2)}, u32[]{:S(2)}) collective-permute-start(bf16[384,768]{1,0:T(8,128)(2,1)} %get-tuple-element.112.refs_27_), channel_id=1, source_target_pairs={{0,1},{1,0},{2,3},{3,2},{4,5},{5,4},{6,7},{7,6},{8,9},{9,8},{10,11... | collective-permute-start | bytes 1769480 | tf_op jit(solution)/shard_map/ppermute | solution.py:587
  576.2 15.7 %collective-permute-start.30 = (bf16[384,768]{1,0:T(8,128)(2,1)}, bf16[384,768]{1,0:T(8,128)(2,1)S(1)}, u32[]{:S(2)}, u32[]{:S(2)}) collective-permute-start(bf16[384,768]{1,0:T(8,128)(2,1)} %get-tuple-element.111.refs_26_), channel_id=1, source_target_pairs={{0,16},{16,0},{1,17},{17,1},{2,18},{18,2},{3,19},{19,3},{4,20},{20... | collective-permute-start | bytes 1769480 | tf_op jit(solution)/shard_map/ppermute | solution.py:587
  577.3 13.3 %copy-start.26 = (f32[384,768]{1,0:T(8,128)S(1)}, f32[384,768]{1,0:T(8,128)}, u32[]{:S(2)}) copy-start(f32[384,768]{1,0:T(8,128)} %shard_map.240) | copy-start | bytes 3538948
  577.4 23.7 %collective-permute-start.27 = (bf16[512,1920]{1,0:T(8,128)(2,1)S(1)}, bf16[512,1920]{1,0:T(8,128)(2,1)S(1)}, u32[]{:S(2)}, u32[]{:S(2)}) collective-permute-start(bf16[512,1920]{1,0:T(8,128)(2,1)S(1)} %copy-done.10), channel_id=1, source_target_pairs={{0,8},{8,0},{1,9},{9,1},{2,10},{10,2},{3,11},{11,3},{4,12},{12,4},... | collective-permute-start | bytes 5898248 | tf_op jit(solution)/shard_map/ppermute | solution.py:517
  578.1 15.7 %collective-permute-start.28 = (f32[16,1920]{1,0:T(8,128)S(1)}, f32[16,1920]{1,0:T(8,128)S(1)}, u32[]{:S(2)}, u32[]{:S(2)}) collective-permute-start(f32[16,1920]{1,0:T(8,128)S(1)} %slice.164), channel_id=1, source_target_pairs={{1,0},{2,1},{3,2},{4,3},{5,4},{6,5},{7,6},{9,8},{10,9},{11,10},{12... | collective-permute-start | bytes 368648 | tf_op jit(solution)/shard_map/ppermute | solution.py:523
  580.7 11.2 %copy-start.27 = (f32[384,768]{1,0:T(8,128)S(1)}, f32[384,768]{1,0:T(8,128)}, u32[]{:S(2)}) copy-start(f32[384,768]{1,0:T(8,128)} %shard_map.239) | copy-start | bytes 3538948
  590.8 6.8 collective-permute-start.33
  592.1 7.8 %collective-permute-start.31 = (bf16[4,48,768]{2,1,0:T(8,128)(2,1)S(1)}, bf16[4,48,768]{2,1,0:T(8,128)(2,1)S(1)}, u32[]{:S(2)}, u32[]{:S(2)}) collective-permute-start(bf16[4,48,768]{2,1,0:T(8,128)(2,1)S(1)} %fusion.17), channel_id=1, source_target_pairs={{0,1},{1,0},{2,3},{3,2},{4,5},{5,4},{6,7},{7,6},{8,9},{9,8},{10,11... | collective-permute-start | bytes 884744 | tf_op jit(solution)/shard_map/ppermute | solution.py:587
  593.9 7.2 %copy-start.38 = (bf16[512,1920]{1,0:T(8,128)(2,1)}, bf16[512,1920]{1,0:T(8,128)(2,1)S(1)}, u32[]{:S(2)}) copy-start(bf16[512,1920]{1,0:T(8,128)(2,1)S(1)} %get-tuple-element.133.refs_1_) | copy-start | bytes 5898244
  593.9 7.2 %copy-start.45 = (bf16[16,1920]{1,0:T(8,128)(2,1)}, bf16[16,1920]{1,0:T(8,128)(2,1)S(1)}, u32[]{:S(2)}) copy-start(bf16[16,1920]{1,0:T(8,128)(2,1)S(1)} %get-tuple-element.134.refs_7_) | copy-start | bytes 184324
  593.9 7.2 %collective-permute-start.29 = (bf16[16,1920]{1,0:T(8,128)(2,1)S(1)}, bf16[16,1920]{1,0:T(8,128)(2,1)S(1)}, u32[]{:S(2)}, u32[]{:S(2)}) collective-permute-start(bf16[16,1920]{1,0:T(8,128)(2,1)S(1)} %get-tuple-element.134.refs_7_), channel_id=1, source_target_pairs={{0,8},{8,0},{1,9},{9,1},{2,10},{10,2},{3,11},{11,3},{4,12},{12,4},... | collective-permute-start | bytes 184328 | tf_op jit(solution)/shard_map/ppermute | solution.py:517
  608.5 30.0 %collective-permute-start.35 = (bf16[384,896]{1,0:T(8,128)(2,1)}, bf16[384,896]{1,0:T(8,128)(2,1)S(1)}, u32[]{:S(2)}, u32[]{:S(2)}) collective-permute-start(bf16[384,896]{1,0:T(8,128)(2,1)} %get-tuple-element.118.refs_7_), channel_id=1, source_target_pairs={{0,1},{1,0},{2,3},{3,2},{4,5},{5,4},{6,7},{7,6},{8,9},{9,8},{10,11... | collective-permute-start | bytes 2064392 | tf_op jit(solution)/shard_map/ppermute | solution.py:587
  616.3 24.8 %collective-permute-start.34 = (bf16[384,1024]{1,0:T(8,128)(2,1)}, bf16[384,1024]{1,0:T(8,128)(2,1)}, u32[]{:S(2)}, u32[]{:S(2)}) collective-permute-start(bf16[384,1024]{1,0:T(8,128)(2,1)} %get-tuple-element.117.refs_6_), channel_id=1, source_target_pairs={{0,16},{16,0},{1,17},{17,1},{2,18},{18,2},{3,19},{19,3},{4,20},{20... | collective-permute-start | bytes 2359304 | tf_op jit(solution)/shard_map/ppermute | solution.py:587
  629.4 29.7 %all-to-all-start.4 = ((f32[4,48,1536]{2,1,0:T(8,128)}), f32[4,48,1536]{2,1,0:T(8,128)S(1)}, u32[]{:S(2)}, u32[]{:S(2)}) async-start(f32[4,48,1536]{2,1,0:T(8,128)} %pad_maximum_fusion.4.refs_9_), calls=%async_computation.4 | async-start | bytes 2359296 | tf_op jit(solution)/shard_map/all_to_all | solution.py:723
  640.0 15.4 %collective-permute-start.37 = (bf16[4,48,896]{2,1,0:T(8,128)(2,1)S(1)}, bf16[4,48,896]{2,1,0:T(8,128)(2,1)}, u32[]{:S(2)}, u32[]{:S(2)}) collective-permute-start(bf16[4,48,896]{2,1,0:T(8,128)(2,1)S(1)} %fusion.15.refs_4_.refs_2_), channel_id=1, source_target_pairs={{0,16},{16,0},{1,17},{17,1},{2,18},{18,2},{3,19},{19,3},{4,20},{20... | collective-permute-start | bytes 1032200 | tf_op jit(solution)/shard_map/ppermute | solution.py:587
  642.6 11.1 %copy-start.41 = (bf16[4,48,1024]{2,1,0:T(8,128)(2,1)}, bf16[4,48,1024]{2,1,0:T(8,128)(2,1)S(1)}, u32[]{:S(2)}) copy-start(bf16[4,48,1024]{2,1,0:T(8,128)(2,1)S(1)} %fusion.14.refs_3_.refs_1_) | copy-start | bytes 1179652
  642.6 14.9 %collective-permute-start.36 = (bf16[4,48,1024]{2,1,0:T(8,128)(2,1)S(1)}, bf16[4,48,1024]{2,1,0:T(8,128)(2,1)}, u32[]{:S(2)}, u32[]{:S(2)}) collective-permute-start(bf16[4,48,1024]{2,1,0:T(8,128)(2,1)S(1)} %fusion.14.refs_3_.refs_1_), channel_id=1, source_target_pairs={{0,1},{1,0},{2,3},{3,2},{4,5},{5,4},{6,7},{7,6},{8,9},{9,8},{10,11... | collective-permute-start | bytes 1179656 | tf_op jit(solution)/shard_map/ppermute | solution.py:587
  659.1 7.8 %copy-start.14 = (f32[4,48,1536]{2,1,0:T(8,128)}, f32[4,48,1536]{2,1,0:T(8,128)S(1)}, u32[]{:S(2)}) copy-start(f32[4,48,1536]{2,1,0:T(8,128)S(1)} %all-to-all-done.4.refs_0_) | copy-start | bytes 3538948
  659.1 13.1 %all-to-all-start.2 = ((f32[32,1,808]{2,1,0:T(1,128)}), f32[32,1,808]{2,1,0:T(1,128)S(1)}, u32[]{:S(2)}, u32[]{:S(2)}) async-start(f32[32,1,808]{2,1,0:T(1,128)} %copy.81), calls=%async_computation.2 | async-start | bytes 229376 | tf_op jit(solution)/shard_map/all_to_all | solution.py:1161
  672.2 38.9 %all-to-all-start.5 = ((f32[4,48,1920]{2,1,0:T(8,128)}), f32[4,48,1920]{2,1,0:T(8,128)S(1)}, u32[]{:S(2)}, u32[]{:S(2)}) async-start(f32[4,48,1920]{2,1,0:T(8,128)} %pad_maximum_fusion.2), calls=%async_computation.5 | async-start | bytes 2949120 | tf_op jit(solution)/shard_map/all_to_all | solution.py:723
  (45 other events, 88.1 us)
Sparse Core Ops, SparseCore 0:
  11.5 90.9 all-gather.2
  106.0 131.5 all-gather.4

commit v4 on v3

--- a/solution.py
+++ b/solution.py
@@ -716,14 +716,20 @@
         self.came_x = travel(self.next_x, "y", ())
         self.came_y = travel(self.next_y, "x", ())
 
-    def third(self, *others):
+    def third(self, *others, kind=F32):
         done_x = total_of(tied(self.own_x, others), self.came_x)
         done_y = total_of(tied(self.own_y, others), self.came_y)
         self.parts = jnp.concatenate([done_x, done_y], axis=2)
-        self.got_z = lax.all_to_all(self.parts, "z", 0, 0, tiled=True)
+        place = lax.axis_index("z")
+        self.mine = pick(self.parts, place) if kind == BF else None
+        self.got_z = lax.all_to_all(self.parts.astype(kind), "z", 0, 0, tiled=True)
 
     def last(self, *others):
-        return jnp.sum(tied(self.got_z, others), axis=0)
+        got = tied(self.got_z, others)
+        if self.mine is None:
+            return jnp.sum(got, axis=0)
+        others_only = lax.broadcasted_iota(jnp.int32, got.shape, 0) != lax.axis_index("z")
+        return self.mine + jnp.sum(jnp.where(others_only, got.astype(F32), 0.0), axis=0)
 
 
 def core_rows(turned, core):
@@ -1001,23 +1007,14 @@
 
     norm_block = 256
 
-    def back_z(wait):
-        back["d_normed"] = call(
-            back_z_body, width // norm_block, 10,
-            [
-                (d_z, whole(row_count, INNER)),
-                (stacked, pl.BlockSpec((2, norm_block, half), lambda g: (0, g, 0))),
-            ],
-            [(out((row_count, width)), lanes(row_count, norm_block))],
-            waits=[wait],
-        )[0]
+    def send_out(wait):
         back["z"].second(wait)
         back["out"].third(wait)
-        return [back["d_normed"], back["out"].parts, *back["z"].next_x, *back["z"].next_y]
+        return [back["out"].parts, *back["z"].next_x, *back["z"].next_y]
 
     returned = entering(
         returned_local, device_decay, True,
-        [out_sums, z_sums, first_within, second_within, back_z],
+        [out_sums, z_sums, first_within, second_within, send_out],
     )
 
     blocks = half // BLOCK
@@ -1090,7 +1087,16 @@
     halo_b = from_behind(edge_b[:LEAD], -1)
     sums_a.second(edge_b)
     sums_a.third()
-    last_b = (edge_b[LEAD:] + halo_b).astype(BF)
+    d_normed_z = call(
+        back_z_body, width // norm_block, 10,
+        [
+            (d_z, whole(row_count, INNER)),
+            (stacked, pl.BlockSpec((2, norm_block, half), lambda g: (0, g, 0))),
+        ],
+        [(out((row_count, width)), lanes(row_count, norm_block))],
+        waits=[edge_b],
+    )[0]
+    last_b = (edge_b[LEAD:] + tie(halo_b, d_normed_z)).astype(BF)
     last_b_theirs = swap(last_b, "core")
     wide_b = d_xb.shape[1]
     sums_b = Reduction(
@@ -1106,7 +1112,7 @@
             (d_xa, whole(row_count, half)),
             (d_xb, whole(row_count, wide_b)),
             (weight_x, rows_of(norm_block, PROJ_X)),
-            (back["d_normed"], lanes(row_count, norm_block)),
+            (d_normed_z, lanes(row_count, norm_block)),
         ],
         [(out((row_count, width)), lanes(row_count, norm_block))],
         waits=sums_b.made(),
@@ -1156,7 +1162,7 @@
         ],
         axis=1,
     )
-    sums_b.third()
+    sums_b.third(kind=BF)
     per_device = tie(per_device, *sums_b.next_x, *sums_b.next_y)
     arrived = lax.all_to_all(per_device, EVERY, 0, 0, tiled=True)
     done = [layer_out]

time: 731 us -> 720 us (0.985)
  waiting for transfers between devices: 175 us -> 166 us
    unnamed x133 -> x141, local copies, waits for them, and re-layouts: 26.4 us -> 29.6 us
  transfers between devices with their start and end apart: 46 -> 46, of which waited for: 14 -> 13; matrix products, arithmetic and copies ran while one was open for 19% -> 19% of each run, Pallas kernels for 32% -> 32%
where the time goes in v4:
time: 720 us; the launch traced here: 708 us
  Pallas kernels  259 us (36%)
  waiting for transfers between devices  166 us (23%)
  starting transfers between devices  99.7 us (14%)
  local copies, waits for them, and re-layouts  74.3 us (10%)
  other arithmetic  67.5 us (9%)
  matrix products  24.4 us (3%)
  between operations  17.6 us (2%)
    pallas_call x23, Pallas kernels, call(): pl.pallas_call(run, grid_spec=pltpu.PrefetchScalarGridSpec(num_scalar_pre...  259 us
    all_gather x1, waiting for transfers between devices, shards(): lax.all_gather(columns(in_weight[:, INNER:], PROJ_X), EVERY, axis=0, tile...  59.4 us
    ppermute x6, waiting for transfers between devices, entering(): arrived = meanwhile(sent, lax.ppermute(sent, 'z', pairs))  42 us
    all_to_all x4, starting transfers between devices, third(): self.got_z = lax.all_to_all(self.parts.astype(kind), 'z', 0, 0, tiled=True)  33.7 us
    unnamed x141, local copies, waits for them, and re-layouts  29.6 us
    ppermute x16, starting transfers between devices, across(): lax.ppermute(array, axis, [(i, i ^ by) for i in range(lax.axis_size(axis))])  27.5 us
    dot_general x3, matrix products, mm(): return jnp.dot(left, right, preferred_element_type=F32)  24.4 us
    add x16, other arithmetic, total_of(): kept = kept + piece.astype(F32)  19.3 us
  transfers between devices with their start and end apart: 46, of which 13 were waited for; matrix products, arithmetic and copies ran while one was open for 19% of the time, Pallas kernels for 32%

profile of v4, /device:TPU:0, one launch (start us, length us, event | category | flops | bytes accessed | tf_op | source)
XLA Modules:
  0.0 708.4 jit_solution(2070394790791725150)
XLA Ops:
  12.0 4.9 collective-permute-start
  19.3 4.9 all-to-all-start
  39.1 3.9 shard_map.203
  43.0 59.4 %all-gather.3.cloned.1.call-done.refs_2_ = bf16[1536,3456]{1,0:T(8,128)(2,1)} async-done(((bf16[48,3456]{1,0:T(8,128)(2,1)}), bf16[1536,3456]{1,0:T(8,128)(2,1)}) %all-gather.3.cloned.1.call-update) | async-done | bytes 10616848 | tf_op jit(solution)/shard_map/all_gather | solution.py:780
  102.4 11.7 %convolution_convert_fusion.refs_0_.refs_1_.refs_4_.refs_17_ = bf16[528,3456]{1,0:T(8,128)(2,1)} fusion(bf16[528,1536]{1,0:T(8,128)(2,1)} %get-tuple-element.68, bf16[1536,3456]{1,0:T(8,128)(2,1)} %all-gather.3.cloned.1.call-done.refs_2_), kind=kOutput, calls=%fused_computation | convolution fusion | flops 5607512064 | bytes 15888384 | tf_op jit(solution)/shard_map/dot_general | solution.py:105
  114.8 4.5 shard_map.204
  120.8 12.5 %shard_map.205 = (f32[512,3072]{1,0:T(8,128)}, f32[512,3072]{1,0:T(8,128)}, f32[2,128,1536]{2,1,0:T(8,128)}, f32[2,8,1536]{2,1,0:T(8,128)}) custom-call(bf16[528,3456]{1,0:T(8,128)(2,1)} %convolution_convert_fusion.refs_0_.refs_1_.refs_4_.refs_17_, f32[8,3072]{1,0:T(8,128)} %slice.174.refs_1_.refs_5_, f32[1,3072]{1,0:T(1,128)} %slice.175.refs_2_, ...), custom_call_target="tpu_custom_call" | custom-call | flops 12000000000 | bytes 36000000 | tf_op jit(solution)/shard_map/pallas_call | solution.py:43
  137.8 13.6 %shard_map.206.refs_1_.refs_0_ = f32[512,1536]{1,0:T(8,128)} custom-call(f32[512,3072]{1,0:T(8,128)} %get-tuple-element.73.refs_0_.refs_5_.refs_1_, f32[512,128]{1,0:T(8,128)} %get-tuple-element.70.refs_5_.refs_1_.refs_2_.refs_11_, f32[1,3072]{1,0:T(1,128)} %broadcast_in_dim_reshape.3.refs_2_.refs_11_.refs_12_, f32[512,512]{1,0:T(8,128)} %get-tuple-element.74.refs_3_, ...), custom_call_target="tpu_custom_call" | custom-call | flops 12000000000 | bytes 36000000 | tf_op jit(solution)/shard_map/pallas_call | solution.py:43
  152.2 11.0 %collective-permute-done.2.refs_0_ = f32[128,1536]{1,0:T(8,128)S(1)} collective-permute-done((f32[128,1536]{1,0:T(8,128)S(1)}, f32[128,1536]{1,0:T(8,128)S(1)}, u32[]{:S(2)}, u32[]{:S(2)}) %collective-permute-start.2) | collective-permute-done | bytes 786464 | tf_op jit(solution)/shard_map/ppermute | solution.py:517
  164.1 2.2 fusion.8.refs_6_
  166.3 3.6 collective-permute-start.3
  169.9 13.7 %shard_map.208.refs_1_ = f32[512,1536]{1,0:T(8,128)} custom-call(f32[512,3072]{1,0:T(8,128)} %get-tuple-element.73.refs_0_.refs_5_.refs_1_, f32[512,128]{1,0:T(8,128)} %get-tuple-element.70.refs_5_.refs_1_.refs_2_.refs_11_, f32[1,3072]{1,0:T(1,128)} %broadcast_in_dim_reshape.3.refs_2_.refs_11_.refs_12_, f32[512,512]{1,0:T(8,128)} %get-tuple-element.74.refs_3_, ...), custom_call_target="tpu_custom_call" | custom-call | flops 12000000000 | bytes 36000000 | tf_op jit(solution)/shard_map/pallas_call | solution.py:43
  183.6 19.1 %collective-permute-done.3.refs_0_ = f32[128,1536]{1,0:T(8,128)S(1)} collective-permute-done((f32[128,1536]{1,0:T(8,128)}, f32[128,1536]{1,0:T(8,128)S(1)}, u32[]{:S(2)}, u32[]{:S(2)}) %collective-permute-start.3) | collective-permute-done | bytes 786464 | tf_op jit(solution)/shard_map/ppermute | solution.py:565
  203.6 2.2 multiply_add_fusion.6
  207.4 2.5 multiply_add_fusion.5
  216.6 2.3 select_bitcast_fusion.1
  218.9 18.8 %all-gather.5.cloned.1.call-done.refs_1_ = bf16[4,1536,1536]{2,1,0:T(8,128)(2,1)} async-done(((bf16[4,48,1536]{2,1,0:T(8,128)(2,1)}), bf16[4,1536,1536]{2,1,0:T(8,128)(2,1)}) %all-gather.5.cloned.1.call-update) | async-done | bytes 18874384 | tf_op jit(solution)/shard_map/all_gather | solution.py:785
  237.7 6.6 fusion.3.refs_3_
  244.3 12.8 %shard_map.212.refs_1_.refs_4_ = f32[512,3072]{1,0:T(8,128)} custom-call(bf16[512,1536]{1,0:T(8,128)(2,1)} %refs_2_.2, bf16[4,1536,1536]{2,1,0:T(8,128)(2,1)} %all-gather.5.cloned.1.call-done.refs_1_, f32[128,1536]{1,0:T(8,128)} %get-tuple-element.146.refs_2_), custom_call_target="tpu_custom_call" | custom-call | flops 7000000000 | bytes 21000000 | tf_op jit(solution)/shard_map/pallas_call | solution.py:43
  257.1 6.0 fusion.2.refs_2_
  264.0 3.6 multiply_add_fusion
  267.5 31.7 %shard_map.214 = (bf16[512,3072]{1,0:T(8,128)(2,1)}, bf16[3072,512]{1,0:T(8,128)(2,1)}, bf16[512,3072]{1,0:T(8,128)(2,1)}, f32[512,3072]{1,0:T(8,128)}, f32[2,12...) custom-call(f32[512,1536]{1,0:T(8,128)} %shard_map.206.refs_1_.refs_0_, ...), custom_call_target="tpu_custom_call" | custom-call | flops 31000000512 | bytes 93000000 | tf_op jit(solution)/shard_map/pallas_call | solution.py:43
  299.9 2.7 constant_dynamic-slice_fusion
  306.3 3.6 collective-permute-done.10.refs_6_
  311.0 7.4 %shard_map.215 = (bf16[768,768]{1,0:T(8,128)(2,1)}, f32[768,768]{1,0:T(8,128)}) custom-call(s32[3]{0:T(128)} %pad_add_fusion.refs_0_, bf16[2,2,768,512]{3,2,1,0:T(8,128)(2,1)} %bitcast.195, bf16[2,2,768,512]{3,2,1,0:T(8,128)(2,1)} %bitcast.196, bf16[2,768,512]{2,1,0:T(8,128)(2,1)} %bitcast.199, bf16[2,768,512]{2,1,0:T(8,128)(2,1)} %bitcast.200, ...), custom_call_target="tpu_custom_call" | custom-call | flops 2949120000 | bytes 8847360 | tf_op jit(solution)/shard_map/pallas_call | solution.py:43
  318.4 7.5 %shard_map.216 = (bf16[768,768]{1,0:T(8,128)(2,1)}, f32[768,768]{1,0:T(8,128)}) custom-call(s32[3]{0:T(128)} %pad_add_fusion.refs_0_, bf16[2,2,4,2,96,512]{5,4,3,2,1,0:T(8,128)(2,1)} %bitcast.197, bf16[2,2,4,2,96,512]{5,4,3,2,1,0:T(8,128)(2,1)} %bitcast.198, bf16[8,2,96,512]{3,2,1,0:T(8,128)(2,1)} %bitcast.201, bf16[8,2,96,512]{3,2,1,0:T(8,128)(2,1)} %bitcast.202, ...), custom_call_target="tpu_custom_call" | custom-call | flops 2949120000 | bytes 8847360 | tf_op jit(solution)/shard_map/pallas_call | solution.py:43
  334.3 7.6 %shard_map.218 = (bf16[384,1536]{1,0:T(8,128)(2,1)}, f32[384,1536]{1,0:T(8,128)}) custom-call(s32[3]{0:T(128)} %pad_add_fusion.refs_0_, bf16[2,2,384,512]{3,2,1,0:T(8,128)(2,1)} %bitcast.169, bf16[2,2,384,512]{3,2,1,0:T(8,128)(2,1)} %bitcast.170, bf16[2,384,512]{2,1,0:T(8,128)(2,1)} %bitcast.182, bf16[2,384,512]{2,1,0:T(8,128)(2,1)} %bitcast.183, ...), custom_call_target="tpu_custom_call" | custom-call | flops 2949120000 | bytes 8847360 | tf_op jit(solution)/shard_map/pallas_call | solution.py:43
  341.9 7.6 %shard_map.219 = (bf16[384,1536]{1,0:T(8,128)(2,1)}, f32[384,1536]{1,0:T(8,128)}) custom-call(s32[3]{0:T(128)} %pad_add_fusion.refs_0_, bf16[2,2,4,2,48,512]{5,4,3,2,1,0:T(8,128)(2,1)} %bitcast.171, bf16[2,2,4,2,48,512]{5,4,3,2,1,0:T(8,128)(2,1)} %bitcast.172, bf16[8,2,48,512]{3,2,1,0:T(8,128)(2,1)} %bitcast.184, bf16[8,2,48,512]{3,2,1,0:T(8,128)(2,1)} %bitcast.185, ...), custom_call_target="tpu_custom_call" | custom-call | flops 2949120000 | bytes 8847360 | tf_op jit(solution)/shard_map/pallas_call | solution.py:43
  352.5 12.0 %collective-permute-start.13 = (f32[128,1536]{1,0:T(8,128)}, f32[128,1536]{1,0:T(8,128)}, u32[]{:S(2)}, u32[]{:S(2)}) collective-permute-start(f32[128,1536]{1,0:T(8,128)} %multiply_add_fusion.3.refs_10_.refs_1_), channel_id=1, source_target_pairs={{4,2},{5,3},{12,10},{13,11},{20,18},{21,19},{28,26},{29,27}} | collective-permute-start | bytes 2359304 | tf_op jit(solution)/shard_map/ppermute | solution.py:565
  374.8 18.3 %shard_map.221 = (f32[512,1536]{1,0:T(8,128)}, f32[512,512]{1,0:T(8,128)}) custom-call(f32[512,3072]{1,0:T(8,128)} %get-tuple-element.73.refs_0_.refs_5_.refs_1_, f32[512,3072]{1,0:T(8,128)} %get-tuple-element.82.refs_1_.refs_2_, f32[512,128]{1,0:T(8,128)} %get-tuple-element.70.refs_5_.refs_1_.refs_2_.refs_11_, f32[512,512]{1,0:T(8,128)} %get-tuple-element.83.refs_3_, ...), custom_call_target="tpu_custom_call" | custom-call | flops 17999998976 | bytes 54000000 | tf_op jit(solution)/shard_map/pallas_call | solution.py:43
  398.9 19.8 %shard_map.223 = (f32[512,1536]{1,0:T(8,128)}, f32[512,512]{1,0:T(8,128)}, f32[512,256]{1,0:T(8,128)}) custom-call(f32[512,3072]{1,0:T(8,128)} %get-tuple-element.73.refs_0_.refs_5_.refs_1_, f32[512,3072]{1,0:T(8,128)} %get-tuple-element.82.refs_1_.refs_2_, f32[512,128]{1,0:T(8,128)} %get-tuple-element.70.refs_5_.refs_1_.refs_2_.refs_11_, ...), custom_call_target="tpu_custom_call" | custom-call | flops 17999998976 | bytes 54000000 | tf_op jit(solution)/shard_map/pallas_call | solution.py:43
  418.7 22.9 %collective-permute-done.14.refs_0_ = f32[128,1536]{1,0:T(8,128)S(1)} collective-permute-done((f32[128,1536]{1,0:T(8,128)S(1)}, f32[128,1536]{1,0:T(8,128)S(1)}, u32[]{:S(2)}, u32[]{:S(2)}) %collective-permute-start.14) | collective-permute-done | bytes 786464 | tf_op jit(solution)/shard_map/ppermute | solution.py:565
  444.0 2.8 select_bitcast_fusion
  452.0 1.8 pad_maximum_fusion.refs_1_
  453.8 20.0 %all-to-all-start.1 = ((f32[4,96,1536]{2,1,0:T(8,128)}), f32[4,96,1536]{2,1,0:T(8,128)S(1)}, u32[]{:S(2)}, u32[]{:S(2)}) async-start(f32[4,96,1536]{2,1,0:T(8,128)} %pad_maximum_fusion.refs_1_), calls=%async_computation.1 | async-start | bytes 4718592 | tf_op jit(solution)/shard_map/all_to_all | solution.py:725
  473.8 2.4 convert_add_fusion
  480.3 2.0 collective-permute-start.25
  485.6 2.7 maximum_select_fusion.1.refs_8_
  489.6 17.5 %shard_map.232 = (bf16[512,1536]{1,0:T(8,128)(2,1)}, f32[32,1536]{1,0:T(8,128)}, f32[8,1536]{1,0:T(8,128)}, f32[512,128]{1,0:T(8,128)}, f32[512,128]{1,0:T(8,128)}, /*index=5*/f32[8,128]{1,0:T(8,128)}) custom-call(f32[512,1536]{1,0:T(8,128)} %get-tuple-element.96.refs_1_.refs_0_, f32[512,3072]{1,0:T(8,128)} %get-tuple-element.73.refs_0_.refs_5_.refs_1_, ...), custom_call_target="tpu_custom_call" | custom-call | flops 14000000000 | bytes 42000000 | tf_op jit(solution)/shard_map/pallas_call | solution.py:43
  513.6 1.8 collective-permute-done.23
  519.7 7.3 %all-to-all-done.1.refs_10_.refs_0_ = f32[4,96,1536]{2,1,0:T(8,128)S(1)} async-done(((f32[4,96,1536]{2,1,0:T(8,128)}), f32[4,96,1536]{2,1,0:T(8,128)S(1)}, u32[]{:S(2)}, u32[]{:S(2)}) %all-to-all-start.1) | async-done | bytes 2359328 | tf_op jit(solution)/shard_map/all_to_all | solution.py:725
  528.4 6.4 all-to-all-start.3
  534.9 5.3 shard_map.236
  540.1 5.3 shard_map.235
  545.4 18.1 %shard_map.237 = (f32[16,128]{1,0:T(8,128)}, bf16[512,1920]{1,0:T(8,128)(2,1)}, f32[32,1920]{1,0:T(8,128)}, f32[8,1920]{1,0:T(8,128)}, f32[512,128]{1,0:T(8,128)}, /*index=5*/f32[512,128]{1,0:T(8,128)}, f32[8,128]{1,0:T(8,128)}) custom-call(f32[512,1536]{1,0:T(8,128)} %get-tuple-element.97.refs_1_.refs_0_, ...), custom_call_target="tpu_custom_call" | custom-call | flops 17999998976 | bytes 54000000 | tf_op jit(solution)/shard_map/pallas_call | solution.py:43
  564.5 2.5 collective-permute-start.32
  571.5 10.7 %shard_map.238.refs_1_.refs_3_ = f32[512,1536]{1,0:T(8,128)} custom-call(bf16[512,3072]{1,0:T(8,128)(2,1)} %get-tuple-element.90.refs_5_.refs_0_, bf16[4,1536,1536]{2,1,0:T(8,128)(2,1)} %all-gather.5.cloned.1.call-done.refs_1_, f32[32,1920]{1,0:T(8,128)} %get-tuple-element.114.refs_2_.refs_1_), custom_call_target="tpu_custom_call" | custom-call | flops 10000000000 | bytes 30000000 | tf_op jit(solution)/shard_map/pallas_call | solution.py:43
  587.7 9.2 %collective-permute-start.31 = (bf16[4,48,768]{2,1,0:T(8,128)(2,1)S(1)}, bf16[4,48,768]{2,1,0:T(8,128)(2,1)S(1)}, u32[]{:S(2)}, u32[]{:S(2)}) collective-permute-start(bf16[4,48,768]{2,1,0:T(8,128)(2,1)S(1)} %fusion.20), channel_id=1, source_target_pairs={{0,1},{1,0},{2,3},{3,2},{4,5},{5,4},{6,7},{7,6},{8,9},{9,8},{10,11... | collective-permute-start | bytes 884744 | tf_op jit(solution)/shard_map/ppermute | solution.py:587
  597.7 6.1 collective-permute-done.31
  605.6 5.4 shard_map.243
  611.1 1.7 collective-permute-start.35
  612.8 5.4 shard_map.242
  618.9 12.0 %shard_map.244.refs_0_ = f32[512,1536]{1,0:T(8,128)} custom-call(bf16[512,1536]{1,0:T(8,128)(2,1)} %copy-done.40, bf16[512,1920]{1,0:T(8,128)(2,1)} %get-tuple-element.133.refs_1_, bf16[1536,3456]{1,0:T(8,128)(2,1)} %all-gather.3.cloned.1.call-done.refs_2_, f32[512,1536]{1,0:T(8,128)} %shard_map.238.refs_1_.refs_3_, ...), custom_call_target="tpu_custom_call" | custom-call | flops 10000000000 | bytes 30000000 | tf_op jit(solution)/shard_map/pallas_call | solution.py:43
  630.9 3.8 all-to-all-start.4
  634.7 5.6 shard_map.245
  652.5 2.4 collective-permute-done.36
  656.1 5.7 all-to-all-done.4.refs_0_
  661.8 2.6 all-to-all-start.2
  665.4 6.7 all-to-all-done.2
  672.1 3.5 all-to-all-start.5
  675.6 12.8 %shard_map.248.refs_1_ = bf16[512,1536]{1,0:T(8,128)(2,1)} custom-call(bf16[512,3072]{1,0:T(8,128)(2,1)} %get-tuple-element.80.refs_0_, bf16[4,1536,1536]{2,1,0:T(8,128)(2,1)} %all-gather.5.cloned.1.call-done.refs_1_, bf16[512,1536]{1,0:T(8,128)(2,1)} %refs_2_.3, bf16[4,48,1024]{2,1,0:T(8,128)(2,1)} %copy-done.41, bf16[4,48,896]{2,1,0:T(8,128)(2,1)} %copy-done.42), custom_call_target="tpu_custom_call" | custom-call | flops 12999999488 | bytes 39000000 | tf_op jit(solution)/shard_map/pallas_call | solution.py:43
  688.4 2.7 reduce_sum.79
  691.1 2.1 reduce_sum.77
  693.1 1.9 reduce_sum.76
  (362 shorter events, 134.0 us)
Async XLA Ops:
  7.2 95.2 %all-gather.3.cloned.1.call-start = ((), (), s32[]{:S(2)}) async-start(), calls=%async_computation.6 | async-start | bytes 10948608 | tf_op jit(solution)/shard_map/all_gather | solution.py:780
  9.0 7.8 %copy-start.57 = (bf16[4,104]{1,0:T(4,128)(2,1)S(1)}, bf16[4,104]{1,0:T(4,128)(2,1)}, u32[]{:S(2)}) copy-start(bf16[4,104]{1,0:T(4,128)(2,1)} %param.17) | copy-start | bytes 2500
  9.1 7.9 %copy-start.59 = (bf16[96]{0:T(256)(128)(2,1)S(1)}, bf16[96]{0:T(256)(128)(2,1)}, u32[]{:S(2)}) copy-start(bf16[96]{0:T(256)(128)(2,1)} %param.22) | copy-start | bytes 580
  9.1 7.9 %copy-start.60 = (bf16[104]{0:T(256)(128)(2,1)S(1)}, bf16[104]{0:T(256)(128)(2,1)}, u32[]{:S(2)}) copy-start(bf16[104]{0:T(256)(128)(2,1)} %param.18) | copy-start | bytes 628
  9.1 7.9 %copy-start.61 = (bf16[48]{0:T(256)(128)(2,1)S(1)}, bf16[48]{0:T(256)(128)(2,1)}, u32[]{:S(2)}) copy-start(bf16[48]{0:T(256)(128)(2,1)} %param.15) | copy-start | bytes 292
  9.1 228.6 %all-gather.5.cloned.1.call-start = ((), (), s32[]{:S(2)}) async-start(), calls=%async_computation.7 | async-start | bytes 19464192 | tf_op jit(solution)/shard_map/all_gather | solution.py:785
  10.2 14.0 %copy-start.64 = (f32[48]{0:T(128)S(1)}, f32[48]{0:T(128)}, u32[]{:S(2)}) copy-start(f32[48]{0:T(128)} %param.19) | copy-start | bytes 580
  10.2 14.5 %copy-start.65 = (f32[48]{0:T(128)S(1)}, f32[48]{0:T(128)}, u32[]{:S(2)}) copy-start(f32[48]{0:T(128)} %param.20) | copy-start | bytes 580
  10.2 15.1 %copy-start.56 = (s32[1,3]{1,0:T(1,128)S(1)}, s32[1,3]{1,0:T(1,128)}, u32[]{:S(2)}) copy-start(s32[1,3]{1,0:T(1,128)} %param.14) | copy-start | bytes 40
  10.2 18.8 %copy-start.62 = (f32[48]{0:T(128)S(1)}, f32[48]{0:T(128)}, u32[]{:S(2)}) copy-start(f32[48]{0:T(128)} %param.21) | copy-start | bytes 580
  12.0 26.5 %collective-permute-start = (bf16[16,1536]{1,0:T(8,128)(2,1)S(1)}, bf16[16,1536]{1,0:T(8,128)(2,1)S(1)}, u32[]{:S(2)}, u32[]{:S(2)}) collective-permute-start(bf16[16,1536]{1,0:T(8,128)(2,1)S(1)} %slice.136), channel_id=1, source_target_pairs={{0,1},{1,2},{2,3},{3,4},{4,5},{5,6},{6,7},{8,9},{9,10},{10,11},{11... | collective-permute-start | bytes 147464 | tf_op jit(solution)/shard_map/ppermute | solution.py:523
  19.3 15.4 %all-to-all-start = ((bf16[32,2,332]{2,1,0:T(2,128)(2,1)}), bf16[32,2,332]{2,1,0:T(2,128)(2,1)S(1)}, u32[]{:S(2)}, u32[]{:S(2)}) async-start(bf16[32,2,332]{2,1,0:T(2,128)(2,1)} %reshape.384), calls=%async_computation | async-start | bytes 98304 | tf_op jit(solution)/shard_map/all_to_all | solution.py:755
  134.2 17.2 %collective-permute-start.1 = (f32[8,1536]{1,0:T(8,128)S(1)}, f32[8,1536]{1,0:T(8,128)S(1)}, u32[]{:S(2)}, u32[]{:S(2)}) collective-permute-start(f32[8,1536]{1,0:T(8,128)S(1)} %dynamic-slice_bitcast_fusion.6), channel_id=1, source_target_pairs={{0,1},{1,0},{2,3},{3,2},{4,5},{5,4},{6,7},{7,6},{8,9},{9,8},{10,11... | collective-permute-start | bytes 147464 | tf_op jit(solution)/shard_map/ppermute | solution.py:517
  136.8 26.4 %collective-permute-start.2 = (f32[128,1536]{1,0:T(8,128)S(1)}, f32[128,1536]{1,0:T(8,128)S(1)}, u32[]{:S(2)}, u32[]{:S(2)}) collective-permute-start(f32[128,1536]{1,0:T(8,128)S(1)} %dynamic-slice_bitcast_fusion.5.refs_6_), channel_id=1, source_target_pairs={{0,1},{1,0},{2,3},{3,2},{4,5},{5,4},{6,7},{7,6},{8,9},{9,8},{10,11... | collective-permute-start | bytes 2359304 | tf_op jit(solution)/shard_map/ppermute | solution.py:517
  152.2 11.9 %copy-start.15 = (f32[2,128,1536]{2,1,0:T(8,128)S(1)}, f32[2,128,1536]{2,1,0:T(8,128)}, u32[]{:S(2)}) copy-start(f32[2,128,1536]{2,1,0:T(8,128)} %get-tuple-element.77) | copy-start | bytes 4718596
  166.3 36.4 %collective-permute-start.3 = (f32[128,1536]{1,0:T(8,128)}, f32[128,1536]{1,0:T(8,128)S(1)}, u32[]{:S(2)}, u32[]{:S(2)}) collective-permute-start(f32[128,1536]{1,0:T(8,128)} %fusion.8.refs_6_), channel_id=1, source_target_pairs={{0,2},{1,3},{8,10},{9,11},{16,18},{17,19},{24,26},{25,27}} | collective-permute-start | bytes 2359304 | tf_op jit(solution)/shard_map/ppermute | solution.py:565
  205.8 0.7 collective-permute-start.4
  209.8 6.8 copy-start.21
  209.8 5.9 collective-permute-start.5
  218.9 44.2 %collective-permute-start.6 = (f32[128,1536]{1,0:T(8,128)}, f32[128,1536]{1,0:T(8,128)S(1)}, u32[]{:S(2)}, u32[]{:S(2)}) collective-permute-start(f32[128,1536]{1,0:T(8,128)} %get-tuple-element.146.refs_2_), channel_id=1, source_target_pairs={{0,1},{1,0},{2,3},{3,2},{4,5},{5,4},{6,7},{7,6},{8,9},{9,8},{10,11... | collective-permute-start | bytes 2359304 | tf_op jit(solution)/shard_map/ppermute | solution.py:517
  244.3 12.8 %copy-start.66 = (bf16[528,1536]{1,0:T(8,128)(2,1)S(1)}, bf16[528,1536]{1,0:T(8,128)(2,1)}, u32[]{:S(2)}) copy-start(bf16[528,1536]{1,0:T(8,128)(2,1)} %get-tuple-element.68) | copy-start | bytes 4866052
  299.3 34.1 %collective-permute-start.12 = (bf16[512,3072]{1,0:T(8,128)(2,1)}, bf16[512,3072]{1,0:T(8,128)(2,1)}, u32[]{:S(2)}, u32[]{:S(2)}) collective-permute-start(bf16[512,3072]{1,0:T(8,128)(2,1)} %get-tuple-element.90.refs_5_.refs_0_), channel_id=1, source_target_pairs={{0,8},{8,0},{1,9},{9,1},{2,10},{10,2},{3,11},{11,3},{4,12},{12,4},... | collective-permute-start | bytes 9437192 | tf_op jit(solution)/shard_map/ppermute | solution.py:517
  299.4 10.4 %collective-permute-start.10 = (bf16[512,1536]{1,0:T(8,128)(2,1)}, bf16[512,1536]{1,0:T(8,128)(2,1)}, u32[]{:S(2)}, u32[]{:S(2)}) collective-permute-start(bf16[512,1536]{1,0:T(8,128)(2,1)} %refs_2_.2), channel_id=1, source_target_pairs={{0,8},{8,0},{1,9},{9,1},{2,10},{10,2},{3,11},{11,3},{4,12},{12,4},... | collective-permute-start | bytes 4718600 | tf_op jit(solution)/shard_map/ppermute | solution.py:517
  302.5 7.3 %collective-permute-start.9 = (bf16[1536,512]{1,0:T(8,128)(2,1)}, bf16[1536,512]{1,0:T(8,128)(2,1)S(1)}, u32[]{:S(2)}, u32[]{:S(2)}) collective-permute-start(bf16[1536,512]{1,0:T(8,128)(2,1)} %bitcast.30), channel_id=1, source_target_pairs={{0,8},{8,0},{1,9},{9,1},{2,10},{10,2},{3,11},{11,3},{4,12},{12,4},... | collective-permute-start | bytes 4718600 | tf_op jit(solution)/shard_map/ppermute | solution.py:517
  303.9 6.0 copy-start.22
  303.9 22.0 %collective-permute-start.8 = (f32[128,1536]{1,0:T(8,128)S(1)}, f32[128,1536]{1,0:T(8,128)}, u32[]{:S(2)}, u32[]{:S(2)}) collective-permute-start(f32[128,1536]{1,0:T(8,128)S(1)} %dynamic-slice_bitcast_fusion.4.refs_7_), channel_id=1, source_target_pairs={{0,1},{1,0},{2,3},{3,2},{4,5},{5,4},{6,7},{7,6},{8,9},{9,8},{10,11... | collective-permute-start | bytes 2359304 | tf_op jit(solution)/shard_map/ppermute | solution.py:517
  306.2 27.2 %collective-permute-start.7 = (bf16[768,512]{1,0:T(8,128)(2,1)}, bf16[768,512]{1,0:T(8,128)(2,1)S(1)}, u32[]{:S(2)}, u32[]{:S(2)}) collective-permute-start(bf16[768,512]{1,0:T(8,128)(2,1)} %bitcast.26), channel_id=1, source_target_pairs={{0,8},{8,0},{1,9},{9,1},{2,10},{10,2},{3,11},{11,3},{4,12},{12,4},... | collective-permute-start | bytes 2359304 | tf_op jit(solution)/shard_map/ppermute | solution.py:517
  328.6 20.9 %collective-permute-start.11 = (f32[128,1536]{1,0:T(8,128)S(1)}, f32[128,1536]{1,0:T(8,128)S(1)}, u32[]{:S(2)}, u32[]{:S(2)}) collective-permute-start(f32[128,1536]{1,0:T(8,128)S(1)} %fusion.7.refs_7_), channel_id=1, source_target_pairs={{6,4},{7,5},{14,12},{15,13},{22,20},{23,21},{30,28},{31,29}} | collective-permute-start | bytes 2359304 | tf_op jit(solution)/shard_map/ppermute | solution.py:565
  330.0 36.6 %collective-permute-start.18 = (bf16[768,768]{1,0:T(8,128)(2,1)}, bf16[768,768]{1,0:T(8,128)(2,1)}, u32[]{:S(2)}, u32[]{:S(2)}) collective-permute-start(bf16[768,768]{1,0:T(8,128)(2,1)} %get-tuple-element.89.refs_4_), channel_id=1, source_target_pairs={{0,1},{1,0},{2,3},{3,2},{4,5},{5,4},{6,7},{7,6},{8,9},{9,8},{10,11... | collective-permute-start | bytes 3538952 | tf_op jit(solution)/shard_map/ppermute | solution.py:587
  332.1 38.5 %collective-permute-start.16 = (bf16[768,768]{1,0:T(8,128)(2,1)}, bf16[768,768]{1,0:T(8,128)(2,1)}, u32[]{:S(2)}, u32[]{:S(2)}) collective-permute-start(bf16[768,768]{1,0:T(8,128)(2,1)} %get-tuple-element.88.refs_3_), channel_id=1, source_target_pairs={{0,16},{16,0},{1,17},{17,1},{2,18},{18,2},{3,19},{19,3},{4,20},{20... | collective-permute-start | bytes 3538952 | tf_op jit(solution)/shard_map/ppermute | solution.py:587
  352.5 14.1 %copy-start.6 = (f32[768,768]{1,0:T(8,128)S(1)}, f32[768,768]{1,0:T(8,128)}, u32[]{:S(2)}) copy-start(f32[768,768]{1,0:T(8,128)} %shard_map.227) | copy-start | bytes 7077892
  352.5 42.8 %collective-permute-start.13 = (f32[128,1536]{1,0:T(8,128)}, f32[128,1536]{1,0:T(8,128)}, u32[]{:S(2)}, u32[]{:S(2)}) collective-permute-start(f32[128,1536]{1,0:T(8,128)} %multiply_add_fusion.3.refs_10_.refs_1_), channel_id=1, source_target_pairs={{4,2},{5,3},{12,10},{13,11},{20,18},{21,19},{28,26},{29,27}} | collective-permute-start | bytes 2359304 | tf_op jit(solution)/shard_map/ppermute | solution.py:565
  364.5 113.3 %collective-permute-start.20 = (bf16[384,1536]{1,0:T(8,128)(2,1)}, bf16[384,1536]{1,0:T(8,128)(2,1)}, u32[]{:S(2)}, u32[]{:S(2)}) collective-permute-start(bf16[384,1536]{1,0:T(8,128)(2,1)} %get-tuple-element.93.refs_3_), channel_id=1, source_target_pairs={{0,16},{16,0},{1,17},{17,1},{2,18},{18,2},{3,19},{19,3},{4,20},{20... | collective-permute-start | bytes 3538952 | tf_op jit(solution)/shard_map/ppermute | solution.py:587
  365.3 108.5 %collective-permute-start.21 = (bf16[384,1536]{1,0:T(8,128)(2,1)}, bf16[384,1536]{1,0:T(8,128)(2,1)}, u32[]{:S(2)}, u32[]{:S(2)}) collective-permute-start(bf16[384,1536]{1,0:T(8,128)(2,1)} %get-tuple-element.94.refs_4_), channel_id=1, source_target_pairs={{0,1},{1,0},{2,3},{3,2},{4,5},{5,4},{6,7},{7,6},{8,9},{9,8},{10,11... | collective-permute-start | bytes 3538952 | tf_op jit(solution)/shard_map/ppermute | solution.py:587
  369.1 79.2 %collective-permute-start.19 = (bf16[4,96,768]{2,1,0:T(8,128)(2,1)}, bf16[4,96,768]{2,1,0:T(8,128)(2,1)}, u32[]{:S(2)}, u32[]{:S(2)}) collective-permute-start(bf16[4,96,768]{2,1,0:T(8,128)(2,1)} %fusion.11), channel_id=1, source_target_pairs={{0,16},{16,0},{1,17},{17,1},{2,18},{18,2},{3,19},{19,3},{4,20},{20... | collective-permute-start | bytes 1769480 | tf_op jit(solution)/shard_map/ppermute | solution.py:587
  373.1 77.7 %collective-permute-start.17 = (bf16[4,96,768]{2,1,0:T(8,128)(2,1)}, bf16[4,96,768]{2,1,0:T(8,128)(2,1)}, u32[]{:S(2)}, u32[]{:S(2)}) collective-permute-start(bf16[4,96,768]{2,1,0:T(8,128)(2,1)} %fusion.13), channel_id=1, source_target_pairs={{0,1},{1,0},{2,3},{3,2},{4,5},{5,4},{6,7},{7,6},{8,9},{9,8},{10,11... | collective-permute-start | bytes 1769480 | tf_op jit(solution)/shard_map/ppermute | solution.py:587
  397.6 44.0 %collective-permute-start.14 = (f32[128,1536]{1,0:T(8,128)S(1)}, f32[128,1536]{1,0:T(8,128)S(1)}, u32[]{:S(2)}, u32[]{:S(2)}) collective-permute-start(f32[128,1536]{1,0:T(8,128)S(1)} %get-tuple-element.139.refs_10_), channel_id=1, source_target_pairs={{2,0},{3,1},{10,8},{11,9},{18,16},{19,17},{26,24},{27,25}} | collective-permute-start | bytes 2359304 | tf_op jit(solution)/shard_map/ppermute | solution.py:565
  448.0 36.5 %collective-permute-start.15 = (f32[128,1536]{1,0:T(8,128)S(1)}, f32[128,1536]{1,0:T(8,128)}, u32[]{:S(2)}, u32[]{:S(2)}) collective-permute-start(f32[128,1536]{1,0:T(8,128)S(1)} %copy-done.9), channel_id=1, source_target_pairs={{0,1},{1,0},{2,3},{3,2},{4,5},{5,4},{6,7},{7,6},{8,9},{9,8},{10,11... | collective-permute-start | bytes 2359304 | tf_op jit(solution)/shard_map/ppermute | solution.py:517
  453.8 73.2 %all-to-all-start.1 = ((f32[4,96,1536]{2,1,0:T(8,128)}), f32[4,96,1536]{2,1,0:T(8,128)S(1)}, u32[]{:S(2)}, u32[]{:S(2)}) async-start(f32[4,96,1536]{2,1,0:T(8,128)} %pad_maximum_fusion.refs_1_), calls=%async_computation.1 | async-start | bytes 4718592 | tf_op jit(solution)/shard_map/all_to_all | solution.py:725
  477.1 32.9 %collective-permute-start.26 = (bf16[4,48,1536]{2,1,0:T(8,128)(2,1)}, bf16[4,48,1536]{2,1,0:T(8,128)(2,1)}, u32[]{:S(2)}, u32[]{:S(2)}) collective-permute-start(bf16[4,48,1536]{2,1,0:T(8,128)(2,1)} %fusion.12.refs_3_), channel_id=1, source_target_pairs={{0,16},{16,0},{1,17},{17,1},{2,18},{18,2},{3,19},{19,3},{4,20},{20... | collective-permute-start | bytes 1769480 | tf_op jit(solution)/shard_map/ppermute | solution.py:587
  480.3 31.4 %collective-permute-start.25 = (bf16[4,48,1536]{2,1,0:T(8,128)(2,1)}, bf16[4,48,1536]{2,1,0:T(8,128)(2,1)}, u32[]{:S(2)}, u32[]{:S(2)}) collective-permute-start(bf16[4,48,1536]{2,1,0:T(8,128)(2,1)} %fusion.14.refs_2_), channel_id=1, source_target_pairs={{0,1},{1,0},{2,3},{3,2},{4,5},{5,4},{6,7},{7,6},{8,9},{9,8},{10,11... | collective-permute-start | bytes 1769480 | tf_op jit(solution)/shard_map/ppermute | solution.py:587
  508.6 6.8 collective-permute-start.23
  509.9 24.9 %collective-permute-start.22 = (bf16[512,1536]{1,0:T(8,128)(2,1)}, bf16[512,1536]{1,0:T(8,128)(2,1)}, u32[]{:S(2)}, u32[]{:S(2)}) collective-permute-start(bf16[512,1536]{1,0:T(8,128)(2,1)} %get-tuple-element.107.refs_5_), channel_id=1, source_target_pairs={{0,8},{8,0},{1,9},{9,1},{2,10},{10,2},{3,11},{11,3},{4,12},{12,4},... | collective-permute-start | bytes 4718600 | tf_op jit(solution)/shard_map/ppermute | solution.py:517
  517.0 17.9 %collective-permute-start.24 = (bf16[16,1536]{1,0:T(8,128)(2,1)}, bf16[16,1536]{1,0:T(8,128)(2,1)}, u32[]{:S(2)}, u32[]{:S(2)}) collective-permute-start(bf16[16,1536]{1,0:T(8,128)(2,1)} %get-tuple-element.136.refs_7_), channel_id=1, source_target_pairs={{0,8},{8,0},{1,9},{9,1},{2,10},{10,2},{3,11},{11,3},{4,12},{12,4},... | collective-permute-start | bytes 147464 | tf_op jit(solution)/shard_map/ppermute | solution.py:517
  528.4 102.5 %all-to-all-start.3 = ((f32[4,48,3072]{2,1,0:T(8,128)}), f32[4,48,3072]{2,1,0:T(8,128)}, u32[]{:S(2)}, u32[]{:S(2)}) async-start(f32[4,48,3072]{2,1,0:T(8,128)} %pad_maximum_fusion.1.refs_9_), calls=%async_computation.3 | async-start | bytes 4718592 | tf_op jit(solution)/shard_map/all_to_all | solution.py:725
  564.5 19.1 %collective-permute-start.32 = (bf16[384,768]{1,0:T(8,128)(2,1)}, bf16[384,768]{1,0:T(8,128)(2,1)}, u32[]{:S(2)}, u32[]{:S(2)}) collective-permute-start(bf16[384,768]{1,0:T(8,128)(2,1)} %get-tuple-element.112.refs_27_), channel_id=1, source_target_pairs={{0,1},{1,0},{2,3},{3,2},{4,5},{5,4},{6,7},{7,6},{8,9},{9,8},{10,11... | collective-permute-start | bytes 1769480 | tf_op jit(solution)/shard_map/ppermute | solution.py:587
  567.0 19.5 %collective-permute-start.30 = (bf16[384,768]{1,0:T(8,128)(2,1)}, bf16[384,768]{1,0:T(8,128)(2,1)}, u32[]{:S(2)}, u32[]{:S(2)}) collective-permute-start(bf16[384,768]{1,0:T(8,128)(2,1)} %get-tuple-element.111.refs_26_), channel_id=1, source_target_pairs={{0,16},{16,0},{1,17},{17,1},{2,18},{18,2},{3,19},{19,3},{4,20},{20... | collective-permute-start | bytes 1769480 | tf_op jit(solution)/shard_map/ppermute | solution.py:587
  570.1 34.9 %collective-permute-start.27 = (bf16[512,1920]{1,0:T(8,128)(2,1)S(1)}, bf16[512,1920]{1,0:T(8,128)(2,1)}, u32[]{:S(2)}, u32[]{:S(2)}) collective-permute-start(bf16[512,1920]{1,0:T(8,128)(2,1)S(1)} %copy-done.10), channel_id=1, source_target_pairs={{0,8},{8,0},{1,9},{9,1},{2,10},{10,2},{3,11},{11,3},{4,12},{12,4},... | collective-permute-start | bytes 5898248 | tf_op jit(solution)/shard_map/ppermute | solution.py:517
  570.1 12.2 %copy-start.52 = (f32[8,1536]{1,0:T(8,128)S(1)}, f32[8,1536]{1,0:T(8,128)}, u32[]{:S(2)}) copy-start(f32[8,1536]{1,0:T(8,128)} %get-tuple-element.121) | copy-start | bytes 147460
  570.1 12.8 %collective-permute-start.28 = (f32[16,1920]{1,0:T(8,128)S(1)}, f32[16,1920]{1,0:T(8,128)S(1)}, u32[]{:S(2)}, u32[]{:S(2)}) collective-permute-start(f32[16,1920]{1,0:T(8,128)S(1)} %slice.164), channel_id=1, source_target_pairs={{1,0},{2,1},{3,2},{4,3},{5,4},{6,5},{7,6},{9,8},{10,9},{11,10},{12... | collective-permute-start | bytes 368648 | tf_op jit(solution)/shard_map/ppermute | solution.py:523
  585.5 11.5 %copy-start.38 = (f32[32,1920]{1,0:T(8,128)S(1)}, f32[32,1920]{1,0:T(8,128)}, u32[]{:S(2)}) copy-start(f32[32,1920]{1,0:T(8,128)} %get-tuple-element.114.refs_2_.refs_1_) | copy-start | bytes 737284
  585.5 11.5 %copy-start.48 = (f32[16,1920]{1,0:T(8,128)S(1)}, f32[16,1920]{1,0:T(8,128)}, u32[]{:S(2)}) copy-start(f32[16,1920]{1,0:T(8,128)} %shard_map.239) | copy-start | bytes 368644
  585.5 12.1 %collective-permute-start.33 = (bf16[4,48,768]{2,1,0:T(8,128)(2,1)S(1)}, bf16[4,48,768]{2,1,0:T(8,128)(2,1)S(1)}, u32[]{:S(2)}, u32[]{:S(2)}) collective-permute-start(bf16[4,48,768]{2,1,0:T(8,128)(2,1)S(1)} %fusion.19), channel_id=1, source_target_pairs={{0,16},{16,0},{1,17},{17,1},{2,18},{18,2},{3,19},{19,3},{4,20},{20... | collective-permute-start | bytes 884744 | tf_op jit(solution)/shard_map/ppermute | solution.py:587
  587.7 16.1 %collective-permute-start.31 = (bf16[4,48,768]{2,1,0:T(8,128)(2,1)S(1)}, bf16[4,48,768]{2,1,0:T(8,128)(2,1)S(1)}, u32[]{:S(2)}, u32[]{:S(2)}) collective-permute-start(bf16[4,48,768]{2,1,0:T(8,128)(2,1)S(1)} %fusion.20), channel_id=1, source_target_pairs={{0,1},{1,0},{2,3},{3,2},{4,5},{5,4},{6,7},{7,6},{8,9},{9,8},{10,11... | collective-permute-start | bytes 884744 | tf_op jit(solution)/shard_map/ppermute | solution.py:587
  597.6 7.4 %copy-start.46 = (bf16[16,1920]{1,0:T(8,128)(2,1)}, bf16[16,1920]{1,0:T(8,128)(2,1)S(1)}, u32[]{:S(2)}) copy-start(bf16[16,1920]{1,0:T(8,128)(2,1)S(1)} %get-tuple-element.134.refs_7_) | copy-start | bytes 184324
  597.6 7.4 %collective-permute-start.29 = (bf16[16,1920]{1,0:T(8,128)(2,1)S(1)}, bf16[16,1920]{1,0:T(8,128)(2,1)S(1)}, u32[]{:S(2)}, u32[]{:S(2)}) collective-permute-start(bf16[16,1920]{1,0:T(8,128)(2,1)S(1)} %get-tuple-element.134.refs_7_), channel_id=1, source_target_pairs={{0,8},{8,0},{1,9},{9,1},{2,10},{10,2},{3,11},{11,3},{4,12},{12,4},... | collective-permute-start | bytes 184328 | tf_op jit(solution)/shard_map/ppermute | solution.py:517
  611.1 29.2 %collective-permute-start.35 = (bf16[384,896]{1,0:T(8,128)(2,1)}, bf16[384,896]{1,0:T(8,128)(2,1)}, u32[]{:S(2)}, u32[]{:S(2)}) collective-permute-start(bf16[384,896]{1,0:T(8,128)(2,1)} %get-tuple-element.118.refs_7_), channel_id=1, source_target_pairs={{0,1},{1,0},{2,3},{3,2},{4,5},{5,4},{6,7},{7,6},{8,9},{9,8},{10,11... | collective-permute-start | bytes 2064392 | tf_op jit(solution)/shard_map/ppermute | solution.py:587
  618.2 26.1 %collective-permute-start.34 = (bf16[384,1024]{1,0:T(8,128)(2,1)}, bf16[384,1024]{1,0:T(8,128)(2,1)S(1)}, u32[]{:S(2)}, u32[]{:S(2)}) collective-permute-start(bf16[384,1024]{1,0:T(8,128)(2,1)} %get-tuple-element.117.refs_6_), channel_id=1, source_target_pairs={{0,16},{16,0},{1,17},{17,1},{2,18},{18,2},{3,19},{19,3},{4,20},{20... | collective-permute-start | bytes 2359304 | tf_op jit(solution)/shard_map/ppermute | solution.py:587
  630.9 30.9 %all-to-all-start.4 = ((f32[4,48,1536]{2,1,0:T(8,128)}), f32[4,48,1536]{2,1,0:T(8,128)S(1)}, u32[]{:S(2)}, u32[]{:S(2)}) async-start(f32[4,48,1536]{2,1,0:T(8,128)} %pad_maximum_fusion.4.refs_9_), calls=%async_computation.4 | async-start | bytes 2359296 | tf_op jit(solution)/shard_map/all_to_all | solution.py:725
  642.9 8.3 %collective-permute-start.37 = (bf16[4,48,896]{2,1,0:T(8,128)(2,1)S(1)}, bf16[4,48,896]{2,1,0:T(8,128)(2,1)}, u32[]{:S(2)}, u32[]{:S(2)}) collective-permute-start(bf16[4,48,896]{2,1,0:T(8,128)(2,1)S(1)} %fusion.18.refs_4_.refs_2_), channel_id=1, source_target_pairs={{0,16},{16,0},{1,17},{17,1},{2,18},{18,2},{3,19},{19,3},{4,20},{20... | collective-permute-start | bytes 1032200 | tf_op jit(solution)/shard_map/ppermute | solution.py:587
  645.9 9.0 %collective-permute-start.36 = (bf16[4,48,1024]{2,1,0:T(8,128)(2,1)S(1)}, bf16[4,48,1024]{2,1,0:T(8,128)(2,1)S(1)}, u32[]{:S(2)}, u32[]{:S(2)}) collective-permute-start(bf16[4,48,1024]{2,1,0:T(8,128)(2,1)S(1)} %fusion.15.refs_3_.refs_1_), channel_id=1, source_target_pairs={{0,1},{1,0},{2,3},{3,2},{4,5},{5,4},{6,7},{7,6},{8,9},{9,8},{10,11... | collective-permute-start | bytes 1179656 | tf_op jit(solution)/shard_map/ppermute | solution.py:587
  661.8 10.3 %copy-start.14 = (f32[4,48,1536]{2,1,0:T(8,128)}, f32[4,48,1536]{2,1,0:T(8,128)S(1)}, u32[]{:S(2)}) copy-start(f32[4,48,1536]{2,1,0:T(8,128)S(1)} %all-to-all-done.4.refs_0_) | copy-start | bytes 3538948
  661.8 10.3 %all-to-all-start.2 = ((f32[32,1,808]{2,1,0:T(1,128)}), f32[32,1,808]{2,1,0:T(1,128)S(1)}, u32[]{:S(2)}, u32[]{:S(2)}) async-start(f32[32,1,808]{2,1,0:T(1,128)} %copy.82), calls=%async_computation.2 | async-start | bytes 229376 | tf_op jit(solution)/shard_map/all_to_all | solution.py:1167
  672.1 27.0 %all-to-all-start.5 = ((bf16[4,48,1920]{2,1,0:T(8,128)(2,1)}), bf16[4,48,1920]{2,1,0:T(8,128)(2,1)S(1)}, u32[]{:S(2)}, u32[]{:S(2)}) async-start(bf16[4,48,1920]{2,1,0:T(8,128)(2,1)} %fusion.4), calls=%async_computation.5 | async-start | bytes 1474560 | tf_op jit(solution)/shard_map/all_to_all | solution.py:725
  (49 other events, 94.9 us)
Sparse Core Ops, SparseCore 0:
  11.5 90.8 all-gather.2
  105.9 131.8 all-gather.4

commit v5 on v4

--- a/solution.py
+++ b/solution.py
@@ -688,6 +688,58 @@
     return [across(tied(piece, others), axis, by + 1) for by, piece in enumerate(sent)]
 
 
+def places_here():
+    return jnp.stack([lax.axis_index(a) for a in ("core", "x", "y")])
+
+
+def second_body(place_ref, *refs):
+    for side in range(2):
+        kept_own, got_own, kept_next, got_next = refs[4 * side : 4 * side + 4]
+        own_ref, next_ref = refs[8 + 2 * side : 10 + 2 * side]
+        own_ref[...] = (kept_own[...] + got_own[...].astype(F32)).reshape(own_ref.shape)
+        next_ref[...] = (kept_next[...] + got_next[...].astype(F32)).reshape(next_ref.shape).astype(BF)
+
+
+def second_stage(kept_x, got_x, kept_y, got_y, depth, waits):
+    rows = kept_x.shape[0] // (2 * depth)
+    ins, outs = [], []
+    for kept, got, by_y in ((kept_x, got_x, True), (kept_y, got_y, False)):
+        width = kept.shape[1]
+        shape = (depth, 2, rows, width) if by_y else (2, depth, rows, width)
+
+        def spec(flip, by_y=by_y, width=width):
+            if by_y:
+                return pl.BlockSpec((1, 1, rows, width), lambda g, p: (g, p[2] ^ flip, 0, 0))
+            return pl.BlockSpec((1, 1, rows, width), lambda g, p: (p[1] ^ flip, g, 0, 0))
+
+        for flip in (0, 1):
+            ins += [(kept.reshape(shape), spec(flip)), (got.reshape(shape), spec(flip))]
+        result = pl.BlockSpec((1, rows, width), lambda g, p: (g, 0, 0))
+        outs += [(out((depth, rows, width)), result), (out((depth, rows, width), BF), result)]
+    return call(second_body, depth, 3, ins, outs, waits=waits, places=places_here())
+
+
+def third_body(own_x, came_x, own_y, came_y, o_ref):
+    width = own_x.shape[2]
+    o_ref[:, :, :width] = (own_x[...] + came_x[...].astype(F32)).astype(o_ref.dtype)
+    o_ref[:, :, width:] = (own_y[...] + came_y[...].astype(F32)).astype(o_ref.dtype)
+
+
+def third_stage(own_x, came_x, own_y, came_y, kind, waits):
+    depth, rows, wide_x = own_x.shape
+    wide_y = own_y.shape[2]
+
+    def spec(width):
+        return pl.BlockSpec((1, rows, width), lambda g: (g, 0, 0))
+
+    return call(
+        third_body, depth, 2,
+        [(own_x, spec(wide_x)), (came_x, spec(wide_x)), (own_y, spec(wide_y)), (came_y, spec(wide_y))],
+        [(out((depth, rows, wide_x + wide_y), kind), spec(wide_x + wide_y))],
+        waits=waits,
+    )[0]
+
+
 class Reduction:
     def __init__(self, left, right, start, middle, end, waits=()):
         if lax.axis_size("x") == 2 and lax.axis_size("y") == 2:
@@ -707,6 +759,15 @@
 
     def second(self, *others):
         sizes = [lax.axis_size(a) for a in ("x", "z", "y")]
+        self.pairs = sizes[0] == 2 and sizes[2] == 2
+        if self.pairs:
+            self.own_x, next_x, self.own_y, next_y = second_stage(
+                self.kept_x, self.got_x[0], self.kept_y, self.got_y[0], sizes[1], others
+            )
+            self.next_x, self.next_y = [next_x], [next_y]
+            self.came_x = travel(self.next_x, "y", ())
+            self.came_y = travel(self.next_y, "x", ())
+            return
         part_x = total_of(tied(self.kept_x, others), self.got_x)
         part_y = total_of(tied(self.kept_y, others), self.got_y)
         view_x = part_x.reshape(sizes[1], sizes[2], -1, part_x.shape[1])
@@ -717,12 +778,22 @@
         self.came_y = travel(self.next_y, "x", ())
 
     def third(self, *others, kind=F32):
-        done_x = total_of(tied(self.own_x, others), self.came_x)
-        done_y = total_of(tied(self.own_y, others), self.came_y)
-        self.parts = jnp.concatenate([done_x, done_y], axis=2)
         place = lax.axis_index("z")
-        self.mine = pick(self.parts, place) if kind == BF else None
-        self.got_z = lax.all_to_all(self.parts.astype(kind), "z", 0, 0, tiled=True)
+        if self.pairs:
+            self.parts = third_stage(
+                self.own_x, self.came_x[0], self.own_y, self.came_y[0], kind, others
+            )
+        else:
+            done_x = total_of(tied(self.own_x, others), self.came_x)
+            done_y = total_of(tied(self.own_y, others), self.came_y)
+            self.parts = jnp.concatenate([done_x, done_y], axis=2).astype(kind)
+        self.mine = None
+        if kind == BF:
+            sides = ((self.own_x, self.came_x), (self.own_y, self.came_y))
+            self.mine = jnp.concatenate(
+                [total_of(pick(own, place), [pick(c, place) for c in came]) for own, came in sides], axis=1
+            )
+        self.got_z = lax.all_to_all(self.parts, "z", 0, 0, tiled=True)
 
     def last(self, *others):
         got = tied(self.got_z, others)

time: 720 us -> 715 us (level)
  Pallas kernels: 259 us -> 297 us
  other arithmetic: 67.5 us -> 43.8 us
  waiting for transfers between devices: 166 us -> 153 us
  local copies, waits for them, and re-layouts: 74.3 us -> 67 us
    pallas_call x23 -> x31, Pallas kernels: 259 us -> 297 us  [call(): pl.pallas_call(run, grid_spec=pltpu.PrefetchScalarGridSpec(num_scalar_pre...]
    add x16 -> x2, other arithmetic: 19.3 us -> 2.01 us  [total_of(): kept = kept + piece.astype(F32)]
    all_to_all x4, waiting for transfers between devices: 13 us -> 0.01 us  [third(): self.got_z = lax.all_to_all(self.parts, 'z', 0, 0, tiled=True)]
    all_to_all x4, starting transfers between devices: 33.7 us -> 42.6 us  [third(): self.got_z = lax.all_to_all(self.parts, 'z', 0, 0, tiled=True)]
    ppermute x16, starting transfers between devices: 27.5 us -> 19.6 us  [across(): lax.ppermute(array, axis, [(i, i ^ by) for i in range(lax.axis_size(axis))])]
    unnamed x141 -> x123, local copies, waits for them, and re-layouts: 29.6 us -> 28.9 us
  transfers between devices with their start and end apart: 46 -> 46, of which waited for: 13 -> 10; matrix products, arithmetic and copies ran while one was open for 19% -> 15% of each run, Pallas kernels for 32% -> 38%
where the time goes in v5:
time: 715 us; the launch traced here: 703 us
  Pallas kernels  297 us (42%)
  waiting for transfers between devices  153 us (21%)
  starting transfers between devices  101 us (14%)
  local copies, waits for them, and re-layouts  67 us (9%)
  other arithmetic  43.8 us (6%)
  matrix products  24.3 us (3%)
  between operations  17.4 us (2%)
    pallas_call x31, Pallas kernels, call(): pl.pallas_call(run, grid_spec=pltpu.PrefetchScalarGridSpec(num_scalar_pre...  297 us
    all_gather x1, waiting for transfers between devices, shards(): lax.all_gather(columns(in_weight[:, INNER:], PROJ_X), EVERY, axis=0, tile...  59.2 us
    all_to_all x4, starting transfers between devices, third(): self.got_z = lax.all_to_all(self.parts, 'z', 0, 0, tiled=True)  42.6 us
    ppermute x6, waiting for transfers between devices, entering(): arrived = meanwhile(sent, lax.ppermute(sent, 'z', pairs))  42.5 us
    unnamed x123, local copies, waits for them, and re-layouts  28.9 us
    dot_general x3, matrix products, mm(): return jnp.dot(left, right, preferred_element_type=F32)  24.3 us
    ppermute x16, starting transfers between devices, across(): lax.ppermute(array, axis, [(i, i ^ by) for i in range(lax.axis_size(axis))])  19.6 us
    all_gather x1, waiting for transfers between devices, shards(): stacked = lax.all_gather(stacked, EVERY, axis=1, tiled=True)  18.9 us
  transfers between devices with their start and end apart: 46, of which 10 were waited for; matrix products, arithmetic and copies ran while one was open for 15% of the time, Pallas kernels for 38%

profile of v5, /device:TPU:0, one launch (start us, length us, event | category | flops | bytes accessed | tf_op | source)
XLA Modules:
  0.0 703.1 jit_solution(11084924271159882610)
XLA Ops:
  12.0 4.9 collective-permute-start
  19.3 4.9 all-to-all-start
  39.1 3.9 shard_map.203
  43.0 59.2 %all-gather.3.cloned.1.call-done.refs_2_ = bf16[1536,3456]{1,0:T(8,128)(2,1)} async-done(((bf16[48,3456]{1,0:T(8,128)(2,1)}), bf16[1536,3456]{1,0:T(8,128)(2,1)}) %all-gather.3.cloned.1.call-update) | async-done | bytes 10616848 | tf_op jit(solution)/shard_map/all_gather | solution.py:851
  102.2 11.7 %convolution_convert_fusion.refs_0_.refs_1_.refs_4_.refs_17_ = bf16[528,3456]{1,0:T(8,128)(2,1)} fusion(bf16[528,1536]{1,0:T(8,128)(2,1)} %get-tuple-element.84, bf16[1536,3456]{1,0:T(8,128)(2,1)} %all-gather.3.cloned.1.call-done.refs_2_), kind=kOutput, calls=%fused_computation | convolution fusion | flops 5607512064 | bytes 15888384 | tf_op jit(solution)/shard_map/dot_general | solution.py:105
  114.6 4.5 shard_map.204
  120.6 12.5 %shard_map.205 = (f32[512,3072]{1,0:T(8,128)}, f32[512,3072]{1,0:T(8,128)}, f32[2,128,1536]{2,1,0:T(8,128)}, f32[2,8,1536]{2,1,0:T(8,128)}) custom-call(bf16[528,3456]{1,0:T(8,128)(2,1)} %convolution_convert_fusion.refs_0_.refs_1_.refs_4_.refs_17_, f32[8,3072]{1,0:T(8,128)} %slice.174.refs_1_.refs_5_, f32[1,3072]{1,0:T(1,128)} %slice.175.refs_2_, ...), custom_call_target="tpu_custom_call" | custom-call | flops 12000000000 | bytes 36000000 | tf_op jit(solution)/shard_map/pallas_call | solution.py:43
  137.6 13.6 %shard_map.206.refs_1_.refs_0_ = f32[512,1536]{1,0:T(8,128)} custom-call(f32[512,3072]{1,0:T(8,128)} %get-tuple-element.89.refs_0_.refs_5_.refs_1_, f32[512,128]{1,0:T(8,128)} %get-tuple-element.86.refs_5_.refs_1_.refs_2_.refs_11_, f32[1,3072]{1,0:T(1,128)} %broadcast_in_dim_reshape.3.refs_2_.refs_11_.refs_12_, f32[512,512]{1,0:T(8,128)} %get-tuple-element.90.refs_3_, ...), custom_call_target="tpu_custom_call" | custom-call | flops 12000000000 | bytes 36000000 | tf_op jit(solution)/shard_map/pallas_call | solution.py:43
  152.0 11.0 %collective-permute-done.2.refs_0_ = f32[128,1536]{1,0:T(8,128)S(1)} collective-permute-done((f32[128,1536]{1,0:T(8,128)S(1)}, f32[128,1536]{1,0:T(8,128)S(1)}, u32[]{:S(2)}, u32[]{:S(2)}) %collective-permute-start.2) | collective-permute-done | bytes 786464 | tf_op jit(solution)/shard_map/ppermute | solution.py:517
  164.0 2.1 fusion.7.refs_6_
  166.1 3.6 collective-permute-start.3
  169.7 13.7 %shard_map.208.refs_1_ = f32[512,1536]{1,0:T(8,128)} custom-call(f32[512,3072]{1,0:T(8,128)} %get-tuple-element.89.refs_0_.refs_5_.refs_1_, f32[512,128]{1,0:T(8,128)} %get-tuple-element.86.refs_5_.refs_1_.refs_2_.refs_11_, f32[1,3072]{1,0:T(1,128)} %broadcast_in_dim_reshape.3.refs_2_.refs_11_.refs_12_, f32[512,512]{1,0:T(8,128)} %get-tuple-element.90.refs_3_, ...), custom_call_target="tpu_custom_call" | custom-call | flops 12000000000 | bytes 36000000 | tf_op jit(solution)/shard_map/pallas_call | solution.py:43
  183.4 19.1 %collective-permute-done.3.refs_0_ = f32[128,1536]{1,0:T(8,128)S(1)} collective-permute-done((f32[128,1536]{1,0:T(8,128)}, f32[128,1536]{1,0:T(8,128)S(1)}, u32[]{:S(2)}, u32[]{:S(2)}) %collective-permute-start.3) | collective-permute-done | bytes 786464 | tf_op jit(solution)/shard_map/ppermute | solution.py:565
  203.4 2.2 multiply_add_fusion.6
  207.2 2.5 multiply_add_fusion.5
  216.3 2.3 select_bitcast_fusion.1
  218.7 18.9 %all-gather.5.cloned.1.call-done.refs_1_ = bf16[4,1536,1536]{2,1,0:T(8,128)(2,1)} async-done(((bf16[4,48,1536]{2,1,0:T(8,128)(2,1)}), bf16[4,1536,1536]{2,1,0:T(8,128)(2,1)}) %all-gather.5.cloned.1.call-update) | async-done | bytes 18874384 | tf_op jit(solution)/shard_map/all_gather | solution.py:856
  237.5 6.6 fusion.3.refs_3_
  244.1 12.8 %shard_map.212.refs_1_.refs_4_ = f32[512,3072]{1,0:T(8,128)} custom-call(bf16[512,1536]{1,0:T(8,128)(2,1)} %refs_2_.2, bf16[4,1536,1536]{2,1,0:T(8,128)(2,1)} %all-gather.5.cloned.1.call-done.refs_1_, f32[128,1536]{1,0:T(8,128)} %get-tuple-element.178.refs_2_), custom_call_target="tpu_custom_call" | custom-call | flops 7000000000 | bytes 21000000 | tf_op jit(solution)/shard_map/pallas_call | solution.py:43
  256.9 6.0 fusion.2.refs_2_
  263.8 3.5 multiply_add_fusion
  267.3 31.8 %shard_map.214 = (bf16[512,3072]{1,0:T(8,128)(2,1)}, bf16[3072,512]{1,0:T(8,128)(2,1)}, bf16[512,3072]{1,0:T(8,128)(2,1)}, f32[512,3072]{1,0:T(8,128)}, f32[2,12...) custom-call(f32[512,1536]{1,0:T(8,128)} %shard_map.206.refs_1_.refs_0_, ...), custom_call_target="tpu_custom_call" | custom-call | flops 31000000512 | bytes 93000000 | tf_op jit(solution)/shard_map/pallas_call | solution.py:43
  299.6 2.7 constant_dynamic-slice_fusion
  306.0 3.6 collective-permute-done.10.refs_6_
  310.8 7.4 %shard_map.215 = (bf16[768,768]{1,0:T(8,128)(2,1)}, f32[768,768]{1,0:T(8,128)}) custom-call(s32[3]{0:T(128)} %pad_add_fusion.refs_0_, bf16[2,2,768,512]{3,2,1,0:T(8,128)(2,1)} %bitcast.157, bf16[2,2,768,512]{3,2,1,0:T(8,128)(2,1)} %bitcast.158, bf16[2,768,512]{2,1,0:T(8,128)(2,1)} %bitcast.161, bf16[2,768,512]{2,1,0:T(8,128)(2,1)} %bitcast.162, ...), custom_call_target="tpu_custom_call" | custom-call | flops 2949120000 | bytes 8847360 | tf_op jit(solution)/shard_map/pallas_call | solution.py:43
  318.3 7.5 %shard_map.216 = (bf16[768,768]{1,0:T(8,128)(2,1)}, f32[768,768]{1,0:T(8,128)}) custom-call(s32[3]{0:T(128)} %pad_add_fusion.refs_0_, bf16[2,2,4,2,96,512]{5,4,3,2,1,0:T(8,128)(2,1)} %bitcast.159, bf16[2,2,4,2,96,512]{5,4,3,2,1,0:T(8,128)(2,1)} %bitcast.160, bf16[8,2,96,512]{3,2,1,0:T(8,128)(2,1)} %bitcast.163, bf16[8,2,96,512]{3,2,1,0:T(8,128)(2,1)} %bitcast.164, ...), custom_call_target="tpu_custom_call" | custom-call | flops 2949120000 | bytes 8847360 | tf_op jit(solution)/shard_map/pallas_call | solution.py:43
  332.1 7.6 %shard_map.218 = (bf16[384,1536]{1,0:T(8,128)(2,1)}, f32[384,1536]{1,0:T(8,128)}) custom-call(s32[3]{0:T(128)} %pad_add_fusion.refs_0_, bf16[2,2,384,512]{3,2,1,0:T(8,128)(2,1)} %bitcast.131, bf16[2,2,384,512]{3,2,1,0:T(8,128)(2,1)} %bitcast.132, bf16[2,384,512]{2,1,0:T(8,128)(2,1)} %bitcast.144, bf16[2,384,512]{2,1,0:T(8,128)(2,1)} %bitcast.145, ...), custom_call_target="tpu_custom_call" | custom-call | flops 2949120000 | bytes 8847360 | tf_op jit(solution)/shard_map/pallas_call | solution.py:43
  340.4 7.6 %shard_map.219 = (bf16[384,1536]{1,0:T(8,128)(2,1)}, f32[384,1536]{1,0:T(8,128)}) custom-call(s32[3]{0:T(128)} %pad_add_fusion.refs_0_, bf16[2,2,4,2,48,512]{5,4,3,2,1,0:T(8,128)(2,1)} %bitcast.133, bf16[2,2,4,2,48,512]{5,4,3,2,1,0:T(8,128)(2,1)} %bitcast.134, bf16[8,2,48,512]{3,2,1,0:T(8,128)(2,1)} %bitcast.146, bf16[8,2,48,512]{3,2,1,0:T(8,128)(2,1)} %bitcast.147, ...), custom_call_target="tpu_custom_call" | custom-call | flops 2949120000 | bytes 8847360 | tf_op jit(solution)/shard_map/pallas_call | solution.py:43
  351.5 10.0 %collective-permute-start.13 = (f32[128,1536]{1,0:T(8,128)S(1)}, f32[128,1536]{1,0:T(8,128)S(1)}, u32[]{:S(2)}, u32[]{:S(2)}) collective-permute-start(f32[128,1536]{1,0:T(8,128)S(1)} %multiply_add_fusion.3.refs_10_.refs_9_), channel_id=1, source_target_pairs={{4,2},{5,3},{12,10},{13,11},{20,18},{21,19},{28,26},{29,27}} | collective-permute-start | bytes 2359304 | tf_op jit(solution)/shard_map/ppermute | solution.py:565
  361.6 5.9 shard_map.225
  370.7 18.3 %shard_map.221 = (f32[512,1536]{1,0:T(8,128)}, f32[512,512]{1,0:T(8,128)}) custom-call(f32[512,3072]{1,0:T(8,128)} %get-tuple-element.89.refs_0_.refs_5_.refs_1_, f32[512,3072]{1,0:T(8,128)} %get-tuple-element.98.refs_1_.refs_2_, f32[512,128]{1,0:T(8,128)} %get-tuple-element.86.refs_5_.refs_1_.refs_2_.refs_11_, f32[512,512]{1,0:T(8,128)} %get-tuple-element.99.refs_3_, ...), custom_call_target="tpu_custom_call" | custom-call | flops 17999998976 | bytes 54000000 | tf_op jit(solution)/shard_map/pallas_call | solution.py:43
  393.4 19.8 %shard_map.223 = (f32[512,1536]{1,0:T(8,128)}, f32[512,512]{1,0:T(8,128)}, f32[512,256]{1,0:T(8,128)}) custom-call(f32[512,3072]{1,0:T(8,128)} %get-tuple-element.89.refs_0_.refs_5_.refs_1_, f32[512,3072]{1,0:T(8,128)} %get-tuple-element.98.refs_1_.refs_2_, f32[512,128]{1,0:T(8,128)} %get-tuple-element.86.refs_5_.refs_1_.refs_2_.refs_11_, ...), custom_call_target="tpu_custom_call" | custom-call | flops 17999998976 | bytes 54000000 | tf_op jit(solution)/shard_map/pallas_call | solution.py:43
  413.2 23.4 %collective-permute-done.14.refs_0_ = f32[128,1536]{1,0:T(8,128)S(1)} collective-permute-done((f32[128,1536]{1,0:T(8,128)S(1)}, f32[128,1536]{1,0:T(8,128)S(1)}, u32[]{:S(2)}, u32[]{:S(2)}) %collective-permute-start.14) | collective-permute-done | bytes 786464 | tf_op jit(solution)/shard_map/ppermute | solution.py:565
  438.9 2.8 select_bitcast_fusion
  442.1 4.1 shard_map.226.refs_1_
  446.2 20.0 %all-to-all-start.1 = ((f32[4,96,1536]{2,1,0:T(8,128)}), f32[4,96,1536]{2,1,0:T(8,128)S(1)}, u32[]{:S(2)}, u32[]{:S(2)}) async-start(f32[4,96,1536]{2,1,0:T(8,128)} %shard_map.226.refs_1_), calls=%async_computation.1 | async-start | bytes 4718592 | tf_op jit(solution)/shard_map/all_to_all | solution.py:796
  467.3 5.9 shard_map.227
  474.3 2.7 maximum_select_fusion.1.refs_8_
  478.3 17.6 %shard_map.229 = (bf16[512,1536]{1,0:T(8,128)(2,1)}, f32[32,1536]{1,0:T(8,128)}, f32[8,1536]{1,0:T(8,128)}, f32[512,128]{1,0:T(8,128)}, f32[512,128]{1,0:T(8,128)}, /*index=5*/f32[8,128]{1,0:T(8,128)}) custom-call(f32[512,1536]{1,0:T(8,128)} %get-tuple-element.112.refs_1_.refs_0_, f32[512,3072]{1,0:T(8,128)} %get-tuple-element.89.refs_0_.refs_5_.refs_1_, ...), custom_call_target="tpu_custom_call" | custom-call | flops 14000000000 | bytes 42000000 | tf_op jit(solution)/shard_map/pallas_call | solution.py:43
  504.7 2.7 copy.76
  507.4 6.5 collective-permute-done.23
  515.5 4.2 shard_map.230.refs_9_
  521.1 7.8 %all-to-all-start.3 = ((f32[4,48,3072]{2,1,0:T(8,128)}), f32[4,48,3072]{2,1,0:T(8,128)}, u32[]{:S(2)}, u32[]{:S(2)}) async-start(f32[4,48,3072]{2,1,0:T(8,128)} %shard_map.230.refs_9_), calls=%async_computation.3 | async-start | bytes 4718592 | tf_op jit(solution)/shard_map/all_to_all | solution.py:796
  529.0 5.3 shard_map.232
  534.2 2.5 collective-permute-start.31
  536.7 5.3 shard_map.231
  543.6 18.1 %shard_map.233 = (f32[16,128]{1,0:T(8,128)}, bf16[512,1920]{1,0:T(8,128)(2,1)}, f32[32,1920]{1,0:T(8,128)}, f32[8,1920]{1,0:T(8,128)}, f32[512,128]{1,0:T(8,128)}, /*index=5*/f32[512,128]{1,0:T(8,128)}, f32[8,128]{1,0:T(8,128)}) custom-call(f32[512,1536]{1,0:T(8,128)} %get-tuple-element.113.refs_1_.refs_0_, ...), custom_call_target="tpu_custom_call" | custom-call | flops 17999998976 | bytes 54000000 | tf_op jit(solution)/shard_map/pallas_call | solution.py:43
  564.1 10.9 %shard_map.234.refs_1_.refs_3_ = f32[512,1536]{1,0:T(8,128)} custom-call(bf16[512,3072]{1,0:T(8,128)(2,1)} %get-tuple-element.106.refs_5_.refs_0_, bf16[4,1536,1536]{2,1,0:T(8,128)(2,1)} %all-gather.5.cloned.1.call-done.refs_1_, f32[32,1920]{1,0:T(8,128)} %get-tuple-element.138.refs_2_.refs_9_), custom_call_target="tpu_custom_call" | custom-call | flops 10000000000 | bytes 30000000 | tf_op jit(solution)/shard_map/pallas_call | solution.py:43
  577.8 4.9 shard_map.236
  582.7 2.7 collective-permute-start.32
  586.4 6.8 collective-permute-done.32.refs_1_
  595.4 3.6 shard_map.237.refs_9_
  599.7 5.4 shard_map.239
  605.5 5.3 shard_map.238
  611.2 11.3 %all-to-all-start.4 = ((f32[4,48,1536]{2,1,0:T(8,128)}), f32[4,48,1536]{2,1,0:T(8,128)S(1)}, u32[]{:S(2)}, u32[]{:S(2)}) async-start(f32[4,48,1536]{2,1,0:T(8,128)} %shard_map.237.refs_9_), calls=%async_computation.4 | async-start | bytes 2359296 | tf_op jit(solution)/shard_map/all_to_all | solution.py:796
  622.4 12.1 %shard_map.240.refs_0_ = f32[512,1536]{1,0:T(8,128)} custom-call(bf16[512,1536]{1,0:T(8,128)(2,1)} %get-tuple-element.167.refs_0_, bf16[512,1920]{1,0:T(8,128)(2,1)} %get-tuple-element.165.refs_1_, bf16[1536,3456]{1,0:T(8,128)(2,1)} %all-gather.3.cloned.1.call-done.refs_2_, f32[512,1536]{1,0:T(8,128)} %shard_map.234.refs_1_.refs_3_, ...), custom_call_target="tpu_custom_call" | custom-call | flops 10000000000 | bytes 30000000 | tf_op jit(solution)/shard_map/pallas_call | solution.py:43
  634.6 5.6 shard_map.241
  641.2 5.1 shard_map.242
  653.9 4.6 all-to-all-start.2
  659.4 3.6 shard_map.248
  663.0 3.1 all-to-all-done.2
  666.1 3.5 all-to-all-start.5
  669.6 12.8 %shard_map.243.refs_1_ = bf16[512,1536]{1,0:T(8,128)(2,1)} custom-call(bf16[512,3072]{1,0:T(8,128)(2,1)} %get-tuple-element.96.refs_0_, bf16[4,1536,1536]{2,1,0:T(8,128)(2,1)} %all-gather.5.cloned.1.call-done.refs_1_, bf16[512,1536]{1,0:T(8,128)(2,1)} %refs_2_.3, bf16[4,48,1024]{2,1,0:T(8,128)(2,1)} %get-tuple-element.148.refs_3_.refs_1_, ...), custom_call_target="tpu_custom_call" | custom-call | flops 12999999488 | bytes 39000000 | tf_op jit(solution)/shard_map/pallas_call | solution.py:43
  682.4 2.7 reduce_sum.79
  (309 shorter events, 111.2 us)
Async XLA Ops:
  7.2 95.0 %all-gather.3.cloned.1.call-start = ((), (), s32[]{:S(2)}) async-start(), calls=%async_computation.6 | async-start | bytes 10948608 | tf_op jit(solution)/shard_map/all_gather | solution.py:851
  9.1 228.4 %all-gather.5.cloned.1.call-start = ((), (), s32[]{:S(2)}) async-start(), calls=%async_computation.7 | async-start | bytes 19464192 | tf_op jit(solution)/shard_map/all_gather | solution.py:856
  10.2 14.0 %copy-start.55 = (f32[48]{0:T(128)S(1)}, f32[48]{0:T(128)}, u32[]{:S(2)}) copy-start(f32[48]{0:T(128)} %param.19) | copy-start | bytes 580
  10.2 14.5 %copy-start.56 = (f32[48]{0:T(128)S(1)}, f32[48]{0:T(128)}, u32[]{:S(2)}) copy-start(f32[48]{0:T(128)} %param.20) | copy-start | bytes 580
  10.2 15.1 %copy-start.45 = (s32[1,3]{1,0:T(1,128)S(1)}, s32[1,3]{1,0:T(1,128)}, u32[]{:S(2)}) copy-start(s32[1,3]{1,0:T(1,128)} %param.14) | copy-start | bytes 40
  10.2 18.8 %copy-start.50 = (f32[48]{0:T(128)S(1)}, f32[48]{0:T(128)}, u32[]{:S(2)}) copy-start(f32[48]{0:T(128)} %param.21) | copy-start | bytes 580
  12.0 26.5 %collective-permute-start = (bf16[16,1536]{1,0:T(8,128)(2,1)S(1)}, bf16[16,1536]{1,0:T(8,128)(2,1)S(1)}, u32[]{:S(2)}, u32[]{:S(2)}) collective-permute-start(bf16[16,1536]{1,0:T(8,128)(2,1)S(1)} %slice.136), channel_id=1, source_target_pairs={{0,1},{1,2},{2,3},{3,4},{4,5},{5,6},{6,7},{8,9},{9,10},{10,11},{11... | collective-permute-start | bytes 147464 | tf_op jit(solution)/shard_map/ppermute | solution.py:523
  19.3 15.5 %all-to-all-start = ((bf16[32,2,332]{2,1,0:T(2,128)(2,1)}), bf16[32,2,332]{2,1,0:T(2,128)(2,1)S(1)}, u32[]{:S(2)}, u32[]{:S(2)}) async-start(bf16[32,2,332]{2,1,0:T(2,128)(2,1)} %reshape.412), calls=%async_computation | async-start | bytes 98304 | tf_op jit(solution)/shard_map/all_to_all | solution.py:826
  134.0 17.2 %collective-permute-start.1 = (f32[8,1536]{1,0:T(8,128)S(1)}, f32[8,1536]{1,0:T(8,128)S(1)}, u32[]{:S(2)}, u32[]{:S(2)}) collective-permute-start(f32[8,1536]{1,0:T(8,128)S(1)} %dynamic-slice_bitcast_fusion.2), channel_id=1, source_target_pairs={{0,1},{1,0},{2,3},{3,2},{4,5},{5,4},{6,7},{7,6},{8,9},{9,8},{10,11... | collective-permute-start | bytes 147464 | tf_op jit(solution)/shard_map/ppermute | solution.py:517
  136.6 26.4 %collective-permute-start.2 = (f32[128,1536]{1,0:T(8,128)S(1)}, f32[128,1536]{1,0:T(8,128)S(1)}, u32[]{:S(2)}, u32[]{:S(2)}) collective-permute-start(f32[128,1536]{1,0:T(8,128)S(1)} %dynamic-slice_bitcast_fusion.1.refs_6_), channel_id=1, source_target_pairs={{0,1},{1,0},{2,3},{3,2},{4,5},{5,4},{6,7},{7,6},{8,9},{9,8},{10,11... | collective-permute-start | bytes 2359304 | tf_op jit(solution)/shard_map/ppermute | solution.py:517
  152.0 11.9 %copy-start.8 = (f32[2,128,1536]{2,1,0:T(8,128)S(1)}, f32[2,128,1536]{2,1,0:T(8,128)}, u32[]{:S(2)}) copy-start(f32[2,128,1536]{2,1,0:T(8,128)} %get-tuple-element.93) | copy-start | bytes 4718596
  166.1 36.4 %collective-permute-start.3 = (f32[128,1536]{1,0:T(8,128)}, f32[128,1536]{1,0:T(8,128)S(1)}, u32[]{:S(2)}, u32[]{:S(2)}) collective-permute-start(f32[128,1536]{1,0:T(8,128)} %fusion.7.refs_6_), channel_id=1, source_target_pairs={{0,2},{1,3},{8,10},{9,11},{16,18},{17,19},{24,26},{25,27}} | collective-permute-start | bytes 2359304 | tf_op jit(solution)/shard_map/ppermute | solution.py:565
  205.6 0.7 collective-permute-start.4
  209.6 5.8 collective-permute-start.5
  218.7 44.2 %collective-permute-start.6 = (f32[128,1536]{1,0:T(8,128)}, f32[128,1536]{1,0:T(8,128)S(1)}, u32[]{:S(2)}, u32[]{:S(2)}) collective-permute-start(f32[128,1536]{1,0:T(8,128)} %get-tuple-element.178.refs_2_), channel_id=1, source_target_pairs={{0,1},{1,0},{2,3},{3,2},{4,5},{5,4},{6,7},{7,6},{8,9},{9,8},{10,11... | collective-permute-start | bytes 2359304 | tf_op jit(solution)/shard_map/ppermute | solution.py:517
  244.1 12.8 %copy-start.57 = (bf16[528,1536]{1,0:T(8,128)(2,1)S(1)}, bf16[528,1536]{1,0:T(8,128)(2,1)}, u32[]{:S(2)}) copy-start(bf16[528,1536]{1,0:T(8,128)(2,1)} %get-tuple-element.84) | copy-start | bytes 4866052
  299.1 32.2 %collective-permute-start.12 = (bf16[512,3072]{1,0:T(8,128)(2,1)}, bf16[512,3072]{1,0:T(8,128)(2,1)}, u32[]{:S(2)}, u32[]{:S(2)}) collective-permute-start(bf16[512,3072]{1,0:T(8,128)(2,1)} %get-tuple-element.106.refs_5_.refs_0_), channel_id=1, source_target_pairs={{0,8},{8,0},{1,9},{9,1},{2,10},{10,2},{3,11},{11,3},{4,12},{12,4},... | collective-permute-start | bytes 9437192 | tf_op jit(solution)/shard_map/ppermute | solution.py:517
  299.2 10.4 %collective-permute-start.10 = (bf16[512,1536]{1,0:T(8,128)(2,1)}, bf16[512,1536]{1,0:T(8,128)(2,1)}, u32[]{:S(2)}, u32[]{:S(2)}) collective-permute-start(bf16[512,1536]{1,0:T(8,128)(2,1)} %refs_2_.2), channel_id=1, source_target_pairs={{0,8},{8,0},{1,9},{9,1},{2,10},{10,2},{3,11},{11,3},{4,12},{12,4},... | collective-permute-start | bytes 4718600 | tf_op jit(solution)/shard_map/ppermute | solution.py:517
  302.3 7.3 %collective-permute-start.9 = (bf16[1536,512]{1,0:T(8,128)(2,1)}, bf16[1536,512]{1,0:T(8,128)(2,1)S(1)}, u32[]{:S(2)}, u32[]{:S(2)}) collective-permute-start(bf16[1536,512]{1,0:T(8,128)(2,1)} %bitcast.30), channel_id=1, source_target_pairs={{0,8},{8,0},{1,9},{9,1},{2,10},{10,2},{3,11},{11,3},{4,12},{12,4},... | collective-permute-start | bytes 4718600 | tf_op jit(solution)/shard_map/ppermute | solution.py:517
  303.7 22.1 %collective-permute-start.8 = (f32[128,1536]{1,0:T(8,128)S(1)}, f32[128,1536]{1,0:T(8,128)}, u32[]{:S(2)}, u32[]{:S(2)}) collective-permute-start(f32[128,1536]{1,0:T(8,128)S(1)} %dynamic-slice_bitcast_fusion.refs_7_), channel_id=1, source_target_pairs={{0,1},{1,0},{2,3},{3,2},{4,5},{5,4},{6,7},{7,6},{8,9},{9,8},{10,11... | collective-permute-start | bytes 2359304 | tf_op jit(solution)/shard_map/ppermute | solution.py:517
  305.9 25.3 %collective-permute-start.7 = (bf16[768,512]{1,0:T(8,128)(2,1)}, bf16[768,512]{1,0:T(8,128)(2,1)S(1)}, u32[]{:S(2)}, u32[]{:S(2)}) collective-permute-start(bf16[768,512]{1,0:T(8,128)(2,1)} %bitcast.26), channel_id=1, source_target_pairs={{0,8},{8,0},{1,9},{9,1},{2,10},{10,2},{3,11},{11,3},{4,12},{12,4},... | collective-permute-start | bytes 2359304 | tf_op jit(solution)/shard_map/ppermute | solution.py:517
  328.4 20.9 %collective-permute-start.11 = (f32[128,1536]{1,0:T(8,128)S(1)}, f32[128,1536]{1,0:T(8,128)S(1)}, u32[]{:S(2)}, u32[]{:S(2)}) collective-permute-start(f32[128,1536]{1,0:T(8,128)S(1)} %fusion.6.refs_7_), channel_id=1, source_target_pairs={{6,4},{7,5},{14,12},{15,13},{22,20},{23,21},{30,28},{31,29}} | collective-permute-start | bytes 2359304 | tf_op jit(solution)/shard_map/ppermute | solution.py:565
  329.2 32.4 %collective-permute-start.16 = (bf16[768,768]{1,0:T(8,128)(2,1)}, bf16[768,768]{1,0:T(8,128)(2,1)}, u32[]{:S(2)}, u32[]{:S(2)}) collective-permute-start(bf16[768,768]{1,0:T(8,128)(2,1)} %get-tuple-element.104.refs_3_), channel_id=1, source_target_pairs={{0,16},{16,0},{1,17},{17,1},{2,18},{18,2},{3,19},{19,3},{4,20},{20... | collective-permute-start | bytes 3538952 | tf_op jit(solution)/shard_map/ppermute | solution.py:587
  330.6 31.0 %collective-permute-start.17 = (bf16[768,768]{1,0:T(8,128)(2,1)}, bf16[768,768]{1,0:T(8,128)(2,1)}, u32[]{:S(2)}, u32[]{:S(2)}) collective-permute-start(bf16[768,768]{1,0:T(8,128)(2,1)} %get-tuple-element.105.refs_4_), channel_id=1, source_target_pairs={{0,1},{1,0},{2,3},{3,2},{4,5},{5,4},{6,7},{7,6},{8,9},{9,8},{10,11... | collective-permute-start | bytes 3538952 | tf_op jit(solution)/shard_map/ppermute | solution.py:587
  339.7 126.6 %collective-permute-start.20 = (bf16[384,1536]{1,0:T(8,128)(2,1)}, bf16[384,1536]{1,0:T(8,128)(2,1)S(1)}, u32[]{:S(2)}, u32[]{:S(2)}) collective-permute-start(bf16[384,1536]{1,0:T(8,128)(2,1)} %get-tuple-element.109.refs_3_), channel_id=1, source_target_pairs={{0,16},{16,0},{1,17},{17,1},{2,18},{18,2},{3,19},{19,3},{4,20},{20... | collective-permute-start | bytes 3538952 | tf_op jit(solution)/shard_map/ppermute | solution.py:587
  348.0 118.3 %collective-permute-start.21 = (bf16[384,1536]{1,0:T(8,128)(2,1)}, bf16[384,1536]{1,0:T(8,128)(2,1)}, u32[]{:S(2)}, u32[]{:S(2)}) collective-permute-start(bf16[384,1536]{1,0:T(8,128)(2,1)} %get-tuple-element.110.refs_4_), channel_id=1, source_target_pairs={{0,1},{1,0},{2,3},{3,2},{4,5},{5,4},{6,7},{7,6},{8,9},{9,8},{10,11... | collective-permute-start | bytes 3538952 | tf_op jit(solution)/shard_map/ppermute | solution.py:587
  351.5 10.1 %copy-start.19 = (f32[128,1536]{1,0:T(8,128)}, f32[128,1536]{1,0:T(8,128)S(1)}, u32[]{:S(2)}) copy-start(f32[128,1536]{1,0:T(8,128)S(1)} %multiply_add_fusion.3.refs_10_.refs_9_) | copy-start | bytes 2359300
  351.5 37.5 %collective-permute-start.13 = (f32[128,1536]{1,0:T(8,128)S(1)}, f32[128,1536]{1,0:T(8,128)S(1)}, u32[]{:S(2)}, u32[]{:S(2)}) collective-permute-start(f32[128,1536]{1,0:T(8,128)S(1)} %multiply_add_fusion.3.refs_10_.refs_9_), channel_id=1, source_target_pairs={{4,2},{5,3},{12,10},{13,11},{20,18},{21,19},{28,26},{29,27}} | collective-permute-start | bytes 2359304 | tf_op jit(solution)/shard_map/ppermute | solution.py:565
  367.5 74.6 %collective-permute-start.18 = (bf16[4,96,768]{2,1,0:T(8,128)(2,1)}, bf16[4,96,768]{2,1,0:T(8,128)(2,1)}, u32[]{:S(2)}, u32[]{:S(2)}) collective-permute-start(bf16[4,96,768]{2,1,0:T(8,128)(2,1)} %get-tuple-element.116), channel_id=1, source_target_pairs={{0,1},{1,0},{2,3},{3,2},{4,5},{5,4},{6,7},{7,6},{8,9},{9,8},{10,11... | collective-permute-start | bytes 1769480 | tf_op jit(solution)/shard_map/ppermute | solution.py:587
  368.2 73.9 %collective-permute-start.19 = (bf16[4,96,768]{2,1,0:T(8,128)(2,1)}, bf16[4,96,768]{2,1,0:T(8,128)(2,1)}, u32[]{:S(2)}, u32[]{:S(2)}) collective-permute-start(bf16[4,96,768]{2,1,0:T(8,128)(2,1)} %get-tuple-element.118), channel_id=1, source_target_pairs={{0,16},{16,0},{1,17},{17,1},{2,18},{18,2},{3,19},{19,3},{4,20},{20... | collective-permute-start | bytes 1769480 | tf_op jit(solution)/shard_map/ppermute | solution.py:587
  392.1 44.5 %collective-permute-start.14 = (f32[128,1536]{1,0:T(8,128)S(1)}, f32[128,1536]{1,0:T(8,128)S(1)}, u32[]{:S(2)}, u32[]{:S(2)}) collective-permute-start(f32[128,1536]{1,0:T(8,128)S(1)} %get-tuple-element.171.refs_10_), channel_id=1, source_target_pairs={{2,0},{3,1},{10,8},{11,9},{18,16},{19,17},{26,24},{27,25}} | collective-permute-start | bytes 2359304 | tf_op jit(solution)/shard_map/ppermute | solution.py:565
  441.7 31.4 %collective-permute-start.15 = (f32[128,1536]{1,0:T(8,128)}, f32[128,1536]{1,0:T(8,128)}, u32[]{:S(2)}, u32[]{:S(2)}) collective-permute-start(f32[128,1536]{1,0:T(8,128)} %get-tuple-element.176.refs_4_.refs_9_), channel_id=1, source_target_pairs={{0,1},{1,0},{2,3},{3,2},{4,5},{5,4},{6,7},{7,6},{8,9},{9,8},{10,11... | collective-permute-start | bytes 2359304 | tf_op jit(solution)/shard_map/ppermute | solution.py:517
  446.2 73.5 %all-to-all-start.1 = ((f32[4,96,1536]{2,1,0:T(8,128)}), f32[4,96,1536]{2,1,0:T(8,128)S(1)}, u32[]{:S(2)}, u32[]{:S(2)}) async-start(f32[4,96,1536]{2,1,0:T(8,128)} %shard_map.226.refs_1_), calls=%async_computation.1 | async-start | bytes 4718592 | tf_op jit(solution)/shard_map/all_to_all | solution.py:796
  478.3 17.7 %copy-start.31 = (bf16[4,48,1536]{2,1,0:T(8,128)(2,1)S(1)}, bf16[4,48,1536]{2,1,0:T(8,128)(2,1)}, u32[]{:S(2)}) copy-start(bf16[4,48,1536]{2,1,0:T(8,128)(2,1)} %get-tuple-element.119.refs_2_) | copy-start | bytes 1769476
  478.3 19.4 %copy-start.30 = (bf16[4,48,1536]{2,1,0:T(8,128)(2,1)S(1)}, bf16[4,48,1536]{2,1,0:T(8,128)(2,1)}, u32[]{:S(2)}) copy-start(bf16[4,48,1536]{2,1,0:T(8,128)(2,1)} %get-tuple-element.120.refs_3_) | copy-start | bytes 1769476
  478.3 22.9 %copy-start.38 = (f32[16,3072]{1,0:T(8,128)S(1)}, f32[16,3072]{1,0:T(8,128)}, u32[]{:S(2)}) copy-start(f32[16,3072]{1,0:T(8,128)} %get-tuple-element.153) | copy-start | bytes 589828
  495.9 33.1 %collective-permute-start.22 = (bf16[512,1536]{1,0:T(8,128)(2,1)}, bf16[512,1536]{1,0:T(8,128)(2,1)}, u32[]{:S(2)}, u32[]{:S(2)}) collective-permute-start(bf16[512,1536]{1,0:T(8,128)(2,1)} %get-tuple-element.129.refs_5_), channel_id=1, source_target_pairs={{0,8},{8,0},{1,9},{9,1},{2,10},{10,2},{3,11},{11,3},{4,12},{12,4},... | collective-permute-start | bytes 4718600 | tf_op jit(solution)/shard_map/ppermute | solution.py:517
  496.0 19.5 %collective-permute-start.25 = (bf16[4,48,1536]{2,1,0:T(8,128)(2,1)S(1)}, bf16[4,48,1536]{2,1,0:T(8,128)(2,1)}, u32[]{:S(2)}, u32[]{:S(2)}) collective-permute-start(bf16[4,48,1536]{2,1,0:T(8,128)(2,1)S(1)} %copy-done.31), channel_id=1, source_target_pairs={{0,1},{1,0},{2,3},{3,2},{4,5},{5,4},{6,7},{7,6},{8,9},{9,8},{10,11... | collective-permute-start | bytes 1769480 | tf_op jit(solution)/shard_map/ppermute | solution.py:587
  497.8 17.7 %collective-permute-start.26 = (bf16[4,48,1536]{2,1,0:T(8,128)(2,1)S(1)}, bf16[4,48,1536]{2,1,0:T(8,128)(2,1)}, u32[]{:S(2)}, u32[]{:S(2)}) collective-permute-start(bf16[4,48,1536]{2,1,0:T(8,128)(2,1)S(1)} %copy-done.30), channel_id=1, source_target_pairs={{0,16},{16,0},{1,17},{17,1},{2,18},{18,2},{3,19},{19,3},{4,20},{20... | collective-permute-start | bytes 1769480 | tf_op jit(solution)/shard_map/ppermute | solution.py:587
  500.0 14.0 %collective-permute-start.23 = (f32[16,1536]{1,0:T(8,128)}, f32[16,1536]{1,0:T(8,128)}, u32[]{:S(2)}, u32[]{:S(2)}) collective-permute-start(f32[16,1536]{1,0:T(8,128)} %slice.162), channel_id=1, source_target_pairs={{1,0},{2,1},{3,2},{4,3},{5,4},{6,5},{7,6},{9,8},{10,9},{11,10},{12... | collective-permute-start | bytes 294920 | tf_op jit(solution)/shard_map/ppermute | solution.py:523
  504.7 9.2 %copy-start.39 = (f32[32,1536]{1,0:T(8,128)S(1)}, f32[32,1536]{1,0:T(8,128)}, u32[]{:S(2)}) copy-start(f32[32,1536]{1,0:T(8,128)} %get-tuple-element.130.refs_4_) | copy-start | bytes 589828
  515.5 13.5 %collective-permute-start.24 = (bf16[16,1536]{1,0:T(8,128)(2,1)}, bf16[16,1536]{1,0:T(8,128)(2,1)}, u32[]{:S(2)}, u32[]{:S(2)}) collective-permute-start(bf16[16,1536]{1,0:T(8,128)(2,1)} %get-tuple-element.168.refs_7_), channel_id=1, source_target_pairs={{0,8},{8,0},{1,9},{9,1},{2,10},{10,2},{3,11},{11,3},{4,12},{12,4},... | collective-permute-start | bytes 147464 | tf_op jit(solution)/shard_map/ppermute | solution.py:517
  521.1 90.0 %all-to-all-start.3 = ((f32[4,48,3072]{2,1,0:T(8,128)}), f32[4,48,3072]{2,1,0:T(8,128)}, u32[]{:S(2)}, u32[]{:S(2)}) async-start(f32[4,48,3072]{2,1,0:T(8,128)} %shard_map.230.refs_9_), calls=%async_computation.3 | async-start | bytes 4718592 | tf_op jit(solution)/shard_map/all_to_all | solution.py:796
  534.2 42.7 %collective-permute-start.31 = (bf16[384,768]{1,0:T(8,128)(2,1)}, bf16[384,768]{1,0:T(8,128)(2,1)S(1)}, u32[]{:S(2)}, u32[]{:S(2)}) collective-permute-start(bf16[384,768]{1,0:T(8,128)(2,1)} %get-tuple-element.136.refs_27_), channel_id=1, source_target_pairs={{0,1},{1,0},{2,3},{3,2},{4,5},{5,4},{6,7},{7,6},{8,9},{9,8},{10,11... | collective-permute-start | bytes 1769480 | tf_op jit(solution)/shard_map/ppermute | solution.py:587
  542.0 35.0 %collective-permute-start.30 = (bf16[384,768]{1,0:T(8,128)(2,1)}, bf16[384,768]{1,0:T(8,128)(2,1)}, u32[]{:S(2)}, u32[]{:S(2)}) collective-permute-start(bf16[384,768]{1,0:T(8,128)(2,1)} %get-tuple-element.135.refs_26_), channel_id=1, source_target_pairs={{0,16},{16,0},{1,17},{17,1},{2,18},{18,2},{3,19},{19,3},{4,20},{20... | collective-permute-start | bytes 1769480 | tf_op jit(solution)/shard_map/ppermute | solution.py:587
  562.7 13.6 %collective-permute-start.28 = (f32[16,1920]{1,0:T(8,128)S(1)}, f32[16,1920]{1,0:T(8,128)S(1)}, u32[]{:S(2)}, u32[]{:S(2)}) collective-permute-start(f32[16,1920]{1,0:T(8,128)S(1)} %slice.164), channel_id=1, source_target_pairs={{1,0},{2,1},{3,2},{4,3},{5,4},{6,5},{7,6},{9,8},{10,9},{11,10},{12... | collective-permute-start | bytes 368648 | tf_op jit(solution)/shard_map/ppermute | solution.py:523
  564.0 11.0 %copy-start.41 = (f32[8,1920]{1,0:T(8,128)S(1)}, f32[8,1920]{1,0:T(8,128)}, u32[]{:S(2)}) copy-start(f32[8,1920]{1,0:T(8,128)} %get-tuple-element.152) | copy-start | bytes 184324
  564.0 11.0 %copy-start.40 = (f32[8,1536]{1,0:T(8,128)S(1)}, f32[8,1536]{1,0:T(8,128)}, u32[]{:S(2)}) copy-start(f32[8,1536]{1,0:T(8,128)} %get-tuple-element.151) | copy-start | bytes 147460
  564.0 35.0 %collective-permute-start.27 = (bf16[512,1920]{1,0:T(8,128)(2,1)}, bf16[512,1920]{1,0:T(8,128)(2,1)}, u32[]{:S(2)}, u32[]{:S(2)}) collective-permute-start(bf16[512,1920]{1,0:T(8,128)(2,1)} %get-tuple-element.137.refs_5_), channel_id=1, source_target_pairs={{0,8},{8,0},{1,9},{9,1},{2,10},{10,2},{3,11},{11,3},{4,12},{12,4},... | collective-permute-start | bytes 5898248 | tf_op jit(solution)/shard_map/ppermute | solution.py:517
  564.1 10.9 %copy-start.6 = (bf16[512,1920]{1,0:T(8,128)(2,1)S(1)}, bf16[512,1920]{1,0:T(8,128)(2,1)}, u32[]{:S(2)}) copy-start(bf16[512,1920]{1,0:T(8,128)(2,1)} %get-tuple-element.137.refs_5_) | copy-start | bytes 5898244
  577.8 8.0 %copy-start.37 = (f32[32,1920]{1,0:T(8,128)S(1)}, f32[32,1920]{1,0:T(8,128)}, u32[]{:S(2)}) copy-start(f32[32,1920]{1,0:T(8,128)} %get-tuple-element.138.refs_2_.refs_9_) | copy-start | bytes 737284
  582.7 10.6 %collective-permute-start.32 = (bf16[4,48,768]{2,1,0:T(8,128)(2,1)}, bf16[4,48,768]{2,1,0:T(8,128)(2,1)S(1)}, u32[]{:S(2)}, u32[]{:S(2)}) collective-permute-start(bf16[4,48,768]{2,1,0:T(8,128)(2,1)} %get-tuple-element.140), channel_id=1, source_target_pairs={{0,1},{1,0},{2,3},{3,2},{4,5},{5,4},{6,7},{7,6},{8,9},{9,8},{10,11... | collective-permute-start | bytes 884744 | tf_op jit(solution)/shard_map/ppermute | solution.py:587
  585.4 9.3 %collective-permute-start.33 = (bf16[4,48,768]{2,1,0:T(8,128)(2,1)}, bf16[4,48,768]{2,1,0:T(8,128)(2,1)S(1)}, u32[]{:S(2)}, u32[]{:S(2)}) collective-permute-start(bf16[4,48,768]{2,1,0:T(8,128)(2,1)} %get-tuple-element.142), channel_id=1, source_target_pairs={{0,16},{16,0},{1,17},{17,1},{2,18},{18,2},{3,19},{19,3},{4,20},{20... | collective-permute-start | bytes 884744 | tf_op jit(solution)/shard_map/ppermute | solution.py:587
  586.4 12.6 %copy-start.32 = (bf16[16,1920]{1,0:T(8,128)(2,1)}, bf16[16,1920]{1,0:T(8,128)(2,1)S(1)}, u32[]{:S(2)}) copy-start(bf16[16,1920]{1,0:T(8,128)(2,1)S(1)} %get-tuple-element.166.refs_7_) | copy-start | bytes 184324
  586.4 12.6 %collective-permute-start.29 = (bf16[16,1920]{1,0:T(8,128)(2,1)S(1)}, bf16[16,1920]{1,0:T(8,128)(2,1)S(1)}, u32[]{:S(2)}, u32[]{:S(2)}) collective-permute-start(bf16[16,1920]{1,0:T(8,128)(2,1)S(1)} %get-tuple-element.166.refs_7_), channel_id=1, source_target_pairs={{0,8},{8,0},{1,9},{9,1},{2,10},{10,2},{3,11},{11,3},{4,12},{12,4},... | collective-permute-start | bytes 184328 | tf_op jit(solution)/shard_map/ppermute | solution.py:517
  605.1 35.1 %collective-permute-start.35 = (bf16[384,896]{1,0:T(8,128)(2,1)}, bf16[384,896]{1,0:T(8,128)(2,1)S(1)}, u32[]{:S(2)}, u32[]{:S(2)}) collective-permute-start(bf16[384,896]{1,0:T(8,128)(2,1)} %get-tuple-element.146.refs_7_), channel_id=1, source_target_pairs={{0,1},{1,0},{2,3},{3,2},{4,5},{5,4},{6,7},{7,6},{8,9},{9,8},{10,11... | collective-permute-start | bytes 2064392 | tf_op jit(solution)/shard_map/ppermute | solution.py:587
  610.8 29.3 %collective-permute-start.34 = (bf16[384,1024]{1,0:T(8,128)(2,1)}, bf16[384,1024]{1,0:T(8,128)(2,1)S(1)}, u32[]{:S(2)}, u32[]{:S(2)}) collective-permute-start(bf16[384,1024]{1,0:T(8,128)(2,1)} %get-tuple-element.144.refs_6_), channel_id=1, source_target_pairs={{0,16},{16,0},{1,17},{17,1},{2,18},{18,2},{3,19},{19,3},{4,20},{20... | collective-permute-start | bytes 2359304 | tf_op jit(solution)/shard_map/ppermute | solution.py:587
  611.2 42.7 %all-to-all-start.4 = ((f32[4,48,1536]{2,1,0:T(8,128)}), f32[4,48,1536]{2,1,0:T(8,128)S(1)}, u32[]{:S(2)}, u32[]{:S(2)}) async-start(f32[4,48,1536]{2,1,0:T(8,128)} %shard_map.237.refs_9_), calls=%async_computation.4 | async-start | bytes 2359296 | tf_op jit(solution)/shard_map/all_to_all | solution.py:796
  641.2 9.2 %copy-start.44 = (f32[48]{0:T(128)S(1)}, f32[48]{0:T(128)}, u32[]{:S(2)}) copy-start(f32[48]{0:T(128)} %reduce_sum.74) | copy-start | bytes 580
  646.3 12.1 %collective-permute-start.37 = (bf16[4,48,896]{2,1,0:T(8,128)(2,1)}, bf16[4,48,896]{2,1,0:T(8,128)(2,1)S(1)}, u32[]{:S(2)}, u32[]{:S(2)}) collective-permute-start(bf16[4,48,896]{2,1,0:T(8,128)(2,1)} %get-tuple-element.149.refs_4_.refs_2_), channel_id=1, source_target_pairs={{0,16},{16,0},{1,17},{17,1},{2,18},{18,2},{3,19},{19,3},{4,20},{20... | collective-permute-start | bytes 1032200 | tf_op jit(solution)/shard_map/ppermute | solution.py:587
  647.7 10.8 %collective-permute-start.36 = (bf16[4,48,1024]{2,1,0:T(8,128)(2,1)}, bf16[4,48,1024]{2,1,0:T(8,128)(2,1)S(1)}, u32[]{:S(2)}, u32[]{:S(2)}) collective-permute-start(bf16[4,48,1024]{2,1,0:T(8,128)(2,1)} %get-tuple-element.148.refs_3_.refs_1_), channel_id=1, source_target_pairs={{0,1},{1,0},{2,3},{3,2},{4,5},{5,4},{6,7},{7,6},{8,9},{9,8},{10,11... | collective-permute-start | bytes 1179656 | tf_op jit(solution)/shard_map/ppermute | solution.py:587
  653.9 9.1 %copy-start.7 = (f32[4,48,1536]{2,1,0:T(8,128)}, f32[4,48,1536]{2,1,0:T(8,128)S(1)}, u32[]{:S(2)}) copy-start(f32[4,48,1536]{2,1,0:T(8,128)S(1)} %all-to-all-done.4.refs_0_) | copy-start | bytes 3538948
  653.9 12.2 %all-to-all-start.2 = ((f32[32,1,808]{2,1,0:T(1,128)}), f32[32,1,808]{2,1,0:T(1,128)S(1)}, u32[]{:S(2)}, u32[]{:S(2)}) async-start(f32[32,1,808]{2,1,0:T(1,128)} %copy.52), calls=%async_computation.2 | async-start | bytes 229376 | tf_op jit(solution)/shard_map/all_to_all | solution.py:1238
  666.1 28.3 %all-to-all-start.5 = ((bf16[4,48,1920]{2,1,0:T(8,128)(2,1)}), bf16[4,48,1920]{2,1,0:T(8,128)(2,1)S(1)}, u32[]{:S(2)}, u32[]{:S(2)}) async-start(bf16[4,48,1920]{2,1,0:T(8,128)(2,1)} %shard_map.248), calls=%async_computation.5 | async-start | bytes 1474560 | tf_op jit(solution)/shard_map/all_to_all | solution.py:796
  (40 other events, 92.9 us)
Sparse Core Ops, SparseCore 0:
  11.5 90.6 all-gather.2
  105.7 131.7 all-gather.4

commit v6 on v5

--- a/solution.py
+++ b/solution.py
@@ -976,6 +976,10 @@
     weight_block = pl.BlockSpec((2, devices * rows_out, width), lambda g: (1, g, 0))
     direct = rows_out % 16 == 0
 
+    def project_z(wait):
+        kept["mixed_z"] = [mm(normed, stacked[side]).astype(BF) for side in range(2)]
+        return kept["mixed_z"]
+
     def project(wait):
         if direct:
             kept["d_final"] = call(
@@ -988,13 +992,12 @@
             weight_o = jnp.moveaxis(stacked[2:].reshape(2, count, rows_out, width), 0, 1)
             kept["weight_o"] = weight_o.reshape(-1, width)
             kept["d_final"] = mm_nt(out_grad, kept["weight_o"])
-        kept["mixed_z"] = [mm(normed, stacked[side]).astype(BF) for side in range(2)]
-        return [kept["d_final"], *kept["mixed_z"]]
+        return [kept["d_final"]]
 
     state_in = entering(
         state_local, device_decay, False,
         [
-            lambda wait: intra(0, wait), lambda wait: intra(1, wait), lambda wait: [], lambda wait: [],
+            lambda wait: intra(0, wait), lambda wait: intra(1, wait), lambda wait: [], project_z,
             project,
         ],
     )
@@ -1070,7 +1073,7 @@
         return [back[index]]
 
     def first_within(wait):
-        back["out"].second(wait)
+        back["z"].second(wait)
         return within(0, wait)
 
     def second_within(wait):
@@ -1079,13 +1082,13 @@
     norm_block = 256
 
     def send_out(wait):
-        back["z"].second(wait)
-        back["out"].third(wait)
-        return [back["out"].parts, *back["z"].next_x, *back["z"].next_y]
+        back["out"].second(wait)
+        back["z"].third(wait)
+        return [back["z"].parts, *back["out"].next_x, *back["out"].next_y]
 
     returned = entering(
         returned_local, device_decay, True,
-        [out_sums, z_sums, first_within, second_within, send_out],
+        [z_sums, out_sums, first_within, second_within, send_out],
     )
 
     blocks = half // BLOCK
@@ -1132,12 +1135,12 @@
 
     none = jnp.zeros((row_count, 128), F32)
     d_xa, edge_a, conv_a, *so_far = carried(0, [none, none, none[:8]], [], [], [])
-    back["z"].third(edge_a)
+    back["out"].third(edge_a)
     d_xa_theirs = swap(d_xa, "core")
     halo_a = from_behind(edge_a[:LEAD], -1)
     last_a = (edge_a[LEAD:] + halo_a).astype(BF)
     last_a_theirs = swap(last_a, "core")
-    sums_a = Reduction(normed_left, [d_xa, d_xa_theirs, last_a, last_a_theirs], 0, half // 2, half, [back["z"].parts, back["out"].got_z])
+    sums_a = Reduction(normed_left, [d_xa, d_xa_theirs, last_a, last_a_theirs], 0, half // 2, half, [back["out"].parts, back["z"].got_z])
     sums_a.launch()
     heads, d_xb, edge_b, conv_b, *_ = carried(
         1, so_far,

time: 715 us -> 707 us (0.989)
    ppermute x6, waiting for transfers between devices: 42.5 us -> 31.8 us  [entering(): arrived = meanwhile(sent, lax.ppermute(sent, 'z', pairs))]
    all_gather x1, waiting for transfers between devices: 18.9 us -> 27.3 us  [shards(): stacked = lax.all_gather(stacked, EVERY, axis=1, tiled=True)]
    all_to_all x4, starting transfers between devices: 42.6 us -> 34.2 us  [third(): self.got_z = lax.all_to_all(self.parts, 'z', 0, 0, tiled=True)]
    unnamed x123 -> x125, local copies, waits for them, and re-layouts: 28.9 us -> 28.2 us
  transfers between devices with their start and end apart: 46 -> 46, of which waited for: 10 -> 13; matrix products, arithmetic and copies ran while one was open for 15% -> 15% of each run, Pallas kernels for 38% -> 38%
where the time goes in v6:
time: 707 us; the launch traced here: 695 us
  Pallas kernels  297 us (42%)
  waiting for transfers between devices  151 us (21%)
  starting transfers between devices  96 us (14%)
  local copies, waits for them, and re-layouts  65.3 us (9%)
  other arithmetic  43.9 us (6%)
  matrix products  24.5 us (3%)
  between operations  17.4 us (2%)
    pallas_call x31, Pallas kernels, call(): pl.pallas_call(run, grid_spec=pltpu.PrefetchScalarGridSpec(num_scalar_pre...  297 us
    all_gather x1, waiting for transfers between devices, shards(): lax.all_gather(columns(in_weight[:, INNER:], PROJ_X), EVERY, axis=0, tile...  59.3 us
    all_to_all x4, starting transfers between devices, third(): self.got_z = lax.all_to_all(self.parts, 'z', 0, 0, tiled=True)  34.2 us
    ppermute x6, waiting for transfers between devices, entering(): arrived = meanwhile(sent, lax.ppermute(sent, 'z', pairs))  31.8 us
    unnamed x125, local copies, waits for them, and re-layouts  28.2 us
    all_gather x1, waiting for transfers between devices, shards(): stacked = lax.all_gather(stacked, EVERY, axis=1, tiled=True)  27.3 us
    dot_general x3, matrix products, mm(): return jnp.dot(left, right, preferred_element_type=F32)  24.5 us
    ppermute x16, starting transfers between devices, across(): lax.ppermute(array, axis, [(i, i ^ by) for i in range(lax.axis_size(axis))])  20.2 us
  transfers between devices with their start and end apart: 46, of which 13 were waited for; matrix products, arithmetic and copies ran while one was open for 15% of the time, Pallas kernels for 38%

profile of v6, /device:TPU:0, one launch (start us, length us, event | category | flops | bytes accessed | tf_op | source)
XLA Modules:
  0.0 694.9 jit_solution(7636452274263097449)
XLA Ops:
  12.0 4.9 collective-permute-start
  19.3 4.9 all-to-all-start
  39.2 3.9 shard_map.203
  43.1 59.3 %all-gather.3.cloned.1.call-done.refs_2_ = bf16[1536,3456]{1,0:T(8,128)(2,1)} async-done(((bf16[48,3456]{1,0:T(8,128)(2,1)}), bf16[1536,3456]{1,0:T(8,128)(2,1)}) %all-gather.3.cloned.1.call-update) | async-done | bytes 10616848 | tf_op jit(solution)/shard_map/all_gather | solution.py:851
  102.4 11.8 %convolution_convert_fusion.refs_0_.refs_1_.refs_4_.refs_17_ = bf16[528,3456]{1,0:T(8,128)(2,1)} fusion(bf16[528,1536]{1,0:T(8,128)(2,1)} %get-tuple-element.84, bf16[1536,3456]{1,0:T(8,128)(2,1)} %all-gather.3.cloned.1.call-done.refs_2_), kind=kOutput, calls=%fused_computation | convolution fusion | flops 5607512064 | bytes 15888384 | tf_op jit(solution)/shard_map/dot_general | solution.py:105
  114.8 4.5 shard_map.204
  120.8 12.4 %shard_map.205 = (f32[512,3072]{1,0:T(8,128)}, f32[512,3072]{1,0:T(8,128)}, f32[2,128,1536]{2,1,0:T(8,128)}, f32[2,8,1536]{2,1,0:T(8,128)}) custom-call(bf16[528,3456]{1,0:T(8,128)(2,1)} %convolution_convert_fusion.refs_0_.refs_1_.refs_4_.refs_17_, f32[8,3072]{1,0:T(8,128)} %slice.174.refs_1_.refs_5_, f32[1,3072]{1,0:T(1,128)} %slice.175.refs_2_, ...), custom_call_target="tpu_custom_call" | custom-call | flops 12000000000 | bytes 36000000 | tf_op jit(solution)/shard_map/pallas_call | solution.py:43
  137.6 13.6 %shard_map.206.refs_1_.refs_0_ = f32[512,1536]{1,0:T(8,128)} custom-call(f32[512,3072]{1,0:T(8,128)} %get-tuple-element.89.refs_0_.refs_5_.refs_1_, f32[512,128]{1,0:T(8,128)} %get-tuple-element.86.refs_5_.refs_1_.refs_2_.refs_11_, f32[1,3072]{1,0:T(1,128)} %broadcast_in_dim_reshape.3.refs_2_.refs_11_.refs_12_, f32[512,512]{1,0:T(8,128)} %get-tuple-element.90.refs_3_, ...), custom_call_target="tpu_custom_call" | custom-call | flops 12000000000 | bytes 36000000 | tf_op jit(solution)/shard_map/pallas_call | solution.py:43
  152.1 11.1 %collective-permute-done.2.refs_0_ = f32[128,1536]{1,0:T(8,128)S(1)} collective-permute-done((f32[128,1536]{1,0:T(8,128)S(1)}, f32[128,1536]{1,0:T(8,128)S(1)}, u32[]{:S(2)}, u32[]{:S(2)}) %collective-permute-start.2) | collective-permute-done | bytes 786464 | tf_op jit(solution)/shard_map/ppermute | solution.py:517
  164.1 2.1 fusion.7.refs_6_
  166.2 3.5 collective-permute-start.3
  169.7 13.7 %shard_map.208.refs_1_ = f32[512,1536]{1,0:T(8,128)} custom-call(f32[512,3072]{1,0:T(8,128)} %get-tuple-element.89.refs_0_.refs_5_.refs_1_, f32[512,128]{1,0:T(8,128)} %get-tuple-element.86.refs_5_.refs_1_.refs_2_.refs_11_, f32[1,3072]{1,0:T(1,128)} %broadcast_in_dim_reshape.3.refs_2_.refs_11_.refs_12_, f32[512,512]{1,0:T(8,128)} %get-tuple-element.90.refs_3_, ...), custom_call_target="tpu_custom_call" | custom-call | flops 12000000000 | bytes 36000000 | tf_op jit(solution)/shard_map/pallas_call | solution.py:43
  183.4 18.8 %collective-permute-done.3.refs_0_ = f32[128,1536]{1,0:T(8,128)S(1)} collective-permute-done((f32[128,1536]{1,0:T(8,128)}, f32[128,1536]{1,0:T(8,128)S(1)}, u32[]{:S(2)}, u32[]{:S(2)}) %collective-permute-start.3) | collective-permute-done | bytes 786464 | tf_op jit(solution)/shard_map/ppermute | solution.py:565
  203.2 2.2 multiply_add_fusion.6
  207.0 2.5 multiply_add_fusion.5
  210.1 27.3 %all-gather.5.cloned.1.call-done.refs_1_ = bf16[4,1536,1536]{2,1,0:T(8,128)(2,1)} async-done(((bf16[4,48,1536]{2,1,0:T(8,128)(2,1)}), bf16[4,1536,1536]{2,1,0:T(8,128)(2,1)}) %all-gather.5.cloned.1.call-update) | async-done | bytes 18874384 | tf_op jit(solution)/shard_map/all_gather | solution.py:856
  237.5 6.7 fusion.3.refs_2_.refs_3_
  244.2 6.0 fusion.2.refs_1_.refs_2_
  251.6 2.3 select_bitcast_fusion.1
  259.8 12.8 %shard_map.212.refs_1_.refs_4_ = f32[512,3072]{1,0:T(8,128)} custom-call(bf16[512,1536]{1,0:T(8,128)(2,1)} %refs_2_.2, bf16[4,1536,1536]{2,1,0:T(8,128)(2,1)} %all-gather.5.cloned.1.call-done.refs_1_, f32[128,1536]{1,0:T(8,128)} %get-tuple-element.178.refs_2_), custom_call_target="tpu_custom_call" | custom-call | flops 7000000000 | bytes 21000000 | tf_op jit(solution)/shard_map/pallas_call | solution.py:43
  274.6 3.6 multiply_add_fusion
  278.2 32.0 %shard_map.214 = (bf16[512,3072]{1,0:T(8,128)(2,1)}, bf16[3072,512]{1,0:T(8,128)(2,1)}, bf16[512,3072]{1,0:T(8,128)(2,1)}, f32[512,3072]{1,0:T(8,128)}, f32[2,12...) custom-call(f32[512,1536]{1,0:T(8,128)} %shard_map.206.refs_1_.refs_0_, ...), custom_call_target="tpu_custom_call" | custom-call | flops 31000000512 | bytes 93000000 | tf_op jit(solution)/shard_map/pallas_call | solution.py:43
  311.7 2.8 constant_dynamic-slice_fusion
  316.4 1.9 collective-permute-done.7
  319.2 7.6 %shard_map.215 = (bf16[384,1536]{1,0:T(8,128)(2,1)}, f32[384,1536]{1,0:T(8,128)}) custom-call(s32[3]{0:T(128)} %pad_add_fusion.refs_0_, bf16[2,2,384,512]{3,2,1,0:T(8,128)(2,1)} %bitcast.131, bf16[2,2,384,512]{3,2,1,0:T(8,128)(2,1)} %bitcast.132, bf16[2,384,512]{2,1,0:T(8,128)(2,1)} %bitcast.144, bf16[2,384,512]{2,1,0:T(8,128)(2,1)} %bitcast.145, ...), custom_call_target="tpu_custom_call" | custom-call | flops 2949120000 | bytes 8847360 | tf_op jit(solution)/shard_map/pallas_call | solution.py:43
  326.8 7.6 %shard_map.216 = (bf16[384,1536]{1,0:T(8,128)(2,1)}, f32[384,1536]{1,0:T(8,128)}) custom-call(s32[3]{0:T(128)} %pad_add_fusion.refs_0_, bf16[2,2,4,2,48,512]{5,4,3,2,1,0:T(8,128)(2,1)} %bitcast.133, bf16[2,2,4,2,48,512]{5,4,3,2,1,0:T(8,128)(2,1)} %bitcast.134, bf16[8,2,48,512]{3,2,1,0:T(8,128)(2,1)} %bitcast.146, bf16[8,2,48,512]{3,2,1,0:T(8,128)(2,1)} %bitcast.147, ...), custom_call_target="tpu_custom_call" | custom-call | flops 2949120000 | bytes 8847360 | tf_op jit(solution)/shard_map/pallas_call | solution.py:43
  336.2 11.6 %collective-permute-start.10 = (f32[128,1536]{1,0:T(8,128)S(1)}, f32[128,1536]{1,0:T(8,128)S(1)}, u32[]{:S(2)}, u32[]{:S(2)}) collective-permute-start(f32[128,1536]{1,0:T(8,128)S(1)} %fusion.6.refs_7_), channel_id=1, source_target_pairs={{6,4},{7,5},{14,12},{15,13},{22,20},{23,21},{30,28},{31,29}} | collective-permute-start | bytes 2359304 | tf_op jit(solution)/shard_map/ppermute | solution.py:565
  351.1 7.6 %shard_map.219 = (bf16[768,768]{1,0:T(8,128)(2,1)}, f32[768,768]{1,0:T(8,128)}) custom-call(s32[3]{0:T(128)} %pad_add_fusion.refs_0_, bf16[2,2,4,2,96,512]{5,4,3,2,1,0:T(8,128)(2,1)} %bitcast.157, bf16[2,2,4,2,96,512]{5,4,3,2,1,0:T(8,128)(2,1)} %bitcast.158, bf16[8,2,96,512]{3,2,1,0:T(8,128)(2,1)} %bitcast.161, bf16[8,2,96,512]{3,2,1,0:T(8,128)(2,1)} %bitcast.162, ...), custom_call_target="tpu_custom_call" | custom-call | flops 2949120000 | bytes 8847360 | tf_op jit(solution)/shard_map/pallas_call | solution.py:43
  360.0 7.5 %shard_map.218 = (bf16[768,768]{1,0:T(8,128)(2,1)}, f32[768,768]{1,0:T(8,128)}) custom-call(s32[3]{0:T(128)} %pad_add_fusion.refs_0_, bf16[2,2,768,512]{3,2,1,0:T(8,128)(2,1)} %bitcast.159, bf16[2,2,768,512]{3,2,1,0:T(8,128)(2,1)} %bitcast.160, bf16[2,768,512]{2,1,0:T(8,128)(2,1)} %bitcast.163, bf16[2,768,512]{2,1,0:T(8,128)(2,1)} %bitcast.164, ...), custom_call_target="tpu_custom_call" | custom-call | flops 2949120000 | bytes 8847360 | tf_op jit(solution)/shard_map/pallas_call | solution.py:43
  372.1 18.3 %shard_map.221 = (f32[512,1536]{1,0:T(8,128)}, f32[512,512]{1,0:T(8,128)}) custom-call(f32[512,3072]{1,0:T(8,128)} %get-tuple-element.89.refs_0_.refs_5_.refs_1_, f32[512,3072]{1,0:T(8,128)} %get-tuple-element.98.refs_1_.refs_2_, f32[512,128]{1,0:T(8,128)} %get-tuple-element.86.refs_5_.refs_1_.refs_2_.refs_11_, f32[512,512]{1,0:T(8,128)} %get-tuple-element.99.refs_3_, ...), custom_call_target="tpu_custom_call" | custom-call | flops 17999998976 | bytes 54000000 | tf_op jit(solution)/shard_map/pallas_call | solution.py:43
  390.4 5.9 shard_map.225
  402.9 19.8 %shard_map.223 = (f32[512,1536]{1,0:T(8,128)}, f32[512,512]{1,0:T(8,128)}, f32[512,256]{1,0:T(8,128)}) custom-call(f32[512,3072]{1,0:T(8,128)} %get-tuple-element.89.refs_0_.refs_5_.refs_1_, f32[512,3072]{1,0:T(8,128)} %get-tuple-element.98.refs_1_.refs_2_, f32[512,128]{1,0:T(8,128)} %get-tuple-element.86.refs_5_.refs_1_.refs_2_.refs_11_, ...), custom_call_target="tpu_custom_call" | custom-call | flops 17999998976 | bytes 54000000 | tf_op jit(solution)/shard_map/pallas_call | solution.py:43
  422.7 12.9 %collective-permute-done.14.refs_0_ = f32[128,1536]{1,0:T(8,128)S(1)} collective-permute-done((f32[128,1536]{1,0:T(8,128)S(1)}, f32[128,1536]{1,0:T(8,128)S(1)}, u32[]{:S(2)}, u32[]{:S(2)}) %collective-permute-start.14) | collective-permute-done | bytes 786464 | tf_op jit(solution)/shard_map/ppermute | solution.py:565
  437.9 2.5 select_bitcast_fusion
  441.5 4.2 shard_map.226.refs_1_
  445.7 11.9 %all-to-all-start.1 = ((f32[4,48,3072]{2,1,0:T(8,128)}), f32[4,48,3072]{2,1,0:T(8,128)S(1)}, u32[]{:S(2)}, u32[]{:S(2)}) async-start(f32[4,48,3072]{2,1,0:T(8,128)} %shard_map.226.refs_1_), calls=%async_computation.1 | async-start | bytes 4718592 | tf_op jit(solution)/shard_map/all_to_all | solution.py:796
  457.5 5.9 shard_map.227
  464.6 2.7 maximum_select_fusion.1.refs_8_
  468.6 17.6 %shard_map.229 = (bf16[512,1536]{1,0:T(8,128)(2,1)}, f32[32,1536]{1,0:T(8,128)}, f32[8,1536]{1,0:T(8,128)}, f32[512,128]{1,0:T(8,128)}, f32[512,128]{1,0:T(8,128)}, /*index=5*/f32[8,128]{1,0:T(8,128)}) custom-call(f32[512,1536]{1,0:T(8,128)} %get-tuple-element.112.refs_1_.refs_0_, f32[512,3072]{1,0:T(8,128)} %get-tuple-element.89.refs_0_.refs_5_.refs_1_, ...), custom_call_target="tpu_custom_call" | custom-call | flops 14000000000 | bytes 42000000 | tf_op jit(solution)/shard_map/pallas_call | solution.py:43
  494.5 2.7 copy.76
  497.2 7.0 %collective-permute-done.23 = f32[16,1536]{1,0:T(8,128)} collective-permute-done((f32[16,1536]{1,0:T(8,128)}, f32[16,1536]{1,0:T(8,128)}, u32[]{:S(2)}, u32[]{:S(2)}) %collective-permute-start.23) | collective-permute-done | bytes 98336 | tf_op jit(solution)/shard_map/ppermute | solution.py:523
  505.8 4.1 shard_map.230.refs_9_
  511.9 7.9 %all-to-all-start.5 = ((f32[4,96,1536]{2,1,0:T(8,128)}), f32[4,96,1536]{2,1,0:T(8,128)}, u32[]{:S(2)}, u32[]{:S(2)}) async-start(f32[4,96,1536]{2,1,0:T(8,128)} %shard_map.230.refs_9_), calls=%async_computation.5 | async-start | bytes 4718592 | tf_op jit(solution)/shard_map/all_to_all | solution.py:796
  519.8 5.3 shard_map.232
  525.1 2.5 collective-permute-start.31
  527.6 5.3 shard_map.231
  533.5 18.1 %shard_map.233 = (f32[16,128]{1,0:T(8,128)}, bf16[512,1920]{1,0:T(8,128)(2,1)}, f32[32,1920]{1,0:T(8,128)}, f32[8,1920]{1,0:T(8,128)}, f32[512,128]{1,0:T(8,128)}, /*index=5*/f32[512,128]{1,0:T(8,128)}, f32[8,128]{1,0:T(8,128)}) custom-call(f32[512,1536]{1,0:T(8,128)} %get-tuple-element.113.refs_1_.refs_0_, ...), custom_call_target="tpu_custom_call" | custom-call | flops 17999998976 | bytes 54000000 | tf_op jit(solution)/shard_map/pallas_call | solution.py:43
  554.0 10.9 %shard_map.234.refs_1_.refs_3_ = f32[512,1536]{1,0:T(8,128)} custom-call(bf16[512,3072]{1,0:T(8,128)(2,1)} %get-tuple-element.101.refs_5_.refs_0_, bf16[4,1536,1536]{2,1,0:T(8,128)(2,1)} %all-gather.5.cloned.1.call-done.refs_1_, f32[32,1920]{1,0:T(8,128)} %get-tuple-element.138.refs_2_.refs_9_), custom_call_target="tpu_custom_call" | custom-call | flops 10000000000 | bytes 30000000 | tf_op jit(solution)/shard_map/pallas_call | solution.py:43
  567.7 4.9 shard_map.236
  572.5 2.7 collective-permute-start.32
  577.3 5.8 collective-permute-done.32.refs_1_
  585.3 3.6 shard_map.237.refs_9_
  590.8 5.4 shard_map.239
  596.6 5.4 shard_map.238
  603.4 10.9 %all-to-all-start.3 = ((f32[4,48,1536]{2,1,0:T(8,128)}), f32[4,48,1536]{2,1,0:T(8,128)S(1)}, u32[]{:S(2)}, u32[]{:S(2)}) async-start(f32[4,48,1536]{2,1,0:T(8,128)} %shard_map.237.refs_9_), calls=%async_computation.3 | async-start | bytes 2359296 | tf_op jit(solution)/shard_map/all_to_all | solution.py:796
  614.4 12.1 %shard_map.240.refs_0_ = f32[512,1536]{1,0:T(8,128)} custom-call(bf16[512,1536]{1,0:T(8,128)(2,1)} %get-tuple-element.167.refs_0_, bf16[512,1920]{1,0:T(8,128)(2,1)} %get-tuple-element.165.refs_1_, bf16[1536,3456]{1,0:T(8,128)(2,1)} %all-gather.3.cloned.1.call-done.refs_2_, f32[512,1536]{1,0:T(8,128)} %shard_map.234.refs_1_.refs_3_, ...), custom_call_target="tpu_custom_call" | custom-call | flops 10000000000 | bytes 30000000 | tf_op jit(solution)/shard_map/pallas_call | solution.py:43
  626.4 5.6 shard_map.241
  633.1 5.1 shard_map.242
  645.8 4.5 all-to-all-start.2
  651.2 3.6 shard_map.248
  654.8 3.1 all-to-all-done.2
  657.9 3.5 all-to-all-start.4
  661.4 12.8 %shard_map.243.refs_1_ = bf16[512,1536]{1,0:T(8,128)(2,1)} custom-call(bf16[512,3072]{1,0:T(8,128)(2,1)} %get-tuple-element.96.refs_0_, bf16[4,1536,1536]{2,1,0:T(8,128)(2,1)} %all-gather.5.cloned.1.call-done.refs_1_, bf16[512,1536]{1,0:T(8,128)(2,1)} %refs_2_.3, bf16[4,48,1024]{2,1,0:T(8,128)(2,1)} %get-tuple-element.148.refs_3_.refs_1_, ...), custom_call_target="tpu_custom_call" | custom-call | flops 12999999488 | bytes 39000000 | tf_op jit(solution)/shard_map/pallas_call | solution.py:43
  674.2 2.7 reduce_sum.79
  (311 shorter events, 113.9 us)
Async XLA Ops:
  7.2 95.2 %all-gather.3.cloned.1.call-start = ((), (), s32[]{:S(2)}) async-start(), calls=%async_computation.6 | async-start | bytes 10948608 | tf_op jit(solution)/shard_map/all_gather | solution.py:851
  9.1 228.4 %all-gather.5.cloned.1.call-start = ((), (), s32[]{:S(2)}) async-start(), calls=%async_computation.7 | async-start | bytes 19464192 | tf_op jit(solution)/shard_map/all_gather | solution.py:856
  10.2 14.0 %copy-start.56 = (f32[48]{0:T(128)S(1)}, f32[48]{0:T(128)}, u32[]{:S(2)}) copy-start(f32[48]{0:T(128)} %param.19) | copy-start | bytes 580
  10.2 14.5 %copy-start.57 = (f32[48]{0:T(128)S(1)}, f32[48]{0:T(128)}, u32[]{:S(2)}) copy-start(f32[48]{0:T(128)} %param.20) | copy-start | bytes 580
  10.2 15.1 %copy-start.46 = (s32[1,3]{1,0:T(1,128)S(1)}, s32[1,3]{1,0:T(1,128)}, u32[]{:S(2)}) copy-start(s32[1,3]{1,0:T(1,128)} %param.14) | copy-start | bytes 40
  10.2 18.9 %copy-start.51 = (f32[48]{0:T(128)S(1)}, f32[48]{0:T(128)}, u32[]{:S(2)}) copy-start(f32[48]{0:T(128)} %param.21) | copy-start | bytes 580
  12.0 26.6 %collective-permute-start = (bf16[16,1536]{1,0:T(8,128)(2,1)S(1)}, bf16[16,1536]{1,0:T(8,128)(2,1)S(1)}, u32[]{:S(2)}, u32[]{:S(2)}) collective-permute-start(bf16[16,1536]{1,0:T(8,128)(2,1)S(1)} %slice.136), channel_id=1, source_target_pairs={{0,1},{1,2},{2,3},{3,4},{4,5},{5,6},{6,7},{8,9},{9,10},{10,11},{11... | collective-permute-start | bytes 147464 | tf_op jit(solution)/shard_map/ppermute | solution.py:523
  19.3 15.5 %all-to-all-start = ((bf16[32,2,332]{2,1,0:T(2,128)(2,1)}), bf16[32,2,332]{2,1,0:T(2,128)(2,1)S(1)}, u32[]{:S(2)}, u32[]{:S(2)}) async-start(bf16[32,2,332]{2,1,0:T(2,128)(2,1)} %reshape.412), calls=%async_computation | async-start | bytes 98304 | tf_op jit(solution)/shard_map/all_to_all | solution.py:826
  134.1 17.1 %collective-permute-start.1 = (f32[8,1536]{1,0:T(8,128)S(1)}, f32[8,1536]{1,0:T(8,128)S(1)}, u32[]{:S(2)}, u32[]{:S(2)}) collective-permute-start(f32[8,1536]{1,0:T(8,128)S(1)} %dynamic-slice_bitcast_fusion.2), channel_id=1, source_target_pairs={{0,1},{1,0},{2,3},{3,2},{4,5},{5,4},{6,7},{7,6},{8,9},{9,8},{10,11... | collective-permute-start | bytes 147464 | tf_op jit(solution)/shard_map/ppermute | solution.py:517
  136.7 26.5 %collective-permute-start.2 = (f32[128,1536]{1,0:T(8,128)S(1)}, f32[128,1536]{1,0:T(8,128)S(1)}, u32[]{:S(2)}, u32[]{:S(2)}) collective-permute-start(f32[128,1536]{1,0:T(8,128)S(1)} %dynamic-slice_bitcast_fusion.1.refs_6_), channel_id=1, source_target_pairs={{0,1},{1,0},{2,3},{3,2},{4,5},{5,4},{6,7},{7,6},{8,9},{9,8},{10,11... | collective-permute-start | bytes 2359304 | tf_op jit(solution)/shard_map/ppermute | solution.py:517
  152.1 12.0 %copy-start.8 = (f32[2,128,1536]{2,1,0:T(8,128)S(1)}, f32[2,128,1536]{2,1,0:T(8,128)}, u32[]{:S(2)}) copy-start(f32[2,128,1536]{2,1,0:T(8,128)} %get-tuple-element.93) | copy-start | bytes 4718596
  166.2 36.1 %collective-permute-start.3 = (f32[128,1536]{1,0:T(8,128)}, f32[128,1536]{1,0:T(8,128)S(1)}, u32[]{:S(2)}, u32[]{:S(2)}) collective-permute-start(f32[128,1536]{1,0:T(8,128)} %fusion.7.refs_6_), channel_id=1, source_target_pairs={{0,2},{1,3},{8,10},{9,11},{16,18},{17,19},{24,26},{25,27}} | collective-permute-start | bytes 2359304 | tf_op jit(solution)/shard_map/ppermute | solution.py:565
  205.4 0.7 collective-permute-start.4
  209.4 40.8 %collective-permute-start.5 = (f32[128,1536]{1,0:T(8,128)}, f32[128,1536]{1,0:T(8,128)S(1)}, u32[]{:S(2)}, u32[]{:S(2)}) collective-permute-start(f32[128,1536]{1,0:T(8,128)} %get-tuple-element.173), channel_id=1, source_target_pairs={{4,6},{5,7},{12,14},{13,15},{20,22},{21,23},{28,30},{29,31}} | collective-permute-start | bytes 2359304 | tf_op jit(solution)/shard_map/ppermute | solution.py:565
  253.9 19.7 %collective-permute-start.6 = (f32[128,1536]{1,0:T(8,128)}, f32[128,1536]{1,0:T(8,128)S(1)}, u32[]{:S(2)}, u32[]{:S(2)}) collective-permute-start(f32[128,1536]{1,0:T(8,128)} %get-tuple-element.178.refs_2_), channel_id=1, source_target_pairs={{0,1},{1,0},{2,3},{3,2},{4,5},{5,4},{6,7},{7,6},{8,9},{9,8},{10,11... | collective-permute-start | bytes 2359304 | tf_op jit(solution)/shard_map/ppermute | solution.py:517
  278.2 32.1 %copy-start = (bf16[1536,512]{1,0:T(8,128)(2,1)S(1)}, bf16[1536,512]{1,0:T(8,128)(2,1)}, u32[]{:S(2)}) copy-start(bf16[1536,512]{1,0:T(8,128)(2,1)} %get-tuple-element.97) | copy-start | bytes 4718596
  310.1 8.2 %collective-permute-start.9 = (bf16[512,3072]{1,0:T(8,128)(2,1)}, bf16[512,3072]{1,0:T(8,128)(2,1)}, u32[]{:S(2)}, u32[]{:S(2)}) collective-permute-start(bf16[512,3072]{1,0:T(8,128)(2,1)} %get-tuple-element.101.refs_5_.refs_0_), channel_id=1, source_target_pairs={{0,8},{8,0},{1,9},{9,1},{2,10},{10,2},{3,11},{11,3},{4,12},{12,4},... | collective-permute-start | bytes 9437192 | tf_op jit(solution)/shard_map/ppermute | solution.py:517
  311.2 7.1 %collective-permute-start.7 = (bf16[768,512]{1,0:T(8,128)(2,1)}, bf16[768,512]{1,0:T(8,128)(2,1)S(1)}, u32[]{:S(2)}, u32[]{:S(2)}) collective-permute-start(bf16[768,512]{1,0:T(8,128)(2,1)} %bitcast.26), channel_id=1, source_target_pairs={{0,8},{8,0},{1,9},{9,1},{2,10},{10,2},{3,11},{11,3},{4,12},{12,4},... | collective-permute-start | bytes 2359304 | tf_op jit(solution)/shard_map/ppermute | solution.py:517
  311.7 38.3 %collective-permute-start.12 = (bf16[512,1536]{1,0:T(8,128)(2,1)}, bf16[512,1536]{1,0:T(8,128)(2,1)}, u32[]{:S(2)}, u32[]{:S(2)}) collective-permute-start(bf16[512,1536]{1,0:T(8,128)(2,1)} %refs_2_.2), channel_id=1, source_target_pairs={{0,8},{8,0},{1,9},{9,1},{2,10},{10,2},{3,11},{11,3},{4,12},{12,4},... | collective-permute-start | bytes 4718600 | tf_op jit(solution)/shard_map/ppermute | solution.py:517
  314.5 35.5 %collective-permute-start.11 = (bf16[1536,512]{1,0:T(8,128)(2,1)}, bf16[1536,512]{1,0:T(8,128)(2,1)S(1)}, u32[]{:S(2)}, u32[]{:S(2)}) collective-permute-start(bf16[1536,512]{1,0:T(8,128)(2,1)} %bitcast.33), channel_id=1, source_target_pairs={{0,8},{8,0},{1,9},{9,1},{2,10},{10,2},{3,11},{11,3},{4,12},{12,4},... | collective-permute-start | bytes 4718600 | tf_op jit(solution)/shard_map/ppermute | solution.py:517
  315.0 19.7 %collective-permute-start.8 = (f32[128,1536]{1,0:T(8,128)S(1)}, f32[128,1536]{1,0:T(8,128)}, u32[]{:S(2)}, u32[]{:S(2)}) collective-permute-start(f32[128,1536]{1,0:T(8,128)S(1)} %dynamic-slice_bitcast_fusion.refs_7_), channel_id=1, source_target_pairs={{0,1},{1,0},{2,3},{3,2},{4,5},{5,4},{6,7},{7,6},{8,9},{9,8},{10,11... | collective-permute-start | bytes 2359304 | tf_op jit(solution)/shard_map/ppermute | solution.py:517
  336.2 13.8 %copy-start.4 = (f32[128,1536]{1,0:T(8,128)}, f32[128,1536]{1,0:T(8,128)S(1)}, u32[]{:S(2)}) copy-start(f32[128,1536]{1,0:T(8,128)S(1)} %fusion.6.refs_7_) | copy-start | bytes 2359300
  336.2 32.0 %collective-permute-start.10 = (f32[128,1536]{1,0:T(8,128)S(1)}, f32[128,1536]{1,0:T(8,128)S(1)}, u32[]{:S(2)}, u32[]{:S(2)}) collective-permute-start(f32[128,1536]{1,0:T(8,128)S(1)} %fusion.6.refs_7_), channel_id=1, source_target_pairs={{6,4},{7,5},{14,12},{15,13},{22,20},{23,21},{30,28},{31,29}} | collective-permute-start | bytes 2359304 | tf_op jit(solution)/shard_map/ppermute | solution.py:565
  347.8 42.6 %collective-permute-start.17 = (bf16[384,1536]{1,0:T(8,128)(2,1)}, bf16[384,1536]{1,0:T(8,128)(2,1)}, u32[]{:S(2)}, u32[]{:S(2)}) collective-permute-start(bf16[384,1536]{1,0:T(8,128)(2,1)} %get-tuple-element.105.refs_4_), channel_id=1, source_target_pairs={{0,1},{1,0},{2,3},{3,2},{4,5},{5,4},{6,7},{7,6},{8,9},{9,8},{10,11... | collective-permute-start | bytes 3538952 | tf_op jit(solution)/shard_map/ppermute | solution.py:587
  348.7 41.8 %collective-permute-start.16 = (bf16[384,1536]{1,0:T(8,128)(2,1)}, bf16[384,1536]{1,0:T(8,128)(2,1)}, u32[]{:S(2)}, u32[]{:S(2)}) collective-permute-start(bf16[384,1536]{1,0:T(8,128)(2,1)} %get-tuple-element.104.refs_3_), channel_id=1, source_target_pairs={{0,16},{16,0},{1,17},{17,1},{2,18},{18,2},{3,19},{19,3},{4,20},{20... | collective-permute-start | bytes 3538952 | tf_op jit(solution)/shard_map/ppermute | solution.py:587
  358.7 98.9 %collective-permute-start.21 = (bf16[768,768]{1,0:T(8,128)(2,1)}, bf16[768,768]{1,0:T(8,128)(2,1)}, u32[]{:S(2)}, u32[]{:S(2)}) collective-permute-start(bf16[768,768]{1,0:T(8,128)(2,1)} %get-tuple-element.110.refs_4_), channel_id=1, source_target_pairs={{0,1},{1,0},{2,3},{3,2},{4,5},{5,4},{6,7},{7,6},{8,9},{9,8},{10,11... | collective-permute-start | bytes 3538952 | tf_op jit(solution)/shard_map/ppermute | solution.py:587
  367.5 90.0 %collective-permute-start.20 = (bf16[768,768]{1,0:T(8,128)(2,1)}, bf16[768,768]{1,0:T(8,128)(2,1)}, u32[]{:S(2)}, u32[]{:S(2)}) collective-permute-start(bf16[768,768]{1,0:T(8,128)(2,1)} %get-tuple-element.109.refs_3_), channel_id=1, source_target_pairs={{0,16},{16,0},{1,17},{17,1},{2,18},{18,2},{3,19},{19,3},{4,20},{20... | collective-permute-start | bytes 3538952 | tf_op jit(solution)/shard_map/ppermute | solution.py:587
  370.3 28.2 %collective-permute-start.13 = (f32[128,1536]{1,0:T(8,128)S(1)}, f32[128,1536]{1,0:T(8,128)S(1)}, u32[]{:S(2)}, u32[]{:S(2)}) collective-permute-start(f32[128,1536]{1,0:T(8,128)S(1)} %multiply_add_fusion.3.refs_10_.refs_9_), channel_id=1, source_target_pairs={{4,2},{5,3},{12,10},{13,11},{20,18},{21,19},{28,26},{29,27}} | collective-permute-start | bytes 2359304 | tf_op jit(solution)/shard_map/ppermute | solution.py:565
  396.4 45.1 %collective-permute-start.18 = (bf16[4,48,1536]{2,1,0:T(8,128)(2,1)}, bf16[4,48,1536]{2,1,0:T(8,128)(2,1)}, u32[]{:S(2)}, u32[]{:S(2)}) collective-permute-start(bf16[4,48,1536]{2,1,0:T(8,128)(2,1)} %get-tuple-element.116), channel_id=1, source_target_pairs={{0,1},{1,0},{2,3},{3,2},{4,5},{5,4},{6,7},{7,6},{8,9},{9,8},{10,11... | collective-permute-start | bytes 1769480 | tf_op jit(solution)/shard_map/ppermute | solution.py:587
  397.2 44.3 %collective-permute-start.19 = (bf16[4,48,1536]{2,1,0:T(8,128)(2,1)}, bf16[4,48,1536]{2,1,0:T(8,128)(2,1)}, u32[]{:S(2)}, u32[]{:S(2)}) collective-permute-start(bf16[4,48,1536]{2,1,0:T(8,128)(2,1)} %get-tuple-element.118), channel_id=1, source_target_pairs={{0,16},{16,0},{1,17},{17,1},{2,18},{18,2},{3,19},{19,3},{4,20},{20... | collective-permute-start | bytes 1769480 | tf_op jit(solution)/shard_map/ppermute | solution.py:587
  401.6 34.0 %collective-permute-start.14 = (f32[128,1536]{1,0:T(8,128)S(1)}, f32[128,1536]{1,0:T(8,128)S(1)}, u32[]{:S(2)}, u32[]{:S(2)}) collective-permute-start(f32[128,1536]{1,0:T(8,128)S(1)} %get-tuple-element.171.refs_10_), channel_id=1, source_target_pairs={{2,0},{3,1},{10,8},{11,9},{18,16},{19,17},{26,24},{27,25}} | collective-permute-start | bytes 2359304 | tf_op jit(solution)/shard_map/ppermute | solution.py:565
  440.5 23.0 %collective-permute-start.15 = (f32[128,1536]{1,0:T(8,128)S(1)}, f32[128,1536]{1,0:T(8,128)}, u32[]{:S(2)}, u32[]{:S(2)}) collective-permute-start(f32[128,1536]{1,0:T(8,128)S(1)} %get-tuple-element.176.refs_4_.refs_9_), channel_id=1, source_target_pairs={{0,1},{1,0},{2,3},{3,2},{4,5},{5,4},{6,7},{7,6},{8,9},{9,8},{10,11... | collective-permute-start | bytes 2359304 | tf_op jit(solution)/shard_map/ppermute | solution.py:517
  445.7 64.8 %all-to-all-start.1 = ((f32[4,48,3072]{2,1,0:T(8,128)}), f32[4,48,3072]{2,1,0:T(8,128)S(1)}, u32[]{:S(2)}, u32[]{:S(2)}) async-start(f32[4,48,3072]{2,1,0:T(8,128)} %shard_map.226.refs_1_), calls=%async_computation.1 | async-start | bytes 4718592 | tf_op jit(solution)/shard_map/all_to_all | solution.py:796
  468.6 17.7 %copy-start.32 = (bf16[4,96,768]{2,1,0:T(8,128)(2,1)S(1)}, bf16[4,96,768]{2,1,0:T(8,128)(2,1)}, u32[]{:S(2)}) copy-start(bf16[4,96,768]{2,1,0:T(8,128)(2,1)} %get-tuple-element.119.refs_2_) | copy-start | bytes 1769476
  468.6 18.9 %copy-start.31 = (bf16[4,96,768]{2,1,0:T(8,128)(2,1)S(1)}, bf16[4,96,768]{2,1,0:T(8,128)(2,1)}, u32[]{:S(2)}) copy-start(bf16[4,96,768]{2,1,0:T(8,128)(2,1)} %get-tuple-element.120.refs_3_) | copy-start | bytes 1769476
  468.6 22.4 %copy-start.39 = (f32[16,3072]{1,0:T(8,128)S(1)}, f32[16,3072]{1,0:T(8,128)}, u32[]{:S(2)}) copy-start(f32[16,3072]{1,0:T(8,128)} %get-tuple-element.153) | copy-start | bytes 589828
  486.2 33.6 %collective-permute-start.22 = (bf16[512,1536]{1,0:T(8,128)(2,1)}, bf16[512,1536]{1,0:T(8,128)(2,1)}, u32[]{:S(2)}, u32[]{:S(2)}) collective-permute-start(bf16[512,1536]{1,0:T(8,128)(2,1)} %get-tuple-element.129.refs_5_), channel_id=1, source_target_pairs={{0,8},{8,0},{1,9},{9,1},{2,10},{10,2},{3,11},{11,3},{4,12},{12,4},... | collective-permute-start | bytes 4718600 | tf_op jit(solution)/shard_map/ppermute | solution.py:517
  486.3 19.5 %collective-permute-start.25 = (bf16[4,96,768]{2,1,0:T(8,128)(2,1)S(1)}, bf16[4,96,768]{2,1,0:T(8,128)(2,1)}, u32[]{:S(2)}, u32[]{:S(2)}) collective-permute-start(bf16[4,96,768]{2,1,0:T(8,128)(2,1)S(1)} %copy-done.32), channel_id=1, source_target_pairs={{0,1},{1,0},{2,3},{3,2},{4,5},{5,4},{6,7},{7,6},{8,9},{9,8},{10,11... | collective-permute-start | bytes 1769480 | tf_op jit(solution)/shard_map/ppermute | solution.py:587
  487.5 18.3 %collective-permute-start.26 = (bf16[4,96,768]{2,1,0:T(8,128)(2,1)S(1)}, bf16[4,96,768]{2,1,0:T(8,128)(2,1)}, u32[]{:S(2)}, u32[]{:S(2)}) collective-permute-start(bf16[4,96,768]{2,1,0:T(8,128)(2,1)S(1)} %copy-done.31), channel_id=1, source_target_pairs={{0,16},{16,0},{1,17},{17,1},{2,18},{18,2},{3,19},{19,3},{4,20},{20... | collective-permute-start | bytes 1769480 | tf_op jit(solution)/shard_map/ppermute | solution.py:587
  489.7 14.5 %collective-permute-start.23 = (f32[16,1536]{1,0:T(8,128)}, f32[16,1536]{1,0:T(8,128)}, u32[]{:S(2)}, u32[]{:S(2)}) collective-permute-start(f32[16,1536]{1,0:T(8,128)} %slice.162), channel_id=1, source_target_pairs={{1,0},{2,1},{3,2},{4,3},{5,4},{6,5},{7,6},{9,8},{10,9},{11,10},{12... | collective-permute-start | bytes 294920 | tf_op jit(solution)/shard_map/ppermute | solution.py:523
  494.5 9.8 %copy-start.40 = (f32[32,1536]{1,0:T(8,128)S(1)}, f32[32,1536]{1,0:T(8,128)}, u32[]{:S(2)}) copy-start(f32[32,1536]{1,0:T(8,128)} %get-tuple-element.130.refs_4_) | copy-start | bytes 589828
  505.8 14.0 %collective-permute-start.24 = (bf16[16,1536]{1,0:T(8,128)(2,1)}, bf16[16,1536]{1,0:T(8,128)(2,1)}, u32[]{:S(2)}, u32[]{:S(2)}) collective-permute-start(bf16[16,1536]{1,0:T(8,128)(2,1)} %get-tuple-element.168.refs_7_), channel_id=1, source_target_pairs={{0,8},{8,0},{1,9},{9,1},{2,10},{10,2},{3,11},{11,3},{4,12},{12,4},... | collective-permute-start | bytes 147464 | tf_op jit(solution)/shard_map/ppermute | solution.py:517
  511.9 91.5 %all-to-all-start.5 = ((f32[4,96,1536]{2,1,0:T(8,128)}), f32[4,96,1536]{2,1,0:T(8,128)}, u32[]{:S(2)}, u32[]{:S(2)}) async-start(f32[4,96,1536]{2,1,0:T(8,128)} %shard_map.230.refs_9_), calls=%async_computation.5 | async-start | bytes 4718592 | tf_op jit(solution)/shard_map/all_to_all | solution.py:796
  525.1 41.7 %collective-permute-start.31 = (bf16[384,768]{1,0:T(8,128)(2,1)}, bf16[384,768]{1,0:T(8,128)(2,1)S(1)}, u32[]{:S(2)}, u32[]{:S(2)}) collective-permute-start(bf16[384,768]{1,0:T(8,128)(2,1)} %get-tuple-element.136.refs_27_), channel_id=1, source_target_pairs={{0,1},{1,0},{2,3},{3,2},{4,5},{5,4},{6,7},{7,6},{8,9},{9,8},{10,11... | collective-permute-start | bytes 1769480 | tf_op jit(solution)/shard_map/ppermute | solution.py:587
  532.9 34.0 %collective-permute-start.30 = (bf16[384,768]{1,0:T(8,128)(2,1)}, bf16[384,768]{1,0:T(8,128)(2,1)}, u32[]{:S(2)}, u32[]{:S(2)}) collective-permute-start(bf16[384,768]{1,0:T(8,128)(2,1)} %get-tuple-element.135.refs_26_), channel_id=1, source_target_pairs={{0,16},{16,0},{1,17},{17,1},{2,18},{18,2},{3,19},{19,3},{4,20},{20... | collective-permute-start | bytes 1769480 | tf_op jit(solution)/shard_map/ppermute | solution.py:587
  552.6 13.6 %collective-permute-start.28 = (f32[16,1920]{1,0:T(8,128)S(1)}, f32[16,1920]{1,0:T(8,128)S(1)}, u32[]{:S(2)}, u32[]{:S(2)}) collective-permute-start(f32[16,1920]{1,0:T(8,128)S(1)} %slice.164), channel_id=1, source_target_pairs={{1,0},{2,1},{3,2},{4,3},{5,4},{6,5},{7,6},{9,8},{10,9},{11,10},{12... | collective-permute-start | bytes 368648 | tf_op jit(solution)/shard_map/ppermute | solution.py:523
  553.9 11.0 %copy-start.42 = (f32[8,1920]{1,0:T(8,128)S(1)}, f32[8,1920]{1,0:T(8,128)}, u32[]{:S(2)}) copy-start(f32[8,1920]{1,0:T(8,128)} %get-tuple-element.152) | copy-start | bytes 184324
  553.9 11.0 %copy-start.41 = (f32[8,1536]{1,0:T(8,128)S(1)}, f32[8,1536]{1,0:T(8,128)}, u32[]{:S(2)}) copy-start(f32[8,1536]{1,0:T(8,128)} %get-tuple-element.151) | copy-start | bytes 147460
  553.9 35.0 %collective-permute-start.27 = (bf16[512,1920]{1,0:T(8,128)(2,1)}, bf16[512,1920]{1,0:T(8,128)(2,1)S(1)}, u32[]{:S(2)}, u32[]{:S(2)}) collective-permute-start(bf16[512,1920]{1,0:T(8,128)(2,1)} %get-tuple-element.137.refs_5_), channel_id=1, source_target_pairs={{0,8},{8,0},{1,9},{9,1},{2,10},{10,2},{3,11},{11,3},{4,12},{12,4},... | collective-permute-start | bytes 5898248 | tf_op jit(solution)/shard_map/ppermute | solution.py:517
  554.0 10.9 %copy-start.6 = (bf16[512,1920]{1,0:T(8,128)(2,1)S(1)}, bf16[512,1920]{1,0:T(8,128)(2,1)}, u32[]{:S(2)}) copy-start(bf16[512,1920]{1,0:T(8,128)(2,1)} %get-tuple-element.137.refs_5_) | copy-start | bytes 5898244
  567.7 9.0 %copy-start.38 = (f32[32,1920]{1,0:T(8,128)S(1)}, f32[32,1920]{1,0:T(8,128)}, u32[]{:S(2)}) copy-start(f32[32,1920]{1,0:T(8,128)} %get-tuple-element.138.refs_2_.refs_9_) | copy-start | bytes 737284
  572.5 10.6 %collective-permute-start.32 = (bf16[4,48,768]{2,1,0:T(8,128)(2,1)}, bf16[4,48,768]{2,1,0:T(8,128)(2,1)S(1)}, u32[]{:S(2)}, u32[]{:S(2)}) collective-permute-start(bf16[4,48,768]{2,1,0:T(8,128)(2,1)} %get-tuple-element.140), channel_id=1, source_target_pairs={{0,1},{1,0},{2,3},{3,2},{4,5},{5,4},{6,7},{7,6},{8,9},{9,8},{10,11... | collective-permute-start | bytes 884744 | tf_op jit(solution)/shard_map/ppermute | solution.py:587
  575.2 9.3 %collective-permute-start.33 = (bf16[4,48,768]{2,1,0:T(8,128)(2,1)}, bf16[4,48,768]{2,1,0:T(8,128)(2,1)S(1)}, u32[]{:S(2)}, u32[]{:S(2)}) collective-permute-start(bf16[4,48,768]{2,1,0:T(8,128)(2,1)} %get-tuple-element.142), channel_id=1, source_target_pairs={{0,16},{16,0},{1,17},{17,1},{2,18},{18,2},{3,19},{19,3},{4,20},{20... | collective-permute-start | bytes 884744 | tf_op jit(solution)/shard_map/ppermute | solution.py:587
  577.3 11.6 %copy-start.33 = (bf16[16,1920]{1,0:T(8,128)(2,1)}, bf16[16,1920]{1,0:T(8,128)(2,1)S(1)}, u32[]{:S(2)}) copy-start(bf16[16,1920]{1,0:T(8,128)(2,1)S(1)} %get-tuple-element.166.refs_7_) | copy-start | bytes 184324
  577.3 11.6 %collective-permute-start.29 = (bf16[16,1920]{1,0:T(8,128)(2,1)S(1)}, bf16[16,1920]{1,0:T(8,128)(2,1)S(1)}, u32[]{:S(2)}, u32[]{:S(2)}) collective-permute-start(bf16[16,1920]{1,0:T(8,128)(2,1)S(1)} %get-tuple-element.166.refs_7_), channel_id=1, source_target_pairs={{0,8},{8,0},{1,9},{9,1},{2,10},{10,2},{3,11},{11,3},{4,12},{12,4},... | collective-permute-start | bytes 184328 | tf_op jit(solution)/shard_map/ppermute | solution.py:517
  596.2 35.7 %collective-permute-start.35 = (bf16[384,896]{1,0:T(8,128)(2,1)}, bf16[384,896]{1,0:T(8,128)(2,1)S(1)}, u32[]{:S(2)}, u32[]{:S(2)}) collective-permute-start(bf16[384,896]{1,0:T(8,128)(2,1)} %get-tuple-element.146.refs_7_), channel_id=1, source_target_pairs={{0,1},{1,0},{2,3},{3,2},{4,5},{5,4},{6,7},{7,6},{8,9},{9,8},{10,11... | collective-permute-start | bytes 2064392 | tf_op jit(solution)/shard_map/ppermute | solution.py:587
  602.0 30.0 %collective-permute-start.34 = (bf16[384,1024]{1,0:T(8,128)(2,1)}, bf16[384,1024]{1,0:T(8,128)(2,1)S(1)}, u32[]{:S(2)}, u32[]{:S(2)}) collective-permute-start(bf16[384,1024]{1,0:T(8,128)(2,1)} %get-tuple-element.144.refs_6_), channel_id=1, source_target_pairs={{0,16},{16,0},{1,17},{17,1},{2,18},{18,2},{3,19},{19,3},{4,20},{20... | collective-permute-start | bytes 2359304 | tf_op jit(solution)/shard_map/ppermute | solution.py:587
  603.4 42.4 %all-to-all-start.3 = ((f32[4,48,1536]{2,1,0:T(8,128)}), f32[4,48,1536]{2,1,0:T(8,128)S(1)}, u32[]{:S(2)}, u32[]{:S(2)}) async-start(f32[4,48,1536]{2,1,0:T(8,128)} %shard_map.237.refs_9_), calls=%async_computation.3 | async-start | bytes 2359296 | tf_op jit(solution)/shard_map/all_to_all | solution.py:796
  633.1 9.3 %copy-start.45 = (f32[48]{0:T(128)S(1)}, f32[48]{0:T(128)}, u32[]{:S(2)}) copy-start(f32[48]{0:T(128)} %reduce_sum.74) | copy-start | bytes 580
  638.2 12.1 %collective-permute-start.37 = (bf16[4,48,896]{2,1,0:T(8,128)(2,1)}, bf16[4,48,896]{2,1,0:T(8,128)(2,1)S(1)}, u32[]{:S(2)}, u32[]{:S(2)}) collective-permute-start(bf16[4,48,896]{2,1,0:T(8,128)(2,1)} %get-tuple-element.149.refs_4_.refs_2_), channel_id=1, source_target_pairs={{0,16},{16,0},{1,17},{17,1},{2,18},{18,2},{3,19},{19,3},{4,20},{20... | collective-permute-start | bytes 1032200 | tf_op jit(solution)/shard_map/ppermute | solution.py:587
  639.7 10.6 %collective-permute-start.36 = (bf16[4,48,1024]{2,1,0:T(8,128)(2,1)}, bf16[4,48,1024]{2,1,0:T(8,128)(2,1)S(1)}, u32[]{:S(2)}, u32[]{:S(2)}) collective-permute-start(bf16[4,48,1024]{2,1,0:T(8,128)(2,1)} %get-tuple-element.148.refs_3_.refs_1_), channel_id=1, source_target_pairs={{0,1},{1,0},{2,3},{3,2},{4,5},{5,4},{6,7},{7,6},{8,9},{9,8},{10,11... | collective-permute-start | bytes 1179656 | tf_op jit(solution)/shard_map/ppermute | solution.py:587
  645.8 9.0 %copy-start.7 = (f32[4,48,1536]{2,1,0:T(8,128)}, f32[4,48,1536]{2,1,0:T(8,128)S(1)}, u32[]{:S(2)}) copy-start(f32[4,48,1536]{2,1,0:T(8,128)S(1)} %all-to-all-done.3.refs_0_) | copy-start | bytes 3538948
  645.8 12.1 %all-to-all-start.2 = ((f32[32,1,808]{2,1,0:T(1,128)}), f32[32,1,808]{2,1,0:T(1,128)S(1)}, u32[]{:S(2)}, u32[]{:S(2)}) async-start(f32[32,1,808]{2,1,0:T(1,128)} %copy.52), calls=%async_computation.2 | async-start | bytes 229376 | tf_op jit(solution)/shard_map/all_to_all | solution.py:1241
  657.9 28.3 %all-to-all-start.4 = ((bf16[4,48,1920]{2,1,0:T(8,128)(2,1)}), bf16[4,48,1920]{2,1,0:T(8,128)(2,1)S(1)}, u32[]{:S(2)}, u32[]{:S(2)}) async-start(bf16[4,48,1920]{2,1,0:T(8,128)(2,1)} %shard_map.248), calls=%async_computation.4 | async-start | bytes 1474560 | tf_op jit(solution)/shard_map/all_to_all | solution.py:796
  (41 other events, 91.9 us)
Sparse Core Ops, SparseCore 0:
  11.5 90.8 all-gather.2
  105.8 131.5 all-gather.4

commit v7 on v6

--- a/solution.py
+++ b/solution.py
@@ -17,7 +17,7 @@
 PROJ_X = 3456
 BLOCK = 512
 BLOCK_HEADS = BLOCK // HEAD_DIM
-PAIRS = 2
+PAIRS = 3
 PAIR_LANES = 128 * PAIRS
 VMEM = 56 * 1024 * 1024
 F32 = jnp.float32

time: 707 us -> 706 us (level)
  no operation moved by 1% of the time
where the time goes in v7:
time: 706 us; the launch traced here: 694 us
  Pallas kernels  294 us (42%)
  waiting for transfers between devices  153 us (22%)
  starting transfers between devices  95.3 us (13%)
  local copies, waits for them, and re-layouts  65.3 us (9%)
  other arithmetic  43.9 us (6%)
  matrix products  24.5 us (3%)
  between operations  17.4 us (2%)
    pallas_call x31, Pallas kernels, call(): pl.pallas_call(run, grid_spec=pltpu.PrefetchScalarGridSpec(num_scalar_pre...  294 us
    all_gather x1, waiting for transfers between devices, shards(): lax.all_gather(columns(in_weight[:, INNER:], PROJ_X), EVERY, axis=0, tile...  59.2 us
    all_to_all x4, starting transfers between devices, third(): self.got_z = lax.all_to_all(self.parts, 'z', 0, 0, tiled=True)  33.8 us
    ppermute x6, waiting for transfers between devices, entering(): arrived = meanwhile(sent, lax.ppermute(sent, 'z', pairs))  33 us
    unnamed x125, local copies, waits for them, and re-layouts  28.2 us
    all_gather x1, waiting for transfers between devices, shards(): stacked = lax.all_gather(stacked, EVERY, axis=1, tiled=True)  27.3 us
    dot_general x3, matrix products, mm(): return jnp.dot(left, right, preferred_element_type=F32)  24.5 us
    ppermute x16, starting transfers between devices, across(): lax.ppermute(array, axis, [(i, i ^ by) for i in range(lax.axis_size(axis))])  20.2 us
  transfers between devices with their start and end apart: 46, of which 13 were waited for; matrix products, arithmetic and copies ran while one was open for 15% of the time, Pallas kernels for 38%

profile of v7, /device:TPU:0, one launch (start us, length us, event | category | flops | bytes accessed | tf_op | source)
XLA Modules:
  0.0 693.7 jit_solution(18114338215750089553)
XLA Ops:
  12.0 4.9 collective-permute-start
  19.3 4.9 all-to-all-start
  39.1 3.9 shard_map.203
  43.0 59.2 %all-gather.3.cloned.1.call-done.refs_2_ = bf16[1536,3456]{1,0:T(8,128)(2,1)} async-done(((bf16[48,3456]{1,0:T(8,128)(2,1)}), bf16[1536,3456]{1,0:T(8,128)(2,1)}) %all-gather.3.cloned.1.call-update) | async-done | bytes 10616848 | tf_op jit(solution)/shard_map/all_gather | solution.py:851
  102.2 11.8 %convolution_convert_fusion.refs_0_.refs_1_.refs_4_.refs_17_ = bf16[528,3456]{1,0:T(8,128)(2,1)} fusion(bf16[528,1536]{1,0:T(8,128)(2,1)} %get-tuple-element.84, bf16[1536,3456]{1,0:T(8,128)(2,1)} %all-gather.3.cloned.1.call-done.refs_2_), kind=kOutput, calls=%fused_computation | convolution fusion | flops 5607512064 | bytes 15888384 | tf_op jit(solution)/shard_map/dot_general | solution.py:105
  114.6 4.5 shard_map.204
  120.6 12.4 %shard_map.205 = (f32[512,3072]{1,0:T(8,128)}, f32[512,3072]{1,0:T(8,128)}, f32[2,128,1536]{2,1,0:T(8,128)}, f32[2,8,1536]{2,1,0:T(8,128)}) custom-call(bf16[528,3456]{1,0:T(8,128)(2,1)} %convolution_convert_fusion.refs_0_.refs_1_.refs_4_.refs_17_, f32[8,3072]{1,0:T(8,128)} %slice.174.refs_1_.refs_5_, f32[1,3072]{1,0:T(1,128)} %slice.175.refs_2_, ...), custom_call_target="tpu_custom_call" | custom-call | flops 12000000000 | bytes 36000000 | tf_op jit(solution)/shard_map/pallas_call | solution.py:43
  137.4 12.7 %shard_map.206.refs_1_.refs_0_ = f32[512,1536]{1,0:T(8,128)} custom-call(f32[512,3072]{1,0:T(8,128)} %get-tuple-element.89.refs_0_.refs_5_.refs_1_, f32[512,128]{1,0:T(8,128)} %get-tuple-element.86.refs_5_.refs_1_.refs_2_.refs_11_, f32[1,3072]{1,0:T(1,128)} %broadcast_in_dim_reshape.3.refs_2_.refs_11_.refs_12_, f32[512,512]{1,0:T(8,128)} %get-tuple-element.90.refs_3_, ...), custom_call_target="tpu_custom_call" | custom-call | flops 12000000000 | bytes 36000000 | tf_op jit(solution)/shard_map/pallas_call | solution.py:43
  151.1 12.0 %collective-permute-done.2.refs_0_ = f32[128,1536]{1,0:T(8,128)S(1)} collective-permute-done((f32[128,1536]{1,0:T(8,128)S(1)}, f32[128,1536]{1,0:T(8,128)S(1)}, u32[]{:S(2)}, u32[]{:S(2)}) %collective-permute-start.2) | collective-permute-done | bytes 786464 | tf_op jit(solution)/shard_map/ppermute | solution.py:517
  163.9 2.1 fusion.7.refs_6_
  166.0 3.5 collective-permute-start.3
  169.6 12.8 %shard_map.208.refs_1_ = f32[512,1536]{1,0:T(8,128)} custom-call(f32[512,3072]{1,0:T(8,128)} %get-tuple-element.89.refs_0_.refs_5_.refs_1_, f32[512,128]{1,0:T(8,128)} %get-tuple-element.86.refs_5_.refs_1_.refs_2_.refs_11_, f32[1,3072]{1,0:T(1,128)} %broadcast_in_dim_reshape.3.refs_2_.refs_11_.refs_12_, f32[512,512]{1,0:T(8,128)} %get-tuple-element.90.refs_3_, ...), custom_call_target="tpu_custom_call" | custom-call | flops 12000000000 | bytes 36000000 | tf_op jit(solution)/shard_map/pallas_call | solution.py:43
  182.4 19.7 %collective-permute-done.3.refs_0_ = f32[128,1536]{1,0:T(8,128)S(1)} collective-permute-done((f32[128,1536]{1,0:T(8,128)}, f32[128,1536]{1,0:T(8,128)S(1)}, u32[]{:S(2)}, u32[]{:S(2)}) %collective-permute-start.3) | collective-permute-done | bytes 786464 | tf_op jit(solution)/shard_map/ppermute | solution.py:565
  203.0 2.2 multiply_add_fusion.6
  206.8 2.5 multiply_add_fusion.5
  210.0 27.3 %all-gather.5.cloned.1.call-done.refs_1_ = bf16[4,1536,1536]{2,1,0:T(8,128)(2,1)} async-done(((bf16[4,48,1536]{2,1,0:T(8,128)(2,1)}), bf16[4,1536,1536]{2,1,0:T(8,128)(2,1)}) %all-gather.5.cloned.1.call-update) | async-done | bytes 18874384 | tf_op jit(solution)/shard_map/all_gather | solution.py:856
  237.3 6.7 fusion.3.refs_2_.refs_3_
  244.0 6.0 fusion.2.refs_1_.refs_2_
  251.5 2.3 select_bitcast_fusion.1
  259.6 12.8 %shard_map.212.refs_1_.refs_4_ = f32[512,3072]{1,0:T(8,128)} custom-call(bf16[512,1536]{1,0:T(8,128)(2,1)} %refs_2_.2, bf16[4,1536,1536]{2,1,0:T(8,128)(2,1)} %all-gather.5.cloned.1.call-done.refs_1_, f32[128,1536]{1,0:T(8,128)} %get-tuple-element.178.refs_2_), custom_call_target="tpu_custom_call" | custom-call | flops 7000000000 | bytes 21000000 | tf_op jit(solution)/shard_map/pallas_call | solution.py:43
  274.4 3.6 multiply_add_fusion
  278.0 32.0 %shard_map.214 = (bf16[512,3072]{1,0:T(8,128)(2,1)}, bf16[3072,512]{1,0:T(8,128)(2,1)}, bf16[512,3072]{1,0:T(8,128)(2,1)}, f32[512,3072]{1,0:T(8,128)}, f32[2,12...) custom-call(f32[512,1536]{1,0:T(8,128)} %shard_map.206.refs_1_.refs_0_, ...), custom_call_target="tpu_custom_call" | custom-call | flops 31000000512 | bytes 93000000 | tf_op jit(solution)/shard_map/pallas_call | solution.py:43
  311.5 2.8 constant_dynamic-slice_fusion
  316.3 1.9 collective-permute-done.7
  319.0 7.6 %shard_map.215 = (bf16[384,1536]{1,0:T(8,128)(2,1)}, f32[384,1536]{1,0:T(8,128)}) custom-call(s32[3]{0:T(128)} %pad_add_fusion.refs_0_, bf16[2,2,384,512]{3,2,1,0:T(8,128)(2,1)} %bitcast.131, bf16[2,2,384,512]{3,2,1,0:T(8,128)(2,1)} %bitcast.132, bf16[2,384,512]{2,1,0:T(8,128)(2,1)} %bitcast.144, bf16[2,384,512]{2,1,0:T(8,128)(2,1)} %bitcast.145, ...), custom_call_target="tpu_custom_call" | custom-call | flops 2949120000 | bytes 8847360 | tf_op jit(solution)/shard_map/pallas_call | solution.py:43
  326.6 7.6 %shard_map.216 = (bf16[384,1536]{1,0:T(8,128)(2,1)}, f32[384,1536]{1,0:T(8,128)}) custom-call(s32[3]{0:T(128)} %pad_add_fusion.refs_0_, bf16[2,2,4,2,48,512]{5,4,3,2,1,0:T(8,128)(2,1)} %bitcast.133, bf16[2,2,4,2,48,512]{5,4,3,2,1,0:T(8,128)(2,1)} %bitcast.134, bf16[8,2,48,512]{3,2,1,0:T(8,128)(2,1)} %bitcast.146, bf16[8,2,48,512]{3,2,1,0:T(8,128)(2,1)} %bitcast.147, ...), custom_call_target="tpu_custom_call" | custom-call | flops 2949120000 | bytes 8847360 | tf_op jit(solution)/shard_map/pallas_call | solution.py:43
  340.0 7.6 %shard_map.219 = (bf16[768,768]{1,0:T(8,128)(2,1)}, f32[768,768]{1,0:T(8,128)}) custom-call(s32[3]{0:T(128)} %pad_add_fusion.refs_0_, bf16[2,2,4,2,96,512]{5,4,3,2,1,0:T(8,128)(2,1)} %bitcast.157, bf16[2,2,4,2,96,512]{5,4,3,2,1,0:T(8,128)(2,1)} %bitcast.158, bf16[8,2,96,512]{3,2,1,0:T(8,128)(2,1)} %bitcast.161, bf16[8,2,96,512]{3,2,1,0:T(8,128)(2,1)} %bitcast.162, ...), custom_call_target="tpu_custom_call" | custom-call | flops 2949120000 | bytes 8847360 | tf_op jit(solution)/shard_map/pallas_call | solution.py:43
  348.9 7.5 %shard_map.218 = (bf16[768,768]{1,0:T(8,128)(2,1)}, f32[768,768]{1,0:T(8,128)}) custom-call(s32[3]{0:T(128)} %pad_add_fusion.refs_0_, bf16[2,2,768,512]{3,2,1,0:T(8,128)(2,1)} %bitcast.159, bf16[2,2,768,512]{3,2,1,0:T(8,128)(2,1)} %bitcast.160, bf16[2,768,512]{2,1,0:T(8,128)(2,1)} %bitcast.163, bf16[2,768,512]{2,1,0:T(8,128)(2,1)} %bitcast.164, ...), custom_call_target="tpu_custom_call" | custom-call | flops 2949120000 | bytes 8847360 | tf_op jit(solution)/shard_map/pallas_call | solution.py:43
  359.2 11.4 %collective-permute-start.13 = (f32[128,1536]{1,0:T(8,128)S(1)}, f32[128,1536]{1,0:T(8,128)S(1)}, u32[]{:S(2)}, u32[]{:S(2)}) collective-permute-start(f32[128,1536]{1,0:T(8,128)S(1)} %multiply_add_fusion.3.refs_10_.refs_9_), channel_id=1, source_target_pairs={{4,2},{5,3},{12,10},{13,11},{20,18},{21,19},{28,26},{29,27}} | collective-permute-start | bytes 2359304 | tf_op jit(solution)/shard_map/ppermute | solution.py:565
  371.7 17.9 %shard_map.221 = (f32[512,1536]{1,0:T(8,128)}, f32[512,512]{1,0:T(8,128)}) custom-call(f32[512,3072]{1,0:T(8,128)} %get-tuple-element.89.refs_0_.refs_5_.refs_1_, f32[512,3072]{1,0:T(8,128)} %get-tuple-element.98.refs_1_.refs_2_, f32[512,128]{1,0:T(8,128)} %get-tuple-element.86.refs_5_.refs_1_.refs_2_.refs_11_, f32[512,512]{1,0:T(8,128)} %get-tuple-element.99.refs_3_, ...), custom_call_target="tpu_custom_call" | custom-call | flops 17999998976 | bytes 54000000 | tf_op jit(solution)/shard_map/pallas_call | solution.py:43
  389.6 5.9 shard_map.225
  402.1 19.4 %shard_map.223 = (f32[512,1536]{1,0:T(8,128)}, f32[512,512]{1,0:T(8,128)}, f32[512,256]{1,0:T(8,128)}) custom-call(f32[512,3072]{1,0:T(8,128)} %get-tuple-element.89.refs_0_.refs_5_.refs_1_, f32[512,3072]{1,0:T(8,128)} %get-tuple-element.98.refs_1_.refs_2_, f32[512,128]{1,0:T(8,128)} %get-tuple-element.86.refs_5_.refs_1_.refs_2_.refs_11_, ...), custom_call_target="tpu_custom_call" | custom-call | flops 17999998976 | bytes 54000000 | tf_op jit(solution)/shard_map/pallas_call | solution.py:43
  421.5 13.3 %collective-permute-done.14.refs_0_ = f32[128,1536]{1,0:T(8,128)S(1)} collective-permute-done((f32[128,1536]{1,0:T(8,128)S(1)}, f32[128,1536]{1,0:T(8,128)S(1)}, u32[]{:S(2)}, u32[]{:S(2)}) %collective-permute-start.14) | collective-permute-done | bytes 786464 | tf_op jit(solution)/shard_map/ppermute | solution.py:565
  437.1 2.5 select_bitcast_fusion
  440.6 4.2 shard_map.226.refs_1_
  444.8 11.5 %all-to-all-start.1 = ((f32[4,48,3072]{2,1,0:T(8,128)}), f32[4,48,3072]{2,1,0:T(8,128)S(1)}, u32[]{:S(2)}, u32[]{:S(2)}) async-start(f32[4,48,3072]{2,1,0:T(8,128)} %shard_map.226.refs_1_), calls=%async_computation.1 | async-start | bytes 4718592 | tf_op jit(solution)/shard_map/all_to_all | solution.py:796
  456.3 5.9 shard_map.227
  463.4 2.7 maximum_select_fusion.1.refs_8_
  467.4 17.6 %shard_map.229 = (bf16[512,1536]{1,0:T(8,128)(2,1)}, f32[32,1536]{1,0:T(8,128)}, f32[8,1536]{1,0:T(8,128)}, f32[512,128]{1,0:T(8,128)}, f32[512,128]{1,0:T(8,128)}, /*index=5*/f32[8,128]{1,0:T(8,128)}) custom-call(f32[512,1536]{1,0:T(8,128)} %get-tuple-element.112.refs_1_.refs_0_, f32[512,3072]{1,0:T(8,128)} %get-tuple-element.89.refs_0_.refs_5_.refs_1_, ...), custom_call_target="tpu_custom_call" | custom-call | flops 14000000000 | bytes 42000000 | tf_op jit(solution)/shard_map/pallas_call | solution.py:43
  493.2 2.7 copy.78
  496.0 7.0 %collective-permute-done.23 = f32[16,1536]{1,0:T(8,128)} collective-permute-done((f32[16,1536]{1,0:T(8,128)}, f32[16,1536]{1,0:T(8,128)}, u32[]{:S(2)}, u32[]{:S(2)}) %collective-permute-start.23) | collective-permute-done | bytes 98336 | tf_op jit(solution)/shard_map/ppermute | solution.py:523
  504.6 4.1 shard_map.230.refs_9_
  510.7 7.9 %all-to-all-start.5 = ((f32[4,96,1536]{2,1,0:T(8,128)}), f32[4,96,1536]{2,1,0:T(8,128)}, u32[]{:S(2)}, u32[]{:S(2)}) async-start(f32[4,96,1536]{2,1,0:T(8,128)} %shard_map.230.refs_9_), calls=%async_computation.5 | async-start | bytes 4718592 | tf_op jit(solution)/shard_map/all_to_all | solution.py:796
  518.6 5.3 shard_map.232
  523.9 2.5 collective-permute-start.31
  526.4 5.3 shard_map.231
  532.3 18.1 %shard_map.233 = (f32[16,128]{1,0:T(8,128)}, bf16[512,1920]{1,0:T(8,128)(2,1)}, f32[32,1920]{1,0:T(8,128)}, f32[8,1920]{1,0:T(8,128)}, f32[512,128]{1,0:T(8,128)}, /*index=5*/f32[512,128]{1,0:T(8,128)}, f32[8,128]{1,0:T(8,128)}) custom-call(f32[512,1536]{1,0:T(8,128)} %get-tuple-element.113.refs_1_.refs_0_, ...), custom_call_target="tpu_custom_call" | custom-call | flops 17999998976 | bytes 54000000 | tf_op jit(solution)/shard_map/pallas_call | solution.py:43
  552.7 10.9 %shard_map.234.refs_1_.refs_3_ = f32[512,1536]{1,0:T(8,128)} custom-call(bf16[512,3072]{1,0:T(8,128)(2,1)} %get-tuple-element.101.refs_5_.refs_0_, bf16[4,1536,1536]{2,1,0:T(8,128)(2,1)} %all-gather.5.cloned.1.call-done.refs_1_, f32[32,1920]{1,0:T(8,128)} %get-tuple-element.138.refs_2_.refs_9_), custom_call_target="tpu_custom_call" | custom-call | flops 10000000000 | bytes 30000000 | tf_op jit(solution)/shard_map/pallas_call | solution.py:43
  566.4 4.9 shard_map.236
  571.3 2.7 collective-permute-start.32
  576.1 5.8 collective-permute-done.32.refs_1_
  584.0 3.6 shard_map.237.refs_9_
  589.6 5.4 shard_map.239
  595.4 5.4 shard_map.238
  602.2 10.9 %all-to-all-start.3 = ((f32[4,48,1536]{2,1,0:T(8,128)}), f32[4,48,1536]{2,1,0:T(8,128)S(1)}, u32[]{:S(2)}, u32[]{:S(2)}) async-start(f32[4,48,1536]{2,1,0:T(8,128)} %shard_map.237.refs_9_), calls=%async_computation.3 | async-start | bytes 2359296 | tf_op jit(solution)/shard_map/all_to_all | solution.py:796
  613.1 12.1 %shard_map.240.refs_0_ = f32[512,1536]{1,0:T(8,128)} custom-call(bf16[512,1536]{1,0:T(8,128)(2,1)} %get-tuple-element.167.refs_0_, bf16[512,1920]{1,0:T(8,128)(2,1)} %get-tuple-element.165.refs_1_, bf16[1536,3456]{1,0:T(8,128)(2,1)} %all-gather.3.cloned.1.call-done.refs_2_, f32[512,1536]{1,0:T(8,128)} %shard_map.234.refs_1_.refs_3_, ...), custom_call_target="tpu_custom_call" | custom-call | flops 10000000000 | bytes 30000000 | tf_op jit(solution)/shard_map/pallas_call | solution.py:43
  625.2 5.6 shard_map.241
  631.9 5.1 shard_map.242
  644.6 4.5 all-to-all-start.2
  649.9 3.6 shard_map.248
  653.5 3.1 all-to-all-done.2
  656.7 3.5 all-to-all-start.4
  660.2 12.8 %shard_map.243.refs_1_ = bf16[512,1536]{1,0:T(8,128)(2,1)} custom-call(bf16[512,3072]{1,0:T(8,128)(2,1)} %get-tuple-element.96.refs_0_, bf16[4,1536,1536]{2,1,0:T(8,128)(2,1)} %all-gather.5.cloned.1.call-done.refs_1_, bf16[512,1536]{1,0:T(8,128)(2,1)} %refs_2_.3, bf16[4,48,1024]{2,1,0:T(8,128)(2,1)} %get-tuple-element.148.refs_3_.refs_1_, ...), custom_call_target="tpu_custom_call" | custom-call | flops 12999999488 | bytes 39000000 | tf_op jit(solution)/shard_map/pallas_call | solution.py:43
  673.0 2.7 reduce_sum.79
  (311 shorter events, 113.8 us)
Async XLA Ops:
  7.2 95.0 %all-gather.3.cloned.1.call-start = ((), (), s32[]{:S(2)}) async-start(), calls=%async_computation.6 | async-start | bytes 10948608 | tf_op jit(solution)/shard_map/all_gather | solution.py:851
  9.1 228.2 %all-gather.5.cloned.1.call-start = ((), (), s32[]{:S(2)}) async-start(), calls=%async_computation.7 | async-start | bytes 19464192 | tf_op jit(solution)/shard_map/all_gather | solution.py:856
  10.2 14.0 %copy-start.56 = (f32[48]{0:T(128)S(1)}, f32[48]{0:T(128)}, u32[]{:S(2)}) copy-start(f32[48]{0:T(128)} %param.19) | copy-start | bytes 580
  10.2 14.5 %copy-start.57 = (f32[48]{0:T(128)S(1)}, f32[48]{0:T(128)}, u32[]{:S(2)}) copy-start(f32[48]{0:T(128)} %param.20) | copy-start | bytes 580
  10.2 15.1 %copy-start.46 = (s32[1,3]{1,0:T(1,128)S(1)}, s32[1,3]{1,0:T(1,128)}, u32[]{:S(2)}) copy-start(s32[1,3]{1,0:T(1,128)} %param.14) | copy-start | bytes 40
  10.2 18.9 %copy-start.51 = (f32[48]{0:T(128)S(1)}, f32[48]{0:T(128)}, u32[]{:S(2)}) copy-start(f32[48]{0:T(128)} %param.21) | copy-start | bytes 580
  12.0 26.5 %collective-permute-start = (bf16[16,1536]{1,0:T(8,128)(2,1)S(1)}, bf16[16,1536]{1,0:T(8,128)(2,1)S(1)}, u32[]{:S(2)}, u32[]{:S(2)}) collective-permute-start(bf16[16,1536]{1,0:T(8,128)(2,1)S(1)} %slice.136), channel_id=1, source_target_pairs={{0,1},{1,2},{2,3},{3,4},{4,5},{5,6},{6,7},{8,9},{9,10},{10,11},{11... | collective-permute-start | bytes 147464 | tf_op jit(solution)/shard_map/ppermute | solution.py:523
  19.3 15.5 %all-to-all-start = ((bf16[32,2,332]{2,1,0:T(2,128)(2,1)}), bf16[32,2,332]{2,1,0:T(2,128)(2,1)S(1)}, u32[]{:S(2)}, u32[]{:S(2)}) async-start(bf16[32,2,332]{2,1,0:T(2,128)(2,1)} %reshape.412), calls=%async_computation | async-start | bytes 98304 | tf_op jit(solution)/shard_map/all_to_all | solution.py:826
  133.9 16.3 %collective-permute-start.1 = (f32[8,1536]{1,0:T(8,128)S(1)}, f32[8,1536]{1,0:T(8,128)S(1)}, u32[]{:S(2)}, u32[]{:S(2)}) collective-permute-start(f32[8,1536]{1,0:T(8,128)S(1)} %dynamic-slice_bitcast_fusion.2), channel_id=1, source_target_pairs={{0,1},{1,0},{2,3},{3,2},{4,5},{5,4},{6,7},{7,6},{8,9},{9,8},{10,11... | collective-permute-start | bytes 147464 | tf_op jit(solution)/shard_map/ppermute | solution.py:517
  136.6 26.5 %collective-permute-start.2 = (f32[128,1536]{1,0:T(8,128)S(1)}, f32[128,1536]{1,0:T(8,128)S(1)}, u32[]{:S(2)}, u32[]{:S(2)}) collective-permute-start(f32[128,1536]{1,0:T(8,128)S(1)} %dynamic-slice_bitcast_fusion.1.refs_6_), channel_id=1, source_target_pairs={{0,1},{1,0},{2,3},{3,2},{4,5},{5,4},{6,7},{7,6},{8,9},{9,8},{10,11... | collective-permute-start | bytes 2359304 | tf_op jit(solution)/shard_map/ppermute | solution.py:517
  151.1 12.8 %copy-start.8 = (f32[2,128,1536]{2,1,0:T(8,128)S(1)}, f32[2,128,1536]{2,1,0:T(8,128)}, u32[]{:S(2)}) copy-start(f32[2,128,1536]{2,1,0:T(8,128)} %get-tuple-element.93) | copy-start | bytes 4718596
  166.0 36.0 %collective-permute-start.3 = (f32[128,1536]{1,0:T(8,128)}, f32[128,1536]{1,0:T(8,128)S(1)}, u32[]{:S(2)}, u32[]{:S(2)}) collective-permute-start(f32[128,1536]{1,0:T(8,128)} %fusion.7.refs_6_), channel_id=1, source_target_pairs={{0,2},{1,3},{8,10},{9,11},{16,18},{17,19},{24,26},{25,27}} | collective-permute-start | bytes 2359304 | tf_op jit(solution)/shard_map/ppermute | solution.py:565
  205.2 0.7 collective-permute-start.4
  209.3 40.8 %collective-permute-start.5 = (f32[128,1536]{1,0:T(8,128)}, f32[128,1536]{1,0:T(8,128)S(1)}, u32[]{:S(2)}, u32[]{:S(2)}) collective-permute-start(f32[128,1536]{1,0:T(8,128)} %get-tuple-element.173), channel_id=1, source_target_pairs={{4,6},{5,7},{12,14},{13,15},{20,22},{21,23},{28,30},{29,31}} | collective-permute-start | bytes 2359304 | tf_op jit(solution)/shard_map/ppermute | solution.py:565
  253.8 19.7 %collective-permute-start.6 = (f32[128,1536]{1,0:T(8,128)}, f32[128,1536]{1,0:T(8,128)S(1)}, u32[]{:S(2)}, u32[]{:S(2)}) collective-permute-start(f32[128,1536]{1,0:T(8,128)} %get-tuple-element.178.refs_2_), channel_id=1, source_target_pairs={{0,1},{1,0},{2,3},{3,2},{4,5},{5,4},{6,7},{7,6},{8,9},{9,8},{10,11... | collective-permute-start | bytes 2359304 | tf_op jit(solution)/shard_map/ppermute | solution.py:517
  278.0 32.1 %copy-start = (bf16[1536,512]{1,0:T(8,128)(2,1)S(1)}, bf16[1536,512]{1,0:T(8,128)(2,1)}, u32[]{:S(2)}) copy-start(bf16[1536,512]{1,0:T(8,128)(2,1)} %get-tuple-element.97) | copy-start | bytes 4718596
  310.0 8.2 %collective-permute-start.9 = (bf16[512,3072]{1,0:T(8,128)(2,1)}, bf16[512,3072]{1,0:T(8,128)(2,1)}, u32[]{:S(2)}, u32[]{:S(2)}) collective-permute-start(bf16[512,3072]{1,0:T(8,128)(2,1)} %get-tuple-element.101.refs_5_.refs_0_), channel_id=1, source_target_pairs={{0,8},{8,0},{1,9},{9,1},{2,10},{10,2},{3,11},{11,3},{4,12},{12,4},... | collective-permute-start | bytes 9437192 | tf_op jit(solution)/shard_map/ppermute | solution.py:517
  311.0 7.1 %collective-permute-start.7 = (bf16[768,512]{1,0:T(8,128)(2,1)}, bf16[768,512]{1,0:T(8,128)(2,1)S(1)}, u32[]{:S(2)}, u32[]{:S(2)}) collective-permute-start(bf16[768,512]{1,0:T(8,128)(2,1)} %bitcast.26), channel_id=1, source_target_pairs={{0,8},{8,0},{1,9},{9,1},{2,10},{10,2},{3,11},{11,3},{4,12},{12,4},... | collective-permute-start | bytes 2359304 | tf_op jit(solution)/shard_map/ppermute | solution.py:517
  311.5 27.4 %collective-permute-start.12 = (bf16[512,1536]{1,0:T(8,128)(2,1)}, bf16[512,1536]{1,0:T(8,128)(2,1)}, u32[]{:S(2)}, u32[]{:S(2)}) collective-permute-start(bf16[512,1536]{1,0:T(8,128)(2,1)} %refs_2_.2), channel_id=1, source_target_pairs={{0,8},{8,0},{1,9},{9,1},{2,10},{10,2},{3,11},{11,3},{4,12},{12,4},... | collective-permute-start | bytes 4718600 | tf_op jit(solution)/shard_map/ppermute | solution.py:517
  314.3 24.6 %collective-permute-start.11 = (bf16[1536,512]{1,0:T(8,128)(2,1)}, bf16[1536,512]{1,0:T(8,128)(2,1)S(1)}, u32[]{:S(2)}, u32[]{:S(2)}) collective-permute-start(bf16[1536,512]{1,0:T(8,128)(2,1)} %bitcast.33), channel_id=1, source_target_pairs={{0,8},{8,0},{1,9},{9,1},{2,10},{10,2},{3,11},{11,3},{4,12},{12,4},... | collective-permute-start | bytes 4718600 | tf_op jit(solution)/shard_map/ppermute | solution.py:517
  314.8 19.7 %collective-permute-start.8 = (f32[128,1536]{1,0:T(8,128)S(1)}, f32[128,1536]{1,0:T(8,128)}, u32[]{:S(2)}, u32[]{:S(2)}) collective-permute-start(f32[128,1536]{1,0:T(8,128)S(1)} %dynamic-slice_bitcast_fusion.refs_7_), channel_id=1, source_target_pairs={{0,1},{1,0},{2,3},{3,2},{4,5},{5,4},{6,7},{7,6},{8,9},{9,8},{10,11... | collective-permute-start | bytes 2359304 | tf_op jit(solution)/shard_map/ppermute | solution.py:517
  336.0 21.0 %collective-permute-start.10 = (f32[128,1536]{1,0:T(8,128)S(1)}, f32[128,1536]{1,0:T(8,128)S(1)}, u32[]{:S(2)}, u32[]{:S(2)}) collective-permute-start(f32[128,1536]{1,0:T(8,128)S(1)} %fusion.6.refs_7_), channel_id=1, source_target_pairs={{6,4},{7,5},{14,12},{15,13},{22,20},{23,21},{30,28},{31,29}} | collective-permute-start | bytes 2359304 | tf_op jit(solution)/shard_map/ppermute | solution.py:565
  336.7 52.8 %collective-permute-start.17 = (bf16[384,1536]{1,0:T(8,128)(2,1)}, bf16[384,1536]{1,0:T(8,128)(2,1)}, u32[]{:S(2)}, u32[]{:S(2)}) collective-permute-start(bf16[384,1536]{1,0:T(8,128)(2,1)} %get-tuple-element.105.refs_4_), channel_id=1, source_target_pairs={{0,1},{1,0},{2,3},{3,2},{4,5},{5,4},{6,7},{7,6},{8,9},{9,8},{10,11... | collective-permute-start | bytes 3538952 | tf_op jit(solution)/shard_map/ppermute | solution.py:587
  337.6 52.0 %collective-permute-start.16 = (bf16[384,1536]{1,0:T(8,128)(2,1)}, bf16[384,1536]{1,0:T(8,128)(2,1)}, u32[]{:S(2)}, u32[]{:S(2)}) collective-permute-start(bf16[384,1536]{1,0:T(8,128)(2,1)} %get-tuple-element.104.refs_3_), channel_id=1, source_target_pairs={{0,16},{16,0},{1,17},{17,1},{2,18},{18,2},{3,19},{19,3},{4,20},{20... | collective-permute-start | bytes 3538952 | tf_op jit(solution)/shard_map/ppermute | solution.py:587
  347.6 108.7 %collective-permute-start.21 = (bf16[768,768]{1,0:T(8,128)(2,1)}, bf16[768,768]{1,0:T(8,128)(2,1)}, u32[]{:S(2)}, u32[]{:S(2)}) collective-permute-start(bf16[768,768]{1,0:T(8,128)(2,1)} %get-tuple-element.110.refs_4_), channel_id=1, source_target_pairs={{0,1},{1,0},{2,3},{3,2},{4,5},{5,4},{6,7},{7,6},{8,9},{9,8},{10,11... | collective-permute-start | bytes 3538952 | tf_op jit(solution)/shard_map/ppermute | solution.py:587
  356.4 99.9 %collective-permute-start.20 = (bf16[768,768]{1,0:T(8,128)(2,1)}, bf16[768,768]{1,0:T(8,128)(2,1)}, u32[]{:S(2)}, u32[]{:S(2)}) collective-permute-start(bf16[768,768]{1,0:T(8,128)(2,1)} %get-tuple-element.109.refs_3_), channel_id=1, source_target_pairs={{0,16},{16,0},{1,17},{17,1},{2,18},{18,2},{3,19},{19,3},{4,20},{20... | collective-permute-start | bytes 3538952 | tf_op jit(solution)/shard_map/ppermute | solution.py:587
  359.2 12.5 %copy-start.19 = (f32[128,1536]{1,0:T(8,128)}, f32[128,1536]{1,0:T(8,128)S(1)}, u32[]{:S(2)}) copy-start(f32[128,1536]{1,0:T(8,128)S(1)} %multiply_add_fusion.3.refs_10_.refs_9_) | copy-start | bytes 2359300
  359.2 38.5 %collective-permute-start.13 = (f32[128,1536]{1,0:T(8,128)S(1)}, f32[128,1536]{1,0:T(8,128)S(1)}, u32[]{:S(2)}, u32[]{:S(2)}) collective-permute-start(f32[128,1536]{1,0:T(8,128)S(1)} %multiply_add_fusion.3.refs_10_.refs_9_), channel_id=1, source_target_pairs={{4,2},{5,3},{12,10},{13,11},{20,18},{21,19},{28,26},{29,27}} | collective-permute-start | bytes 2359304 | tf_op jit(solution)/shard_map/ppermute | solution.py:565
  395.5 45.1 %collective-permute-start.18 = (bf16[4,48,1536]{2,1,0:T(8,128)(2,1)}, bf16[4,48,1536]{2,1,0:T(8,128)(2,1)}, u32[]{:S(2)}, u32[]{:S(2)}) collective-permute-start(bf16[4,48,1536]{2,1,0:T(8,128)(2,1)} %get-tuple-element.116), channel_id=1, source_target_pairs={{0,1},{1,0},{2,3},{3,2},{4,5},{5,4},{6,7},{7,6},{8,9},{9,8},{10,11... | collective-permute-start | bytes 1769480 | tf_op jit(solution)/shard_map/ppermute | solution.py:587
  396.3 44.3 %collective-permute-start.19 = (bf16[4,48,1536]{2,1,0:T(8,128)(2,1)}, bf16[4,48,1536]{2,1,0:T(8,128)(2,1)}, u32[]{:S(2)}, u32[]{:S(2)}) collective-permute-start(bf16[4,48,1536]{2,1,0:T(8,128)(2,1)} %get-tuple-element.118), channel_id=1, source_target_pairs={{0,16},{16,0},{1,17},{17,1},{2,18},{18,2},{3,19},{19,3},{4,20},{20... | collective-permute-start | bytes 1769480 | tf_op jit(solution)/shard_map/ppermute | solution.py:587
  400.8 34.0 %collective-permute-start.14 = (f32[128,1536]{1,0:T(8,128)S(1)}, f32[128,1536]{1,0:T(8,128)S(1)}, u32[]{:S(2)}, u32[]{:S(2)}) collective-permute-start(f32[128,1536]{1,0:T(8,128)S(1)} %get-tuple-element.171.refs_10_), channel_id=1, source_target_pairs={{2,0},{3,1},{10,8},{11,9},{18,16},{19,17},{26,24},{27,25}} | collective-permute-start | bytes 2359304 | tf_op jit(solution)/shard_map/ppermute | solution.py:565
  439.6 22.6 %collective-permute-start.15 = (f32[128,1536]{1,0:T(8,128)S(1)}, f32[128,1536]{1,0:T(8,128)}, u32[]{:S(2)}, u32[]{:S(2)}) collective-permute-start(f32[128,1536]{1,0:T(8,128)S(1)} %get-tuple-element.176.refs_4_.refs_9_), channel_id=1, source_target_pairs={{0,1},{1,0},{2,3},{3,2},{4,5},{5,4},{6,7},{7,6},{8,9},{9,8},{10,11... | collective-permute-start | bytes 2359304 | tf_op jit(solution)/shard_map/ppermute | solution.py:517
  444.8 64.4 %all-to-all-start.1 = ((f32[4,48,3072]{2,1,0:T(8,128)}), f32[4,48,3072]{2,1,0:T(8,128)S(1)}, u32[]{:S(2)}, u32[]{:S(2)}) async-start(f32[4,48,3072]{2,1,0:T(8,128)} %shard_map.226.refs_1_), calls=%async_computation.1 | async-start | bytes 4718592 | tf_op jit(solution)/shard_map/all_to_all | solution.py:796
  467.4 17.7 %copy-start.32 = (bf16[4,96,768]{2,1,0:T(8,128)(2,1)S(1)}, bf16[4,96,768]{2,1,0:T(8,128)(2,1)}, u32[]{:S(2)}) copy-start(bf16[4,96,768]{2,1,0:T(8,128)(2,1)} %get-tuple-element.119.refs_2_) | copy-start | bytes 1769476
  467.4 18.9 %copy-start.31 = (bf16[4,96,768]{2,1,0:T(8,128)(2,1)S(1)}, bf16[4,96,768]{2,1,0:T(8,128)(2,1)}, u32[]{:S(2)}) copy-start(bf16[4,96,768]{2,1,0:T(8,128)(2,1)} %get-tuple-element.120.refs_3_) | copy-start | bytes 1769476
  467.4 22.4 %copy-start.39 = (f32[16,3072]{1,0:T(8,128)S(1)}, f32[16,3072]{1,0:T(8,128)}, u32[]{:S(2)}) copy-start(f32[16,3072]{1,0:T(8,128)} %get-tuple-element.153) | copy-start | bytes 589828
  485.0 33.6 %collective-permute-start.22 = (bf16[512,1536]{1,0:T(8,128)(2,1)}, bf16[512,1536]{1,0:T(8,128)(2,1)}, u32[]{:S(2)}, u32[]{:S(2)}) collective-permute-start(bf16[512,1536]{1,0:T(8,128)(2,1)} %get-tuple-element.129.refs_5_), channel_id=1, source_target_pairs={{0,8},{8,0},{1,9},{9,1},{2,10},{10,2},{3,11},{11,3},{4,12},{12,4},... | collective-permute-start | bytes 4718600 | tf_op jit(solution)/shard_map/ppermute | solution.py:517
  485.1 19.5 %collective-permute-start.25 = (bf16[4,96,768]{2,1,0:T(8,128)(2,1)S(1)}, bf16[4,96,768]{2,1,0:T(8,128)(2,1)}, u32[]{:S(2)}, u32[]{:S(2)}) collective-permute-start(bf16[4,96,768]{2,1,0:T(8,128)(2,1)S(1)} %copy-done.32), channel_id=1, source_target_pairs={{0,1},{1,0},{2,3},{3,2},{4,5},{5,4},{6,7},{7,6},{8,9},{9,8},{10,11... | collective-permute-start | bytes 1769480 | tf_op jit(solution)/shard_map/ppermute | solution.py:587
  486.3 18.3 %collective-permute-start.26 = (bf16[4,96,768]{2,1,0:T(8,128)(2,1)S(1)}, bf16[4,96,768]{2,1,0:T(8,128)(2,1)}, u32[]{:S(2)}, u32[]{:S(2)}) collective-permute-start(bf16[4,96,768]{2,1,0:T(8,128)(2,1)S(1)} %copy-done.31), channel_id=1, source_target_pairs={{0,16},{16,0},{1,17},{17,1},{2,18},{18,2},{3,19},{19,3},{4,20},{20... | collective-permute-start | bytes 1769480 | tf_op jit(solution)/shard_map/ppermute | solution.py:587
  488.5 14.5 %collective-permute-start.23 = (f32[16,1536]{1,0:T(8,128)}, f32[16,1536]{1,0:T(8,128)}, u32[]{:S(2)}, u32[]{:S(2)}) collective-permute-start(f32[16,1536]{1,0:T(8,128)} %slice.162), channel_id=1, source_target_pairs={{1,0},{2,1},{3,2},{4,3},{5,4},{6,5},{7,6},{9,8},{10,9},{11,10},{12... | collective-permute-start | bytes 294920 | tf_op jit(solution)/shard_map/ppermute | solution.py:523
  493.2 9.8 %copy-start.40 = (f32[32,1536]{1,0:T(8,128)S(1)}, f32[32,1536]{1,0:T(8,128)}, u32[]{:S(2)}) copy-start(f32[32,1536]{1,0:T(8,128)} %get-tuple-element.130.refs_4_) | copy-start | bytes 589828
  504.5 14.0 %collective-permute-start.24 = (bf16[16,1536]{1,0:T(8,128)(2,1)}, bf16[16,1536]{1,0:T(8,128)(2,1)}, u32[]{:S(2)}, u32[]{:S(2)}) collective-permute-start(bf16[16,1536]{1,0:T(8,128)(2,1)} %get-tuple-element.168.refs_7_), channel_id=1, source_target_pairs={{0,8},{8,0},{1,9},{9,1},{2,10},{10,2},{3,11},{11,3},{4,12},{12,4},... | collective-permute-start | bytes 147464 | tf_op jit(solution)/shard_map/ppermute | solution.py:517
  510.7 91.5 %all-to-all-start.5 = ((f32[4,96,1536]{2,1,0:T(8,128)}), f32[4,96,1536]{2,1,0:T(8,128)}, u32[]{:S(2)}, u32[]{:S(2)}) async-start(f32[4,96,1536]{2,1,0:T(8,128)} %shard_map.230.refs_9_), calls=%async_computation.5 | async-start | bytes 4718592 | tf_op jit(solution)/shard_map/all_to_all | solution.py:796
  523.9 41.7 %collective-permute-start.31 = (bf16[384,768]{1,0:T(8,128)(2,1)}, bf16[384,768]{1,0:T(8,128)(2,1)S(1)}, u32[]{:S(2)}, u32[]{:S(2)}) collective-permute-start(bf16[384,768]{1,0:T(8,128)(2,1)} %get-tuple-element.136.refs_27_), channel_id=1, source_target_pairs={{0,1},{1,0},{2,3},{3,2},{4,5},{5,4},{6,7},{7,6},{8,9},{9,8},{10,11... | collective-permute-start | bytes 1769480 | tf_op jit(solution)/shard_map/ppermute | solution.py:587
  531.7 34.0 %collective-permute-start.30 = (bf16[384,768]{1,0:T(8,128)(2,1)}, bf16[384,768]{1,0:T(8,128)(2,1)}, u32[]{:S(2)}, u32[]{:S(2)}) collective-permute-start(bf16[384,768]{1,0:T(8,128)(2,1)} %get-tuple-element.135.refs_26_), channel_id=1, source_target_pairs={{0,16},{16,0},{1,17},{17,1},{2,18},{18,2},{3,19},{19,3},{4,20},{20... | collective-permute-start | bytes 1769480 | tf_op jit(solution)/shard_map/ppermute | solution.py:587
  551.3 13.6 %collective-permute-start.28 = (f32[16,1920]{1,0:T(8,128)S(1)}, f32[16,1920]{1,0:T(8,128)S(1)}, u32[]{:S(2)}, u32[]{:S(2)}) collective-permute-start(f32[16,1920]{1,0:T(8,128)S(1)} %slice.164), channel_id=1, source_target_pairs={{1,0},{2,1},{3,2},{4,3},{5,4},{6,5},{7,6},{9,8},{10,9},{11,10},{12... | collective-permute-start | bytes 368648 | tf_op jit(solution)/shard_map/ppermute | solution.py:523
  552.6 11.0 %copy-start.42 = (f32[8,1920]{1,0:T(8,128)S(1)}, f32[8,1920]{1,0:T(8,128)}, u32[]{:S(2)}) copy-start(f32[8,1920]{1,0:T(8,128)} %get-tuple-element.152) | copy-start | bytes 184324
  552.6 11.0 %copy-start.41 = (f32[8,1536]{1,0:T(8,128)S(1)}, f32[8,1536]{1,0:T(8,128)}, u32[]{:S(2)}) copy-start(f32[8,1536]{1,0:T(8,128)} %get-tuple-element.151) | copy-start | bytes 147460
  552.7 35.0 %collective-permute-start.27 = (bf16[512,1920]{1,0:T(8,128)(2,1)}, bf16[512,1920]{1,0:T(8,128)(2,1)S(1)}, u32[]{:S(2)}, u32[]{:S(2)}) collective-permute-start(bf16[512,1920]{1,0:T(8,128)(2,1)} %get-tuple-element.137.refs_5_), channel_id=1, source_target_pairs={{0,8},{8,0},{1,9},{9,1},{2,10},{10,2},{3,11},{11,3},{4,12},{12,4},... | collective-permute-start | bytes 5898248 | tf_op jit(solution)/shard_map/ppermute | solution.py:517
  552.7 10.9 %copy-start.6 = (bf16[512,1920]{1,0:T(8,128)(2,1)S(1)}, bf16[512,1920]{1,0:T(8,128)(2,1)}, u32[]{:S(2)}) copy-start(bf16[512,1920]{1,0:T(8,128)(2,1)} %get-tuple-element.137.refs_5_) | copy-start | bytes 5898244
  566.4 9.0 %copy-start.38 = (f32[32,1920]{1,0:T(8,128)S(1)}, f32[32,1920]{1,0:T(8,128)}, u32[]{:S(2)}) copy-start(f32[32,1920]{1,0:T(8,128)} %get-tuple-element.138.refs_2_.refs_9_) | copy-start | bytes 737284
  571.3 10.6 %collective-permute-start.32 = (bf16[4,48,768]{2,1,0:T(8,128)(2,1)}, bf16[4,48,768]{2,1,0:T(8,128)(2,1)S(1)}, u32[]{:S(2)}, u32[]{:S(2)}) collective-permute-start(bf16[4,48,768]{2,1,0:T(8,128)(2,1)} %get-tuple-element.140), channel_id=1, source_target_pairs={{0,1},{1,0},{2,3},{3,2},{4,5},{5,4},{6,7},{7,6},{8,9},{9,8},{10,11... | collective-permute-start | bytes 884744 | tf_op jit(solution)/shard_map/ppermute | solution.py:587
  574.0 9.3 %collective-permute-start.33 = (bf16[4,48,768]{2,1,0:T(8,128)(2,1)}, bf16[4,48,768]{2,1,0:T(8,128)(2,1)S(1)}, u32[]{:S(2)}, u32[]{:S(2)}) collective-permute-start(bf16[4,48,768]{2,1,0:T(8,128)(2,1)} %get-tuple-element.142), channel_id=1, source_target_pairs={{0,16},{16,0},{1,17},{17,1},{2,18},{18,2},{3,19},{19,3},{4,20},{20... | collective-permute-start | bytes 884744 | tf_op jit(solution)/shard_map/ppermute | solution.py:587
  576.1 11.6 %copy-start.33 = (bf16[16,1920]{1,0:T(8,128)(2,1)}, bf16[16,1920]{1,0:T(8,128)(2,1)S(1)}, u32[]{:S(2)}) copy-start(bf16[16,1920]{1,0:T(8,128)(2,1)S(1)} %get-tuple-element.166.refs_7_) | copy-start | bytes 184324
  576.1 11.6 %collective-permute-start.29 = (bf16[16,1920]{1,0:T(8,128)(2,1)S(1)}, bf16[16,1920]{1,0:T(8,128)(2,1)S(1)}, u32[]{:S(2)}, u32[]{:S(2)}) collective-permute-start(bf16[16,1920]{1,0:T(8,128)(2,1)S(1)} %get-tuple-element.166.refs_7_), channel_id=1, source_target_pairs={{0,8},{8,0},{1,9},{9,1},{2,10},{10,2},{3,11},{11,3},{4,12},{12,4},... | collective-permute-start | bytes 184328 | tf_op jit(solution)/shard_map/ppermute | solution.py:517
  595.0 35.7 %collective-permute-start.35 = (bf16[384,896]{1,0:T(8,128)(2,1)}, bf16[384,896]{1,0:T(8,128)(2,1)S(1)}, u32[]{:S(2)}, u32[]{:S(2)}) collective-permute-start(bf16[384,896]{1,0:T(8,128)(2,1)} %get-tuple-element.146.refs_7_), channel_id=1, source_target_pairs={{0,1},{1,0},{2,3},{3,2},{4,5},{5,4},{6,7},{7,6},{8,9},{9,8},{10,11... | collective-permute-start | bytes 2064392 | tf_op jit(solution)/shard_map/ppermute | solution.py:587
  600.8 30.0 %collective-permute-start.34 = (bf16[384,1024]{1,0:T(8,128)(2,1)}, bf16[384,1024]{1,0:T(8,128)(2,1)S(1)}, u32[]{:S(2)}, u32[]{:S(2)}) collective-permute-start(bf16[384,1024]{1,0:T(8,128)(2,1)} %get-tuple-element.144.refs_6_), channel_id=1, source_target_pairs={{0,16},{16,0},{1,17},{17,1},{2,18},{18,2},{3,19},{19,3},{4,20},{20... | collective-permute-start | bytes 2359304 | tf_op jit(solution)/shard_map/ppermute | solution.py:587
  602.2 42.4 %all-to-all-start.3 = ((f32[4,48,1536]{2,1,0:T(8,128)}), f32[4,48,1536]{2,1,0:T(8,128)S(1)}, u32[]{:S(2)}, u32[]{:S(2)}) async-start(f32[4,48,1536]{2,1,0:T(8,128)} %shard_map.237.refs_9_), calls=%async_computation.3 | async-start | bytes 2359296 | tf_op jit(solution)/shard_map/all_to_all | solution.py:796
  631.9 9.3 %copy-start.45 = (f32[48]{0:T(128)S(1)}, f32[48]{0:T(128)}, u32[]{:S(2)}) copy-start(f32[48]{0:T(128)} %reduce_sum.74) | copy-start | bytes 580
  637.0 12.1 %collective-permute-start.37 = (bf16[4,48,896]{2,1,0:T(8,128)(2,1)}, bf16[4,48,896]{2,1,0:T(8,128)(2,1)S(1)}, u32[]{:S(2)}, u32[]{:S(2)}) collective-permute-start(bf16[4,48,896]{2,1,0:T(8,128)(2,1)} %get-tuple-element.149.refs_4_.refs_2_), channel_id=1, source_target_pairs={{0,16},{16,0},{1,17},{17,1},{2,18},{18,2},{3,19},{19,3},{4,20},{20... | collective-permute-start | bytes 1032200 | tf_op jit(solution)/shard_map/ppermute | solution.py:587
  638.4 10.7 %collective-permute-start.36 = (bf16[4,48,1024]{2,1,0:T(8,128)(2,1)}, bf16[4,48,1024]{2,1,0:T(8,128)(2,1)S(1)}, u32[]{:S(2)}, u32[]{:S(2)}) collective-permute-start(bf16[4,48,1024]{2,1,0:T(8,128)(2,1)} %get-tuple-element.148.refs_3_.refs_1_), channel_id=1, source_target_pairs={{0,1},{1,0},{2,3},{3,2},{4,5},{5,4},{6,7},{7,6},{8,9},{9,8},{10,11... | collective-permute-start | bytes 1179656 | tf_op jit(solution)/shard_map/ppermute | solution.py:587
  644.6 9.0 %copy-start.7 = (f32[4,48,1536]{2,1,0:T(8,128)}, f32[4,48,1536]{2,1,0:T(8,128)S(1)}, u32[]{:S(2)}) copy-start(f32[4,48,1536]{2,1,0:T(8,128)S(1)} %all-to-all-done.3.refs_0_) | copy-start | bytes 3538948
  644.6 12.1 %all-to-all-start.2 = ((f32[32,1,808]{2,1,0:T(1,128)}), f32[32,1,808]{2,1,0:T(1,128)S(1)}, u32[]{:S(2)}, u32[]{:S(2)}) async-start(f32[32,1,808]{2,1,0:T(1,128)} %copy.54), calls=%async_computation.2 | async-start | bytes 229376 | tf_op jit(solution)/shard_map/all_to_all | solution.py:1241
  656.7 28.3 %all-to-all-start.4 = ((bf16[4,48,1920]{2,1,0:T(8,128)(2,1)}), bf16[4,48,1920]{2,1,0:T(8,128)(2,1)S(1)}, u32[]{:S(2)}, u32[]{:S(2)}) async-start(bf16[4,48,1920]{2,1,0:T(8,128)(2,1)} %shard_map.248), calls=%async_computation.4 | async-start | bytes 1474560 | tf_op jit(solution)/shard_map/all_to_all | solution.py:796
  (41 other events, 93.0 us)
Sparse Core Ops, SparseCore 0:
  11.5 90.6 all-gather.2
  105.7 131.5 all-gather.4
